TPU v7x, 128 devices: a whole 4x4x4 slice. The times are simulated.
128 devices in a mesh: rep: 8 (over z, x_lo), tr: 16 (over y, x_hi, core).
Axes of the slice: x: 4 (x_hi: 2, x_lo: 2; x = x_hi * 2 + x_lo), y: 4, z: 4, core: 2. Of those that a mesh axis runs over, the one named last changes fastest.
Arguments:
- taps: bfloat16 [64, 96, 3, 4096], P('rep', None, None, 'tr'), may hold values from -6 to 6
- routes: int32 [64, 1], replicated, may hold values from 0 to 7; in each aligned block of 8 rows (0 to 7, 8 to 15, ...) at most 2 rows name the same one
- lengths: int32 [64], replicated, may hold values from 4 to 96, as said below
- merge_weight: bfloat16 [3, 4096, 4096], P(None, 'tr'), may hold values from -0.0546875 to 0.0546875
- norm_gain: float32 [4096], P('tr'), may hold values from 0.5 to 1.5
- head_scale: float32 [32], P('tr'), may hold values from 0.02 to 1
Outputs:
- grad: float32 [3, 4096, 4096], P(None, 'tr', 'rep')
- new_weights: bfloat16 [3, 4096, 4096], P(None, 'tr')
Inputs may be any that keep to these rules, and one draw needn't show every extreme that they name: routes[s, 0] names the trainer group of rollout s. Within each aligned block of the 8 rollouts of one replica group, no trainer group is named more than 2 times; some group is named exactly 2 times, and every trainer group is named by some rollout. `lengths`: some rollout has exactly 96 live tokens.
All inputs are finite; a program needn't handle non-finite values.
Results may differ from a plain program's by a relative error of at most 0.0034.
Values may be sent and summed in bfloat16 or wider, within the bound.
No kernel may reach another device: no remote copies, remote signals or barrier semaphores. Data moves between devices by JAX's collectives and lax.ppermute only.
A program may use at most 128 MiB of HBM per device.

v0:
```python
import jax
import jax.numpy as jnp
from jax import lax
from jax.experimental import pallas as pl
from jax.experimental.layout import Layout, with_layout_constraint
from jax.experimental.pallas import tpu as pltpu
from jax.sharding import PartitionSpec as P

epsilon = 1e-06
step_size = 0.004
SEND = 128.0
SPAN = 96
HEAD = 128
RING = 4
ORDER = (((2, 1), (1, 1), (3, 1), (1, 0)), ((3, 0), (2, 0), (0, 1), (0, 0)))

f32 = jnp.float32
bf16 = jnp.bfloat16
f16 = jnp.float16

ROWS_ROWS = (((1,), (1,)), ((), ()))
ROWS_COLS = (((1,), (0,)), ((), ()))
COLS_COLS = (((0,), (0,)), ((), ()))


def split(a):
    high = a.astype(bf16)
    return high, (a - high.astype(f32)).astype(bf16)


def product(a, b, dims):
    ka, kb = dims[0][0][0], dims[0][1][0]
    return lax.dot_general(
        jnp.concatenate([a[0], a[0], a[1]], axis=ka),
        jnp.concatenate([b[0], b[1], b[0]], axis=kb),
        dims,
        preferred_element_type=f32,
    )


def attention_kernel(lens_ref, weights_ref, scale_ref, merged_ref, square_ref, gain_ref, tap_ref, scaled_ref, cross_ref):
    slots = merged_ref.shape[0]
    heads = scale_ref.shape[0]
    first = pl.program_id(0) * slots
    place = lax.broadcasted_iota(jnp.int32, (SPAN, HEAD), 0)
    key = lax.broadcasted_iota(jnp.int32, (SPAN, HEAD), 1)
    eye = lax.broadcasted_iota(jnp.int32, (SPAN, SPAN), 0) == lax.broadcasted_iota(jnp.int32, (SPAN, SPAN), 1)
    pad = jnp.zeros((HEAD - SPAN, HEAD), f32)
    chains = [(s, h) for s in range(slots) for h in range(heads)]
    every = range(len(chains))
    width = 16 * heads * HEAD
    lens = [lens_ref[first + s] for s, _ in chains]
    weights = [weights_ref[first + s] for s, _ in chains]
    scales = [scale_ref[h] for _, h in chains]
    columns = [pl.ds(h * HEAD, HEAD) for _, h in chains]
    allowed = [(key <= place) & (key < lens[c]) for c in every]
    inverse = []
    for s in range(slots):
        across = lax.rsqrt(square_ref[s] / width + epsilon)
        inverse.append(jnp.sum(jnp.where(eye, across, 0.0), axis=1, keepdims=True))
    gains = [gain_ref[:, columns[c]] for c in every]
    start = [merged_ref[chains[c][0], :, columns[c]] * inverse[chains[c][0]] * gains[c] for c in every]
    keys = [split(jnp.concatenate([start[c], pad], axis=0)) for c in every]
    current = list(start)
    queries, shares, loss_grads = [], [], []
    for step in range(3):
        parts = [split(current[c]) for c in every]
        logits = [product(parts[c], keys[c], ROWS_ROWS) * scales[c] for c in every]
        logits = [jnp.where(allowed[c], logits[c], -1e30) for c in every]
        raised = [jnp.exp(logits[c] - jnp.max(logits[c], axis=1, keepdims=True)) for c in every]
        share = [raised[c] / jnp.sum(raised[c], axis=1, keepdims=True) for c in every]
        share_parts = [split(share[c]) for c in every]
        attended = [product(share_parts[c], keys[c], ROWS_COLS) for c in every]
        current = [current[c] + attended[c] for c in every]
        queries.append(parts)
        shares.append((share, share_parts))
        grads = []
        for c in every:
            later = pltpu.roll(tap_ref[chains[c][0], :, columns[c]].astype(f32), SPAN - (step + 1), 0)
            active = jnp.where(place + (step + 1) < lens[c], 2.0 * weights[c], 0.0)
            grads.append(active * (current[c] - later))
        loss_grads.append(grads)
    grad = loss_grads[2]
    key_grad = None
    for step in (2, 1, 0):
        share, share_parts = shares[step]
        parts = [split(grad[c]) for c in every]
        share_grad = [product(parts[c], keys[c], ROWS_ROWS) for c in every]
        inner = [jnp.sum(share_grad[c] * share[c], axis=1, keepdims=True) for c in every]
        logit_parts = [split(share[c] * (share_grad[c] - inner[c]) * scales[c]) for c in every]
        left = [tuple(jnp.concatenate(z, axis=0) for z in zip(share_parts[c], logit_parts[c])) for c in every]
        right = [tuple(jnp.concatenate(z, axis=0) for z in zip(parts[c], queries[step][c])) for c in every]
        added = [product(left[c], right[c], COLS_COLS) for c in every]
        key_grad = added if key_grad is None else [key_grad[c] + added[c] for c in every]
        grad = [grad[c] + product(logit_parts[c], keys[c], ROWS_COLS) for c in every]
        if step > 0:
            grad = [grad[c] + loss_grads[step - 1][c] for c in every]
    crossed = [None] * slots
    for c in every:
        s = chains[c][0]
        scaled = (grad[c] + key_grad[c][:SPAN]) * gains[c]
        scaled_ref[s, :, columns[c]] = scaled
        inner = jnp.sum(scaled * merged_ref[s, :, columns[c]], axis=1, keepdims=True)
        crossed[s] = inner if crossed[s] is None else crossed[s] + inner
    for s in range(slots):
        cross_ref[s] = jnp.sum(jnp.where(eye, crossed[s], 0.0), axis=0, keepdims=True)


def attention(lens, weights, scales, merged, squares, gain, taps, slots=2):
    count, span, wide = merged.shape
    scalar = pl.BlockSpec(memory_space=pltpu.SMEM)
    block = pl.BlockSpec((slots, span, wide), lambda i: (i, 0, 0))
    flat = pl.BlockSpec((slots, 1, span), lambda i: (i, 0, 0))
    return pl.pallas_call(
        attention_kernel,
        grid=(count // slots,),
        in_specs=[scalar, scalar, scalar, block, flat, pl.BlockSpec((1, wide), lambda i: (0, 0)), block],
        out_specs=[block, flat],
        out_shape=[
            jax.ShapeDtypeStruct((count, span, wide), f32),
            jax.ShapeDtypeStruct((count, 1, span), f32),
        ],
        compiler_params=pltpu.CompilerParams(vmem_limit_bytes=48 * 2**20),
        cost_estimate=pl.CostEstimate(flops=2 * 10**9, bytes_accessed=3 * 10**6, transcendentals=10**6),
    )(lens, weights, scales, merged, squares, gain, taps)


def row_major(a):
    return with_layout_constraint(a, Layout(major_to_minor=tuple(range(a.ndim))))


def buffer(shape, dtype):
    return pl.pallas_call(
        lambda out_ref: None,
        out_specs=pl.BlockSpec(memory_space=pl.ANY),
        out_shape=jax.ShapeDtypeStruct(shape, dtype),
    )()


def tr_index(y, x, core):
    return (y % RING * 2 + x % 2) * 2 + core % 2


def to_chip(value, dy, dx, dcore=0):
    pairs = [
        (tr_index(y, x, core), tr_index(y + dy, x + dx, core + dcore))
        for y in range(RING)
        for x in range(2)
        for core in range(2)
    ]
    return lax.ppermute(value, "tr", pairs)


def to_group(value, dz, dx):
    pairs = [(z * 2 + x, (z + dz) % RING * 2 + (x + dx) % 2) for z in range(RING) for x in range(2)]
    return lax.ppermute(value, "rep", pairs)


def to_sibling(value):
    return to_chip(value, 0, 0, 1)


def gather(value, send):
    got = {(0, 0): value}
    got[1, 0] = send(value, 1, 0)
    got[3, 0] = send(value, 3, 0)
    got[0, 1] = send(value, 0, 1)
    got[2, 0] = send(value, 2, 0)
    got[1, 1] = send(got[0, 1], 1, 0)
    got[3, 1] = send(got[0, 1], 3, 0)
    got[2, 1] = send(got[2, 0], 0, 1)
    return got


def gather_relayed(value, send):
    half = value.shape[0] // 2
    up, down, across = send(value, 1, 0), send(value, 3, 0), send(value, 0, 1)
    far_first = send(up[:half], 1, 0)
    far_last = send(down[half:], 3, 0)
    up_across, down_across = send(across, 1, 0), send(across, 3, 0)
    far_across = send(jnp.concatenate([far_first, far_last], axis=0), 0, 1)
    return [
        (0, 0, 0, value),
        (1, 0, 0, up),
        (3, 0, 0, down),
        (0, 1, 0, across),
        (2, 0, 0, far_first),
        (2, 0, half, far_last),
        (1, 1, 0, up_across),
        (3, 1, 0, down_across),
        (2, 1, 0, far_across),
    ]


def product_kernel(blocks_ref, rows_ref, weight_ref, out_ref):
    out_ref[0] = jnp.dot(rows_ref[...], weight_ref[...], preferred_element_type=f32)


def products(rows, weight, blocks, wide):
    count, depth = rows.shape
    number = blocks.shape[0]
    return pl.pallas_call(
        product_kernel,
        grid_spec=pltpu.PrefetchScalarGridSpec(
            num_scalar_prefetch=1,
            grid=(number,),
            in_specs=[
                pl.BlockSpec((count, depth), lambda i, blocks: (0, 0)),
                pl.BlockSpec((depth, wide), lambda i, blocks: (0, blocks[i])),
            ],
            out_specs=pl.BlockSpec((1, count, wide), lambda i, blocks: (i, 0, 0)),
        ),
        out_shape=jax.ShapeDtypeStruct((number, count, wide), f32),
        compiler_params=pltpu.CompilerParams(vmem_limit_bytes=8 * 2**20),
        cost_estimate=pl.CostEstimate(
            flops=2 * count * depth * wide * number,
            bytes_accessed=count * depth * 2 + number * wide * (count * 4 + depth * 2),
            transcendentals=0,
        ),
    )(blocks, rows, weight)


def sum_over_tr(value):
    value = value + to_sibling(value)
    value = value + to_chip(value, 0, 1)
    return value + to_chip(value, 1, 0) + to_chip(value, 2, 0) + to_chip(value, 3, 0)


def per_device(taps, routes, lengths, merge_weight, norm_gain, head_scale):
    rep = lax.axis_index("rep")
    tr = lax.axis_index("tr")
    core = tr % 2
    x_high = tr // 2 % 2
    y = tr // 4
    x_low = rep % 2
    z = rep // 2
    slots, span, tap_count, wide = taps.shape
    width_all = merge_weight.shape[2]
    flat_in = tap_count * wide
    block = width_all // lax.axis_size("rep")
    rows = row_major(taps.reshape(slots * span, flat_in))
    weight = merge_weight.reshape(flat_in, width_all)

    dest = routes[:, 0]
    target = jnp.maximum(lengths - 1, 0) + jnp.maximum(lengths - 2, 0) + jnp.maximum(lengths - 3, 0)
    own_dest = lax.dynamic_slice_in_dim(dest, rep * slots, slots)
    lens = lax.dynamic_slice_in_dim(lengths, rep * slots, slots)
    count = jnp.sum(jnp.where(own_dest[:, None] == dest[None, :], target[None, :], 0), axis=1)
    weights = 1.0 / count.astype(f32)

    along_z = [[at_z * 2 + at_x for at_z in range(RING)] for at_x in range(2)]

    def gather_taps(value):
        return row_major(lax.all_gather(value, "rep", axis=0, tiled=True, axis_index_groups=along_z))

    rows_across = row_major(to_group(rows, 0, 1))
    taps_here = gather_taps(rows)

    def sums(offsets, parity):
        blocks = jnp.stack([tr_index(y + dy, x_high + dx, parity) for dy, dx in offsets])
        return products(rows, weight, blocks.astype(jnp.int32), wide)

    crossing = [to_sibling(sums(offsets, 1 - core)) for offsets in ORDER]
    pairs_of = {}
    for offsets, other in zip(ORDER, crossing):
        own = sums(offsets, core)
        for i, offset in enumerate(offsets):
            pairs_of[offset] = (own[i], other[i])

    def chip_sum(dy, dx):
        own, other = pairs_of[dy, dx]
        return (own + other) * SEND

    def send(value, dy, dx):
        return to_chip(value.astype(f16), dy, dx)

    far_across = send(chip_sum(2, 1), 0, 1)
    up_across = send(chip_sum(1, 1), 1, 0).astype(f32)
    down_across = send(chip_sum(3, 1), 3, 0).astype(f32)
    up = send(chip_sum(1, 0), 1, 0).astype(f32)
    down = send(chip_sum(3, 0), 3, 0).astype(f32)
    far_across, rows_across = lax.optimization_barrier((far_across, rows_across))
    taps_across = gather_taps(rows_across)
    far = send(chip_sum(2, 0) + far_across.astype(f32), 2, 0).astype(f32)
    across = send(chip_sum(0, 1) + up_across + down_across, 0, 1).astype(f32)
    merged = (chip_sum(0, 0) + up + down + far + across) * (1.0 / SEND)
    merged = merged.reshape(slots, span, wide)
    squares = sum_over_tr(jnp.sum(merged * merged, axis=2))

    scaled, crossed = attention(
        lens,
        weights,
        head_scale,
        merged,
        squares.reshape(slots, 1, span),
        norm_gain.reshape(1, wide),
        taps[:, :, 2, :],
    )
    crossed = sum_over_tr(crossed.reshape(slots, span))
    inverse = lax.rsqrt(squares / width_all + epsilon)
    merged_grad = (
        scaled * inverse[:, :, None]
        - merged * (inverse * inverse * inverse * crossed / width_all)[:, :, None]
    ).astype(bf16)

    chips = lax.axis_size("tr")
    pairs = [
        (
            (at_z * 2 + at_x) * chips + tr_index(at_y, at_high, at_core),
            (at_y * 2 + at_high) * chips + tr_index(at_y + at_z, at_x, at_core),
        )
        for at_z in range(RING)
        for at_x in range(2)
        for at_y in range(RING)
        for at_high in range(2)
        for at_core in range(2)
    ]
    turned = lax.ppermute(merged_grad.reshape(slots * span, wide), ("rep", "tr"), pairs)
    own_half = gather(turned, to_chip)
    other_half = {k: to_sibling(v) for k, v in own_half.items()}

    def gradient(half):
        total = None
        same = x_low == x_high
        for a in (0, 1, 3, 2):
            straight, crossed = half[a, 0], half[a, 1]
            for taps_of, piece in (
                (taps_here, jnp.where(same, straight, crossed)),
                (taps_across, jnp.where(same, crossed, straight)),
            ):
                at_z = (y - a - z) % RING
                source = lax.dynamic_slice_in_dim(taps_of, at_z * slots * span, slots * span, 0)
                part = lax.dot_general(source, piece, COLS_COLS, preferred_element_type=f32)
                total = part if total is None else total + part
        return total

    grad = buffer((flat_in, block), f32)
    for half, parity in ((own_half, core), (other_half, 1 - core)):
        grad = lax.dynamic_update_slice_in_dim(grad, gradient(half), parity * wide, 1)
    old = lax.dynamic_slice_in_dim(weight, rep * block, block, 1)
    new_block = (old.astype(f32) - step_size * grad).astype(bf16)
    new = buffer((flat_in, width_all), bf16)
    for a, b, first, piece in gather_relayed(new_block, to_group):
        owner = (z - a) % RING * 2 + (x_low - b) % 2
        new = lax.dynamic_update_slice(new, piece, (first, owner * block))
    return grad.reshape(tap_count, wide, block), new.reshape(tap_count, wide, width_all)


def solution(mesh):
    in_specs = (P("rep", None, None, "tr"), P(), P(), P(None, "tr", None), P("tr"), P("tr"))
    out_specs = (P(None, "tr", "rep"), P(None, "tr", None))
    return jax.shard_map(
        per_device, mesh=mesh, in_specs=in_specs, out_specs=out_specs, check_vma=False
    )
```

profile of v0, /device:TPU:0, one launch (start us, length us, event | category | flops | bytes accessed | tf_op | source)
XLA Modules:
  0.0 276.6 jit_solution(8076946021968468554)
XLA Ops:
  11.2 2.8 %copy-done = bf16[3,256,4096]{2,1,0:T(8,128)(2,1)S(1)} copy-done((bf16[3,256,4096]{2,1,0:T(8,128)(2,1)S(1)}, bf16[3,256,4096]{2,1,0:T(8,128)(2,1)}, u32[]{:S(2)}) %copy-start) | copy-done | bytes 6291480
  14.0 5.5 %shard_map.81 = f32[4,768,256]{2,1,0:T(8,128)} custom-call(s32[4]{0:T(128)S(1)} %get-tuple-element.23.blocks_ref, bf16[768,768]{1,0:T(8,128)(2,1)} %bitcast.39.rows_ref, bf16[768,4096]{1,0:T(8,128)(2,1)S(1)} %bitcast.72), custom_call_target="tpu_custom_call" | custom-call | flops 1207959552 | bytes 5898240 | tf_op jit(solution)/shard_map/pallas_call | solution.py:202
  21.1 5.3 %shard_map.79 = f32[4,768,256]{2,1,0:T(8,128)} custom-call(s32[4]{0:T(128)S(1)} %get-tuple-element.22.blocks_ref, bf16[768,768]{1,0:T(8,128)(2,1)} %bitcast.39.rows_ref, bf16[768,4096]{1,0:T(8,128)(2,1)S(1)} %bitcast.75), custom_call_target="tpu_custom_call" | custom-call | flops 1207959552 | bytes 5898240 | tf_op jit(solution)/shard_map/pallas_call | solution.py:202
  26.7 2.8 %copy-done.1 = bf16[3,256,4096]{2,1,0:T(8,128)(2,1)S(1)} copy-done((bf16[3,256,4096]{2,1,0:T(8,128)(2,1)S(1)}, bf16[3,256,4096]{2,1,0:T(8,128)(2,1)}, u32[]{:S(2)}) %copy-start.1) | copy-done | bytes 6291480
  29.4 4.0 %shard_map.80 = f32[4,768,256]{2,1,0:T(8,128)S(1)} custom-call(s32[4]{0:T(128)S(1)} %pad_add_fusion.2.blocks_ref, bf16[768,768]{1,0:T(8,128)(2,1)} %bitcast.39.rows_ref, bf16[768,4096]{1,0:T(8,128)(2,1)S(1)} %bitcast.76), custom_call_target="tpu_custom_call" | custom-call | flops 1207959552 | bytes 5898240 | tf_op jit(solution)/shard_map/pallas_call | solution.py:202
  33.4 3.3 %fusion.66 = (f16[768,256]{1,0:T(8,128)(2,1)}, f16[768,256]{1,0:T(8,128)(2,1)}, f16[768,256]{1,0:T(8,128)(2,1)}, f16[768,256]{1,0:T(8,128)(2,1)}) fusion(f32[4,768,256]{2,1,0:T(8,128)} %collective-permute-done.1, f32[4,768,256]{2,1,0:T(8,128)S(1)} %shard_map.80), kind=kLoop, calls=%fused_computation.82 | loop fusion | flops 2359296 | bytes 7864320 | tf_op jit(solution)/shard_map/convert_element_type | solution.py:275
  39.5 9.1 %collective-permute-done.5 = bf16[768,768]{1,0:T(8,128)(2,1)} collective-permute-done((bf16[768,768]{1,0:T(8,128)(2,1)}, bf16[768,768]{1,0:T(8,128)(2,1)}, u32[]{:S(2)}, u32[]{:S(2)}) %collective-permute-start.5) | collective-permute-done | bytes 1179680 | tf_op jit(solution)/shard_map/ppermute | solution.py:156
  48.6 10.2 %collective-permute-done.4 = f16[768,256]{1,0:T(8,128)(2,1)S(1)} collective-permute-done((f16[768,256]{1,0:T(8,128)(2,1)}, f16[768,256]{1,0:T(8,128)(2,1)S(1)}, u32[]{:S(2)}, u32[]{:S(2)}) %collective-permute-start.4) | collective-permute-done | bytes 393248 | tf_op jit(solution)/shard_map/ppermute | solution.py:151
  58.8 3.1 %collective-permute-start.8 = (f16[768,256]{1,0:T(8,128)(2,1)}, f16[768,256]{1,0:T(8,128)(2,1)}, u32[]{:S(2)}, u32[]{:S(2)}) collective-permute-start(f16[768,256]{1,0:T(8,128)(2,1)} %get-tuple-element.17), channel_id=1, source_target_pairs={{0,12},{1,13},{2,14},{3,15},{4,0},{5,1},{6,2},{7,3},{8,4},{9,5},{1... | collective-permute-start | bytes 1179656 | tf_op jit(solution)/shard_map/ppermute | solution.py:151
  62.0 2.8 %copy-done.2 = bf16[3,256,4096]{2,1,0:T(8,128)(2,1)S(1)} copy-done((bf16[3,256,4096]{2,1,0:T(8,128)(2,1)S(1)}, bf16[3,256,4096]{2,1,0:T(8,128)(2,1)}, u32[]{:S(2)}) %copy-start.2) | copy-done | bytes 6291480
  64.8 4.0 %shard_map.78 = f32[4,768,256]{2,1,0:T(8,128)S(1)} custom-call(s32[4]{0:T(128)S(1)} %pad_add_fusion.blocks_ref, bf16[768,768]{1,0:T(8,128)(2,1)} %bitcast.39.rows_ref, bf16[768,4096]{1,0:T(8,128)(2,1)S(1)} %bitcast.77), custom_call_target="tpu_custom_call" | custom-call | flops 1207959552 | bytes 5898240 | tf_op jit(solution)/shard_map/pallas_call | solution.py:202
  68.9 3.3 %collective-permute-start.3 = (f16[768,256]{1,0:T(8,128)(2,1)S(1)}, f16[768,256]{1,0:T(8,128)(2,1)S(1)}, u32[]{:S(2)}, u32[]{:S(2)}) collective-permute-start(f16[768,256]{1,0:T(8,128)(2,1)S(1)} %fusion.67), channel_id=1, source_target_pairs={{0,12},{1,13},{2,14},{3,15},{4,0},{5,1},{6,2},{7,3},{8,4},{9,5},{1... | collective-permute-start | bytes 1179656 | tf_op jit(solution)/shard_map/ppermute | solution.py:151
  77.6 10.8 %collective-permute-done.3 = f16[768,256]{1,0:T(8,128)(2,1)S(1)} collective-permute-done((f16[768,256]{1,0:T(8,128)(2,1)S(1)}, f16[768,256]{1,0:T(8,128)(2,1)S(1)}, u32[]{:S(2)}, u32[]{:S(2)}) %collective-permute-start.3) | collective-permute-done | bytes 393248 | tf_op jit(solution)/shard_map/ppermute | solution.py:151
  88.4 3.4 %collective-permute-done.2 = f16[768,256]{1,0:T(8,128)(2,1)S(1)} collective-permute-done((f16[768,256]{1,0:T(8,128)(2,1)S(1)}, f16[768,256]{1,0:T(8,128)(2,1)S(1)}, u32[]{:S(2)}, u32[]{:S(2)}) %collective-permute-start.2) | collective-permute-done | bytes 393248 | tf_op jit(solution)/shard_map/ppermute | solution.py:151
  95.7 4.0 %collective-permute-done.11 = f32[8,96]{1,0:T(8,128)S(1)} collective-permute-done((f32[8,96]{1,0:T(8,128)S(1)}, f32[8,96]{1,0:T(8,128)S(1)}, u32[]{:S(2)}, u32[]{:S(2)}) %collective-permute-start.11) | collective-permute-done | bytes 3104 | tf_op jit(solution)/shard_map/ppermute | solution.py:151
  106.1 15.8 %shard_map.82 = (f32[8,96,256]{2,1,0:T(8,128)S(1)}, f32[8,1,96]{2,1,0:T(1,128)S(1)}) custom-call(s32[8]{0:T(128)S(1)} %dynamic_slice.42.lens_ref, f32[8]{0:T(128)S(1)} %convert_divide_fusion.weights_ref, f32[2]{0:T(128)S(1)} %copy-done.4, f32[8,96,256]{2,1,0:T(8,128)S(1)} %bitcast.78, f32[8,1,96]{2,1,0:T(1,128)S(1)} %bitcast.80, f32[1,256]{1,0:T(1,128)S(1)} %bitcast.83, ...), custom_call_target="tpu_custom_call" | custom-call | flops 2000000000 | bytes 3000000 | tf_op jit(solution)/shard_map/pallas_call | solution.py:114
  124.0 4.2 %collective-permute-done.16 = f32[8,96]{1,0:T(8,128)S(1)} collective-permute-done((f32[8,96]{1,0:T(8,128)S(1)}, f32[8,96]{1,0:T(8,128)S(1)}, u32[]{:S(2)}, u32[]{:S(2)}) %collective-permute-start.16) | collective-permute-done | bytes 3104 | tf_op jit(solution)/shard_map/ppermute | solution.py:151
  131.8 3.5 %collective-permute-done.18 = f32[8,96]{1,0:T(8,128)S(1)} collective-permute-done((f32[8,96]{1,0:T(8,128)S(1)}, f32[8,96]{1,0:T(8,128)S(1)}, u32[]{:S(2)}, u32[]{:S(2)}) %collective-permute-start.18) | collective-permute-done | bytes 3104 | tf_op jit(solution)/shard_map/ppermute | solution.py:151
  137.0 14.8 %collective-permute-start.26 = (bf16[768,256]{1,0:T(8,128)(2,1)S(1)}, bf16[768,256]{1,0:T(8,128)(2,1)S(1)}, u32[]{:S(2)}, u32[]{:S(2)}) collective-permute-start(bf16[768,256]{1,0:T(8,128)(2,1)S(1)} %collective-permute-done.20), channel_id=1, source_target_pairs={{0,8},{1,9},{2,10},{3,11},{4,12},{5,13},{6,14},{7,15},{8,0},{9,1},... | collective-permute-start | bytes 1179656 | tf_op jit(solution)/shard_map/ppermute | solution.py:151
  153.6 3.9 %collective-permute-done.26 = bf16[768,256]{1,0:T(8,128)(2,1)S(1)} collective-permute-done((bf16[768,256]{1,0:T(8,128)(2,1)S(1)}, bf16[768,256]{1,0:T(8,128)(2,1)S(1)}, u32[]{:S(2)}, u32[]{:S(2)}) %collective-permute-start.26) | collective-permute-done | bytes 393248 | tf_op jit(solution)/shard_map/ppermute | solution.py:151
  159.4 4.2 %collective-permute-start.24 = (bf16[768,256]{1,0:T(8,128)(2,1)S(1)}, bf16[768,256]{1,0:T(8,128)(2,1)}, u32[]{:S(2)}, u32[]{:S(2)}) collective-permute-start(bf16[768,256]{1,0:T(8,128)(2,1)S(1)} %collective-permute-done.20), channel_id=1, source_target_pairs={{0,12},{1,13},{2,14},{3,15},{4,0},{5,1},{6,2},{7,3},{8,4},{9,5},{1... | collective-permute-start | bytes 1179656 | tf_op jit(solution)/shard_map/ppermute | solution.py:151
  172.1 3.0 %collective-permute-done.25 = bf16[768,256]{1,0:T(8,128)(2,1)} collective-permute-done((bf16[768,256]{1,0:T(8,128)(2,1)S(1)}, bf16[768,256]{1,0:T(8,128)(2,1)}, u32[]{:S(2)}, u32[]{:S(2)}) %collective-permute-start.25) | collective-permute-done | bytes 393248 | tf_op jit(solution)/shard_map/ppermute | solution.py:151
  175.6 2.8 %fusion.26 = f32[768,256]{1,0:T(8,128)} fusion(bf16[3072,768]{1,0:T(8,128)(2,1)} %all-gather.3.cloned.1.call-done, s32[]{:T(128)S(6)} %select_n.385, bf16[768,256]{1,0:T(8,128)(2,1)} %collective-permute-done.24, bf16[768,256]{1,0:T(8,128)(2,1)} %collective-permute-done.25, pred[]{:T(512)S(6)} %eq.107), kind=kOutput, calls=%fused_computation.31 | convolution fusion | flops 302186496 | bytes 2752517 | tf_op jit(solution)/shard_map/dot_general | solution.py:333
  181.2 5.1 %collective-permute-done.23 = bf16[768,256]{1,0:T(8,128)(2,1)} collective-permute-done((bf16[768,256]{1,0:T(8,128)(2,1)S(1)}, bf16[768,256]{1,0:T(8,128)(2,1)}, u32[]{:S(2)}, u32[]{:S(2)}) %collective-permute-start.23) | collective-permute-done | bytes 393248 | tf_op jit(solution)/shard_map/ppermute | solution.py:151
  204.9 2.9 %constant_dynamic-update-slice_fusion.7 = (bf16[768,4096]{1,0:T(8,128)(2,1)}, bf16[768,512]{1,0:T(8,128)(2,1)S(1)}) fusion(bf16[768,4096]{1,0:T(8,128)(2,1)} %shard_map.83, s32[]{:T(128)S(6)} %select_n.405, f32[768,512]{1,0:T(8,128)S(1)} %fusion.5, bf16[768,4096]{1,0:T(8,128)(2,1)} %bitcast.71, s32[]{:T(128)S(6)} %select_n.402), kind=kLoop, calls=%fused_computation.134 | loop fusion | flops 1572864 | bytes 3932168 | tf_op jit(solution)/shard_map/dynamic_update_slice | solution.py:345
  207.8 4.9 %collective-permute-start.36 = (bf16[768,512]{1,0:T(8,128)(2,1)S(1)}, bf16[768,512]{1,0:T(8,128)(2,1)S(1)}, u32[]{:S(2)}, u32[]{:S(2)}) collective-permute-start(bf16[768,512]{1,0:T(8,128)(2,1)S(1)} %get-tuple-element.11), channel_id=1, source_target_pairs={{0,32},{16,48},{32,64},{48,80},{64,96},{80,112},{96,0},{112,16},{1... | collective-permute-start | bytes 2359304 | tf_op jit(solution)/shard_map/ppermute | solution.py:156
  212.7 4.8 %collective-permute-start.37 = (bf16[768,512]{1,0:T(8,128)(2,1)S(1)}, bf16[768,512]{1,0:T(8,128)(2,1)S(1)}, u32[]{:S(2)}, u32[]{:S(2)}) collective-permute-start(bf16[768,512]{1,0:T(8,128)(2,1)S(1)} %get-tuple-element.11), channel_id=1, source_target_pairs={{0,96},{16,112},{32,0},{48,16},{64,32},{80,48},{96,64},{112,80},{1... | collective-permute-start | bytes 2359304 | tf_op jit(solution)/shard_map/ppermute | solution.py:156
  217.5 18.2 %collective-permute-done.36 = bf16[768,512]{1,0:T(8,128)(2,1)S(1)} collective-permute-done((bf16[768,512]{1,0:T(8,128)(2,1)S(1)}, bf16[768,512]{1,0:T(8,128)(2,1)S(1)}, u32[]{:S(2)}, u32[]{:S(2)}) %collective-permute-start.36) | collective-permute-done | bytes 786464 | tf_op jit(solution)/shard_map/ppermute | solution.py:156
  237.3 3.2 %collective-permute-start.40 = (bf16[384,512]{1,0:T(8,128)(2,1)}, bf16[384,512]{1,0:T(8,128)(2,1)}, u32[]{:S(2)}, u32[]{:S(2)}) collective-permute-start(bf16[384,512]{1,0:T(8,128)(2,1)} %slice.93), channel_id=1, source_target_pairs={{0,96},{16,112},{32,0},{48,16},{64,32},{80,48},{96,64},{112,80},{1... | collective-permute-start | bytes 1179656 | tf_op jit(solution)/shard_map/ppermute | solution.py:156
  240.5 3.2 %collective-permute-start.42 = (bf16[768,512]{1,0:T(8,128)(2,1)}, bf16[768,512]{1,0:T(8,128)(2,1)S(1)}, u32[]{:S(2)}, u32[]{:S(2)}) collective-permute-start(bf16[768,512]{1,0:T(8,128)(2,1)} %collective-permute-done.38), channel_id=1, source_target_pairs={{0,96},{16,112},{32,0},{48,16},{64,32},{80,48},{96,64},{112,80},{1... | collective-permute-start | bytes 2359304 | tf_op jit(solution)/shard_map/ppermute | solution.py:156
  243.7 6.2 %collective-permute-done.39 = bf16[384,512]{1,0:T(8,128)(2,1)S(1)} collective-permute-done((bf16[384,512]{1,0:T(8,128)(2,1)}, bf16[384,512]{1,0:T(8,128)(2,1)S(1)}, u32[]{:S(2)}, u32[]{:S(2)}) %collective-permute-start.39) | collective-permute-done | bytes 393248 | tf_op jit(solution)/shard_map/ppermute | solution.py:156
  258.0 7.8 %collective-permute-done.41 = bf16[768,512]{1,0:T(8,128)(2,1)} collective-permute-done((bf16[768,512]{1,0:T(8,128)(2,1)}, bf16[768,512]{1,0:T(8,128)(2,1)}, u32[]{:S(2)}, u32[]{:S(2)}) %collective-permute-start.41) | collective-permute-done | bytes 786464 | tf_op jit(solution)/shard_map/ppermute | solution.py:156
  (176 shorter events, 78.9 us)
Async XLA Ops:
  7.2 162.4 %all-gather.3.cloned.1.call-start = ((), (), s32[]{:S(2)}) async-start(), calls=%async_computation | async-start | bytes 5898240 | tf_op jit(solution)/shard_map/all_gather | solution.py:254
  10.9 178.3 %all-gather.5.cloned.1.call-start = ((), (), s32[]{:S(2)}) async-start(), calls=%async_computation.1 | async-start | bytes 5898240 | tf_op jit(solution)/shard_map/all_gather | solution.py:254
  19.5 13.9 %collective-permute-start.1 = (f32[4,768,256]{2,1,0:T(8,128)}, f32[4,768,256]{2,1,0:T(8,128)}, u32[]{:S(2)}, u32[]{:S(2)}) collective-permute-start(f32[4,768,256]{2,1,0:T(8,128)} %shard_map.81), channel_id=1, source_target_pairs={{0,1},{1,0},{2,3},{3,2},{4,5},{5,4},{6,7},{7,6},{8,9},{9,8},{10,11... | collective-permute-start | bytes 9437192 | tf_op jit(solution)/shard_map/ppermute | solution.py:151
  19.5 29.1 %collective-permute-start.5 = (bf16[768,768]{1,0:T(8,128)(2,1)}, bf16[768,768]{1,0:T(8,128)(2,1)}, u32[]{:S(2)}, u32[]{:S(2)}) collective-permute-start(bf16[768,768]{1,0:T(8,128)(2,1)} %bitcast.39.rows_ref), channel_id=1, source_target_pairs={{0,16},{16,0},{32,48},{48,32},{64,80},{80,64},{96,112},{112,96},{1... | collective-permute-start | bytes 3538952 | tf_op jit(solution)/shard_map/ppermute | solution.py:156
  26.4 42.4 %collective-permute-start = (f32[4,768,256]{2,1,0:T(8,128)}, f32[4,768,256]{2,1,0:T(8,128)S(1)}, u32[]{:S(2)}, u32[]{:S(2)}) collective-permute-start(f32[4,768,256]{2,1,0:T(8,128)} %shard_map.79), channel_id=1, source_target_pairs={{0,1},{1,0},{2,3},{3,2},{4,5},{5,4},{6,7},{7,6},{8,9},{9,8},{10,11... | collective-permute-start | bytes 9437192 | tf_op jit(solution)/shard_map/ppermute | solution.py:151
  36.8 22.0 %collective-permute-start.4 = (f16[768,256]{1,0:T(8,128)(2,1)}, f16[768,256]{1,0:T(8,128)(2,1)S(1)}, u32[]{:S(2)}, u32[]{:S(2)}) collective-permute-start(f16[768,256]{1,0:T(8,128)(2,1)} %get-tuple-element.19), channel_id=1, source_target_pairs={{0,2},{1,3},{2,0},{3,1},{4,6},{5,7},{6,4},{7,5},{8,10},{9,11},{10,... | collective-permute-start | bytes 1179656 | tf_op jit(solution)/shard_map/ppermute | solution.py:151
  58.8 13.4 %collective-permute-start.8 = (f16[768,256]{1,0:T(8,128)(2,1)}, f16[768,256]{1,0:T(8,128)(2,1)}, u32[]{:S(2)}, u32[]{:S(2)}) collective-permute-start(f16[768,256]{1,0:T(8,128)(2,1)} %get-tuple-element.17), channel_id=1, source_target_pairs={{0,12},{1,13},{2,14},{3,15},{4,0},{5,1},{6,2},{7,3},{8,4},{9,5},{1... | collective-permute-start | bytes 1179656 | tf_op jit(solution)/shard_map/ppermute | solution.py:151
  61.9 12.0 %collective-permute-start.7 = (f16[768,256]{1,0:T(8,128)(2,1)}, f16[768,256]{1,0:T(8,128)(2,1)}, u32[]{:S(2)}, u32[]{:S(2)}) collective-permute-start(f16[768,256]{1,0:T(8,128)(2,1)} %get-tuple-element.18), channel_id=1, source_target_pairs={{0,4},{1,5},{2,6},{3,7},{4,8},{5,9},{6,10},{7,11},{8,12},{9,13},{1... | collective-permute-start | bytes 1179656 | tf_op jit(solution)/shard_map/ppermute | solution.py:151
  68.9 19.4 %collective-permute-start.3 = (f16[768,256]{1,0:T(8,128)(2,1)S(1)}, f16[768,256]{1,0:T(8,128)(2,1)S(1)}, u32[]{:S(2)}, u32[]{:S(2)}) collective-permute-start(f16[768,256]{1,0:T(8,128)(2,1)S(1)} %fusion.67), channel_id=1, source_target_pairs={{0,12},{1,13},{2,14},{3,15},{4,0},{5,1},{6,2},{7,3},{8,4},{9,5},{1... | collective-permute-start | bytes 1179656 | tf_op jit(solution)/shard_map/ppermute | solution.py:151
  72.3 19.5 %collective-permute-start.2 = (f16[768,256]{1,0:T(8,128)(2,1)S(1)}, f16[768,256]{1,0:T(8,128)(2,1)S(1)}, u32[]{:S(2)}, u32[]{:S(2)}) collective-permute-start(f16[768,256]{1,0:T(8,128)(2,1)S(1)} %copy-done.11), channel_id=1, source_target_pairs={{0,4},{1,5},{2,6},{3,7},{4,8},{5,9},{6,10},{7,11},{8,12},{9,13},{1... | collective-permute-start | bytes 1179656 | tf_op jit(solution)/shard_map/ppermute | solution.py:151
  75.5 16.3 %collective-permute-start.9 = (f16[768,256]{1,0:T(8,128)(2,1)S(1)}, f16[768,256]{1,0:T(8,128)(2,1)S(1)}, u32[]{:S(2)}, u32[]{:S(2)}) collective-permute-start(f16[768,256]{1,0:T(8,128)(2,1)S(1)} %get-tuple-element.21), channel_id=1, source_target_pairs={{0,2},{1,3},{2,0},{3,1},{4,6},{5,7},{6,4},{7,5},{8,10},{9,11},{10,... | collective-permute-start | bytes 1179656 | tf_op jit(solution)/shard_map/ppermute | solution.py:151
  76.5 15.3 %collective-permute-start.6 = (f16[768,256]{1,0:T(8,128)(2,1)S(1)}, f16[768,256]{1,0:T(8,128)(2,1)S(1)}, u32[]{:S(2)}, u32[]{:S(2)}) collective-permute-start(f16[768,256]{1,0:T(8,128)(2,1)S(1)} %get-tuple-element.20), channel_id=1, source_target_pairs={{0,8},{1,9},{2,10},{3,11},{4,12},{5,13},{6,14},{7,15},{8,0},{9,1},... | collective-permute-start | bytes 1179656 | tf_op jit(solution)/shard_map/ppermute | solution.py:151
  137.0 20.6 %collective-permute-start.26 = (bf16[768,256]{1,0:T(8,128)(2,1)S(1)}, bf16[768,256]{1,0:T(8,128)(2,1)S(1)}, u32[]{:S(2)}, u32[]{:S(2)}) collective-permute-start(bf16[768,256]{1,0:T(8,128)(2,1)S(1)} %collective-permute-done.20), channel_id=1, source_target_pairs={{0,8},{1,9},{2,10},{3,11},{4,12},{5,13},{6,14},{7,15},{8,0},{9,1},... | collective-permute-start | bytes 1179656 | tf_op jit(solution)/shard_map/ppermute | solution.py:151
  151.8 13.2 %collective-permute-start.21 = (bf16[768,256]{1,0:T(8,128)(2,1)S(1)}, bf16[768,256]{1,0:T(8,128)(2,1)S(1)}, u32[]{:S(2)}, u32[]{:S(2)}) collective-permute-start(bf16[768,256]{1,0:T(8,128)(2,1)S(1)} %collective-permute-done.20), channel_id=1, source_target_pairs={{0,2},{1,3},{2,0},{3,1},{4,6},{5,7},{6,4},{7,5},{8,10},{9,11},{10,... | collective-permute-start | bytes 1179656 | tf_op jit(solution)/shard_map/ppermute | solution.py:151
  157.6 12.0 %collective-permute-start.27 = (bf16[768,256]{1,0:T(8,128)(2,1)S(1)}, bf16[768,256]{1,0:T(8,128)(2,1)S(1)}, u32[]{:S(2)}, u32[]{:S(2)}) collective-permute-start(bf16[768,256]{1,0:T(8,128)(2,1)S(1)} %collective-permute-done.26), channel_id=1, source_target_pairs={{0,2},{1,3},{2,0},{3,1},{4,6},{5,7},{6,4},{7,5},{8,10},{9,11},{10,... | collective-permute-start | bytes 1179656 | tf_op jit(solution)/shard_map/ppermute | solution.py:151
  159.4 12.1 %collective-permute-start.24 = (bf16[768,256]{1,0:T(8,128)(2,1)S(1)}, bf16[768,256]{1,0:T(8,128)(2,1)}, u32[]{:S(2)}, u32[]{:S(2)}) collective-permute-start(bf16[768,256]{1,0:T(8,128)(2,1)S(1)} %collective-permute-done.20), channel_id=1, source_target_pairs={{0,12},{1,13},{2,14},{3,15},{4,0},{5,1},{6,2},{7,3},{8,4},{9,5},{1... | collective-permute-start | bytes 1179656 | tf_op jit(solution)/shard_map/ppermute | solution.py:151
  165.1 15.7 %collective-permute-start.22 = (bf16[768,256]{1,0:T(8,128)(2,1)S(1)}, bf16[768,256]{1,0:T(8,128)(2,1)S(1)}, u32[]{:S(2)}, u32[]{:S(2)}) collective-permute-start(bf16[768,256]{1,0:T(8,128)(2,1)S(1)} %collective-permute-done.20), channel_id=1, source_target_pairs={{0,4},{1,5},{2,6},{3,7},{4,8},{5,9},{6,10},{7,11},{8,12},{9,13},{1... | collective-permute-start | bytes 1179656 | tf_op jit(solution)/shard_map/ppermute | solution.py:151
  171.5 14.8 %collective-permute-start.23 = (bf16[768,256]{1,0:T(8,128)(2,1)S(1)}, bf16[768,256]{1,0:T(8,128)(2,1)}, u32[]{:S(2)}, u32[]{:S(2)}) collective-permute-start(bf16[768,256]{1,0:T(8,128)(2,1)S(1)} %collective-permute-done.21), channel_id=1, source_target_pairs={{0,4},{1,5},{2,6},{3,7},{4,8},{5,9},{6,10},{7,11},{8,12},{9,13},{1... | collective-permute-start | bytes 1179656 | tf_op jit(solution)/shard_map/ppermute | solution.py:151
  175.1 11.3 %collective-permute-start.32 = (bf16[768,256]{1,0:T(8,128)(2,1)}, bf16[768,256]{1,0:T(8,128)(2,1)S(1)}, u32[]{:S(2)}, u32[]{:S(2)}) collective-permute-start(bf16[768,256]{1,0:T(8,128)(2,1)} %collective-permute-done.24), channel_id=1, source_target_pairs={{0,1},{1,0},{2,3},{3,2},{4,5},{5,4},{6,7},{7,6},{8,9},{9,8},{10,11... | collective-permute-start | bytes 1179656 | tf_op jit(solution)/shard_map/ppermute | solution.py:151
  175.1 11.8 %collective-permute-start.33 = (bf16[768,256]{1,0:T(8,128)(2,1)}, bf16[768,256]{1,0:T(8,128)(2,1)S(1)}, u32[]{:S(2)}, u32[]{:S(2)}) collective-permute-start(bf16[768,256]{1,0:T(8,128)(2,1)} %collective-permute-done.25), channel_id=1, source_target_pairs={{0,1},{1,0},{2,3},{3,2},{4,5},{5,4},{6,7},{7,6},{8,9},{9,8},{10,11... | collective-permute-start | bytes 1179656 | tf_op jit(solution)/shard_map/ppermute | solution.py:151
  179.1 18.1 %collective-permute-start.28 = (bf16[768,256]{1,0:T(8,128)(2,1)S(1)}, bf16[768,256]{1,0:T(8,128)(2,1)}, u32[]{:S(2)}, u32[]{:S(2)}) collective-permute-start(bf16[768,256]{1,0:T(8,128)(2,1)S(1)} %collective-permute-done.20), channel_id=1, source_target_pairs={{0,1},{1,0},{2,3},{3,2},{4,5},{5,4},{6,7},{7,6},{8,9},{9,8},{10,11... | collective-permute-start | bytes 1179656 | tf_op jit(solution)/shard_map/ppermute | solution.py:151
  180.8 16.5 %collective-permute-start.29 = (bf16[768,256]{1,0:T(8,128)(2,1)S(1)}, bf16[768,256]{1,0:T(8,128)(2,1)}, u32[]{:S(2)}, u32[]{:S(2)}) collective-permute-start(bf16[768,256]{1,0:T(8,128)(2,1)S(1)} %collective-permute-done.21), channel_id=1, source_target_pairs={{0,1},{1,0},{2,3},{3,2},{4,5},{5,4},{6,7},{7,6},{8,9},{9,8},{10,11... | collective-permute-start | bytes 1179656 | tf_op jit(solution)/shard_map/ppermute | solution.py:151
  186.3 14.2 %collective-permute-start.30 = (bf16[768,256]{1,0:T(8,128)(2,1)S(1)}, bf16[768,256]{1,0:T(8,128)(2,1)}, u32[]{:S(2)}, u32[]{:S(2)}) collective-permute-start(bf16[768,256]{1,0:T(8,128)(2,1)S(1)} %collective-permute-done.22), channel_id=1, source_target_pairs={{0,1},{1,0},{2,3},{3,2},{4,5},{5,4},{6,7},{7,6},{8,9},{9,8},{10,11... | collective-permute-start | bytes 1179656 | tf_op jit(solution)/shard_map/ppermute | solution.py:151
  186.3 14.2 %collective-permute-start.31 = (bf16[768,256]{1,0:T(8,128)(2,1)}, bf16[768,256]{1,0:T(8,128)(2,1)}, u32[]{:S(2)}, u32[]{:S(2)}) collective-permute-start(bf16[768,256]{1,0:T(8,128)(2,1)} %collective-permute-done.23), channel_id=1, source_target_pairs={{0,1},{1,0},{2,3},{3,2},{4,5},{5,4},{6,7},{7,6},{8,9},{9,8},{10,11... | collective-permute-start | bytes 1179656 | tf_op jit(solution)/shard_map/ppermute | solution.py:151
  207.8 27.9 %collective-permute-start.36 = (bf16[768,512]{1,0:T(8,128)(2,1)S(1)}, bf16[768,512]{1,0:T(8,128)(2,1)S(1)}, u32[]{:S(2)}, u32[]{:S(2)}) collective-permute-start(bf16[768,512]{1,0:T(8,128)(2,1)S(1)} %get-tuple-element.11), channel_id=1, source_target_pairs={{0,32},{16,48},{32,64},{48,80},{64,96},{80,112},{96,0},{112,16},{1... | collective-permute-start | bytes 2359304 | tf_op jit(solution)/shard_map/ppermute | solution.py:156
  212.7 23.8 %collective-permute-start.37 = (bf16[768,512]{1,0:T(8,128)(2,1)S(1)}, bf16[768,512]{1,0:T(8,128)(2,1)S(1)}, u32[]{:S(2)}, u32[]{:S(2)}) collective-permute-start(bf16[768,512]{1,0:T(8,128)(2,1)S(1)} %get-tuple-element.11), channel_id=1, source_target_pairs={{0,96},{16,112},{32,0},{48,16},{64,32},{80,48},{96,64},{112,80},{1... | collective-permute-start | bytes 2359304 | tf_op jit(solution)/shard_map/ppermute | solution.py:156
  217.5 23.0 %collective-permute-start.38 = (bf16[768,512]{1,0:T(8,128)(2,1)S(1)}, bf16[768,512]{1,0:T(8,128)(2,1)}, u32[]{:S(2)}, u32[]{:S(2)}) collective-permute-start(bf16[768,512]{1,0:T(8,128)(2,1)S(1)} %get-tuple-element.11), channel_id=1, source_target_pairs={{0,16},{16,0},{32,48},{48,32},{64,80},{80,64},{96,112},{112,96},{1... | collective-permute-start | bytes 2359304 | tf_op jit(solution)/shard_map/ppermute | solution.py:156
  236.5 13.4 %collective-permute-start.39 = (bf16[384,512]{1,0:T(8,128)(2,1)}, bf16[384,512]{1,0:T(8,128)(2,1)S(1)}, u32[]{:S(2)}, u32[]{:S(2)}) collective-permute-start(bf16[384,512]{1,0:T(8,128)(2,1)} %slice.92), channel_id=1, source_target_pairs={{0,32},{16,48},{32,64},{48,80},{64,96},{80,112},{96,0},{112,16},{1... | collective-permute-start | bytes 1179656 | tf_op jit(solution)/shard_map/ppermute | solution.py:156
  237.3 13.1 %collective-permute-start.40 = (bf16[384,512]{1,0:T(8,128)(2,1)}, bf16[384,512]{1,0:T(8,128)(2,1)}, u32[]{:S(2)}, u32[]{:S(2)}) collective-permute-start(bf16[384,512]{1,0:T(8,128)(2,1)} %slice.93), channel_id=1, source_target_pairs={{0,96},{16,112},{32,0},{48,16},{64,32},{80,48},{96,64},{112,80},{1... | collective-permute-start | bytes 1179656 | tf_op jit(solution)/shard_map/ppermute | solution.py:156
  240.5 25.3 %collective-permute-start.41 = (bf16[768,512]{1,0:T(8,128)(2,1)}, bf16[768,512]{1,0:T(8,128)(2,1)}, u32[]{:S(2)}, u32[]{:S(2)}) collective-permute-start(bf16[768,512]{1,0:T(8,128)(2,1)} %collective-permute-done.38), channel_id=1, source_target_pairs={{0,32},{16,48},{32,64},{48,80},{64,96},{80,112},{96,0},{112,16},{1... | collective-permute-start | bytes 2359304 | tf_op jit(solution)/shard_map/ppermute | solution.py:156
  240.5 27.4 %collective-permute-start.42 = (bf16[768,512]{1,0:T(8,128)(2,1)}, bf16[768,512]{1,0:T(8,128)(2,1)S(1)}, u32[]{:S(2)}, u32[]{:S(2)}) collective-permute-start(bf16[768,512]{1,0:T(8,128)(2,1)} %collective-permute-done.38), channel_id=1, source_target_pairs={{0,96},{16,112},{32,0},{48,16},{64,32},{80,48},{96,64},{112,80},{1... | collective-permute-start | bytes 2359304 | tf_op jit(solution)/shard_map/ppermute | solution.py:156
  251.4 17.4 %collective-permute-start.43 = (bf16[768,512]{1,0:T(8,128)(2,1)S(1)}, bf16[768,512]{1,0:T(8,128)(2,1)S(1)}, u32[]{:S(2)}, u32[]{:S(2)}) collective-permute-start(bf16[768,512]{1,0:T(8,128)(2,1)S(1)} %pad_maximum_fusion), channel_id=1, source_target_pairs={{0,16},{16,0},{32,48},{48,32},{64,80},{80,64},{96,112},{112,96},{1... | collective-permute-start | bytes 2359304 | tf_op jit(solution)/shard_map/ppermute | solution.py:156
  (41 other events, 289.6 us)
Sparse Core Ops, SparseCore 0:
  11.0 55.3 all-gather.2
  68.0 53.1 all-gather.4
where the time goes:
time: 278 us; the launch traced here: 277 us
  waiting for transfers between devices  103 us (37%)
  starting transfers between devices  62.6 us (23%)
  Pallas kernels  34.5 us (12%)
  local copies, waits for them, and re-layouts  27.6 us (10%)
  matrix products  22.5 us (8%)
  between operations  14.8 us (5%)
  other arithmetic  11.3 us (4%)
    ppermute x34, waiting for transfers between devices, to_chip(): return lax.ppermute(value, 'tr', pairs)  61.5 us
    ppermute x34, starting transfers between devices, to_chip(): return lax.ppermute(value, 'tr', pairs)  44 us
    ppermute x9, waiting for transfers between devices, to_group(): return lax.ppermute(value, 'rep', pairs)  41.7 us
    dot_general x16, matrix products, gradient(): part = lax.dot_general(source, piece, COLS_COLS, preferred_element_type=f32)  22.5 us
    pallas_call x4, Pallas kernels, products(): pl.pallas_call(product_kernel, grid_spec=pltpu.PrefetchScalarGridSpec(num...  18.7 us
    ppermute x9, starting transfers between devices, to_group(): return lax.ppermute(value, 'rep', pairs)  17.9 us
    pallas_call x1, Pallas kernels, attention(): pl.pallas_call(attention_kernel, grid=(count // slots,), in_specs=[scalar...  15.8 us
    unnamed x55, local copies, waits for them, and re-layouts  12.1 us
  transfers between devices with their start and end apart: 46, of which 24 were waited for; matrix products, arithmetic and copies ran while one was open for 14% of the time, Pallas kernels for 12%

commit v1 on v0

--- a/solution.py
+++ b/solution.py
@@ -12,7 +12,7 @@
 SPAN = 96
 HEAD = 128
 RING = 4
-ORDER = (((2, 1), (1, 1), (3, 1), (1, 0)), ((3, 0), (2, 0), (0, 1), (0, 0)))
+ORDER = (((2, 1), (1, 1), (3, 1)), ((1, 0), (3, 0), (2, 0), (0, 1), (0, 0)))
 
 f32 = jnp.float32
 bf16 = jnp.bfloat16
@@ -120,7 +120,7 @@
             jax.ShapeDtypeStruct((count, span, wide), f32),
             jax.ShapeDtypeStruct((count, 1, span), f32),
         ],
-        compiler_params=pltpu.CompilerParams(vmem_limit_bytes=48 * 2**20),
+        compiler_params=pltpu.CompilerParams(vmem_limit_bytes=16 * 2**20),
         cost_estimate=pl.CostEstimate(flops=2 * 10**9, bytes_accessed=3 * 10**6, transcendentals=10**6),
     )(lens, weights, scales, merged, squares, gain, taps)
 
@@ -253,39 +253,39 @@
     def gather_taps(value):
         return row_major(lax.all_gather(value, "rep", axis=0, tiled=True, axis_index_groups=along_z))
 
-    rows_across = row_major(to_group(rows, 0, 1))
     taps_here = gather_taps(rows)
 
-    def sums(offsets, parity):
+    def sums(rows, offsets, parity):
         blocks = jnp.stack([tr_index(y + dy, x_high + dx, parity) for dy, dx in offsets])
         return products(rows, weight, blocks.astype(jnp.int32), wide)
 
-    crossing = [to_sibling(sums(offsets, 1 - core)) for offsets in ORDER]
-    pairs_of = {}
-    for offsets, other in zip(ORDER, crossing):
-        own = sums(offsets, core)
-        for i, offset in enumerate(offsets):
-            pairs_of[offset] = (own[i], other[i])
-
-    def chip_sum(dy, dx):
-        own, other = pairs_of[dy, dx]
-        return (own + other) * SEND
+    def chip_sums(rows, offsets):
+        other = to_sibling(sums(rows, offsets, 1 - core))
+        own = sums(rows, offsets, core)
+        return {offset: (own[i] + other[i]) * SEND for i, offset in enumerate(offsets)}
 
     def send(value, dy, dx):
         return to_chip(value.astype(f16), dy, dx)
 
-    far_across = send(chip_sum(2, 1), 0, 1)
-    up_across = send(chip_sum(1, 1), 1, 0).astype(f32)
-    down_across = send(chip_sum(3, 1), 3, 0).astype(f32)
-    up = send(chip_sum(1, 0), 1, 0).astype(f32)
-    down = send(chip_sum(3, 0), 3, 0).astype(f32)
-    far_across, rows_across = lax.optimization_barrier((far_across, rows_across))
-    taps_across = gather_taps(rows_across)
-    far = send(chip_sum(2, 0) + far_across.astype(f32), 2, 0).astype(f32)
-    across = send(chip_sum(0, 1) + up_across + down_across, 0, 1).astype(f32)
-    merged = (chip_sum(0, 0) + up + down + far + across) * (1.0 / SEND)
+    first = chip_sums(rows, ORDER[0])
+    far_across, up_across, down_across, rows_now = lax.optimization_barrier(
+        tuple(first[offset].astype(f16) for offset in ORDER[0]) + (rows,)
+    )
+    far_across = send(far_across, 0, 1)
+    up_across = send(up_across, 1, 0)
+    down_across = send(down_across, 3, 0)
+    second = chip_sums(rows_now, ORDER[1])
+    far_across, rows_now = lax.optimization_barrier((far_across, rows_now))
+    rows_across = row_major(to_group(rows_now, 0, 1))
+    up = send(second[1, 0], 1, 0).astype(f32)
+    down = send(second[3, 0], 3, 0).astype(f32)
+    far = send(second[2, 0] + far_across.astype(f32), 2, 0).astype(f32)
+    across = send(second[0, 1] + up_across.astype(f32) + down_across.astype(f32), 0, 1).astype(f32)
+    merged = (second[0, 0] + up + down + far + across) * (1.0 / SEND)
     merged = merged.reshape(slots, span, wide)
     squares = sum_over_tr(jnp.sum(merged * merged, axis=2))
+    squares, rows_across = lax.optimization_barrier((squares, rows_across))
+    taps_across = gather_taps(rows_across)
 
     scaled, crossed = attention(
         lens,
@@ -319,19 +319,18 @@
     own_half = gather(turned, to_chip)
     other_half = {k: to_sibling(v) for k, v in own_half.items()}
 
+    all_rows = buffer((2, RING * slots * span, flat_in), bf16)
+    all_rows = lax.dynamic_update_slice(all_rows, taps_here[None], (0, 0, 0))
+    all_rows = lax.dynamic_update_slice(all_rows, taps_across[None], (1, 0, 0))
+    all_rows = all_rows.reshape(2 * RING, slots * span, flat_in)
+
     def gradient(half):
         total = None
-        same = x_low == x_high
-        for a in (0, 1, 3, 2):
-            straight, crossed = half[a, 0], half[a, 1]
-            for taps_of, piece in (
-                (taps_here, jnp.where(same, straight, crossed)),
-                (taps_across, jnp.where(same, crossed, straight)),
-            ):
-                at_z = (y - a - z) % RING
-                source = lax.dynamic_slice_in_dim(taps_of, at_z * slots * span, slots * span, 0)
-                part = lax.dot_general(source, piece, COLS_COLS, preferred_element_type=f32)
-                total = part if total is None else total + part
+        for (a, b), piece in half.items():
+            place = (x_low + x_high - b) % 2 * RING + (y - a - z) % RING
+            source = lax.dynamic_index_in_dim(all_rows, place, 0, keepdims=False)
+            part = lax.dot_general(source, piece, COLS_COLS, preferred_element_type=f32)
+            total = part if total is None else total + part
         return total
 
     grad = buffer((flat_in, block), f32)

time: 278 us -> 257 us (0.924)
  waiting for transfers between devices: 103 us -> 80.4 us
  local copies, waits for them, and re-layouts: 27.6 us -> 36.7 us
  matrix products: 22.5 us -> 13.5 us
  Pallas kernels: 34.5 us -> 29.5 us
  starting transfers between devices: 62.6 us -> 67.6 us
    ppermute x34, waiting for transfers between devices: 61.5 us -> 50 us  [to_chip(): return lax.ppermute(value, 'tr', pairs)]
    ppermute x9, waiting for transfers between devices: 41.7 us -> 30.3 us  [to_group(): return lax.ppermute(value, 'rep', pairs)]
    ppermute x34, starting transfers between devices: 44 us -> 53.7 us  [to_chip(): return lax.ppermute(value, 'tr', pairs)]
    dynamic_update_slice x0 -> x2, local copies, waits for them, and re-layouts: none -> 9.63 us  [the longest x1 4.82 us: per_device(): all_rows = lax.dynamic_update_slice(all_rows, taps_across[None], (1, 0, 0))]
    dot_general x16, matrix products: 22.5 us -> 13.5 us  [gradient(): part = lax.dot_general(source, piece, COLS_COLS, preferred_element_type=f32)]
    pallas_call x4, Pallas kernels: 18.7 us -> 13.7 us  [products(): pl.pallas_call(product_kernel, grid_spec=pltpu.PrefetchScalarGridSpec(num...]
    ppermute x9, starting transfers between devices: 17.9 us -> 13.1 us  [to_group(): return lax.ppermute(value, 'rep', pairs)]
    convert_element_type x0 -> x1, other arithmetic: none -> 3.01 us  [per_device(): first[offset].astype(f16)]
  transfers between devices with their start and end apart: 46 -> 46, of which waited for: 24 -> 19; matrix products, arithmetic and copies ran while one was open for 14% -> 18% of each run, Pallas kernels for 12% -> 10%
where the time goes in v1:
time: 257 us; the launch traced here: 255 us
  waiting for transfers between devices  80.4 us (31%)
  starting transfers between devices  67.6 us (26%)
  local copies, waits for them, and re-layouts  36.7 us (14%)
  Pallas kernels  29.5 us (11%)
  between operations  15 us (6%)
  matrix products  13.5 us (5%)
  other arithmetic  12.8 us (5%)
    ppermute x34, starting transfers between devices, to_chip(): return lax.ppermute(value, 'tr', pairs)  53.7 us
    ppermute x34, waiting for transfers between devices, to_chip(): return lax.ppermute(value, 'tr', pairs)  50 us
    ppermute x9, waiting for transfers between devices, to_group(): return lax.ppermute(value, 'rep', pairs)  30.3 us
    pallas_call x1, Pallas kernels, attention(): pl.pallas_call(attention_kernel, grid=(count // slots,), in_specs=[scalar...  15.8 us
    pallas_call x4, Pallas kernels, products(): pl.pallas_call(product_kernel, grid_spec=pltpu.PrefetchScalarGridSpec(num...  13.7 us
    dot_general x16, matrix products, gradient(): part = lax.dot_general(source, piece, COLS_COLS, preferred_element_type=f32)  13.5 us
    ppermute x9, starting transfers between devices, to_group(): return lax.ppermute(value, 'rep', pairs)  13.1 us
    unnamed x33, local copies, waits for them, and re-layouts  11.4 us
  transfers between devices with their start and end apart: 46, of which 19 were waited for; matrix products, arithmetic and copies ran while one was open for 18% of the time, Pallas kernels for 10%

profile of v1, /device:TPU:0, one launch (start us, length us, event | category | flops | bytes accessed | tf_op | source)
XLA Modules:
  0.0 255.5 jit_solution(10115632161728790995)
XLA Ops:
  7.3 2.3 copy.16
  10.0 3.1 %copy-done = bf16[3,256,4096]{2,1,0:T(8,128)(2,1)S(1)} copy-done((bf16[3,256,4096]{2,1,0:T(8,128)(2,1)S(1)}, bf16[3,256,4096]{2,1,0:T(8,128)(2,1)}, u32[]{:S(2)}) %copy-start) | copy-done | bytes 6291480
  13.1 3.4 %shard_map.80 = f32[3,768,256]{2,1,0:T(8,128)} custom-call(s32[3]{0:T(128)S(1)} %pad_add_fusion.1.blocks_ref, bf16[768,768]{1,0:T(8,128)(2,1)S(1)} %bitcast.139, bf16[768,4096]{1,0:T(8,128)(2,1)S(1)} %bitcast.133), custom_call_target="tpu_custom_call" | custom-call | flops 905969664 | bytes 4718592 | tf_op jit(solution)/shard_map/pallas_call | solution.py:202
  16.9 2.8 %copy-done.1 = bf16[3,256,4096]{2,1,0:T(8,128)(2,1)S(1)} copy-done((bf16[3,256,4096]{2,1,0:T(8,128)(2,1)S(1)}, bf16[3,256,4096]{2,1,0:T(8,128)(2,1)}, u32[]{:S(2)}) %copy-start.1) | copy-done | bytes 6291480
  20.9 2.2 shard_map.79
  23.2 3.0 %fusion.80 = (f16[768,256]{1,0:T(8,128)(2,1)}, f16[768,256]{1,0:T(8,128)(2,1)}, f16[768,256]{1,0:T(8,128)(2,1)}) fusion(f32[3,768,256]{2,1,0:T(8,128)} %collective-permute-done, f32[3,768,256]{2,1,0:T(8,128)S(1)} %shard_map.79), kind=kLoop, calls=%fused_computation.100 | loop fusion | flops 1769472 | bytes 5898240 | tf_op jit(solution)/shard_map/convert_element_type | solution.py:272
  26.2 4.8 %shard_map.82 = f32[5,768,256]{2,1,0:T(8,128)} custom-call(s32[5]{0:T(128)S(1)} %stack.79.blocks_ref, bf16[768,768]{1,0:T(8,128)(2,1)S(1)} %bitcast.142, bf16[768,4096]{1,0:T(8,128)(2,1)S(1)} %bitcast.137), custom_call_target="tpu_custom_call" | custom-call | flops 1509949440 | bytes 7077888 | tf_op jit(solution)/shard_map/pallas_call | solution.py:202
  31.5 3.1 %collective-permute-start.4 = (f16[768,256]{1,0:T(8,128)(2,1)}, f16[768,256]{1,0:T(8,128)(2,1)S(1)}, u32[]{:S(2)}, u32[]{:S(2)}) collective-permute-start(f16[768,256]{1,0:T(8,128)(2,1)} %get-tuple-element.13), channel_id=1, source_target_pairs={{0,2},{1,3},{2,0},{3,1},{4,6},{5,7},{6,4},{7,5},{8,10},{9,11},{10,... | collective-permute-start | bytes 1179656 | tf_op jit(solution)/shard_map/ppermute | solution.py:151
  34.6 3.0 %collective-permute-start.7 = (f16[768,256]{1,0:T(8,128)(2,1)}, f16[768,256]{1,0:T(8,128)(2,1)S(1)}, u32[]{:S(2)}, u32[]{:S(2)}) collective-permute-start(f16[768,256]{1,0:T(8,128)(2,1)} %get-tuple-element.16), channel_id=1, source_target_pairs={{0,12},{1,13},{2,14},{3,15},{4,0},{5,1},{6,2},{7,3},{8,4},{9,5},{1... | collective-permute-start | bytes 1179656 | tf_op jit(solution)/shard_map/ppermute | solution.py:151
  37.7 2.9 %copy-done.2 = bf16[3,256,4096]{2,1,0:T(8,128)(2,1)S(1)} copy-done((bf16[3,256,4096]{2,1,0:T(8,128)(2,1)S(1)}, bf16[3,256,4096]{2,1,0:T(8,128)(2,1)}, u32[]{:S(2)}) %copy-start.2) | copy-done | bytes 6291480
  40.6 3.3 %shard_map.81 = f32[5,768,256]{2,1,0:T(8,128)S(1)} custom-call(s32[5]{0:T(128)S(1)} %stack.65.blocks_ref, bf16[768,768]{1,0:T(8,128)(2,1)S(1)} %bitcast.143, bf16[768,4096]{1,0:T(8,128)(2,1)S(1)} %bitcast.138), custom_call_target="tpu_custom_call" | custom-call | flops 1509949440 | bytes 7077888 | tf_op jit(solution)/shard_map/pallas_call | solution.py:202
  46.2 3.4 %collective-permute-done.6 = f16[768,256]{1,0:T(8,128)(2,1)} collective-permute-done((f16[768,256]{1,0:T(8,128)(2,1)}, f16[768,256]{1,0:T(8,128)(2,1)}, u32[]{:S(2)}, u32[]{:S(2)}) %collective-permute-start.6) | collective-permute-done | bytes 393248 | tf_op jit(solution)/shard_map/ppermute | solution.py:151
  57.7 24.3 %collective-permute-done.8 = f16[768,256]{1,0:T(8,128)(2,1)S(1)} collective-permute-done((f16[768,256]{1,0:T(8,128)(2,1)S(1)}, f16[768,256]{1,0:T(8,128)(2,1)S(1)}, u32[]{:S(2)}, u32[]{:S(2)}) %collective-permute-start.8) | collective-permute-done | bytes 393248 | tf_op jit(solution)/shard_map/ppermute | solution.py:151
  85.8 4.2 %collective-permute-done.10 = f32[8,96]{1,0:T(8,128)S(1)} collective-permute-done((f32[8,96]{1,0:T(8,128)S(1)}, f32[8,96]{1,0:T(8,128)S(1)}, u32[]{:S(2)}, u32[]{:S(2)}) %collective-permute-start.10) | collective-permute-done | bytes 3104 | tf_op jit(solution)/shard_map/ppermute | solution.py:151
  90.0 3.0 %collective-permute-start.13 = (f32[8,96]{1,0:T(8,128)S(1)}, f32[8,96]{1,0:T(8,128)S(1)}, u32[]{:S(2)}, u32[]{:S(2)}) collective-permute-start(f32[8,96]{1,0:T(8,128)S(1)} %add.607), channel_id=1, source_target_pairs={{0,12},{1,13},{2,14},{3,15},{4,0},{5,1},{6,2},{7,3},{8,4},{9,5},{1... | collective-permute-start | bytes 9224 | tf_op jit(solution)/shard_map/ppermute | solution.py:151
  94.6 3.5 %collective-permute-done.12 = f32[8,96]{1,0:T(8,128)S(1)} collective-permute-done((f32[8,96]{1,0:T(8,128)S(1)}, f32[8,96]{1,0:T(8,128)S(1)}, u32[]{:S(2)}, u32[]{:S(2)}) %collective-permute-start.12) | collective-permute-done | bytes 3104 | tf_op jit(solution)/shard_map/ppermute | solution.py:151
  100.9 15.8 %shard_map.83 = (f32[8,96,256]{2,1,0:T(8,128)S(1)}, f32[8,1,96]{2,1,0:T(1,128)S(1)}) custom-call(s32[8]{0:T(128)S(1)} %dynamic_slice.43.lens_ref, f32[8]{0:T(128)S(1)} %convert_divide_fusion.weights_ref, f32[2]{0:T(128)S(1)} %copy-done.7, f32[8,96,256]{2,1,0:T(8,128)S(1)} %bitcast.145, f32[8,1,96]{2,1,0:T(1,128)S(1)} %bitcast.147, f32[1,256]{1,0:T(1,128)S(1)} %bitcast.150, ...), custom_call_target="tpu_custom_call" | custom-call | flops 2000000000 | bytes 3000000 | tf_op jit(solution)/shard_map/pallas_call | solution.py:114
  118.8 4.2 %collective-permute-done.16 = f32[8,96]{1,0:T(8,128)S(1)} collective-permute-done((f32[8,96]{1,0:T(8,128)S(1)}, f32[8,96]{1,0:T(8,128)S(1)}, u32[]{:S(2)}, u32[]{:S(2)}) %collective-permute-start.16) | collective-permute-done | bytes 3104 | tf_op jit(solution)/shard_map/ppermute | solution.py:151
  131.0 11.1 %collective-permute-start.23 = (bf16[768,256]{1,0:T(8,128)(2,1)S(1)}, bf16[768,256]{1,0:T(8,128)(2,1)S(1)}, u32[]{:S(2)}, u32[]{:S(2)}) collective-permute-start(bf16[768,256]{1,0:T(8,128)(2,1)S(1)} %collective-permute-done.20), channel_id=1, source_target_pairs={{0,2},{1,3},{2,0},{3,1},{4,6},{5,7},{6,4},{7,5},{8,10},{9,11},{10,... | collective-permute-start | bytes 1179656 | tf_op jit(solution)/shard_map/ppermute | solution.py:151
  142.1 4.8 %bitcast_dynamic-update-slice_fusion.1 = bf16[2,3072,768]{2,1,0:T(8,128)(2,1)} fusion(bf16[2,3072,768]{2,1,0:T(8,128)(2,1)} %shard_map.78, bf16[3072,768]{1,0:T(8,128)(2,1)} %all-gather.3.cloned.1.call-done), kind=kLoop, calls=%fused_computation.1 | loop fusion | bytes 9437184 | tf_op jit(solution)/shard_map/dynamic_update_slice | solution.py:323
  146.9 11.4 %collective-permute-start.24 = (bf16[768,256]{1,0:T(8,128)(2,1)S(1)}, bf16[768,256]{1,0:T(8,128)(2,1)S(1)}, u32[]{:S(2)}, u32[]{:S(2)}) collective-permute-start(bf16[768,256]{1,0:T(8,128)(2,1)S(1)} %collective-permute-done.20), channel_id=1, source_target_pairs={{0,8},{1,9},{2,10},{3,11},{4,12},{5,13},{6,14},{7,15},{8,0},{9,1},... | collective-permute-start | bytes 1179656 | tf_op jit(solution)/shard_map/ppermute | solution.py:151
  161.5 2.3 collective-permute-start.26
  163.8 4.8 %bitcast_dynamic-update-slice_fusion = bf16[2,3072,768]{2,1,0:T(8,128)(2,1)} fusion(bf16[2,3072,768]{2,1,0:T(8,128)(2,1)} %bitcast_dynamic-update-slice_fusion.1, bf16[3072,768]{1,0:T(8,128)(2,1)} %all-gather.5.cloned.1.call-done), kind=kLoop, calls=%fused_computation | loop fusion | bytes 9437184 | tf_op jit(solution)/shard_map/dynamic_update_slice | solution.py:324
  170.7 3.0 %collective-permute-done.21 = bf16[768,256]{1,0:T(8,128)(2,1)S(1)} collective-permute-done((bf16[768,256]{1,0:T(8,128)(2,1)S(1)}, bf16[768,256]{1,0:T(8,128)(2,1)S(1)}, u32[]{:S(2)}, u32[]{:S(2)}) %collective-permute-start.21) | collective-permute-done | bytes 393248 | tf_op jit(solution)/shard_map/ppermute | solution.py:151
  173.7 2.9 %collective-permute-start.27 = (bf16[768,256]{1,0:T(8,128)(2,1)S(1)}, bf16[768,256]{1,0:T(8,128)(2,1)S(1)}, u32[]{:S(2)}, u32[]{:S(2)}) collective-permute-start(bf16[768,256]{1,0:T(8,128)(2,1)S(1)} %collective-permute-done.24), channel_id=1, source_target_pairs={{0,2},{1,3},{2,0},{3,1},{4,6},{5,7},{6,4},{7,5},{8,10},{9,11},{10,... | collective-permute-start | bytes 1179656 | tf_op jit(solution)/shard_map/ppermute | solution.py:151
  190.9 2.9 %constant_dynamic-update-slice_fusion.7 = (bf16[768,4096]{1,0:T(8,128)(2,1)}, bf16[768,512]{1,0:T(8,128)(2,1)S(1)}) fusion(bf16[768,4096]{1,0:T(8,128)(2,1)} %shard_map.84, s32[]{:T(128)S(6)} %select_n.371, f32[768,512]{1,0:T(8,128)S(1)} %fusion.2, bf16[768,4096]{1,0:T(8,128)(2,1)} %bitcast.132, s32[]{:T(128)S(6)} %select_n.368), kind=kLoop, calls=%fused_computation.118 | loop fusion | flops 1572864 | bytes 3932168 | tf_op jit(solution)/shard_map/dynamic_update_slice | solution.py:344
  193.8 3.2 %collective-permute-start.37 = (bf16[768,512]{1,0:T(8,128)(2,1)S(1)}, bf16[768,512]{1,0:T(8,128)(2,1)S(1)}, u32[]{:S(2)}, u32[]{:S(2)}) collective-permute-start(bf16[768,512]{1,0:T(8,128)(2,1)S(1)} %get-tuple-element.23), channel_id=1, source_target_pairs={{0,96},{16,112},{32,0},{48,16},{64,32},{80,48},{96,64},{112,80},{1... | collective-permute-start | bytes 2359304 | tf_op jit(solution)/shard_map/ppermute | solution.py:156
  197.9 17.0 %collective-permute-done.36 = bf16[768,512]{1,0:T(8,128)(2,1)S(1)} collective-permute-done((bf16[768,512]{1,0:T(8,128)(2,1)S(1)}, bf16[768,512]{1,0:T(8,128)(2,1)S(1)}, u32[]{:S(2)}, u32[]{:S(2)}) %collective-permute-start.36) | collective-permute-done | bytes 786464 | tf_op jit(solution)/shard_map/ppermute | solution.py:156
  216.6 3.1 %collective-permute-start.40 = (bf16[384,512]{1,0:T(8,128)(2,1)}, bf16[384,512]{1,0:T(8,128)(2,1)}, u32[]{:S(2)}, u32[]{:S(2)}) collective-permute-start(bf16[384,512]{1,0:T(8,128)(2,1)} %slice.93), channel_id=1, source_target_pairs={{0,96},{16,112},{32,0},{48,16},{64,32},{80,48},{96,64},{112,80},{1... | collective-permute-start | bytes 1179656 | tf_op jit(solution)/shard_map/ppermute | solution.py:156
  219.7 3.2 %collective-permute-start.42 = (bf16[768,512]{1,0:T(8,128)(2,1)}, bf16[768,512]{1,0:T(8,128)(2,1)S(1)}, u32[]{:S(2)}, u32[]{:S(2)}) collective-permute-start(bf16[768,512]{1,0:T(8,128)(2,1)} %collective-permute-done.38), channel_id=1, source_target_pairs={{0,96},{16,112},{32,0},{48,16},{64,32},{80,48},{96,64},{112,80},{1... | collective-permute-start | bytes 2359304 | tf_op jit(solution)/shard_map/ppermute | solution.py:156
  222.9 6.2 %collective-permute-done.39 = bf16[384,512]{1,0:T(8,128)(2,1)S(1)} collective-permute-done((bf16[384,512]{1,0:T(8,128)(2,1)}, bf16[384,512]{1,0:T(8,128)(2,1)S(1)}, u32[]{:S(2)}, u32[]{:S(2)}) %collective-permute-start.39) | collective-permute-done | bytes 393248 | tf_op jit(solution)/shard_map/ppermute | solution.py:156
  238.0 6.7 %collective-permute-done.41 = bf16[768,512]{1,0:T(8,128)(2,1)} collective-permute-done((bf16[768,512]{1,0:T(8,128)(2,1)}, bf16[768,512]{1,0:T(8,128)(2,1)}, u32[]{:S(2)}, u32[]{:S(2)}) %collective-permute-start.41) | collective-permute-done | bytes 786464 | tf_op jit(solution)/shard_map/ppermute | solution.py:156
  (157 shorter events, 65.4 us)
Async XLA Ops:
  7.2 134.9 %all-gather.3.cloned.1.call-start = ((), (), s32[]{:S(2)}) async-start(), calls=%async_computation | async-start | bytes 5898240 | tf_op jit(solution)/shard_map/all_gather | solution.py:254
  16.5 6.6 %collective-permute-start = (f32[3,768,256]{2,1,0:T(8,128)}, f32[3,768,256]{2,1,0:T(8,128)}, u32[]{:S(2)}, u32[]{:S(2)}) collective-permute-start(f32[3,768,256]{2,1,0:T(8,128)} %shard_map.80), channel_id=1, source_target_pairs={{0,1},{1,0},{2,3},{3,2},{4,5},{5,4},{6,7},{7,6},{8,9},{9,8},{10,11... | collective-permute-start | bytes 7077896 | tf_op jit(solution)/shard_map/ppermute | solution.py:151
  16.6 147.3 %all-gather.5.cloned.1.call-start = ((), (), s32[]{:S(2)}) async-start(), calls=%async_computation.1 | async-start | bytes 5898240 | tf_op jit(solution)/shard_map/all_gather | solution.py:254
  31.0 18.6 %collective-permute-start.1 = (f32[5,768,256]{2,1,0:T(8,128)}, f32[5,768,256]{2,1,0:T(8,128)}, u32[]{:S(2)}, u32[]{:S(2)}) collective-permute-start(f32[5,768,256]{2,1,0:T(8,128)} %shard_map.82), channel_id=1, source_target_pairs={{0,1},{1,0},{2,3},{3,2},{4,5},{5,4},{6,7},{7,6},{8,9},{9,8},{10,11... | collective-permute-start | bytes 11796488 | tf_op jit(solution)/shard_map/ppermute | solution.py:151
  31.5 12.7 %collective-permute-start.4 = (f16[768,256]{1,0:T(8,128)(2,1)}, f16[768,256]{1,0:T(8,128)(2,1)S(1)}, u32[]{:S(2)}, u32[]{:S(2)}) collective-permute-start(f16[768,256]{1,0:T(8,128)(2,1)} %get-tuple-element.13), channel_id=1, source_target_pairs={{0,2},{1,3},{2,0},{3,1},{4,6},{5,7},{6,4},{7,5},{8,10},{9,11},{10,... | collective-permute-start | bytes 1179656 | tf_op jit(solution)/shard_map/ppermute | solution.py:151
  34.6 11.6 %collective-permute-start.7 = (f16[768,256]{1,0:T(8,128)(2,1)}, f16[768,256]{1,0:T(8,128)(2,1)S(1)}, u32[]{:S(2)}, u32[]{:S(2)}) collective-permute-start(f16[768,256]{1,0:T(8,128)(2,1)} %get-tuple-element.16), channel_id=1, source_target_pairs={{0,12},{1,13},{2,14},{3,15},{4,0},{5,1},{6,2},{7,3},{8,4},{9,5},{1... | collective-permute-start | bytes 1179656 | tf_op jit(solution)/shard_map/ppermute | solution.py:151
  37.7 12.0 %collective-permute-start.6 = (f16[768,256]{1,0:T(8,128)(2,1)}, f16[768,256]{1,0:T(8,128)(2,1)}, u32[]{:S(2)}, u32[]{:S(2)}) collective-permute-start(f16[768,256]{1,0:T(8,128)(2,1)} %get-tuple-element.15), channel_id=1, source_target_pairs={{0,4},{1,5},{2,6},{3,7},{4,8},{5,9},{6,10},{7,11},{8,12},{9,13},{1... | collective-permute-start | bytes 1179656 | tf_op jit(solution)/shard_map/ppermute | solution.py:151
  44.3 54.2 %collective-permute-start.14 = (bf16[768,768]{1,0:T(8,128)(2,1)S(1)}, bf16[768,768]{1,0:T(8,128)(2,1)S(1)}, u32[]{:S(2)}, u32[]{:S(2)}) collective-permute-start(bf16[768,768]{1,0:T(8,128)(2,1)S(1)} %bitcast.144), channel_id=1, source_target_pairs={{0,16},{16,0},{32,48},{48,32},{64,80},{80,64},{96,112},{112,96},{1... | collective-permute-start | bytes 3538952 | tf_op jit(solution)/shard_map/ppermute | solution.py:156
  51.6 30.4 %collective-permute-start.8 = (f16[768,256]{1,0:T(8,128)(2,1)S(1)}, f16[768,256]{1,0:T(8,128)(2,1)S(1)}, u32[]{:S(2)}, u32[]{:S(2)}) collective-permute-start(f16[768,256]{1,0:T(8,128)(2,1)S(1)} %get-tuple-element.29), channel_id=1, source_target_pairs={{0,2},{1,3},{2,0},{3,1},{4,6},{5,7},{6,4},{7,5},{8,10},{9,11},{10,... | collective-permute-start | bytes 1179656 | tf_op jit(solution)/shard_map/ppermute | solution.py:151
  52.3 29.8 %collective-permute-start.5 = (f16[768,256]{1,0:T(8,128)(2,1)S(1)}, f16[768,256]{1,0:T(8,128)(2,1)S(1)}, u32[]{:S(2)}, u32[]{:S(2)}) collective-permute-start(f16[768,256]{1,0:T(8,128)(2,1)S(1)} %get-tuple-element.28), channel_id=1, source_target_pairs={{0,8},{1,9},{2,10},{3,11},{4,12},{5,13},{6,14},{7,15},{8,0},{9,1},... | collective-permute-start | bytes 1179656 | tf_op jit(solution)/shard_map/ppermute | solution.py:151
  55.6 26.4 %collective-permute-start.3 = (f16[768,256]{1,0:T(8,128)(2,1)S(1)}, f16[768,256]{1,0:T(8,128)(2,1)S(1)}, u32[]{:S(2)}, u32[]{:S(2)}) collective-permute-start(f16[768,256]{1,0:T(8,128)(2,1)S(1)} %get-tuple-element.27), channel_id=1, source_target_pairs={{0,12},{1,13},{2,14},{3,15},{4,0},{5,1},{6,2},{7,3},{8,4},{9,5},{1... | collective-permute-start | bytes 1179656 | tf_op jit(solution)/shard_map/ppermute | solution.py:151
  56.7 25.4 %collective-permute-start.2 = (f16[768,256]{1,0:T(8,128)(2,1)S(1)}, f16[768,256]{1,0:T(8,128)(2,1)S(1)}, u32[]{:S(2)}, u32[]{:S(2)}) collective-permute-start(f16[768,256]{1,0:T(8,128)(2,1)S(1)} %get-tuple-element.26), channel_id=1, source_target_pairs={{0,4},{1,5},{2,6},{3,7},{4,8},{5,9},{6,10},{7,11},{8,12},{9,13},{1... | collective-permute-start | bytes 1179656 | tf_op jit(solution)/shard_map/ppermute | solution.py:151
  84.9 5.1 %collective-permute-start.10 = (f32[8,96]{1,0:T(8,128)S(1)}, f32[8,96]{1,0:T(8,128)S(1)}, u32[]{:S(2)}, u32[]{:S(2)}) collective-permute-start(f32[8,96]{1,0:T(8,128)S(1)} %add.606), channel_id=1, source_target_pairs={{0,2},{1,3},{2,0},{3,1},{4,6},{5,7},{6,4},{7,5},{8,10},{9,11},{10,... | collective-permute-start | bytes 9224 | tf_op jit(solution)/shard_map/ppermute | solution.py:151
  93.0 5.1 %collective-permute-start.12 = (f32[8,96]{1,0:T(8,128)S(1)}, f32[8,96]{1,0:T(8,128)S(1)}, u32[]{:S(2)}, u32[]{:S(2)}) collective-permute-start(f32[8,96]{1,0:T(8,128)S(1)} %add.607), channel_id=1, source_target_pairs={{0,8},{1,9},{2,10},{3,11},{4,12},{5,13},{6,14},{7,15},{8,0},{9,1},... | collective-permute-start | bytes 9224 | tf_op jit(solution)/shard_map/ppermute | solution.py:151
  117.9 5.1 %collective-permute-start.16 = (f32[8,96]{1,0:T(8,128)S(1)}, f32[8,96]{1,0:T(8,128)S(1)}, u32[]{:S(2)}, u32[]{:S(2)}) collective-permute-start(f32[8,96]{1,0:T(8,128)S(1)} %add.622), channel_id=1, source_target_pairs={{0,2},{1,3},{2,0},{3,1},{4,6},{5,7},{6,4},{7,5},{8,10},{9,11},{10,... | collective-permute-start | bytes 9224 | tf_op jit(solution)/shard_map/ppermute | solution.py:151
  123.5 5.1 %collective-permute-start.18 = (f32[8,96]{1,0:T(8,128)S(1)}, f32[8,96]{1,0:T(8,128)S(1)}, u32[]{:S(2)}, u32[]{:S(2)}) collective-permute-start(f32[8,96]{1,0:T(8,128)S(1)} %add.623), channel_id=1, source_target_pairs={{0,8},{1,9},{2,10},{3,11},{4,12},{5,13},{6,14},{7,15},{8,0},{9,1},... | collective-permute-start | bytes 9224 | tf_op jit(solution)/shard_map/ppermute | solution.py:151
  131.0 30.5 %collective-permute-start.23 = (bf16[768,256]{1,0:T(8,128)(2,1)S(1)}, bf16[768,256]{1,0:T(8,128)(2,1)S(1)}, u32[]{:S(2)}, u32[]{:S(2)}) collective-permute-start(bf16[768,256]{1,0:T(8,128)(2,1)S(1)} %collective-permute-done.20), channel_id=1, source_target_pairs={{0,2},{1,3},{2,0},{3,1},{4,6},{5,7},{6,4},{7,5},{8,10},{9,11},{10,... | collective-permute-start | bytes 1179656 | tf_op jit(solution)/shard_map/ppermute | solution.py:151
  146.9 23.7 %collective-permute-start.24 = (bf16[768,256]{1,0:T(8,128)(2,1)S(1)}, bf16[768,256]{1,0:T(8,128)(2,1)S(1)}, u32[]{:S(2)}, u32[]{:S(2)}) collective-permute-start(bf16[768,256]{1,0:T(8,128)(2,1)S(1)} %collective-permute-done.20), channel_id=1, source_target_pairs={{0,8},{1,9},{2,10},{3,11},{4,12},{5,13},{6,14},{7,15},{8,0},{9,1},... | collective-permute-start | bytes 1179656 | tf_op jit(solution)/shard_map/ppermute | solution.py:151
  158.3 15.4 %collective-permute-start.21 = (bf16[768,256]{1,0:T(8,128)(2,1)S(1)}, bf16[768,256]{1,0:T(8,128)(2,1)S(1)}, u32[]{:S(2)}, u32[]{:S(2)}) collective-permute-start(bf16[768,256]{1,0:T(8,128)(2,1)S(1)} %collective-permute-done.20), channel_id=1, source_target_pairs={{0,4},{1,5},{2,6},{3,7},{4,8},{5,9},{6,10},{7,11},{8,12},{9,13},{1... | collective-permute-start | bytes 1179656 | tf_op jit(solution)/shard_map/ppermute | solution.py:151
  160.1 22.5 %collective-permute-start.22 = (bf16[768,256]{1,0:T(8,128)(2,1)S(1)}, bf16[768,256]{1,0:T(8,128)(2,1)S(1)}, u32[]{:S(2)}, u32[]{:S(2)}) collective-permute-start(bf16[768,256]{1,0:T(8,128)(2,1)S(1)} %collective-permute-done.20), channel_id=1, source_target_pairs={{0,12},{1,13},{2,14},{3,15},{4,0},{5,1},{6,2},{7,3},{8,4},{9,5},{1... | collective-permute-start | bytes 1179656 | tf_op jit(solution)/shard_map/ppermute | solution.py:151
  161.5 20.4 %collective-permute-start.28 = (bf16[768,256]{1,0:T(8,128)(2,1)S(1)}, bf16[768,256]{1,0:T(8,128)(2,1)S(1)}, u32[]{:S(2)}, u32[]{:S(2)}) collective-permute-start(bf16[768,256]{1,0:T(8,128)(2,1)S(1)} %collective-permute-done.20), channel_id=1, source_target_pairs={{0,1},{1,0},{2,3},{3,2},{4,5},{5,4},{6,7},{7,6},{8,9},{9,8},{10,11... | collective-permute-start | bytes 1179656 | tf_op jit(solution)/shard_map/ppermute | solution.py:151
  161.5 24.3 %collective-permute-start.26 = (bf16[768,256]{1,0:T(8,128)(2,1)S(1)}, bf16[768,256]{1,0:T(8,128)(2,1)S(1)}, u32[]{:S(2)}, u32[]{:S(2)}) collective-permute-start(bf16[768,256]{1,0:T(8,128)(2,1)S(1)} %collective-permute-done.23), channel_id=1, source_target_pairs={{0,12},{1,13},{2,14},{3,15},{4,0},{5,1},{6,2},{7,3},{8,4},{9,5},{1... | collective-permute-start | bytes 1179656 | tf_op jit(solution)/shard_map/ppermute | solution.py:151
  170.6 15.9 %collective-permute-start.25 = (bf16[768,256]{1,0:T(8,128)(2,1)S(1)}, bf16[768,256]{1,0:T(8,128)(2,1)S(1)}, u32[]{:S(2)}, u32[]{:S(2)}) collective-permute-start(bf16[768,256]{1,0:T(8,128)(2,1)S(1)} %collective-permute-done.23), channel_id=1, source_target_pairs={{0,4},{1,5},{2,6},{3,7},{4,8},{5,9},{6,10},{7,11},{8,12},{9,13},{1... | collective-permute-start | bytes 1179656 | tf_op jit(solution)/shard_map/ppermute | solution.py:151
  173.7 10.6 %collective-permute-start.27 = (bf16[768,256]{1,0:T(8,128)(2,1)S(1)}, bf16[768,256]{1,0:T(8,128)(2,1)S(1)}, u32[]{:S(2)}, u32[]{:S(2)}) collective-permute-start(bf16[768,256]{1,0:T(8,128)(2,1)S(1)} %collective-permute-done.24), channel_id=1, source_target_pairs={{0,2},{1,3},{2,0},{3,1},{4,6},{5,7},{6,4},{7,5},{8,10},{9,11},{10,... | collective-permute-start | bytes 1179656 | tf_op jit(solution)/shard_map/ppermute | solution.py:151
  193.8 21.1 %collective-permute-start.36 = (bf16[768,512]{1,0:T(8,128)(2,1)S(1)}, bf16[768,512]{1,0:T(8,128)(2,1)S(1)}, u32[]{:S(2)}, u32[]{:S(2)}) collective-permute-start(bf16[768,512]{1,0:T(8,128)(2,1)S(1)} %get-tuple-element.23), channel_id=1, source_target_pairs={{0,32},{16,48},{32,64},{48,80},{64,96},{80,112},{96,0},{112,16},{1... | collective-permute-start | bytes 2359304 | tf_op jit(solution)/shard_map/ppermute | solution.py:156
  193.8 22.0 %collective-permute-start.37 = (bf16[768,512]{1,0:T(8,128)(2,1)S(1)}, bf16[768,512]{1,0:T(8,128)(2,1)S(1)}, u32[]{:S(2)}, u32[]{:S(2)}) collective-permute-start(bf16[768,512]{1,0:T(8,128)(2,1)S(1)} %get-tuple-element.23), channel_id=1, source_target_pairs={{0,96},{16,112},{32,0},{48,16},{64,32},{80,48},{96,64},{112,80},{1... | collective-permute-start | bytes 2359304 | tf_op jit(solution)/shard_map/ppermute | solution.py:156
  197.0 22.7 %collective-permute-start.38 = (bf16[768,512]{1,0:T(8,128)(2,1)S(1)}, bf16[768,512]{1,0:T(8,128)(2,1)}, u32[]{:S(2)}, u32[]{:S(2)}) collective-permute-start(bf16[768,512]{1,0:T(8,128)(2,1)S(1)} %get-tuple-element.23), channel_id=1, source_target_pairs={{0,16},{16,0},{32,48},{48,32},{64,80},{80,64},{96,112},{112,96},{1... | collective-permute-start | bytes 2359304 | tf_op jit(solution)/shard_map/ppermute | solution.py:156
  215.7 13.5 %collective-permute-start.39 = (bf16[384,512]{1,0:T(8,128)(2,1)}, bf16[384,512]{1,0:T(8,128)(2,1)S(1)}, u32[]{:S(2)}, u32[]{:S(2)}) collective-permute-start(bf16[384,512]{1,0:T(8,128)(2,1)} %slice.92), channel_id=1, source_target_pairs={{0,32},{16,48},{32,64},{48,80},{64,96},{80,112},{96,0},{112,16},{1... | collective-permute-start | bytes 1179656 | tf_op jit(solution)/shard_map/ppermute | solution.py:156
  216.6 13.0 %collective-permute-start.40 = (bf16[384,512]{1,0:T(8,128)(2,1)}, bf16[384,512]{1,0:T(8,128)(2,1)}, u32[]{:S(2)}, u32[]{:S(2)}) collective-permute-start(bf16[384,512]{1,0:T(8,128)(2,1)} %slice.93), channel_id=1, source_target_pairs={{0,96},{16,112},{32,0},{48,16},{64,32},{80,48},{96,64},{112,80},{1... | collective-permute-start | bytes 1179656 | tf_op jit(solution)/shard_map/ppermute | solution.py:156
  219.7 25.0 %collective-permute-start.41 = (bf16[768,512]{1,0:T(8,128)(2,1)}, bf16[768,512]{1,0:T(8,128)(2,1)}, u32[]{:S(2)}, u32[]{:S(2)}) collective-permute-start(bf16[768,512]{1,0:T(8,128)(2,1)} %collective-permute-done.38), channel_id=1, source_target_pairs={{0,32},{16,48},{32,64},{48,80},{64,96},{80,112},{96,0},{112,16},{1... | collective-permute-start | bytes 2359304 | tf_op jit(solution)/shard_map/ppermute | solution.py:156
  219.7 27.1 %collective-permute-start.42 = (bf16[768,512]{1,0:T(8,128)(2,1)}, bf16[768,512]{1,0:T(8,128)(2,1)S(1)}, u32[]{:S(2)}, u32[]{:S(2)}) collective-permute-start(bf16[768,512]{1,0:T(8,128)(2,1)} %collective-permute-done.38), channel_id=1, source_target_pairs={{0,96},{16,112},{32,0},{48,16},{64,32},{80,48},{96,64},{112,80},{1... | collective-permute-start | bytes 2359304 | tf_op jit(solution)/shard_map/ppermute | solution.py:156
  230.6 17.1 %collective-permute-start.43 = (bf16[768,512]{1,0:T(8,128)(2,1)S(1)}, bf16[768,512]{1,0:T(8,128)(2,1)S(1)}, u32[]{:S(2)}, u32[]{:S(2)}) collective-permute-start(bf16[768,512]{1,0:T(8,128)(2,1)S(1)} %pad_maximum_fusion), channel_id=1, source_target_pairs={{0,16},{16,0},{32,48},{48,32},{64,80},{80,64},{96,112},{112,96},{1... | collective-permute-start | bytes 2359304 | tf_op jit(solution)/shard_map/ppermute | solution.py:156
  (30 other events, 334.2 us)
Sparse Core Ops, SparseCore 0:
  16.7 55.4 all-gather.2
  99.6 59.2 all-gather.4

commit v2 on v1

--- a/solution.py
+++ b/solution.py
@@ -12,7 +12,7 @@
 SPAN = 96
 HEAD = 128
 RING = 4
-ORDER = (((2, 1), (1, 1), (3, 1)), ((1, 0), (3, 0), (2, 0), (0, 1), (0, 0)))
+ORDER = ((2, 1), (1, 1), (3, 1), (1, 0), (3, 0), (2, 0), (0, 1), (0, 0))
 
 f32 = jnp.float32
 bf16 = jnp.bfloat16
@@ -248,12 +248,9 @@
     count = jnp.sum(jnp.where(own_dest[:, None] == dest[None, :], target[None, :], 0), axis=1)
     weights = 1.0 / count.astype(f32)
 
-    along_z = [[at_z * 2 + at_x for at_z in range(RING)] for at_x in range(2)]
-
-    def gather_taps(value):
-        return row_major(lax.all_gather(value, "rep", axis=0, tiled=True, axis_index_groups=along_z))
-
-    taps_here = gather_taps(rows)
+    tap_rows = {(0, 0): rows}
+    for a, b in ((1, 0), (3, 0), (0, 1)):
+        tap_rows[a, b] = to_group(rows, a, b)
 
     def sums(rows, offsets, parity):
         blocks = jnp.stack([tr_index(y + dy, x_high + dx, parity) for dy, dx in offsets])
@@ -267,25 +264,25 @@
     def send(value, dy, dx):
         return to_chip(value.astype(f16), dy, dx)
 
-    first = chip_sums(rows, ORDER[0])
-    far_across, up_across, down_across, rows_now = lax.optimization_barrier(
-        tuple(first[offset].astype(f16) for offset in ORDER[0]) + (rows,)
-    )
-    far_across = send(far_across, 0, 1)
-    up_across = send(up_across, 1, 0)
-    down_across = send(down_across, 3, 0)
-    second = chip_sums(rows_now, ORDER[1])
-    far_across, rows_now = lax.optimization_barrier((far_across, rows_now))
-    rows_across = row_major(to_group(rows_now, 0, 1))
-    up = send(second[1, 0], 1, 0).astype(f32)
-    down = send(second[3, 0], 3, 0).astype(f32)
-    far = send(second[2, 0] + far_across.astype(f32), 2, 0).astype(f32)
-    across = send(second[0, 1] + up_across.astype(f32) + down_across.astype(f32), 0, 1).astype(f32)
-    merged = (second[0, 0] + up + down + far + across) * (1.0 / SEND)
+    total = chip_sums(rows, ORDER)
+    far_across = send(total[2, 1], 0, 1)
+    up_across = send(total[1, 1], 1, 0)
+    down_across = send(total[3, 1], 3, 0)
+    far_across, up_across, down_across, tap_rows[1, 0], tap_rows[3, 0], tap_rows[0, 1], rows = lax.optimization_barrier(
+        (far_across, up_across, down_across, tap_rows[1, 0], tap_rows[3, 0], tap_rows[0, 1], rows)
+    )
+    up = send(total[1, 0], 1, 0).astype(f32)
+    down = send(total[3, 0], 3, 0).astype(f32)
+    far = send(total[2, 0] + far_across.astype(f32), 2, 0).astype(f32)
+    across = send(total[0, 1] + up_across.astype(f32) + down_across.astype(f32), 0, 1).astype(f32)
+    tap_rows[2, 0] = to_group(rows, 2, 0)
+    merged = (total[0, 0] + up + down + far + across) * (1.0 / SEND)
     merged = merged.reshape(slots, span, wide)
+    merged, tap_rows[0, 1] = lax.optimization_barrier((merged, tap_rows[0, 1]))
+    tap_rows[1, 1] = to_group(tap_rows[0, 1], 1, 0)
+    tap_rows[3, 1] = to_group(tap_rows[0, 1], 3, 0)
     squares = sum_over_tr(jnp.sum(merged * merged, axis=2))
-    squares, rows_across = lax.optimization_barrier((squares, rows_across))
-    taps_across = gather_taps(rows_across)
+    squares, tap_rows[2, 0] = lax.optimization_barrier((squares, tap_rows[2, 0]))
 
     scaled, crossed = attention(
         lens,
@@ -296,6 +293,10 @@
         norm_gain.reshape(1, wide),
         taps[:, :, 2, :],
     )
+    crossed, tap_rows[0, 1], tap_rows[1, 1], tap_rows[3, 1] = lax.optimization_barrier(
+        (crossed, tap_rows[0, 1], tap_rows[1, 1], tap_rows[3, 1])
+    )
+    tap_rows[2, 1] = to_group(tap_rows[0, 1], 2, 0)
     crossed = sum_over_tr(crossed.reshape(slots, span))
     inverse = lax.rsqrt(squares / width_all + epsilon)
     merged_grad = (
@@ -316,26 +317,24 @@
         for at_core in range(2)
     ]
     turned = lax.ppermute(merged_grad.reshape(slots * span, wide), ("rep", "tr"), pairs)
+    turned, tap_rows[2, 1] = lax.optimization_barrier((turned, tap_rows[2, 1]))
     own_half = gather(turned, to_chip)
-    other_half = {k: to_sibling(v) for k, v in own_half.items()}
-
-    all_rows = buffer((2, RING * slots * span, flat_in), bf16)
-    all_rows = lax.dynamic_update_slice(all_rows, taps_here[None], (0, 0, 0))
-    all_rows = lax.dynamic_update_slice(all_rows, taps_across[None], (1, 0, 0))
-    all_rows = all_rows.reshape(2 * RING, slots * span, flat_in)
-
-    def gradient(half):
-        total = None
-        for (a, b), piece in half.items():
-            place = (x_low + x_high - b) % 2 * RING + (y - a - z) % RING
-            source = lax.dynamic_index_in_dim(all_rows, place, 0, keepdims=False)
-            part = lax.dot_general(source, piece, COLS_COLS, preferred_element_type=f32)
-            total = part if total is None else total + part
-        return total
-
-    grad = buffer((flat_in, block), f32)
-    for half, parity in ((own_half, core), (other_half, 1 - core)):
-        grad = lax.dynamic_update_slice_in_dim(grad, gradient(half), parity * wide, 1)
+    all_grads = buffer((RING * 2, slots * span, block), bf16)
+    for (a, b), piece in own_half.items():
+        all_grads = lax.dynamic_update_slice(all_grads, piece[None], (a * 2 + b, 0, core * wide))
+        other = to_sibling(piece)
+        all_grads = lax.dynamic_update_slice(all_grads, other[None], (a * 2 + b, 0, (1 - core) * wide))
+
+    grad = None
+    for a, b in ((0, 0), (1, 0), (3, 0), (2, 0), (0, 1), (1, 1), (3, 1), (2, 1)):
+        place = (y - 2 * z + a) % RING * 2 + (x_high - x_low + b) % 2
+        part = lax.dot_general(
+            tap_rows[a, b],
+            lax.dynamic_index_in_dim(all_grads, place, 0, keepdims=False),
+            COLS_COLS,
+            preferred_element_type=f32,
+        )
+        grad = part if grad is None else grad + part
     old = lax.dynamic_slice_in_dim(weight, rep * block, block, 1)
     new_block = (old.astype(f32) - step_size * grad).astype(bf16)
     new = buffer((flat_in, width_all), bf16)

time: 257 us -> 274 us (1.066)
  waiting for transfers between devices: 80.4 us -> 107 us
  starting transfers between devices: 67.6 us -> 82.2 us
  between operations: 15 us -> 1.11 us
  other arithmetic: 12.8 us -> 6.95 us
  local copies, waits for them, and re-layouts: 36.7 us -> 31.3 us
  matrix products: 13.5 us -> 17.8 us
    ppermute x9 -> x15, waiting for transfers between devices: 30.3 us -> 68.4 us  [to_group(): return lax.ppermute(value, 'rep', pairs)]
    ppermute x34 -> x33, waiting for transfers between devices: 50 us -> 38.6 us  [to_chip(): return lax.ppermute(value, 'tr', pairs)]
    ppermute x9 -> x15, starting transfers between devices: 13.1 us -> 23.5 us  [to_group(): return lax.ppermute(value, 'rep', pairs)]
    unnamed x33 -> x19, local copies, waits for them, and re-layouts: 11.4 us -> 5.89 us
    ppermute x34 -> x33, starting transfers between devices: 53.7 us -> 58.1 us  [to_chip(): return lax.ppermute(value, 'tr', pairs)]
    dot_general x16 -> x8, matrix products: 13.5 us -> 17.8 us  [per_device(): lax.dot_general(tap_rows[a, b], lax.dynamic_index_in_dim(all_grads, place...]
    dynamic_update_slice x2 -> x16, local copies, waits for them, and re-layouts: 9.63 us -> 12.7 us  [the longest x8 6.37 us: per_device(): lax.dynamic_update_slice(all_grads, piece[None], (a * 2 + b, 0, core * wi...]
    convert_element_type x1 -> x0, other arithmetic: 3.01 us -> none  [per_device(): first[offset].astype(f16)]
  transfers between devices with their start and end apart: 46 -> 49, of which waited for: 19 -> 22; matrix products, arithmetic and copies ran while one was open for 18% -> 10% of each run, Pallas kernels for 10% -> 8%
where the time goes in v2:
time: 274 us
  waiting for transfers between devices  107 us (39%)
  starting transfers between devices  82.2 us (30%)
  local copies, waits for them, and re-layouts  31.3 us (11%)
  Pallas kernels  27.5 us (10%)
  matrix products  17.8 us (6%)
  other arithmetic  6.95 us (3%)
    ppermute x15, waiting for transfers between devices, to_group(): return lax.ppermute(value, 'rep', pairs)  68.4 us
    ppermute x33, starting transfers between devices, to_chip(): return lax.ppermute(value, 'tr', pairs)  58.1 us
    ppermute x33, waiting for transfers between devices, to_chip(): return lax.ppermute(value, 'tr', pairs)  38.6 us
    ppermute x15, starting transfers between devices, to_group(): return lax.ppermute(value, 'rep', pairs)  23.5 us
    dot_general x8, matrix products, per_device(): lax.dot_general(tap_rows[a, b], lax.dynamic_index_in_dim(all_grads, place...  17.8 us
    pallas_call x1, Pallas kernels, attention(): pl.pallas_call(attention_kernel, grid=(count // slots,), in_specs=[scalar...  15.8 us
    pallas_call x2, Pallas kernels, products(): pl.pallas_call(product_kernel, grid_spec=pltpu.PrefetchScalarGridSpec(num...  11.7 us
    dynamic_update_slice x8, local copies, waits for them, and re-layouts, per_device(): new = lax.dynamic_update_slice(new, piece, (first, owner * block))  8.25 us
  transfers between devices with their start and end apart: 49, of which 22 were waited for; matrix products, arithmetic and copies ran while one was open for 10% of the time, Pallas kernels for 8%

profile of v2, /device:TPU:0, one launch (start us, length us, event | category | flops | bytes accessed | tf_op | source)
XLA Modules:
  0.0 273.8 jit_solution(11740084506848742726)
XLA Ops:
  3.5 2.8 %copy-done = bf16[3,256,4096]{2,1,0:T(8,128)(2,1)S(1)} copy-done((bf16[3,256,4096]{2,1,0:T(8,128)(2,1)S(1)}, bf16[3,256,4096]{2,1,0:T(8,128)(2,1)}, u32[]{:S(2)}) %copy-start) | copy-done | bytes 6291480
  6.3 6.8 %shard_map.79 = f32[8,768,256]{2,1,0:T(8,128)} custom-call(s32[8]{0:T(128)S(1)} %stack.71.blocks_ref, bf16[768,768]{1,0:T(8,128)(2,1)S(1)} %bitcast.153, bf16[768,4096]{1,0:T(8,128)(2,1)S(1)} %bitcast.151), custom_call_target="tpu_custom_call" | custom-call | flops 2415919104 | bytes 10616832 | tf_op jit(solution)/shard_map/pallas_call | solution.py:202
  18.7 2.8 %copy-done.1 = bf16[3,256,4096]{2,1,0:T(8,128)(2,1)S(1)} copy-done((bf16[3,256,4096]{2,1,0:T(8,128)(2,1)S(1)}, bf16[3,256,4096]{2,1,0:T(8,128)(2,1)}, u32[]{:S(2)}) %copy-start.1) | copy-done | bytes 6291480
  21.5 4.9 %shard_map.78 = f32[8,768,256]{2,1,0:T(8,128)S(1)} custom-call(s32[8]{0:T(128)S(1)} %stack.62.blocks_ref, bf16[768,768]{1,0:T(8,128)(2,1)S(1)} %bitcast.157, bf16[768,4096]{1,0:T(8,128)(2,1)S(1)} %bitcast.152), custom_call_target="tpu_custom_call" | custom-call | flops 2415919104 | bytes 10616832 | tf_op jit(solution)/shard_map/pallas_call | solution.py:202
  26.5 2.8 %fusion.55 = (f16[768,256]{1,0:T(8,128)(2,1)S(1)}, f16[768,256]{1,0:T(8,128)(2,1)S(1)}, f16[768,256]{1,0:T(8,128)(2,1)S(1)}, f16[768,256]{1,0:T(8,128)(2,1)S(1)}, f16[768,256]{1,0:T(8,128)(2,1)S(1)}) fusion(f32[8,768,256]{2,1,0:T(8,128)} %collective-permute-done, f32[8,768,256]{2,1,0:T(8,128)S(1)} %shard_map.78), kind=kLoop, calls=%fused_computation.68 | loop fusion | flops 2949120 | bytes 9830400 | tf_op jit(solution)/shard_map/convert_element_type | solution.py:265
  29.3 2.8 %collective-permute-start.3 = (f16[768,256]{1,0:T(8,128)(2,1)S(1)}, f16[768,256]{1,0:T(8,128)(2,1)S(1)}, u32[]{:S(2)}, u32[]{:S(2)}) collective-permute-start(f16[768,256]{1,0:T(8,128)(2,1)S(1)} %get-tuple-element.45), channel_id=1, source_target_pairs={{0,2},{1,3},{2,0},{3,1},{4,6},{5,7},{6,4},{7,5},{8,10},{9,11},{10,... | collective-permute-start | bytes 1179656 | tf_op jit(solution)/shard_map/ppermute | solution.py:151
  33.7 10.2 %collective-permute-done.6 = bf16[768,768]{1,0:T(8,128)(2,1)} collective-permute-done((bf16[768,768]{1,0:T(8,128)(2,1)S(1)}, bf16[768,768]{1,0:T(8,128)(2,1)}, u32[]{:S(2)}, u32[]{:S(2)}) %collective-permute-start.6) | collective-permute-done | bytes 1179680 | tf_op jit(solution)/shard_map/ppermute | solution.py:156
  43.9 3.0 %collective-permute-start.5 = (f16[768,256]{1,0:T(8,128)(2,1)S(1)}, f16[768,256]{1,0:T(8,128)(2,1)S(1)}, u32[]{:S(2)}, u32[]{:S(2)}) collective-permute-start(f16[768,256]{1,0:T(8,128)(2,1)S(1)} %get-tuple-element.43), channel_id=1, source_target_pairs={{0,12},{1,13},{2,14},{3,15},{4,0},{5,1},{6,2},{7,3},{8,4},{9,5},{1... | collective-permute-start | bytes 1179656 | tf_op jit(solution)/shard_map/ppermute | solution.py:151
  46.9 3.2 %collective-permute-start.2 = (f16[768,256]{1,0:T(8,128)(2,1)S(1)}, f16[768,256]{1,0:T(8,128)(2,1)S(1)}, u32[]{:S(2)}, u32[]{:S(2)}) collective-permute-start(f16[768,256]{1,0:T(8,128)(2,1)S(1)} %get-tuple-element.46), channel_id=1, source_target_pairs={{0,12},{1,13},{2,14},{3,15},{4,0},{5,1},{6,2},{7,3},{8,4},{9,5},{1... | collective-permute-start | bytes 1179656 | tf_op jit(solution)/shard_map/ppermute | solution.py:151
  50.2 5.7 %collective-permute-done.3 = f16[768,256]{1,0:T(8,128)(2,1)S(1)} collective-permute-done((f16[768,256]{1,0:T(8,128)(2,1)S(1)}, f16[768,256]{1,0:T(8,128)(2,1)S(1)}, u32[]{:S(2)}, u32[]{:S(2)}) %collective-permute-start.3) | collective-permute-done | bytes 393248 | tf_op jit(solution)/shard_map/ppermute | solution.py:151
  58.3 3.1 %collective-permute-start.10 = (f16[768,256]{1,0:T(8,128)(2,1)S(1)}, f16[768,256]{1,0:T(8,128)(2,1)S(1)}, u32[]{:S(2)}, u32[]{:S(2)}) collective-permute-start(f16[768,256]{1,0:T(8,128)(2,1)S(1)} %get-tuple-element.48), channel_id=1, source_target_pairs={{0,2},{1,3},{2,0},{3,1},{4,6},{5,7},{6,4},{7,5},{8,10},{9,11},{10,... | collective-permute-start | bytes 1179656 | tf_op jit(solution)/shard_map/ppermute | solution.py:151
  66.7 5.5 %collective-permute-done.2 = f16[768,256]{1,0:T(8,128)(2,1)S(1)} collective-permute-done((f16[768,256]{1,0:T(8,128)(2,1)S(1)}, f16[768,256]{1,0:T(8,128)(2,1)S(1)}, u32[]{:S(2)}, u32[]{:S(2)}) %collective-permute-start.2) | collective-permute-done | bytes 393248 | tf_op jit(solution)/shard_map/ppermute | solution.py:151
  73.9 3.2 %collective-permute-start.18 = (bf16[768,768]{1,0:T(8,128)(2,1)}, bf16[768,768]{1,0:T(8,128)(2,1)}, u32[]{:S(2)}, u32[]{:S(2)}) collective-permute-start(bf16[768,768]{1,0:T(8,128)(2,1)} %collective-permute-done.8), channel_id=1, source_target_pairs={{0,96},{16,112},{32,0},{48,16},{64,32},{80,48},{96,64},{112,80},{1... | collective-permute-start | bytes 3538952 | tf_op jit(solution)/shard_map/ppermute | solution.py:156
  78.6 3.0 %collective-permute-start.12 = (f32[8,96]{1,0:T(8,128)S(1)}, f32[8,96]{1,0:T(8,128)S(1)}, u32[]{:S(2)}, u32[]{:S(2)}) collective-permute-start(f32[8,96]{1,0:T(8,128)S(1)} %add.566), channel_id=1, source_target_pairs={{0,2},{1,3},{2,0},{3,1},{4,6},{5,7},{6,4},{7,5},{8,10},{9,11},{10,... | collective-permute-start | bytes 9224 | tf_op jit(solution)/shard_map/ppermute | solution.py:151
  85.9 3.2 %collective-permute-start.14 = (f32[8,96]{1,0:T(8,128)S(1)}, f32[8,96]{1,0:T(8,128)S(1)}, u32[]{:S(2)}, u32[]{:S(2)}) collective-permute-start(f32[8,96]{1,0:T(8,128)S(1)} %add.567), channel_id=1, source_target_pairs={{0,8},{1,9},{2,10},{3,11},{4,12},{5,13},{6,14},{7,15},{8,0},{9,1},... | collective-permute-start | bytes 9224 | tf_op jit(solution)/shard_map/ppermute | solution.py:151
  92.7 3.0 %collective-permute-done.16 = bf16[768,768]{1,0:T(8,128)(2,1)} collective-permute-done((bf16[768,768]{1,0:T(8,128)(2,1)S(1)}, bf16[768,768]{1,0:T(8,128)(2,1)}, u32[]{:S(2)}, u32[]{:S(2)}) %collective-permute-start.16) | collective-permute-done | bytes 1179680 | tf_op jit(solution)/shard_map/ppermute | solution.py:156
  95.7 15.8 %shard_map.80 = (f32[8,96,256]{2,1,0:T(8,128)S(1)}, f32[8,1,96]{2,1,0:T(1,128)S(1)}) custom-call(s32[8]{0:T(128)S(1)} %dynamic_slice.34.lens_ref, f32[8]{0:T(128)S(1)} %convert_divide_fusion.weights_ref, f32[2]{0:T(128)S(1)} %copy-done.3, f32[8,96,256]{2,1,0:T(8,128)S(1)} %bitcast.161, f32[8,1,96]{2,1,0:T(1,128)S(1)} %bitcast.163, f32[1,256]{1,0:T(1,128)S(1)} %bitcast.166, ...), custom_call_target="tpu_custom_call" | custom-call | flops 2000000000 | bytes 3000000 | tf_op jit(solution)/shard_map/pallas_call | solution.py:114
  111.5 5.9 %collective-permute-done.17 = bf16[768,768]{1,0:T(8,128)(2,1)} collective-permute-done((bf16[768,768]{1,0:T(8,128)(2,1)}, bf16[768,768]{1,0:T(8,128)(2,1)}, u32[]{:S(2)}, u32[]{:S(2)}) %collective-permute-start.17) | collective-permute-done | bytes 1179680 | tf_op jit(solution)/shard_map/ppermute | solution.py:156
  121.7 3.1 %collective-permute-done.20 = f32[8,96]{1,0:T(8,128)S(1)} collective-permute-done((f32[8,96]{1,0:T(8,128)S(1)}, f32[8,96]{1,0:T(8,128)S(1)}, u32[]{:S(2)}, u32[]{:S(2)}) %collective-permute-start.20) | collective-permute-done | bytes 3104 | tf_op jit(solution)/shard_map/ppermute | solution.py:151
  132.8 14.2 %collective-permute-done.25 = bf16[768,768]{1,0:T(8,128)(2,1)S(1)} collective-permute-done((bf16[768,768]{1,0:T(8,128)(2,1)}, bf16[768,768]{1,0:T(8,128)(2,1)S(1)}, u32[]{:S(2)}, u32[]{:S(2)}) %collective-permute-start.25) | collective-permute-done | bytes 1179680 | tf_op jit(solution)/shard_map/ppermute | solution.py:156
  148.9 9.4 %collective-permute-start.27 = (bf16[768,256]{1,0:T(8,128)(2,1)S(1)}, bf16[768,256]{1,0:T(8,128)(2,1)S(1)}, u32[]{:S(2)}, u32[]{:S(2)}) collective-permute-start(bf16[768,256]{1,0:T(8,128)(2,1)S(1)} %collective-permute-done.24), channel_id=1, source_target_pairs={{0,4},{1,5},{2,6},{3,7},{4,8},{5,9},{6,10},{7,11},{8,12},{9,13},{1... | collective-permute-start | bytes 1179656 | tf_op jit(solution)/shard_map/ppermute | solution.py:151
  161.3 7.6 %collective-permute-start.35 = (bf16[768,256]{1,0:T(8,128)(2,1)S(1)}, bf16[768,256]{1,0:T(8,128)(2,1)S(1)}, u32[]{:S(2)}, u32[]{:S(2)}) collective-permute-start(bf16[768,256]{1,0:T(8,128)(2,1)S(1)} %collective-permute-done.31), channel_id=1, source_target_pairs={{0,4},{1,5},{2,6},{3,7},{4,8},{5,9},{6,10},{7,11},{8,12},{9,13},{1... | collective-permute-start | bytes 1179656 | tf_op jit(solution)/shard_map/ppermute | solution.py:151
  171.9 6.3 %collective-permute-done.33 = bf16[768,256]{1,0:T(8,128)(2,1)S(1)} collective-permute-done((bf16[768,256]{1,0:T(8,128)(2,1)S(1)}, bf16[768,256]{1,0:T(8,128)(2,1)S(1)}, u32[]{:S(2)}, u32[]{:S(2)}) %collective-permute-start.33) | collective-permute-done | bytes 393248 | tf_op jit(solution)/shard_map/ppermute | solution.py:151
  181.9 4.2 %collective-permute-done.35 = bf16[768,256]{1,0:T(8,128)(2,1)S(1)} collective-permute-done((bf16[768,256]{1,0:T(8,128)(2,1)S(1)}, bf16[768,256]{1,0:T(8,128)(2,1)S(1)}, u32[]{:S(2)}, u32[]{:S(2)}) %collective-permute-start.35) | collective-permute-done | bytes 393248 | tf_op jit(solution)/shard_map/ppermute | solution.py:151
  186.7 4.5 %collective-permute-done.39 = bf16[768,256]{1,0:T(8,128)(2,1)S(1)} collective-permute-done((bf16[768,256]{1,0:T(8,128)(2,1)S(1)}, bf16[768,256]{1,0:T(8,128)(2,1)S(1)}, u32[]{:S(2)}, u32[]{:S(2)}) %collective-permute-start.39) | collective-permute-done | bytes 393248 | tf_op jit(solution)/shard_map/ppermute | solution.py:151
  213.9 3.9 %constant_dynamic-update-slice_fusion.7 = (bf16[768,4096]{1,0:T(8,128)(2,1)}, bf16[768,512]{1,0:T(8,128)(2,1)S(1)}, f32[768,512]{1,0:T(8,128)}) fusion(bf16[768,4096]{1,0:T(8,128)(2,1)} %shard_map.81, s32[]{:T(128)S(6)} %select_n.345, bf16[768,4096]{1,0:T(8,128)(2,1)} %bitcast.150, s32[]{:T(128)S(6)} %select_n.342, f32[768,512]{1,0:T(8,128)S(1)} %fusion.32, ...), kind=kOutput, calls=%fused_computation.97 | convolution fusion | flops 608305152 | bytes 16908300 | tf_op jit(solution)/shard_map/dot_general | solution.py:331
  217.8 2.9 %collective-permute-start.41 = (bf16[768,512]{1,0:T(8,128)(2,1)S(1)}, bf16[768,512]{1,0:T(8,128)(2,1)S(1)}, u32[]{:S(2)}, u32[]{:S(2)}) collective-permute-start(bf16[768,512]{1,0:T(8,128)(2,1)S(1)} %get-tuple-element.41), channel_id=1, source_target_pairs={{0,32},{16,48},{32,64},{48,80},{64,96},{80,112},{96,0},{112,16},{1... | collective-permute-start | bytes 2359304 | tf_op jit(solution)/shard_map/ppermute | solution.py:156
  222.7 18.0 %collective-permute-done.41 = bf16[768,512]{1,0:T(8,128)(2,1)S(1)} collective-permute-done((bf16[768,512]{1,0:T(8,128)(2,1)S(1)}, bf16[768,512]{1,0:T(8,128)(2,1)S(1)}, u32[]{:S(2)}, u32[]{:S(2)}) %collective-permute-start.41) | collective-permute-done | bytes 786464 | tf_op jit(solution)/shard_map/ppermute | solution.py:156
  241.5 3.2 %collective-permute-start.45 = (bf16[384,512]{1,0:T(8,128)(2,1)}, bf16[384,512]{1,0:T(8,128)(2,1)S(1)}, u32[]{:S(2)}, u32[]{:S(2)}) collective-permute-start(bf16[384,512]{1,0:T(8,128)(2,1)} %slice.93), channel_id=1, source_target_pairs={{0,96},{16,112},{32,0},{48,16},{64,32},{80,48},{96,64},{112,80},{1... | collective-permute-start | bytes 1179656 | tf_op jit(solution)/shard_map/ppermute | solution.py:156
  244.8 3.2 %collective-permute-start.47 = (bf16[768,512]{1,0:T(8,128)(2,1)S(1)}, bf16[768,512]{1,0:T(8,128)(2,1)S(1)}, u32[]{:S(2)}, u32[]{:S(2)}) collective-permute-start(bf16[768,512]{1,0:T(8,128)(2,1)S(1)} %collective-permute-done.43), channel_id=1, source_target_pairs={{0,96},{16,112},{32,0},{48,16},{64,32},{80,48},{96,64},{112,80},{1... | collective-permute-start | bytes 2359304 | tf_op jit(solution)/shard_map/ppermute | solution.py:156
  248.0 5.9 %collective-permute-done.44 = bf16[384,512]{1,0:T(8,128)(2,1)S(1)} collective-permute-done((bf16[384,512]{1,0:T(8,128)(2,1)S(1)}, bf16[384,512]{1,0:T(8,128)(2,1)S(1)}, u32[]{:S(2)}, u32[]{:S(2)}) %collective-permute-start.44) | collective-permute-done | bytes 393248 | tf_op jit(solution)/shard_map/ppermute | solution.py:156
  259.3 10.5 %collective-permute-done.46 = bf16[768,512]{1,0:T(8,128)(2,1)} collective-permute-done((bf16[768,512]{1,0:T(8,128)(2,1)S(1)}, bf16[768,512]{1,0:T(8,128)(2,1)}, u32[]{:S(2)}, u32[]{:S(2)}) %collective-permute-start.46) | collective-permute-done | bytes 786464 | tf_op jit(solution)/shard_map/ppermute | solution.py:156
  (145 shorter events, 87.9 us)
Async XLA Ops:
  13.0 13.4 %collective-permute-start = (f32[8,768,256]{2,1,0:T(8,128)}, f32[8,768,256]{2,1,0:T(8,128)}, u32[]{:S(2)}, u32[]{:S(2)}) collective-permute-start(f32[8,768,256]{2,1,0:T(8,128)} %shard_map.79), channel_id=1, source_target_pairs={{0,1},{1,0},{2,3},{3,2},{4,5},{5,4},{6,7},{7,6},{8,9},{9,8},{10,11... | collective-permute-start | bytes 18874376 | tf_op jit(solution)/shard_map/ppermute | solution.py:151
  13.0 30.9 %collective-permute-start.6 = (bf16[768,768]{1,0:T(8,128)(2,1)S(1)}, bf16[768,768]{1,0:T(8,128)(2,1)}, u32[]{:S(2)}, u32[]{:S(2)}) collective-permute-start(bf16[768,768]{1,0:T(8,128)(2,1)S(1)} %bitcast.154), channel_id=1, source_target_pairs={{0,32},{16,48},{32,64},{48,80},{64,96},{80,112},{96,0},{112,16},{1... | collective-permute-start | bytes 3538952 | tf_op jit(solution)/shard_map/ppermute | solution.py:156
  15.0 31.9 %collective-permute-start.7 = (bf16[768,768]{1,0:T(8,128)(2,1)S(1)}, bf16[768,768]{1,0:T(8,128)(2,1)}, u32[]{:S(2)}, u32[]{:S(2)}) collective-permute-start(bf16[768,768]{1,0:T(8,128)(2,1)S(1)} %bitcast.155), channel_id=1, source_target_pairs={{0,96},{16,112},{32,0},{48,16},{64,32},{80,48},{96,64},{112,80},{1... | collective-permute-start | bytes 3538952 | tf_op jit(solution)/shard_map/ppermute | solution.py:156
  17.2 29.8 %collective-permute-start.8 = (bf16[768,768]{1,0:T(8,128)(2,1)S(1)}, bf16[768,768]{1,0:T(8,128)(2,1)}, u32[]{:S(2)}, u32[]{:S(2)}) collective-permute-start(bf16[768,768]{1,0:T(8,128)(2,1)S(1)} %bitcast.156), channel_id=1, source_target_pairs={{0,16},{16,0},{32,48},{48,32},{64,80},{80,64},{96,112},{112,96},{1... | collective-permute-start | bytes 3538952 | tf_op jit(solution)/shard_map/ppermute | solution.py:156
  29.3 26.6 %collective-permute-start.3 = (f16[768,256]{1,0:T(8,128)(2,1)S(1)}, f16[768,256]{1,0:T(8,128)(2,1)S(1)}, u32[]{:S(2)}, u32[]{:S(2)}) collective-permute-start(f16[768,256]{1,0:T(8,128)(2,1)S(1)} %get-tuple-element.45), channel_id=1, source_target_pairs={{0,2},{1,3},{2,0},{3,1},{4,6},{5,7},{6,4},{7,5},{8,10},{9,11},{10,... | collective-permute-start | bytes 1179656 | tf_op jit(solution)/shard_map/ppermute | solution.py:151
  32.1 23.8 %collective-permute-start.4 = (f16[768,256]{1,0:T(8,128)(2,1)S(1)}, f16[768,256]{1,0:T(8,128)(2,1)S(1)}, u32[]{:S(2)}, u32[]{:S(2)}) collective-permute-start(f16[768,256]{1,0:T(8,128)(2,1)S(1)} %get-tuple-element.44), channel_id=1, source_target_pairs={{0,4},{1,5},{2,6},{3,7},{4,8},{5,9},{6,10},{7,11},{8,12},{9,13},{1... | collective-permute-start | bytes 1179656 | tf_op jit(solution)/shard_map/ppermute | solution.py:151
  43.9 12.5 %collective-permute-start.5 = (f16[768,256]{1,0:T(8,128)(2,1)S(1)}, f16[768,256]{1,0:T(8,128)(2,1)S(1)}, u32[]{:S(2)}, u32[]{:S(2)}) collective-permute-start(f16[768,256]{1,0:T(8,128)(2,1)S(1)} %get-tuple-element.43), channel_id=1, source_target_pairs={{0,12},{1,13},{2,14},{3,15},{4,0},{5,1},{6,2},{7,3},{8,4},{9,5},{1... | collective-permute-start | bytes 1179656 | tf_op jit(solution)/shard_map/ppermute | solution.py:151
  46.9 19.8 %collective-permute-start.1 = (f16[768,256]{1,0:T(8,128)(2,1)S(1)}, f16[768,256]{1,0:T(8,128)(2,1)S(1)}, u32[]{:S(2)}, u32[]{:S(2)}) collective-permute-start(f16[768,256]{1,0:T(8,128)(2,1)S(1)} %get-tuple-element.42), channel_id=1, source_target_pairs={{0,4},{1,5},{2,6},{3,7},{4,8},{5,9},{6,10},{7,11},{8,12},{9,13},{1... | collective-permute-start | bytes 1179656 | tf_op jit(solution)/shard_map/ppermute | solution.py:151
  46.9 25.3 %collective-permute-start.2 = (f16[768,256]{1,0:T(8,128)(2,1)S(1)}, f16[768,256]{1,0:T(8,128)(2,1)S(1)}, u32[]{:S(2)}, u32[]{:S(2)}) collective-permute-start(f16[768,256]{1,0:T(8,128)(2,1)S(1)} %get-tuple-element.46), channel_id=1, source_target_pairs={{0,12},{1,13},{2,14},{3,15},{4,0},{5,1},{6,2},{7,3},{8,4},{9,5},{1... | collective-permute-start | bytes 1179656 | tf_op jit(solution)/shard_map/ppermute | solution.py:151
  58.3 14.0 %collective-permute-start.10 = (f16[768,256]{1,0:T(8,128)(2,1)S(1)}, f16[768,256]{1,0:T(8,128)(2,1)S(1)}, u32[]{:S(2)}, u32[]{:S(2)}) collective-permute-start(f16[768,256]{1,0:T(8,128)(2,1)S(1)} %get-tuple-element.48), channel_id=1, source_target_pairs={{0,2},{1,3},{2,0},{3,1},{4,6},{5,7},{6,4},{7,5},{8,10},{9,11},{10,... | collective-permute-start | bytes 1179656 | tf_op jit(solution)/shard_map/ppermute | solution.py:151
  65.1 30.6 %collective-permute-start.16 = (bf16[768,768]{1,0:T(8,128)(2,1)S(1)}, bf16[768,768]{1,0:T(8,128)(2,1)}, u32[]{:S(2)}, u32[]{:S(2)}) collective-permute-start(bf16[768,768]{1,0:T(8,128)(2,1)S(1)} %bitcast.158), channel_id=1, source_target_pairs={{0,64},{16,80},{32,96},{48,112},{64,0},{80,16},{96,32},{112,48},{1... | collective-permute-start | bytes 3538952 | tf_op jit(solution)/shard_map/ppermute | solution.py:156
  73.8 43.5 %collective-permute-start.17 = (bf16[768,768]{1,0:T(8,128)(2,1)}, bf16[768,768]{1,0:T(8,128)(2,1)}, u32[]{:S(2)}, u32[]{:S(2)}) collective-permute-start(bf16[768,768]{1,0:T(8,128)(2,1)} %collective-permute-done.8), channel_id=1, source_target_pairs={{0,32},{16,48},{32,64},{48,80},{64,96},{80,112},{96,0},{112,16},{1... | collective-permute-start | bytes 3538952 | tf_op jit(solution)/shard_map/ppermute | solution.py:156
  73.9 43.4 %collective-permute-start.18 = (bf16[768,768]{1,0:T(8,128)(2,1)}, bf16[768,768]{1,0:T(8,128)(2,1)}, u32[]{:S(2)}, u32[]{:S(2)}) collective-permute-start(bf16[768,768]{1,0:T(8,128)(2,1)} %collective-permute-done.8), channel_id=1, source_target_pairs={{0,96},{16,112},{32,0},{48,16},{64,32},{80,48},{96,64},{112,80},{1... | collective-permute-start | bytes 3538952 | tf_op jit(solution)/shard_map/ppermute | solution.py:156
  117.4 29.6 %collective-permute-start.25 = (bf16[768,768]{1,0:T(8,128)(2,1)}, bf16[768,768]{1,0:T(8,128)(2,1)S(1)}, u32[]{:S(2)}, u32[]{:S(2)}) collective-permute-start(bf16[768,768]{1,0:T(8,128)(2,1)} %collective-permute-done.8), channel_id=1, source_target_pairs={{0,64},{16,80},{32,96},{48,112},{64,0},{80,16},{96,32},{112,48},{1... | collective-permute-start | bytes 3538952 | tf_op jit(solution)/shard_map/ppermute | solution.py:156
  147.0 14.4 %collective-permute-start.31 = (bf16[768,256]{1,0:T(8,128)(2,1)S(1)}, bf16[768,256]{1,0:T(8,128)(2,1)S(1)}, u32[]{:S(2)}, u32[]{:S(2)}) collective-permute-start(bf16[768,256]{1,0:T(8,128)(2,1)S(1)} %collective-permute-done.24), channel_id=1, source_target_pairs={{0,2},{1,3},{2,0},{3,1},{4,6},{5,7},{6,4},{7,5},{8,10},{9,11},{10,... | collective-permute-start | bytes 1179656 | tf_op jit(solution)/shard_map/ppermute | solution.py:151
  148.9 12.5 %collective-permute-start.26 = (bf16[768,256]{1,0:T(8,128)(2,1)S(1)}, bf16[768,256]{1,0:T(8,128)(2,1)S(1)}, u32[]{:S(2)}, u32[]{:S(2)}) collective-permute-start(bf16[768,256]{1,0:T(8,128)(2,1)S(1)} %collective-permute-done.24), channel_id=1, source_target_pairs={{0,1},{1,0},{2,3},{3,2},{4,5},{5,4},{6,7},{7,6},{8,9},{9,8},{10,11... | collective-permute-start | bytes 1179656 | tf_op jit(solution)/shard_map/ppermute | solution.py:151
  148.9 20.1 %collective-permute-start.27 = (bf16[768,256]{1,0:T(8,128)(2,1)S(1)}, bf16[768,256]{1,0:T(8,128)(2,1)S(1)}, u32[]{:S(2)}, u32[]{:S(2)}) collective-permute-start(bf16[768,256]{1,0:T(8,128)(2,1)S(1)} %collective-permute-done.24), channel_id=1, source_target_pairs={{0,4},{1,5},{2,6},{3,7},{4,8},{5,9},{6,10},{7,11},{8,12},{9,13},{1... | collective-permute-start | bytes 1179656 | tf_op jit(solution)/shard_map/ppermute | solution.py:151
  158.3 12.5 %collective-permute-start.29 = (bf16[768,256]{1,0:T(8,128)(2,1)S(1)}, bf16[768,256]{1,0:T(8,128)(2,1)S(1)}, u32[]{:S(2)}, u32[]{:S(2)}) collective-permute-start(bf16[768,256]{1,0:T(8,128)(2,1)S(1)} %collective-permute-done.24), channel_id=1, source_target_pairs={{0,12},{1,13},{2,14},{3,15},{4,0},{5,1},{6,2},{7,3},{8,4},{9,5},{1... | collective-permute-start | bytes 1179656 | tf_op jit(solution)/shard_map/ppermute | solution.py:151
  158.7 19.5 %collective-permute-start.33 = (bf16[768,256]{1,0:T(8,128)(2,1)S(1)}, bf16[768,256]{1,0:T(8,128)(2,1)S(1)}, u32[]{:S(2)}, u32[]{:S(2)}) collective-permute-start(bf16[768,256]{1,0:T(8,128)(2,1)S(1)} %collective-permute-done.24), channel_id=1, source_target_pairs={{0,8},{1,9},{2,10},{3,11},{4,12},{5,13},{6,14},{7,15},{8,0},{9,1},... | collective-permute-start | bytes 1179656 | tf_op jit(solution)/shard_map/ppermute | solution.py:151
  161.3 31.5 %collective-permute-start.32 = (bf16[768,256]{1,0:T(8,128)(2,1)S(1)}, bf16[768,256]{1,0:T(8,128)(2,1)S(1)}, u32[]{:S(2)}, u32[]{:S(2)}) collective-permute-start(bf16[768,256]{1,0:T(8,128)(2,1)S(1)} %collective-permute-done.31), channel_id=1, source_target_pairs={{0,1},{1,0},{2,3},{3,2},{4,5},{5,4},{6,7},{7,6},{8,9},{9,8},{10,11... | collective-permute-start | bytes 1179656 | tf_op jit(solution)/shard_map/ppermute | solution.py:151
  161.3 24.8 %collective-permute-start.35 = (bf16[768,256]{1,0:T(8,128)(2,1)S(1)}, bf16[768,256]{1,0:T(8,128)(2,1)S(1)}, u32[]{:S(2)}, u32[]{:S(2)}) collective-permute-start(bf16[768,256]{1,0:T(8,128)(2,1)S(1)} %collective-permute-done.31), channel_id=1, source_target_pairs={{0,4},{1,5},{2,6},{3,7},{4,8},{5,9},{6,10},{7,11},{8,12},{9,13},{1... | collective-permute-start | bytes 1179656 | tf_op jit(solution)/shard_map/ppermute | solution.py:151
  170.8 15.6 %collective-permute-start.37 = (bf16[768,256]{1,0:T(8,128)(2,1)S(1)}, bf16[768,256]{1,0:T(8,128)(2,1)S(1)}, u32[]{:S(2)}, u32[]{:S(2)}) collective-permute-start(bf16[768,256]{1,0:T(8,128)(2,1)S(1)} %collective-permute-done.31), channel_id=1, source_target_pairs={{0,12},{1,13},{2,14},{3,15},{4,0},{5,1},{6,2},{7,3},{8,4},{9,5},{1... | collective-permute-start | bytes 1179656 | tf_op jit(solution)/shard_map/ppermute | solution.py:151
  178.2 13.0 %collective-permute-start.39 = (bf16[768,256]{1,0:T(8,128)(2,1)S(1)}, bf16[768,256]{1,0:T(8,128)(2,1)S(1)}, u32[]{:S(2)}, u32[]{:S(2)}) collective-permute-start(bf16[768,256]{1,0:T(8,128)(2,1)S(1)} %collective-permute-done.33), channel_id=1, source_target_pairs={{0,2},{1,3},{2,0},{3,1},{4,6},{5,7},{6,4},{7,5},{8,10},{9,11},{10,... | collective-permute-start | bytes 1179656 | tf_op jit(solution)/shard_map/ppermute | solution.py:151
  181.7 12.7 %collective-permute-start.34 = (bf16[768,256]{1,0:T(8,128)(2,1)S(1)}, bf16[768,256]{1,0:T(8,128)(2,1)S(1)}, u32[]{:S(2)}, u32[]{:S(2)}) collective-permute-start(bf16[768,256]{1,0:T(8,128)(2,1)S(1)} %collective-permute-done.33), channel_id=1, source_target_pairs={{0,1},{1,0},{2,3},{3,2},{4,5},{5,4},{6,7},{7,6},{8,9},{9,8},{10,11... | collective-permute-start | bytes 1179656 | tf_op jit(solution)/shard_map/ppermute | solution.py:151
  217.8 22.9 %collective-permute-start.41 = (bf16[768,512]{1,0:T(8,128)(2,1)S(1)}, bf16[768,512]{1,0:T(8,128)(2,1)S(1)}, u32[]{:S(2)}, u32[]{:S(2)}) collective-permute-start(bf16[768,512]{1,0:T(8,128)(2,1)S(1)} %get-tuple-element.41), channel_id=1, source_target_pairs={{0,32},{16,48},{32,64},{48,80},{64,96},{80,112},{96,0},{112,16},{1... | collective-permute-start | bytes 2359304 | tf_op jit(solution)/shard_map/ppermute | solution.py:156
  220.7 20.1 %collective-permute-start.42 = (bf16[768,512]{1,0:T(8,128)(2,1)S(1)}, bf16[768,512]{1,0:T(8,128)(2,1)S(1)}, u32[]{:S(2)}, u32[]{:S(2)}) collective-permute-start(bf16[768,512]{1,0:T(8,128)(2,1)S(1)} %get-tuple-element.41), channel_id=1, source_target_pairs={{0,96},{16,112},{32,0},{48,16},{64,32},{80,48},{96,64},{112,80},{1... | collective-permute-start | bytes 2359304 | tf_op jit(solution)/shard_map/ppermute | solution.py:156
  222.4 22.3 %collective-permute-start.43 = (bf16[768,512]{1,0:T(8,128)(2,1)S(1)}, bf16[768,512]{1,0:T(8,128)(2,1)S(1)}, u32[]{:S(2)}, u32[]{:S(2)}) collective-permute-start(bf16[768,512]{1,0:T(8,128)(2,1)S(1)} %get-tuple-element.41), channel_id=1, source_target_pairs={{0,16},{16,0},{32,48},{48,32},{64,80},{80,64},{96,112},{112,96},{1... | collective-permute-start | bytes 2359304 | tf_op jit(solution)/shard_map/ppermute | solution.py:156
  240.7 13.3 %collective-permute-start.44 = (bf16[384,512]{1,0:T(8,128)(2,1)S(1)}, bf16[384,512]{1,0:T(8,128)(2,1)S(1)}, u32[]{:S(2)}, u32[]{:S(2)}) collective-permute-start(bf16[384,512]{1,0:T(8,128)(2,1)S(1)} %slice.92), channel_id=1, source_target_pairs={{0,32},{16,48},{32,64},{48,80},{64,96},{80,112},{96,0},{112,16},{1... | collective-permute-start | bytes 1179656 | tf_op jit(solution)/shard_map/ppermute | solution.py:156
  241.5 13.1 %collective-permute-start.45 = (bf16[384,512]{1,0:T(8,128)(2,1)}, bf16[384,512]{1,0:T(8,128)(2,1)S(1)}, u32[]{:S(2)}, u32[]{:S(2)}) collective-permute-start(bf16[384,512]{1,0:T(8,128)(2,1)} %slice.93), channel_id=1, source_target_pairs={{0,96},{16,112},{32,0},{48,16},{64,32},{80,48},{96,64},{112,80},{1... | collective-permute-start | bytes 1179656 | tf_op jit(solution)/shard_map/ppermute | solution.py:156
  244.8 25.1 %collective-permute-start.46 = (bf16[768,512]{1,0:T(8,128)(2,1)S(1)}, bf16[768,512]{1,0:T(8,128)(2,1)}, u32[]{:S(2)}, u32[]{:S(2)}) collective-permute-start(bf16[768,512]{1,0:T(8,128)(2,1)S(1)} %collective-permute-done.43), channel_id=1, source_target_pairs={{0,32},{16,48},{32,64},{48,80},{64,96},{80,112},{96,0},{112,16},{1... | collective-permute-start | bytes 2359304 | tf_op jit(solution)/shard_map/ppermute | solution.py:156
  244.8 27.2 %collective-permute-start.47 = (bf16[768,512]{1,0:T(8,128)(2,1)S(1)}, bf16[768,512]{1,0:T(8,128)(2,1)S(1)}, u32[]{:S(2)}, u32[]{:S(2)}) collective-permute-start(bf16[768,512]{1,0:T(8,128)(2,1)S(1)} %collective-permute-done.43), channel_id=1, source_target_pairs={{0,96},{16,112},{32,0},{48,16},{64,32},{80,48},{96,64},{112,80},{1... | collective-permute-start | bytes 2359304 | tf_op jit(solution)/shard_map/ppermute | solution.py:156
  254.7 18.2 %collective-permute-start.48 = (bf16[768,512]{1,0:T(8,128)(2,1)S(1)}, bf16[768,512]{1,0:T(8,128)(2,1)S(1)}, u32[]{:S(2)}, u32[]{:S(2)}) collective-permute-start(bf16[768,512]{1,0:T(8,128)(2,1)S(1)} %pad_maximum_fusion), channel_id=1, source_target_pairs={{0,16},{16,0},{32,48},{48,32},{64,80},{80,64},{96,112},{112,96},{1... | collective-permute-start | bytes 2359304 | tf_op jit(solution)/shard_map/ppermute | solution.py:156
  (26 other events, 346.0 us)

commit v3 on v1

--- a/solution.py
+++ b/solution.py
@@ -221,9 +221,8 @@
 
 
 def sum_over_tr(value):
-    value = value + to_sibling(value)
-    value = value + to_chip(value, 0, 1)
-    return value + to_chip(value, 1, 0) + to_chip(value, 2, 0) + to_chip(value, 3, 0)
+    value = value + to_sibling(value) + to_chip(value, 0, 1) + to_chip(value, 0, 1, 1)
+    return value + to_chip(value, 1, 0) + to_chip(value, 3, 0) + to_chip(value, 2, 0)
 
 
 def per_device(taps, routes, lengths, merge_weight, norm_gain, head_scale):
@@ -287,6 +286,8 @@
     squares, rows_across = lax.optimization_barrier((squares, rows_across))
     taps_across = gather_taps(rows_across)
 
+    squares, taps_here = lax.optimization_barrier((squares, taps_here))
+
     scaled, crossed = attention(
         lens,
         weights,
@@ -319,18 +320,19 @@
     own_half = gather(turned, to_chip)
     other_half = {k: to_sibling(v) for k, v in own_half.items()}
 
-    all_rows = buffer((2, RING * slots * span, flat_in), bf16)
-    all_rows = lax.dynamic_update_slice(all_rows, taps_here[None], (0, 0, 0))
-    all_rows = lax.dynamic_update_slice(all_rows, taps_across[None], (1, 0, 0))
-    all_rows = all_rows.reshape(2 * RING, slots * span, flat_in)
-
     def gradient(half):
         total = None
-        for (a, b), piece in half.items():
-            place = (x_low + x_high - b) % 2 * RING + (y - a - z) % RING
-            source = lax.dynamic_index_in_dim(all_rows, place, 0, keepdims=False)
-            part = lax.dot_general(source, piece, COLS_COLS, preferred_element_type=f32)
-            total = part if total is None else total + part
+        same = x_low == x_high
+        for a in (0, 1, 3, 2):
+            straight, crossed = half[a, 0], half[a, 1]
+            for taps_of, piece in (
+                (taps_here, jnp.where(same, straight, crossed)),
+                (taps_across, jnp.where(same, crossed, straight)),
+            ):
+                at_z = (y - a - z) % RING
+                source = lax.dynamic_slice_in_dim(taps_of, at_z * slots * span, slots * span, 0)
+                part = lax.dot_general(source, piece, COLS_COLS, preferred_element_type=f32)
+                total = part if total is None else total + part
         return total
 
     grad = buffer((flat_in, block), f32)

time: 257 us -> 273 us (1.062)
  matrix products: 13.5 us -> 24.2 us
  local copies, waits for them, and re-layouts: 36.7 us -> 28.6 us
  waiting for transfers between devices: 80.4 us -> 88 us
  starting transfers between devices: 67.6 us -> 73.4 us
    dot_general x16, matrix products: 13.5 us -> 24.2 us  [gradient(): part = lax.dot_general(source, piece, COLS_COLS, preferred_element_type=f32)]
    ppermute x34 -> x36, waiting for transfers between devices: 50 us -> 59.7 us  [to_chip(): return lax.ppermute(value, 'tr', pairs)]
    dynamic_update_slice x2 -> x0, local copies, waits for them, and re-layouts: 9.63 us -> none  [the longest x1 4.82 us: per_device(): all_rows = lax.dynamic_update_slice(all_rows, taps_across[None], (1, 0, 0))]
    ppermute x34 -> x36, starting transfers between devices: 53.7 us -> 56.8 us  [to_chip(): return lax.ppermute(value, 'tr', pairs)]
    ppermute x9, starting transfers between devices: 13.1 us -> 15.8 us  [to_group(): return lax.ppermute(value, 'rep', pairs)]
    unnamed x33 -> x57, local copies, waits for them, and re-layouts: 11.4 us -> 12.9 us
  transfers between devices with their start and end apart: 46 -> 48, of which waited for: 19 -> 22; matrix products, arithmetic and copies ran while one was open for 18% -> 16% of each run, Pallas kernels for 10% -> 10%
where the time goes in v3:
time: 273 us; the launch traced here: 271 us
  waiting for transfers between devices  88 us (32%)
  starting transfers between devices  73.4 us (27%)
  Pallas kernels  29.5 us (11%)
  local copies, waits for them, and re-layouts  28.6 us (10%)
  matrix products  24.2 us (9%)
  between operations  15 us (5%)
  other arithmetic  12.8 us (5%)
    ppermute x36, waiting for transfers between devices, to_chip(): return lax.ppermute(value, 'tr', pairs)  59.7 us
    ppermute x36, starting transfers between devices, to_chip(): return lax.ppermute(value, 'tr', pairs)  56.8 us
    ppermute x9, waiting for transfers between devices, to_group(): return lax.ppermute(value, 'rep', pairs)  28.3 us
    dot_general x16, matrix products, gradient(): part = lax.dot_general(source, piece, COLS_COLS, preferred_element_type=f32)  24.2 us
    ppermute x9, starting transfers between devices, to_group(): return lax.ppermute(value, 'rep', pairs)  15.8 us
    pallas_call x1, Pallas kernels, attention(): pl.pallas_call(attention_kernel, grid=(count // slots,), in_specs=[scalar...  15.8 us
    pallas_call x4, Pallas kernels, products(): pl.pallas_call(product_kernel, grid_spec=pltpu.PrefetchScalarGridSpec(num...  13.7 us
    unnamed x57, local copies, waits for them, and re-layouts  12.9 us
  transfers between devices with their start and end apart: 48, of which 22 were waited for; matrix products, arithmetic and copies ran while one was open for 16% of the time, Pallas kernels for 10%

profile of v3, /device:TPU:0, one launch (start us, length us, event | category | flops | bytes accessed | tf_op | source)
XLA Modules:
  0.0 271.4 jit_solution(3013532692255843467)
XLA Ops:
  7.3 2.3 copy.16
  10.0 3.1 %copy-done = bf16[3,256,4096]{2,1,0:T(8,128)(2,1)S(1)} copy-done((bf16[3,256,4096]{2,1,0:T(8,128)(2,1)S(1)}, bf16[3,256,4096]{2,1,0:T(8,128)(2,1)}, u32[]{:S(2)}) %copy-start) | copy-done | bytes 6291480
  13.1 3.4 %shard_map.79 = f32[3,768,256]{2,1,0:T(8,128)} custom-call(s32[3]{0:T(128)S(1)} %pad_add_fusion.1.blocks_ref, bf16[768,768]{1,0:T(8,128)(2,1)S(1)} %bitcast.78, bf16[768,4096]{1,0:T(8,128)(2,1)S(1)} %bitcast.72), custom_call_target="tpu_custom_call" | custom-call | flops 905969664 | bytes 4718592 | tf_op jit(solution)/shard_map/pallas_call | solution.py:202
  16.9 2.8 %copy-done.1 = bf16[3,256,4096]{2,1,0:T(8,128)(2,1)S(1)} copy-done((bf16[3,256,4096]{2,1,0:T(8,128)(2,1)S(1)}, bf16[3,256,4096]{2,1,0:T(8,128)(2,1)}, u32[]{:S(2)}) %copy-start.1) | copy-done | bytes 6291480
  20.9 2.2 shard_map.78
  23.2 3.0 %fusion.68 = (f16[768,256]{1,0:T(8,128)(2,1)}, f16[768,256]{1,0:T(8,128)(2,1)}, f16[768,256]{1,0:T(8,128)(2,1)}) fusion(f32[3,768,256]{2,1,0:T(8,128)} %collective-permute-done, f32[3,768,256]{2,1,0:T(8,128)S(1)} %shard_map.78), kind=kLoop, calls=%fused_computation.84 | loop fusion | flops 1769472 | bytes 5898240 | tf_op jit(solution)/shard_map/convert_element_type | solution.py:271
  26.2 4.8 %shard_map.81 = f32[5,768,256]{2,1,0:T(8,128)} custom-call(s32[5]{0:T(128)S(1)} %stack.79.blocks_ref, bf16[768,768]{1,0:T(8,128)(2,1)S(1)} %bitcast.81, bf16[768,4096]{1,0:T(8,128)(2,1)S(1)} %bitcast.76), custom_call_target="tpu_custom_call" | custom-call | flops 1509949440 | bytes 7077888 | tf_op jit(solution)/shard_map/pallas_call | solution.py:202
  31.5 3.1 %collective-permute-start.4 = (f16[768,256]{1,0:T(8,128)(2,1)}, f16[768,256]{1,0:T(8,128)(2,1)S(1)}, u32[]{:S(2)}, u32[]{:S(2)}) collective-permute-start(f16[768,256]{1,0:T(8,128)(2,1)} %get-tuple-element.15), channel_id=1, source_target_pairs={{0,2},{1,3},{2,0},{3,1},{4,6},{5,7},{6,4},{7,5},{8,10},{9,11},{10,... | collective-permute-start | bytes 1179656 | tf_op jit(solution)/shard_map/ppermute | solution.py:151
  34.6 3.0 %collective-permute-start.7 = (f16[768,256]{1,0:T(8,128)(2,1)}, f16[768,256]{1,0:T(8,128)(2,1)S(1)}, u32[]{:S(2)}, u32[]{:S(2)}) collective-permute-start(f16[768,256]{1,0:T(8,128)(2,1)} %get-tuple-element.18), channel_id=1, source_target_pairs={{0,12},{1,13},{2,14},{3,15},{4,0},{5,1},{6,2},{7,3},{8,4},{9,5},{1... | collective-permute-start | bytes 1179656 | tf_op jit(solution)/shard_map/ppermute | solution.py:151
  37.8 2.9 %copy-done.2 = bf16[3,256,4096]{2,1,0:T(8,128)(2,1)S(1)} copy-done((bf16[3,256,4096]{2,1,0:T(8,128)(2,1)S(1)}, bf16[3,256,4096]{2,1,0:T(8,128)(2,1)}, u32[]{:S(2)}) %copy-start.2) | copy-done | bytes 6291480
  40.6 3.3 %shard_map.80 = f32[5,768,256]{2,1,0:T(8,128)S(1)} custom-call(s32[5]{0:T(128)S(1)} %stack.65.blocks_ref, bf16[768,768]{1,0:T(8,128)(2,1)S(1)} %bitcast.82, bf16[768,4096]{1,0:T(8,128)(2,1)S(1)} %bitcast.77), custom_call_target="tpu_custom_call" | custom-call | flops 1509949440 | bytes 7077888 | tf_op jit(solution)/shard_map/pallas_call | solution.py:202
  46.2 3.4 %collective-permute-done.6 = f16[768,256]{1,0:T(8,128)(2,1)} collective-permute-done((f16[768,256]{1,0:T(8,128)(2,1)}, f16[768,256]{1,0:T(8,128)(2,1)}, u32[]{:S(2)}, u32[]{:S(2)}) %collective-permute-start.6) | collective-permute-done | bytes 393248 | tf_op jit(solution)/shard_map/ppermute | solution.py:151
  57.6 24.4 %collective-permute-done.8 = f16[768,256]{1,0:T(8,128)(2,1)S(1)} collective-permute-done((f16[768,256]{1,0:T(8,128)(2,1)S(1)}, f16[768,256]{1,0:T(8,128)(2,1)S(1)}, u32[]{:S(2)}, u32[]{:S(2)}) %collective-permute-start.8) | collective-permute-done | bytes 393248 | tf_op jit(solution)/shard_map/ppermute | solution.py:151
  88.9 3.3 %collective-permute-start.14 = (f32[8,96]{1,0:T(8,128)S(1)}, f32[8,96]{1,0:T(8,128)S(1)}, u32[]{:S(2)}, u32[]{:S(2)}) collective-permute-start(f32[8,96]{1,0:T(8,128)S(1)} %add_add_fusion.2), channel_id=1, source_target_pairs={{0,8},{1,9},{2,10},{3,11},{4,12},{5,13},{6,14},{7,15},{8,0},{9,1},... | collective-permute-start | bytes 9224 | tf_op jit(solution)/shard_map/ppermute | solution.py:151
  95.8 2.3 collective-permute-done.12
  100.6 15.8 %shard_map.82 = (f32[8,96,256]{2,1,0:T(8,128)S(1)}, f32[8,1,96]{2,1,0:T(1,128)S(1)}) custom-call(s32[8]{0:T(128)S(1)} %dynamic_slice.42.lens_ref, f32[8]{0:T(128)S(1)} %convert_divide_fusion.weights_ref, f32[2]{0:T(128)S(1)} %copy-done.7, f32[8,96,256]{2,1,0:T(8,128)S(1)} %bitcast.84, f32[8,1,96]{2,1,0:T(1,128)S(1)} %bitcast.86, f32[1,256]{1,0:T(1,128)S(1)} %bitcast.91, ...), custom_call_target="tpu_custom_call" | custom-call | flops 2000000000 | bytes 3000000 | tf_op jit(solution)/shard_map/pallas_call | solution.py:114
  124.4 2.6 collective-permute-done.21
  130.2 22.2 %collective-permute-start.28 = (bf16[768,256]{1,0:T(8,128)(2,1)S(1)}, bf16[768,256]{1,0:T(8,128)(2,1)S(1)}, u32[]{:S(2)}, u32[]{:S(2)}) collective-permute-start(bf16[768,256]{1,0:T(8,128)(2,1)S(1)} %collective-permute-done.22), channel_id=1, source_target_pairs={{0,8},{1,9},{2,10},{3,11},{4,12},{5,13},{6,14},{7,15},{8,0},{9,1},... | collective-permute-start | bytes 1179656 | tf_op jit(solution)/shard_map/ppermute | solution.py:151
  152.4 7.5 %collective-permute-done.28 = bf16[768,256]{1,0:T(8,128)(2,1)S(1)} collective-permute-done((bf16[768,256]{1,0:T(8,128)(2,1)S(1)}, bf16[768,256]{1,0:T(8,128)(2,1)S(1)}, u32[]{:S(2)}, u32[]{:S(2)}) %collective-permute-start.28) | collective-permute-done | bytes 393248 | tf_op jit(solution)/shard_map/ppermute | solution.py:151
  159.9 4.2 %collective-permute-start.26 = (bf16[768,256]{1,0:T(8,128)(2,1)S(1)}, bf16[768,256]{1,0:T(8,128)(2,1)}, u32[]{:S(2)}, u32[]{:S(2)}) collective-permute-start(bf16[768,256]{1,0:T(8,128)(2,1)S(1)} %collective-permute-done.22), channel_id=1, source_target_pairs={{0,12},{1,13},{2,14},{3,15},{4,0},{5,1},{6,2},{7,3},{8,4},{9,5},{1... | collective-permute-start | bytes 1179656 | tf_op jit(solution)/shard_map/ppermute | solution.py:151
  166.2 5.1 %collective-permute-done.29 = bf16[768,256]{1,0:T(8,128)(2,1)S(1)} collective-permute-done((bf16[768,256]{1,0:T(8,128)(2,1)S(1)}, bf16[768,256]{1,0:T(8,128)(2,1)S(1)}, u32[]{:S(2)}, u32[]{:S(2)}) %collective-permute-start.29) | collective-permute-done | bytes 393248 | tf_op jit(solution)/shard_map/ppermute | solution.py:151
  174.4 3.4 %collective-permute-done.27 = bf16[768,256]{1,0:T(8,128)(2,1)} collective-permute-done((bf16[768,256]{1,0:T(8,128)(2,1)S(1)}, bf16[768,256]{1,0:T(8,128)(2,1)}, u32[]{:S(2)}, u32[]{:S(2)}) %collective-permute-start.27) | collective-permute-done | bytes 393248 | tf_op jit(solution)/shard_map/ppermute | solution.py:151
  178.3 2.8 %fusion.26 = f32[768,256]{1,0:T(8,128)} fusion(bf16[3072,768]{1,0:T(8,128)(2,1)} %all-gather.3.cloned.1.call-done, s32[]{:T(128)S(6)} %select_n.385, bf16[768,256]{1,0:T(8,128)(2,1)} %collective-permute-done.26, bf16[768,256]{1,0:T(8,128)(2,1)} %collective-permute-done.27, pred[]{:T(512)S(6)} %eq.107), kind=kOutput, calls=%fused_computation.31 | convolution fusion | flops 302186496 | bytes 2752517 | tf_op jit(solution)/shard_map/dot_general | solution.py:334
  183.6 2.4 collective-permute-done.25
  187.6 2.7 %fusion.24 = f32[768,256]{1,0:T(8,128)} fusion(bf16[3072,768]{1,0:T(8,128)(2,1)} %all-gather.3.cloned.1.call-done, s32[]{:T(128)S(6)} %select_n.385, bf16[768,256]{1,0:T(8,128)(2,1)S(1)} %collective-permute-done.34, bf16[768,256]{1,0:T(8,128)(2,1)S(1)} %collective-permute-done.35, pred[]{:T(512)S(6)} %eq.107), kind=kOutput, calls=%fused_computation.29 | convolution fusion | flops 302186496 | bytes 2752517 | tf_op jit(solution)/shard_map/dot_general | solution.py:334
  206.2 2.9 %constant_dynamic-update-slice_fusion.7 = (bf16[768,4096]{1,0:T(8,128)(2,1)}, bf16[768,512]{1,0:T(8,128)(2,1)S(1)}) fusion(bf16[768,4096]{1,0:T(8,128)(2,1)} %shard_map.83, s32[]{:T(128)S(6)} %select_n.405, f32[768,512]{1,0:T(8,128)S(1)} %fusion.5, bf16[768,4096]{1,0:T(8,128)(2,1)} %bitcast.71, s32[]{:T(128)S(6)} %select_n.402), kind=kLoop, calls=%fused_computation.134 | loop fusion | flops 1572864 | bytes 3932168 | tf_op jit(solution)/shard_map/dynamic_update_slice | solution.py:346
  214.4 15.8 %collective-permute-done.38 = bf16[768,512]{1,0:T(8,128)(2,1)S(1)} collective-permute-done((bf16[768,512]{1,0:T(8,128)(2,1)S(1)}, bf16[768,512]{1,0:T(8,128)(2,1)S(1)}, u32[]{:S(2)}, u32[]{:S(2)}) %collective-permute-start.38) | collective-permute-done | bytes 786464 | tf_op jit(solution)/shard_map/ppermute | solution.py:156
  232.0 3.0 %collective-permute-start.42 = (bf16[384,512]{1,0:T(8,128)(2,1)}, bf16[384,512]{1,0:T(8,128)(2,1)}, u32[]{:S(2)}, u32[]{:S(2)}) collective-permute-start(bf16[384,512]{1,0:T(8,128)(2,1)} %slice.93), channel_id=1, source_target_pairs={{0,96},{16,112},{32,0},{48,16},{64,32},{80,48},{96,64},{112,80},{1... | collective-permute-start | bytes 1179656 | tf_op jit(solution)/shard_map/ppermute | solution.py:156
  235.0 3.2 %collective-permute-start.44 = (bf16[768,512]{1,0:T(8,128)(2,1)}, bf16[768,512]{1,0:T(8,128)(2,1)S(1)}, u32[]{:S(2)}, u32[]{:S(2)}) collective-permute-start(bf16[768,512]{1,0:T(8,128)(2,1)} %collective-permute-done.40), channel_id=1, source_target_pairs={{0,96},{16,112},{32,0},{48,16},{64,32},{80,48},{96,64},{112,80},{1... | collective-permute-start | bytes 2359304 | tf_op jit(solution)/shard_map/ppermute | solution.py:156
  238.2 6.2 %collective-permute-done.41 = bf16[384,512]{1,0:T(8,128)(2,1)S(1)} collective-permute-done((bf16[384,512]{1,0:T(8,128)(2,1)}, bf16[384,512]{1,0:T(8,128)(2,1)S(1)}, u32[]{:S(2)}, u32[]{:S(2)}) %collective-permute-start.41) | collective-permute-done | bytes 393248 | tf_op jit(solution)/shard_map/ppermute | solution.py:156
  245.9 2.4 collective-permute-start.45
  254.8 5.3 %collective-permute-done.43 = bf16[768,512]{1,0:T(8,128)(2,1)} collective-permute-done((bf16[768,512]{1,0:T(8,128)(2,1)}, bf16[768,512]{1,0:T(8,128)(2,1)}, u32[]{:S(2)}, u32[]{:S(2)}) %collective-permute-start.43) | collective-permute-done | bytes 786464 | tf_op jit(solution)/shard_map/ppermute | solution.py:156
  (181 shorter events, 81.6 us)
Async XLA Ops:
  7.2 93.4 %all-gather.3.cloned.1.call-start = ((), (), s32[]{:S(2)}) async-start(), calls=%async_computation | async-start | bytes 5898240 | tf_op jit(solution)/shard_map/all_gather | solution.py:253
  16.6 173.7 %all-gather.5.cloned.1.call-start = ((), (), s32[]{:S(2)}) async-start(), calls=%async_computation.1 | async-start | bytes 5898240 | tf_op jit(solution)/shard_map/all_gather | solution.py:253
  31.0 18.6 %collective-permute-start.1 = (f32[5,768,256]{2,1,0:T(8,128)}, f32[5,768,256]{2,1,0:T(8,128)}, u32[]{:S(2)}, u32[]{:S(2)}) collective-permute-start(f32[5,768,256]{2,1,0:T(8,128)} %shard_map.81), channel_id=1, source_target_pairs={{0,1},{1,0},{2,3},{3,2},{4,5},{5,4},{6,7},{7,6},{8,9},{9,8},{10,11... | collective-permute-start | bytes 11796488 | tf_op jit(solution)/shard_map/ppermute | solution.py:151
  31.5 12.7 %collective-permute-start.4 = (f16[768,256]{1,0:T(8,128)(2,1)}, f16[768,256]{1,0:T(8,128)(2,1)S(1)}, u32[]{:S(2)}, u32[]{:S(2)}) collective-permute-start(f16[768,256]{1,0:T(8,128)(2,1)} %get-tuple-element.15), channel_id=1, source_target_pairs={{0,2},{1,3},{2,0},{3,1},{4,6},{5,7},{6,4},{7,5},{8,10},{9,11},{10,... | collective-permute-start | bytes 1179656 | tf_op jit(solution)/shard_map/ppermute | solution.py:151
  34.6 11.6 %collective-permute-start.7 = (f16[768,256]{1,0:T(8,128)(2,1)}, f16[768,256]{1,0:T(8,128)(2,1)S(1)}, u32[]{:S(2)}, u32[]{:S(2)}) collective-permute-start(f16[768,256]{1,0:T(8,128)(2,1)} %get-tuple-element.18), channel_id=1, source_target_pairs={{0,12},{1,13},{2,14},{3,15},{4,0},{5,1},{6,2},{7,3},{8,4},{9,5},{1... | collective-permute-start | bytes 1179656 | tf_op jit(solution)/shard_map/ppermute | solution.py:151
  37.7 12.0 %collective-permute-start.6 = (f16[768,256]{1,0:T(8,128)(2,1)}, f16[768,256]{1,0:T(8,128)(2,1)}, u32[]{:S(2)}, u32[]{:S(2)}) collective-permute-start(f16[768,256]{1,0:T(8,128)(2,1)} %get-tuple-element.17), channel_id=1, source_target_pairs={{0,4},{1,5},{2,6},{3,7},{4,8},{5,9},{6,10},{7,11},{8,12},{9,13},{1... | collective-permute-start | bytes 1179656 | tf_op jit(solution)/shard_map/ppermute | solution.py:151
  44.3 53.8 %collective-permute-start.15 = (bf16[768,768]{1,0:T(8,128)(2,1)S(1)}, bf16[768,768]{1,0:T(8,128)(2,1)S(1)}, u32[]{:S(2)}, u32[]{:S(2)}) collective-permute-start(bf16[768,768]{1,0:T(8,128)(2,1)S(1)} %bitcast.83), channel_id=1, source_target_pairs={{0,16},{16,0},{32,48},{48,32},{64,80},{80,64},{96,112},{112,96},{1... | collective-permute-start | bytes 3538952 | tf_op jit(solution)/shard_map/ppermute | solution.py:156
  51.6 30.5 %collective-permute-start.8 = (f16[768,256]{1,0:T(8,128)(2,1)S(1)}, f16[768,256]{1,0:T(8,128)(2,1)S(1)}, u32[]{:S(2)}, u32[]{:S(2)}) collective-permute-start(f16[768,256]{1,0:T(8,128)(2,1)S(1)} %get-tuple-element.33), channel_id=1, source_target_pairs={{0,2},{1,3},{2,0},{3,1},{4,6},{5,7},{6,4},{7,5},{8,10},{9,11},{10,... | collective-permute-start | bytes 1179656 | tf_op jit(solution)/shard_map/ppermute | solution.py:151
  52.2 29.8 %collective-permute-start.5 = (f16[768,256]{1,0:T(8,128)(2,1)S(1)}, f16[768,256]{1,0:T(8,128)(2,1)S(1)}, u32[]{:S(2)}, u32[]{:S(2)}) collective-permute-start(f16[768,256]{1,0:T(8,128)(2,1)S(1)} %get-tuple-element.32), channel_id=1, source_target_pairs={{0,8},{1,9},{2,10},{3,11},{4,12},{5,13},{6,14},{7,15},{8,0},{9,1},... | collective-permute-start | bytes 1179656 | tf_op jit(solution)/shard_map/ppermute | solution.py:151
  55.5 26.5 %collective-permute-start.3 = (f16[768,256]{1,0:T(8,128)(2,1)S(1)}, f16[768,256]{1,0:T(8,128)(2,1)S(1)}, u32[]{:S(2)}, u32[]{:S(2)}) collective-permute-start(f16[768,256]{1,0:T(8,128)(2,1)S(1)} %get-tuple-element.31), channel_id=1, source_target_pairs={{0,12},{1,13},{2,14},{3,15},{4,0},{5,1},{6,2},{7,3},{8,4},{9,5},{1... | collective-permute-start | bytes 1179656 | tf_op jit(solution)/shard_map/ppermute | solution.py:151
  56.6 25.4 %collective-permute-start.2 = (f16[768,256]{1,0:T(8,128)(2,1)S(1)}, f16[768,256]{1,0:T(8,128)(2,1)S(1)}, u32[]{:S(2)}, u32[]{:S(2)}) collective-permute-start(f16[768,256]{1,0:T(8,128)(2,1)S(1)} %get-tuple-element.30), channel_id=1, source_target_pairs={{0,4},{1,5},{2,6},{3,7},{4,8},{5,9},{6,10},{7,11},{8,12},{9,13},{1... | collective-permute-start | bytes 1179656 | tf_op jit(solution)/shard_map/ppermute | solution.py:151
  130.2 29.7 %collective-permute-start.28 = (bf16[768,256]{1,0:T(8,128)(2,1)S(1)}, bf16[768,256]{1,0:T(8,128)(2,1)S(1)}, u32[]{:S(2)}, u32[]{:S(2)}) collective-permute-start(bf16[768,256]{1,0:T(8,128)(2,1)S(1)} %collective-permute-done.22), channel_id=1, source_target_pairs={{0,8},{1,9},{2,10},{3,11},{4,12},{5,13},{6,14},{7,15},{8,0},{9,1},... | collective-permute-start | bytes 1179656 | tf_op jit(solution)/shard_map/ppermute | solution.py:151
  152.4 11.8 %collective-permute-start.23 = (bf16[768,256]{1,0:T(8,128)(2,1)S(1)}, bf16[768,256]{1,0:T(8,128)(2,1)S(1)}, u32[]{:S(2)}, u32[]{:S(2)}) collective-permute-start(bf16[768,256]{1,0:T(8,128)(2,1)S(1)} %collective-permute-done.22), channel_id=1, source_target_pairs={{0,2},{1,3},{2,0},{3,1},{4,6},{5,7},{6,4},{7,5},{8,10},{9,11},{10,... | collective-permute-start | bytes 1179656 | tf_op jit(solution)/shard_map/ppermute | solution.py:151
  159.9 11.4 %collective-permute-start.29 = (bf16[768,256]{1,0:T(8,128)(2,1)S(1)}, bf16[768,256]{1,0:T(8,128)(2,1)S(1)}, u32[]{:S(2)}, u32[]{:S(2)}) collective-permute-start(bf16[768,256]{1,0:T(8,128)(2,1)S(1)} %collective-permute-done.28), channel_id=1, source_target_pairs={{0,2},{1,3},{2,0},{3,1},{4,6},{5,7},{6,4},{7,5},{8,10},{9,11},{10,... | collective-permute-start | bytes 1179656 | tf_op jit(solution)/shard_map/ppermute | solution.py:151
  159.9 13.4 %collective-permute-start.26 = (bf16[768,256]{1,0:T(8,128)(2,1)S(1)}, bf16[768,256]{1,0:T(8,128)(2,1)}, u32[]{:S(2)}, u32[]{:S(2)}) collective-permute-start(bf16[768,256]{1,0:T(8,128)(2,1)S(1)} %collective-permute-done.22), channel_id=1, source_target_pairs={{0,12},{1,13},{2,14},{3,15},{4,0},{5,1},{6,2},{7,3},{8,4},{9,5},{1... | collective-permute-start | bytes 1179656 | tf_op jit(solution)/shard_map/ppermute | solution.py:151
  164.2 13.6 %collective-permute-start.27 = (bf16[768,256]{1,0:T(8,128)(2,1)S(1)}, bf16[768,256]{1,0:T(8,128)(2,1)}, u32[]{:S(2)}, u32[]{:S(2)}) collective-permute-start(bf16[768,256]{1,0:T(8,128)(2,1)S(1)} %collective-permute-done.23), channel_id=1, source_target_pairs={{0,12},{1,13},{2,14},{3,15},{4,0},{5,1},{6,2},{7,3},{8,4},{9,5},{1... | collective-permute-start | bytes 1179656 | tf_op jit(solution)/shard_map/ppermute | solution.py:151
  164.2 13.6 %collective-permute-start.36 = (bf16[768,256]{1,0:T(8,128)(2,1)S(1)}, bf16[768,256]{1,0:T(8,128)(2,1)S(1)}, u32[]{:S(2)}, u32[]{:S(2)}) collective-permute-start(bf16[768,256]{1,0:T(8,128)(2,1)S(1)} %collective-permute-done.28), channel_id=1, source_target_pairs={{0,1},{1,0},{2,3},{3,2},{4,5},{5,4},{6,7},{7,6},{8,9},{9,8},{10,11... | collective-permute-start | bytes 1179656 | tf_op jit(solution)/shard_map/ppermute | solution.py:151
  164.4 18.8 %collective-permute-start.24 = (bf16[768,256]{1,0:T(8,128)(2,1)S(1)}, bf16[768,256]{1,0:T(8,128)(2,1)S(1)}, u32[]{:S(2)}, u32[]{:S(2)}) collective-permute-start(bf16[768,256]{1,0:T(8,128)(2,1)S(1)} %collective-permute-done.22), channel_id=1, source_target_pairs={{0,4},{1,5},{2,6},{3,7},{4,8},{5,9},{6,10},{7,11},{8,12},{9,13},{1... | collective-permute-start | bytes 1179656 | tf_op jit(solution)/shard_map/ppermute | solution.py:151
  171.3 9.8 %collective-permute-start.37 = (bf16[768,256]{1,0:T(8,128)(2,1)S(1)}, bf16[768,256]{1,0:T(8,128)(2,1)S(1)}, u32[]{:S(2)}, u32[]{:S(2)}) collective-permute-start(bf16[768,256]{1,0:T(8,128)(2,1)S(1)} %collective-permute-done.29), channel_id=1, source_target_pairs={{0,1},{1,0},{2,3},{3,2},{4,5},{5,4},{6,7},{7,6},{8,9},{9,8},{10,11... | collective-permute-start | bytes 1179656 | tf_op jit(solution)/shard_map/ppermute | solution.py:151
  173.3 12.8 %collective-permute-start.25 = (bf16[768,256]{1,0:T(8,128)(2,1)S(1)}, bf16[768,256]{1,0:T(8,128)(2,1)}, u32[]{:S(2)}, u32[]{:S(2)}) collective-permute-start(bf16[768,256]{1,0:T(8,128)(2,1)S(1)} %collective-permute-done.23), channel_id=1, source_target_pairs={{0,4},{1,5},{2,6},{3,7},{4,8},{5,9},{6,10},{7,11},{8,12},{9,13},{1... | collective-permute-start | bytes 1179656 | tf_op jit(solution)/shard_map/ppermute | solution.py:151
  181.1 17.4 %collective-permute-start.30 = (bf16[768,256]{1,0:T(8,128)(2,1)S(1)}, bf16[768,256]{1,0:T(8,128)(2,1)}, u32[]{:S(2)}, u32[]{:S(2)}) collective-permute-start(bf16[768,256]{1,0:T(8,128)(2,1)S(1)} %collective-permute-done.22), channel_id=1, source_target_pairs={{0,1},{1,0},{2,3},{3,2},{4,5},{5,4},{6,7},{7,6},{8,9},{9,8},{10,11... | collective-permute-start | bytes 1179656 | tf_op jit(solution)/shard_map/ppermute | solution.py:151
  183.2 15.3 %collective-permute-start.31 = (bf16[768,256]{1,0:T(8,128)(2,1)S(1)}, bf16[768,256]{1,0:T(8,128)(2,1)}, u32[]{:S(2)}, u32[]{:S(2)}) collective-permute-start(bf16[768,256]{1,0:T(8,128)(2,1)S(1)} %collective-permute-done.23), channel_id=1, source_target_pairs={{0,1},{1,0},{2,3},{3,2},{4,5},{5,4},{6,7},{7,6},{8,9},{9,8},{10,11... | collective-permute-start | bytes 1179656 | tf_op jit(solution)/shard_map/ppermute | solution.py:151
  186.1 15.7 %collective-permute-start.32 = (bf16[768,256]{1,0:T(8,128)(2,1)S(1)}, bf16[768,256]{1,0:T(8,128)(2,1)}, u32[]{:S(2)}, u32[]{:S(2)}) collective-permute-start(bf16[768,256]{1,0:T(8,128)(2,1)S(1)} %collective-permute-done.24), channel_id=1, source_target_pairs={{0,1},{1,0},{2,3},{3,2},{4,5},{5,4},{6,7},{7,6},{8,9},{9,8},{10,11... | collective-permute-start | bytes 1179656 | tf_op jit(solution)/shard_map/ppermute | solution.py:151
  186.1 15.7 %collective-permute-start.33 = (bf16[768,256]{1,0:T(8,128)(2,1)}, bf16[768,256]{1,0:T(8,128)(2,1)}, u32[]{:S(2)}, u32[]{:S(2)}) collective-permute-start(bf16[768,256]{1,0:T(8,128)(2,1)} %collective-permute-done.25), channel_id=1, source_target_pairs={{0,1},{1,0},{2,3},{3,2},{4,5},{5,4},{6,7},{7,6},{8,9},{9,8},{10,11... | collective-permute-start | bytes 1179656 | tf_op jit(solution)/shard_map/ppermute | solution.py:151
  209.0 21.2 %collective-permute-start.38 = (bf16[768,512]{1,0:T(8,128)(2,1)S(1)}, bf16[768,512]{1,0:T(8,128)(2,1)S(1)}, u32[]{:S(2)}, u32[]{:S(2)}) collective-permute-start(bf16[768,512]{1,0:T(8,128)(2,1)S(1)} %get-tuple-element.27), channel_id=1, source_target_pairs={{0,32},{16,48},{32,64},{48,80},{64,96},{80,112},{96,0},{112,16},{1... | collective-permute-start | bytes 2359304 | tf_op jit(solution)/shard_map/ppermute | solution.py:156
  210.5 20.7 %collective-permute-start.39 = (bf16[768,512]{1,0:T(8,128)(2,1)S(1)}, bf16[768,512]{1,0:T(8,128)(2,1)S(1)}, u32[]{:S(2)}, u32[]{:S(2)}) collective-permute-start(bf16[768,512]{1,0:T(8,128)(2,1)S(1)} %get-tuple-element.27), channel_id=1, source_target_pairs={{0,96},{16,112},{32,0},{48,16},{64,32},{80,48},{96,64},{112,80},{1... | collective-permute-start | bytes 2359304 | tf_op jit(solution)/shard_map/ppermute | solution.py:156
  212.2 22.8 %collective-permute-start.40 = (bf16[768,512]{1,0:T(8,128)(2,1)S(1)}, bf16[768,512]{1,0:T(8,128)(2,1)}, u32[]{:S(2)}, u32[]{:S(2)}) collective-permute-start(bf16[768,512]{1,0:T(8,128)(2,1)S(1)} %get-tuple-element.27), channel_id=1, source_target_pairs={{0,16},{16,0},{32,48},{48,32},{64,80},{80,64},{96,112},{112,96},{1... | collective-permute-start | bytes 2359304 | tf_op jit(solution)/shard_map/ppermute | solution.py:156
  231.0 13.4 %collective-permute-start.41 = (bf16[384,512]{1,0:T(8,128)(2,1)}, bf16[384,512]{1,0:T(8,128)(2,1)S(1)}, u32[]{:S(2)}, u32[]{:S(2)}) collective-permute-start(bf16[384,512]{1,0:T(8,128)(2,1)} %slice.92), channel_id=1, source_target_pairs={{0,32},{16,48},{32,64},{48,80},{64,96},{80,112},{96,0},{112,16},{1... | collective-permute-start | bytes 1179656 | tf_op jit(solution)/shard_map/ppermute | solution.py:156
  232.0 12.9 %collective-permute-start.42 = (bf16[384,512]{1,0:T(8,128)(2,1)}, bf16[384,512]{1,0:T(8,128)(2,1)}, u32[]{:S(2)}, u32[]{:S(2)}) collective-permute-start(bf16[384,512]{1,0:T(8,128)(2,1)} %slice.93), channel_id=1, source_target_pairs={{0,96},{16,112},{32,0},{48,16},{64,32},{80,48},{96,64},{112,80},{1... | collective-permute-start | bytes 1179656 | tf_op jit(solution)/shard_map/ppermute | solution.py:156
  235.0 25.1 %collective-permute-start.43 = (bf16[768,512]{1,0:T(8,128)(2,1)}, bf16[768,512]{1,0:T(8,128)(2,1)}, u32[]{:S(2)}, u32[]{:S(2)}) collective-permute-start(bf16[768,512]{1,0:T(8,128)(2,1)} %collective-permute-done.40), channel_id=1, source_target_pairs={{0,32},{16,48},{32,64},{48,80},{64,96},{80,112},{96,0},{112,16},{1... | collective-permute-start | bytes 2359304 | tf_op jit(solution)/shard_map/ppermute | solution.py:156
  235.0 27.2 %collective-permute-start.44 = (bf16[768,512]{1,0:T(8,128)(2,1)}, bf16[768,512]{1,0:T(8,128)(2,1)S(1)}, u32[]{:S(2)}, u32[]{:S(2)}) collective-permute-start(bf16[768,512]{1,0:T(8,128)(2,1)} %collective-permute-done.40), channel_id=1, source_target_pairs={{0,96},{16,112},{32,0},{48,16},{64,32},{80,48},{96,64},{112,80},{1... | collective-permute-start | bytes 2359304 | tf_op jit(solution)/shard_map/ppermute | solution.py:156
  245.9 17.7 %collective-permute-start.45 = (bf16[768,512]{1,0:T(8,128)(2,1)S(1)}, bf16[768,512]{1,0:T(8,128)(2,1)S(1)}, u32[]{:S(2)}, u32[]{:S(2)}) collective-permute-start(bf16[768,512]{1,0:T(8,128)(2,1)S(1)} %pad_maximum_fusion), channel_id=1, source_target_pairs={{0,16},{16,0},{32,48},{48,32},{64,80},{80,64},{96,112},{112,96},{1... | collective-permute-start | bytes 2359304 | tf_op jit(solution)/shard_map/ppermute | solution.py:156
  (44 other events, 392.0 us)
Sparse Core Ops, SparseCore 0:
  16.7 55.4 all-gather.2
  99.2 58.5 all-gather.4

commit v4 on v1

--- a/solution.py
+++ b/solution.py
@@ -13,6 +13,8 @@
 HEAD = 128
 RING = 4
 ORDER = (((2, 1), (1, 1), (3, 1)), ((1, 0), (3, 0), (2, 0), (0, 1), (0, 0)))
+
+GRAD_ORDER = (0, 1, 3, 2)
 
 f32 = jnp.float32
 bf16 = jnp.bfloat16
@@ -125,6 +127,62 @@
     )(lens, weights, scales, merged, squares, gain, taps)
 
 
+def gradient_kernel(places_ref, here_ref, across_ref, *refs):
+    number = 2 * len(GRAD_ORDER)
+    own, other, old_ref, grad_ref, new_ref = refs[:number], refs[number : 2 * number], *refs[2 * number :]
+    step = pl.program_id(0)
+    same, core = places_ref[len(GRAD_ORDER)], places_ref[len(GRAD_ORDER) + 1]
+    wide = own[0].shape[1]
+
+    @pl.when(step == 0)
+    def _():
+        grad_ref[...] = jnp.zeros_like(grad_ref)
+
+    for k in range(len(GRAD_ORDER)):
+
+        @pl.when(step == k)
+        def _():
+            for half, parity in ((own, core), (other, 1 - core)):
+                straight, crossed = half[2 * k][...], half[2 * k + 1][...]
+                here = jnp.where(same == 1, straight, crossed)
+                across = jnp.where(same == 1, crossed, straight)
+                columns = pl.ds(pl.multiple_of(parity * wide, wide), wide)
+                grad_ref[:, columns] += lax.dot_general(
+                    here_ref[...], here, COLS_COLS, preferred_element_type=f32
+                ) + lax.dot_general(across_ref[...], across, COLS_COLS, preferred_element_type=f32)
+
+    @pl.when(step == len(GRAD_ORDER) - 1)
+    def _():
+        new_ref[...] = (old_ref[...].astype(f32) - step_size * grad_ref[...]).astype(bf16)
+
+
+def gradient(places, here, across, own, other, weight):
+    steps = len(GRAD_ORDER)
+    rows, wide = own[0].shape
+    depth = weight.shape[0]
+    piece = pl.BlockSpec((rows, wide), lambda i, places: (0, 0))
+    taps = pl.BlockSpec((rows, depth), lambda i, places: (places[i], 0))
+    out = pl.BlockSpec((depth, 2 * wide), lambda i, places: (0, 0))
+    old = pl.BlockSpec((depth, 2 * wide), lambda i, places: (0, places[steps + 2]))
+    return pl.pallas_call(
+        gradient_kernel,
+        grid_spec=pltpu.PrefetchScalarGridSpec(
+            num_scalar_prefetch=1,
+            grid=(steps,),
+            in_specs=[taps, taps] + [piece] * (4 * steps) + [old],
+            out_specs=[out, out],
+        ),
+        out_shape=[
+            jax.ShapeDtypeStruct((depth, 2 * wide), f32),
+            jax.ShapeDtypeStruct((depth, 2 * wide), bf16),
+        ],
+        compiler_params=pltpu.CompilerParams(vmem_limit_bytes=56 * 2**20),
+        cost_estimate=pl.CostEstimate(
+            flops=8 * steps * rows * depth * wide, bytes_accessed=20 * 2**20, transcendentals=0
+        ),
+    )(places, here, across, *own, *other, weight)
+
+
 def row_major(a):
     return with_layout_constraint(a, Layout(major_to_minor=tuple(range(a.ndim))))
 
@@ -283,9 +341,9 @@
     across = send(second[0, 1] + up_across.astype(f32) + down_across.astype(f32), 0, 1).astype(f32)
     merged = (second[0, 0] + up + down + far + across) * (1.0 / SEND)
     merged = merged.reshape(slots, span, wide)
+    merged, rows_across = lax.optimization_barrier((merged, rows_across))
+    taps_across = gather_taps(rows_across)
     squares = sum_over_tr(jnp.sum(merged * merged, axis=2))
-    squares, rows_across = lax.optimization_barrier((squares, rows_across))
-    taps_across = gather_taps(rows_across)
 
     scaled, crossed = attention(
         lens,
@@ -319,25 +377,16 @@
     own_half = gather(turned, to_chip)
     other_half = {k: to_sibling(v) for k, v in own_half.items()}
 
-    all_rows = buffer((2, RING * slots * span, flat_in), bf16)
-    all_rows = lax.dynamic_update_slice(all_rows, taps_here[None], (0, 0, 0))
-    all_rows = lax.dynamic_update_slice(all_rows, taps_across[None], (1, 0, 0))
-    all_rows = all_rows.reshape(2 * RING, slots * span, flat_in)
-
-    def gradient(half):
-        total = None
-        for (a, b), piece in half.items():
-            place = (x_low + x_high - b) % 2 * RING + (y - a - z) % RING
-            source = lax.dynamic_index_in_dim(all_rows, place, 0, keepdims=False)
-            part = lax.dot_general(source, piece, COLS_COLS, preferred_element_type=f32)
-            total = part if total is None else total + part
-        return total
-
-    grad = buffer((flat_in, block), f32)
-    for half, parity in ((own_half, core), (other_half, 1 - core)):
-        grad = lax.dynamic_update_slice_in_dim(grad, gradient(half), parity * wide, 1)
-    old = lax.dynamic_slice_in_dim(weight, rep * block, block, 1)
-    new_block = (old.astype(f32) - step_size * grad).astype(bf16)
+    offsets = [(a, b) for a in GRAD_ORDER for b in range(2)]
+    places = [(y - a - z) % RING for a in GRAD_ORDER] + [jnp.where(x_low == x_high, 1, 0), core, rep]
+    grad, new_block = gradient(
+        jnp.stack(places).astype(jnp.int32),
+        taps_here,
+        taps_across,
+        [own_half[k] for k in offsets],
+        [other_half[k] for k in offsets],
+        weight,
+    )
     new = buffer((flat_in, width_all), bf16)
     for a, b, first, piece in gather_relayed(new_block, to_group):
         owner = (z - a) % RING * 2 + (x_low - b) % 2

time: 257 us -> 258 us (level)
  matrix products: 13.5 us -> 0 us
  Pallas kernels: 29.5 us -> 42 us
  starting transfers between devices: 67.6 us -> 79.2 us
  local copies, waits for them, and re-layouts: 36.7 us -> 26.7 us
  waiting for transfers between devices: 80.4 us -> 84.4 us
  other arithmetic: 12.8 us -> 8.95 us
    dot_general x16 -> x0, matrix products: 13.5 us -> none  [gradient(): part = lax.dot_general(source, piece, COLS_COLS, preferred_element_type=f32)]
    pallas_call x0 -> x1, Pallas kernels: none -> 12.6 us  [gradient(): pl.pallas_call(gradient_kernel, grid_spec=pltpu.PrefetchScalarGridSpec(nu...]
    dynamic_update_slice x2 -> x0, local copies, waits for them, and re-layouts: 9.63 us -> none  [the longest x1 4.82 us: per_device(): all_rows = lax.dynamic_update_slice(all_rows, taps_across[None], (1, 0, 0))]
    ppermute x9, starting transfers between devices: 13.1 us -> 21.2 us  [to_group(): return lax.ppermute(value, 'rep', pairs)]
    ppermute x34, waiting for transfers between devices: 50 us -> 57.3 us  [to_chip(): return lax.ppermute(value, 'tr', pairs)]
    ppermute x34, starting transfers between devices: 53.7 us -> 57.2 us  [to_chip(): return lax.ppermute(value, 'tr', pairs)]
    ppermute x9, waiting for transfers between devices: 30.3 us -> 27 us  [to_group(): return lax.ppermute(value, 'rep', pairs)]
    dynamic_update_slice x1 -> x0, other arithmetic: 2.86 us -> none  [per_device(): new = lax.dynamic_update_slice(new, piece, (first, owner * block))]
  transfers between devices with their start and end apart: 46 -> 46, of which waited for: 19 -> 24; matrix products, arithmetic and copies ran while one was open for 18% -> 8% of each run, Pallas kernels for 10% -> 10%
where the time goes in v4:
time: 258 us; the launch traced here: 256 us
  waiting for transfers between devices  84.4 us (33%)
  starting transfers between devices  79.2 us (31%)
  Pallas kernels  42 us (16%)
  local copies, waits for them, and re-layouts  26.7 us (10%)
  between operations  14.7 us (6%)
  other arithmetic  8.95 us (3%)
    ppermute x34, waiting for transfers between devices, to_chip(): return lax.ppermute(value, 'tr', pairs)  57.3 us
    ppermute x34, starting transfers between devices, to_chip(): return lax.ppermute(value, 'tr', pairs)  57.2 us
    ppermute x9, waiting for transfers between devices, to_group(): return lax.ppermute(value, 'rep', pairs)  27 us
    ppermute x9, starting transfers between devices, to_group(): return lax.ppermute(value, 'rep', pairs)  21.2 us
    pallas_call x1, Pallas kernels, attention(): pl.pallas_call(attention_kernel, grid=(count // slots,), in_specs=[scalar...  15.8 us
    pallas_call x4, Pallas kernels, products(): pl.pallas_call(product_kernel, grid_spec=pltpu.PrefetchScalarGridSpec(num...  13.7 us
    pallas_call x1, Pallas kernels, gradient(): pl.pallas_call(gradient_kernel, grid_spec=pltpu.PrefetchScalarGridSpec(nu...  12.6 us
    unnamed x49, local copies, waits for them, and re-layouts  12.4 us
  transfers between devices with their start and end apart: 46, of which 24 were waited for; matrix products, arithmetic and copies ran while one was open for 8% of the time, Pallas kernels for 10%

profile of v4, /device:TPU:0, one launch (start us, length us, event | category | flops | bytes accessed | tf_op | source)
XLA Modules:
  0.0 255.9 jit_solution(15655951320632605303)
XLA Ops:
  10.0 3.1 %copy-done = bf16[3,256,4096]{2,1,0:T(8,128)(2,1)S(1)} copy-done((bf16[3,256,4096]{2,1,0:T(8,128)(2,1)S(1)}, bf16[3,256,4096]{2,1,0:T(8,128)(2,1)}, u32[]{:S(2)}) %copy-start) | copy-done | bytes 6291480
  13.1 3.4 %shard_map.78 = f32[3,768,256]{2,1,0:T(8,128)} custom-call(s32[3]{0:T(128)S(1)} %pad_add_fusion.1.blocks_ref, bf16[768,768]{1,0:T(8,128)(2,1)S(1)} %bitcast.84, bf16[768,4096]{1,0:T(8,128)(2,1)S(1)} %bitcast.78), custom_call_target="tpu_custom_call" | custom-call | flops 905969664 | bytes 4718592 | tf_op jit(solution)/shard_map/pallas_call | solution.py:260
  16.9 2.8 %copy-done.1 = bf16[3,256,4096]{2,1,0:T(8,128)(2,1)S(1)} copy-done((bf16[3,256,4096]{2,1,0:T(8,128)(2,1)S(1)}, bf16[3,256,4096]{2,1,0:T(8,128)(2,1)}, u32[]{:S(2)}) %copy-start.1) | copy-done | bytes 6291480
  23.2 3.0 %fusion.28 = (f16[768,256]{1,0:T(8,128)(2,1)}, f16[768,256]{1,0:T(8,128)(2,1)}, f16[768,256]{1,0:T(8,128)(2,1)}) fusion(f32[3,768,256]{2,1,0:T(8,128)} %collective-permute-done, f32[3,768,256]{2,1,0:T(8,128)S(1)} %shard_map.77), kind=kLoop, calls=%fused_computation.39 | loop fusion | flops 1769472 | bytes 5898240 | tf_op jit(solution)/shard_map/convert_element_type | solution.py:330
  26.1 4.8 %shard_map.80 = f32[5,768,256]{2,1,0:T(8,128)} custom-call(s32[5]{0:T(128)S(1)} %stack.111.blocks_ref, bf16[768,768]{1,0:T(8,128)(2,1)S(1)} %bitcast.87, bf16[768,4096]{1,0:T(8,128)(2,1)S(1)} %bitcast.82), custom_call_target="tpu_custom_call" | custom-call | flops 1509949440 | bytes 7077888 | tf_op jit(solution)/shard_map/pallas_call | solution.py:260
  31.5 3.1 %collective-permute-start.4 = (f16[768,256]{1,0:T(8,128)(2,1)}, f16[768,256]{1,0:T(8,128)(2,1)S(1)}, u32[]{:S(2)}, u32[]{:S(2)}) collective-permute-start(f16[768,256]{1,0:T(8,128)(2,1)} %get-tuple-element.15), channel_id=1, source_target_pairs={{0,2},{1,3},{2,0},{3,1},{4,6},{5,7},{6,4},{7,5},{8,10},{9,11},{10,... | collective-permute-start | bytes 1179656 | tf_op jit(solution)/shard_map/ppermute | solution.py:209
  37.9 2.9 %copy-done.2 = bf16[3,256,4096]{2,1,0:T(8,128)(2,1)S(1)} copy-done((bf16[3,256,4096]{2,1,0:T(8,128)(2,1)S(1)}, bf16[3,256,4096]{2,1,0:T(8,128)(2,1)}, u32[]{:S(2)}) %copy-start.2) | copy-done | bytes 6291480
  40.8 3.3 %shard_map.79 = f32[5,768,256]{2,1,0:T(8,128)S(1)} custom-call(s32[5]{0:T(128)S(1)} %stack.97.blocks_ref, bf16[768,768]{1,0:T(8,128)(2,1)S(1)} %bitcast.88, bf16[768,4096]{1,0:T(8,128)(2,1)S(1)} %bitcast.83), custom_call_target="tpu_custom_call" | custom-call | flops 1509949440 | bytes 7077888 | tf_op jit(solution)/shard_map/pallas_call | solution.py:260
  59.7 6.9 %collective-permute-done.3 = f16[768,256]{1,0:T(8,128)(2,1)S(1)} collective-permute-done((f16[768,256]{1,0:T(8,128)(2,1)S(1)}, f16[768,256]{1,0:T(8,128)(2,1)S(1)}, u32[]{:S(2)}, u32[]{:S(2)}) %collective-permute-start.3) | collective-permute-done | bytes 393248 | tf_op jit(solution)/shard_map/ppermute | solution.py:209
  68.5 13.5 %collective-permute-done.8 = f16[768,256]{1,0:T(8,128)(2,1)S(1)} collective-permute-done((f16[768,256]{1,0:T(8,128)(2,1)S(1)}, f16[768,256]{1,0:T(8,128)(2,1)S(1)}, u32[]{:S(2)}, u32[]{:S(2)}) %collective-permute-start.8) | collective-permute-done | bytes 393248 | tf_op jit(solution)/shard_map/ppermute | solution.py:209
  88.1 4.0 %collective-permute-done.11 = f32[8,96]{1,0:T(8,128)S(1)} collective-permute-done((f32[8,96]{1,0:T(8,128)S(1)}, f32[8,96]{1,0:T(8,128)S(1)}, u32[]{:S(2)}, u32[]{:S(2)}) %collective-permute-start.11) | collective-permute-done | bytes 3104 | tf_op jit(solution)/shard_map/ppermute | solution.py:209
  93.7 2.9 %collective-permute-start.13 = (f32[8,96]{1,0:T(8,128)S(1)}, f32[8,96]{1,0:T(8,128)S(1)}, u32[]{:S(2)}, u32[]{:S(2)}) collective-permute-start(f32[8,96]{1,0:T(8,128)S(1)} %add.448), channel_id=1, source_target_pairs={{0,8},{1,9},{2,10},{3,11},{4,12},{5,13},{6,14},{7,15},{8,0},{9,1},... | collective-permute-start | bytes 9224 | tf_op jit(solution)/shard_map/ppermute | solution.py:209
  100.2 15.8 %shard_map.81 = (f32[8,96,256]{2,1,0:T(8,128)S(1)}, f32[8,1,96]{2,1,0:T(1,128)S(1)}) custom-call(s32[8]{0:T(128)S(1)} %dynamic_slice.6.lens_ref, f32[8]{0:T(128)S(1)} %convert_divide_fusion.weights_ref, f32[2]{0:T(128)S(1)} %copy-done.7, f32[8,96,256]{2,1,0:T(8,128)S(1)} %bitcast.91, f32[8,1,96]{2,1,0:T(1,128)S(1)} %bitcast.93, f32[1,256]{1,0:T(1,128)S(1)} %bitcast.96, ...), custom_call_target="tpu_custom_call" | custom-call | flops 2000000000 | bytes 3000000 | tf_op jit(solution)/shard_map/pallas_call | solution.py:116
  118.2 4.2 %collective-permute-done.16 = f32[8,96]{1,0:T(8,128)S(1)} collective-permute-done((f32[8,96]{1,0:T(8,128)S(1)}, f32[8,96]{1,0:T(8,128)S(1)}, u32[]{:S(2)}, u32[]{:S(2)}) %collective-permute-start.16) | collective-permute-done | bytes 3104 | tf_op jit(solution)/shard_map/ppermute | solution.py:209
  122.5 3.8 %collective-permute-start.18 = (f32[8,96]{1,0:T(8,128)S(1)}, f32[8,96]{1,0:T(8,128)S(1)}, u32[]{:S(2)}, u32[]{:S(2)}) collective-permute-start(f32[8,96]{1,0:T(8,128)S(1)} %add.455), channel_id=1, source_target_pairs={{0,8},{1,9},{2,10},{3,11},{4,12},{5,13},{6,14},{7,15},{8,0},{9,1},... | collective-permute-start | bytes 9224 | tf_op jit(solution)/shard_map/ppermute | solution.py:209
  131.0 11.2 %collective-permute-start.21 = (bf16[768,256]{1,0:T(8,128)(2,1)S(1)}, bf16[768,256]{1,0:T(8,128)(2,1)S(1)}, u32[]{:S(2)}, u32[]{:S(2)}) collective-permute-start(bf16[768,256]{1,0:T(8,128)(2,1)S(1)} %collective-permute-done.20.refs_0_), channel_id=1, source_target_pairs={{0,2},{1,3},{2,0},{3,1},{4,6},{5,7},{6,4},{7,5},{8,10},{9,11},{10,... | collective-permute-start | bytes 1179656 | tf_op jit(solution)/shard_map/ppermute | solution.py:209
  142.2 6.8 %collective-permute-start.26 = (bf16[768,256]{1,0:T(8,128)(2,1)S(1)}, bf16[768,256]{1,0:T(8,128)(2,1)S(1)}, u32[]{:S(2)}, u32[]{:S(2)}) collective-permute-start(bf16[768,256]{1,0:T(8,128)(2,1)S(1)} %collective-permute-done.20.refs_0_), channel_id=1, source_target_pairs={{0,8},{1,9},{2,10},{3,11},{4,12},{5,13},{6,14},{7,15},{8,0},{9,1},... | collective-permute-start | bytes 1179656 | tf_op jit(solution)/shard_map/ppermute | solution.py:209
  149.1 3.1 %collective-permute-start.24 = (bf16[768,256]{1,0:T(8,128)(2,1)S(1)}, bf16[768,256]{1,0:T(8,128)(2,1)S(1)}, u32[]{:S(2)}, u32[]{:S(2)}) collective-permute-start(bf16[768,256]{1,0:T(8,128)(2,1)S(1)} %collective-permute-done.20.refs_0_), channel_id=1, source_target_pairs={{0,12},{1,13},{2,14},{3,15},{4,0},{5,1},{6,2},{7,3},{8,4},{9,5},{1... | collective-permute-start | bytes 1179656 | tf_op jit(solution)/shard_map/ppermute | solution.py:209
  152.2 3.2 %collective-permute-start.23 = (bf16[768,256]{1,0:T(8,128)(2,1)S(1)}, bf16[768,256]{1,0:T(8,128)(2,1)S(1)}, u32[]{:S(2)}, u32[]{:S(2)}) collective-permute-start(bf16[768,256]{1,0:T(8,128)(2,1)S(1)} %collective-permute-done.21.refs_1_), channel_id=1, source_target_pairs={{0,4},{1,5},{2,6},{3,7},{4,8},{5,9},{6,10},{7,11},{8,12},{9,13},{1... | collective-permute-start | bytes 1179656 | tf_op jit(solution)/shard_map/ppermute | solution.py:209
  155.4 3.7 %collective-permute-done.26.refs_6_ = bf16[768,256]{1,0:T(8,128)(2,1)S(1)} collective-permute-done((bf16[768,256]{1,0:T(8,128)(2,1)S(1)}, bf16[768,256]{1,0:T(8,128)(2,1)S(1)}, u32[]{:S(2)}, u32[]{:S(2)}) %collective-permute-start.26) | collective-permute-done | bytes 393248 | tf_op jit(solution)/shard_map/ppermute | solution.py:209
  161.8 5.2 %collective-permute-done.22.refs_2_ = bf16[768,256]{1,0:T(8,128)(2,1)S(1)} collective-permute-done((bf16[768,256]{1,0:T(8,128)(2,1)S(1)}, bf16[768,256]{1,0:T(8,128)(2,1)S(1)}, u32[]{:S(2)}, u32[]{:S(2)}) %collective-permute-start.22) | collective-permute-done | bytes 393248 | tf_op jit(solution)/shard_map/ppermute | solution.py:209
  168.8 3.4 %collective-permute-done.23.refs_3_ = bf16[768,256]{1,0:T(8,128)(2,1)S(1)} collective-permute-done((bf16[768,256]{1,0:T(8,128)(2,1)S(1)}, bf16[768,256]{1,0:T(8,128)(2,1)S(1)}, u32[]{:S(2)}, u32[]{:S(2)}) %collective-permute-start.23) | collective-permute-done | bytes 393248 | tf_op jit(solution)/shard_map/ppermute | solution.py:209
  172.7 3.6 %collective-permute-done.27.refs_7_ = bf16[768,256]{1,0:T(8,128)(2,1)S(1)} collective-permute-done((bf16[768,256]{1,0:T(8,128)(2,1)S(1)}, bf16[768,256]{1,0:T(8,128)(2,1)S(1)}, u32[]{:S(2)}, u32[]{:S(2)}) %collective-permute-start.27) | collective-permute-done | bytes 393248 | tf_op jit(solution)/shard_map/ppermute | solution.py:209
  179.9 12.6 %shard_map.82 = (f32[768,512]{1,0:T(8,128)}, bf16[768,512]{1,0:T(8,128)(2,1)}) custom-call(s32[7]{0:T(128)} %stack.91.places_ref, bf16[3072,768]{1,0:T(8,128)(2,1)} %all-gather.3.cloned.1.call-done.here_ref, bf16[3072,768]{1,0:T(8,128)(2,1)} %all-gather.5.cloned.1.call-done.across_ref, bf16[768,256]{1,0:T(8,128)(2,1)} %copy-done.9, ...), custom_call_target="tpu_custom_call" | custom-call | flops 4831838208 | bytes 20971520 | tf_op jit(solution)/shard_map/pallas_call | solution.py:167
  192.5 4.2 %collective-permute-start.37 = (bf16[768,512]{1,0:T(8,128)(2,1)}, bf16[768,512]{1,0:T(8,128)(2,1)S(1)}, u32[]{:S(2)}, u32[]{:S(2)}) collective-permute-start(bf16[768,512]{1,0:T(8,128)(2,1)} %get-tuple-element.25), channel_id=1, source_target_pairs={{0,96},{16,112},{32,0},{48,16},{64,32},{80,48},{96,64},{112,80},{1... | collective-permute-start | bytes 2359304 | tf_op jit(solution)/shard_map/ppermute | solution.py:214
  196.8 4.3 %collective-permute-start.38 = (bf16[768,512]{1,0:T(8,128)(2,1)}, bf16[768,512]{1,0:T(8,128)(2,1)S(1)}, u32[]{:S(2)}, u32[]{:S(2)}) collective-permute-start(bf16[768,512]{1,0:T(8,128)(2,1)} %get-tuple-element.25), channel_id=1, source_target_pairs={{0,16},{16,0},{32,48},{48,32},{64,80},{80,64},{96,112},{112,96},{1... | collective-permute-start | bytes 2359304 | tf_op jit(solution)/shard_map/ppermute | solution.py:214
  201.1 13.8 %collective-permute-done.36 = bf16[768,512]{1,0:T(8,128)(2,1)S(1)} collective-permute-done((bf16[768,512]{1,0:T(8,128)(2,1)}, bf16[768,512]{1,0:T(8,128)(2,1)S(1)}, u32[]{:S(2)}, u32[]{:S(2)}) %collective-permute-start.36) | collective-permute-done | bytes 786464 | tf_op jit(solution)/shard_map/ppermute | solution.py:214
  215.8 3.2 %collective-permute-start.40 = (bf16[384,512]{1,0:T(8,128)(2,1)}, bf16[384,512]{1,0:T(8,128)(2,1)S(1)}, u32[]{:S(2)}, u32[]{:S(2)}) collective-permute-start(bf16[384,512]{1,0:T(8,128)(2,1)} %slice.93), channel_id=1, source_target_pairs={{0,96},{16,112},{32,0},{48,16},{64,32},{80,48},{96,64},{112,80},{1... | collective-permute-start | bytes 1179656 | tf_op jit(solution)/shard_map/ppermute | solution.py:214
  221.1 3.2 %collective-permute-start.42 = (bf16[768,512]{1,0:T(8,128)(2,1)S(1)}, bf16[768,512]{1,0:T(8,128)(2,1)S(1)}, u32[]{:S(2)}, u32[]{:S(2)}) collective-permute-start(bf16[768,512]{1,0:T(8,128)(2,1)S(1)} %collective-permute-done.38), channel_id=1, source_target_pairs={{0,96},{16,112},{32,0},{48,16},{64,32},{80,48},{96,64},{112,80},{1... | collective-permute-start | bytes 2359304 | tf_op jit(solution)/shard_map/ppermute | solution.py:214
  224.3 3.9 %collective-permute-done.39 = bf16[384,512]{1,0:T(8,128)(2,1)S(1)} collective-permute-done((bf16[384,512]{1,0:T(8,128)(2,1)S(1)}, bf16[384,512]{1,0:T(8,128)(2,1)S(1)}, u32[]{:S(2)}, u32[]{:S(2)}) %collective-permute-start.39) | collective-permute-done | bytes 393248 | tf_op jit(solution)/shard_map/ppermute | solution.py:214
  228.9 4.4 %collective-permute-start.43 = (bf16[768,512]{1,0:T(8,128)(2,1)S(1)}, bf16[768,512]{1,0:T(8,128)(2,1)S(1)}, u32[]{:S(2)}, u32[]{:S(2)}) collective-permute-start(bf16[768,512]{1,0:T(8,128)(2,1)S(1)} %pad_maximum_fusion), channel_id=1, source_target_pairs={{0,16},{16,0},{32,48},{48,32},{64,80},{80,64},{96,112},{112,96},{1... | collective-permute-start | bytes 2359304 | tf_op jit(solution)/shard_map/ppermute | solution.py:214
  237.7 6.2 %collective-permute-done.41 = bf16[768,512]{1,0:T(8,128)(2,1)S(1)} collective-permute-done((bf16[768,512]{1,0:T(8,128)(2,1)S(1)}, bf16[768,512]{1,0:T(8,128)(2,1)S(1)}, u32[]{:S(2)}, u32[]{:S(2)}) %collective-permute-start.41) | collective-permute-done | bytes 786464 | tf_op jit(solution)/shard_map/ppermute | solution.py:214
  (155 shorter events, 67.9 us)
Async XLA Ops:
  7.2 171.8 %all-gather.3.cloned.1.call-start = ((), (), s32[]{:S(2)}) async-start(), calls=%async_computation | async-start | bytes 5898240 | tf_op jit(solution)/shard_map/all_gather | solution.py:312
  16.5 6.6 %collective-permute-start = (f32[3,768,256]{2,1,0:T(8,128)}, f32[3,768,256]{2,1,0:T(8,128)}, u32[]{:S(2)}, u32[]{:S(2)}) collective-permute-start(f32[3,768,256]{2,1,0:T(8,128)} %shard_map.78), channel_id=1, source_target_pairs={{0,1},{1,0},{2,3},{3,2},{4,5},{5,4},{6,7},{7,6},{8,9},{9,8},{10,11... | collective-permute-start | bytes 7077896 | tf_op jit(solution)/shard_map/ppermute | solution.py:209
  16.6 163.2 %all-gather.5.cloned.1.call-start = ((), (), s32[]{:S(2)}) async-start(), calls=%async_computation.1 | async-start | bytes 5898240 | tf_op jit(solution)/shard_map/all_gather | solution.py:312
  31.0 14.8 %collective-permute-start.1 = (f32[5,768,256]{2,1,0:T(8,128)}, f32[5,768,256]{2,1,0:T(8,128)}, u32[]{:S(2)}, u32[]{:S(2)}) collective-permute-start(f32[5,768,256]{2,1,0:T(8,128)} %shard_map.80), channel_id=1, source_target_pairs={{0,1},{1,0},{2,3},{3,2},{4,5},{5,4},{6,7},{7,6},{8,9},{9,8},{10,11... | collective-permute-start | bytes 11796488 | tf_op jit(solution)/shard_map/ppermute | solution.py:209
  31.5 12.7 %collective-permute-start.4 = (f16[768,256]{1,0:T(8,128)(2,1)}, f16[768,256]{1,0:T(8,128)(2,1)S(1)}, u32[]{:S(2)}, u32[]{:S(2)}) collective-permute-start(f16[768,256]{1,0:T(8,128)(2,1)} %get-tuple-element.15), channel_id=1, source_target_pairs={{0,2},{1,3},{2,0},{3,1},{4,6},{5,7},{6,4},{7,5},{8,10},{9,11},{10,... | collective-permute-start | bytes 1179656 | tf_op jit(solution)/shard_map/ppermute | solution.py:209
  34.7 16.2 %collective-permute-start.6 = (f16[768,256]{1,0:T(8,128)(2,1)}, f16[768,256]{1,0:T(8,128)(2,1)S(1)}, u32[]{:S(2)}, u32[]{:S(2)}) collective-permute-start(f16[768,256]{1,0:T(8,128)(2,1)} %get-tuple-element.17), channel_id=1, source_target_pairs={{0,4},{1,5},{2,6},{3,7},{4,8},{5,9},{6,10},{7,11},{8,12},{9,13},{1... | collective-permute-start | bytes 1179656 | tf_op jit(solution)/shard_map/ppermute | solution.py:209
  36.2 14.6 %collective-permute-start.7 = (f16[768,256]{1,0:T(8,128)(2,1)}, f16[768,256]{1,0:T(8,128)(2,1)S(1)}, u32[]{:S(2)}, u32[]{:S(2)}) collective-permute-start(f16[768,256]{1,0:T(8,128)(2,1)} %get-tuple-element.18), channel_id=1, source_target_pairs={{0,12},{1,13},{2,14},{3,15},{4,0},{5,1},{6,2},{7,3},{8,4},{9,5},{1... | collective-permute-start | bytes 1179656 | tf_op jit(solution)/shard_map/ppermute | solution.py:209
  44.2 39.2 %collective-permute-start.9 = (bf16[768,768]{1,0:T(8,128)(2,1)S(1)}, bf16[768,768]{1,0:T(8,128)(2,1)S(1)}, u32[]{:S(2)}, u32[]{:S(2)}) collective-permute-start(bf16[768,768]{1,0:T(8,128)(2,1)S(1)} %bitcast.89), channel_id=1, source_target_pairs={{0,16},{16,0},{32,48},{48,32},{64,80},{80,64},{96,112},{112,96},{1... | collective-permute-start | bytes 3538952 | tf_op jit(solution)/shard_map/ppermute | solution.py:214
  47.5 12.2 %collective-permute-start.2 = (f16[768,256]{1,0:T(8,128)(2,1)S(1)}, f16[768,256]{1,0:T(8,128)(2,1)S(1)}, u32[]{:S(2)}, u32[]{:S(2)}) collective-permute-start(f16[768,256]{1,0:T(8,128)(2,1)S(1)} %get-tuple-element.28), channel_id=1, source_target_pairs={{0,4},{1,5},{2,6},{3,7},{4,8},{5,9},{6,10},{7,11},{8,12},{9,13},{1... | collective-permute-start | bytes 1179656 | tf_op jit(solution)/shard_map/ppermute | solution.py:209
  49.2 17.5 %collective-permute-start.3 = (f16[768,256]{1,0:T(8,128)(2,1)S(1)}, f16[768,256]{1,0:T(8,128)(2,1)S(1)}, u32[]{:S(2)}, u32[]{:S(2)}) collective-permute-start(f16[768,256]{1,0:T(8,128)(2,1)S(1)} %get-tuple-element.29), channel_id=1, source_target_pairs={{0,12},{1,13},{2,14},{3,15},{4,0},{5,1},{6,2},{7,3},{8,4},{9,5},{1... | collective-permute-start | bytes 1179656 | tf_op jit(solution)/shard_map/ppermute | solution.py:209
  52.7 15.8 %collective-permute-start.5 = (f16[768,256]{1,0:T(8,128)(2,1)S(1)}, f16[768,256]{1,0:T(8,128)(2,1)S(1)}, u32[]{:S(2)}, u32[]{:S(2)}) collective-permute-start(f16[768,256]{1,0:T(8,128)(2,1)S(1)} %get-tuple-element.30), channel_id=1, source_target_pairs={{0,8},{1,9},{2,10},{3,11},{4,12},{5,13},{6,14},{7,15},{8,0},{9,1},... | collective-permute-start | bytes 1179656 | tf_op jit(solution)/shard_map/ppermute | solution.py:209
  54.7 27.2 %collective-permute-start.8 = (f16[768,256]{1,0:T(8,128)(2,1)S(1)}, f16[768,256]{1,0:T(8,128)(2,1)S(1)}, u32[]{:S(2)}, u32[]{:S(2)}) collective-permute-start(f16[768,256]{1,0:T(8,128)(2,1)S(1)} %get-tuple-element.31), channel_id=1, source_target_pairs={{0,2},{1,3},{2,0},{3,1},{4,6},{5,7},{6,4},{7,5},{8,10},{9,11},{10,... | collective-permute-start | bytes 1179656 | tf_op jit(solution)/shard_map/ppermute | solution.py:209
  131.0 21.2 %collective-permute-start.21 = (bf16[768,256]{1,0:T(8,128)(2,1)S(1)}, bf16[768,256]{1,0:T(8,128)(2,1)S(1)}, u32[]{:S(2)}, u32[]{:S(2)}) collective-permute-start(bf16[768,256]{1,0:T(8,128)(2,1)S(1)} %collective-permute-done.20.refs_0_), channel_id=1, source_target_pairs={{0,2},{1,3},{2,0},{3,1},{4,6},{5,7},{6,4},{7,5},{8,10},{9,11},{10,... | collective-permute-start | bytes 1179656 | tf_op jit(solution)/shard_map/ppermute | solution.py:209
  142.2 16.8 %collective-permute-start.26 = (bf16[768,256]{1,0:T(8,128)(2,1)S(1)}, bf16[768,256]{1,0:T(8,128)(2,1)S(1)}, u32[]{:S(2)}, u32[]{:S(2)}) collective-permute-start(bf16[768,256]{1,0:T(8,128)(2,1)S(1)} %collective-permute-done.20.refs_0_), channel_id=1, source_target_pairs={{0,8},{1,9},{2,10},{3,11},{4,12},{5,13},{6,14},{7,15},{8,0},{9,1},... | collective-permute-start | bytes 1179656 | tf_op jit(solution)/shard_map/ppermute | solution.py:209
  149.0 18.0 %collective-permute-start.22 = (bf16[768,256]{1,0:T(8,128)(2,1)S(1)}, bf16[768,256]{1,0:T(8,128)(2,1)S(1)}, u32[]{:S(2)}, u32[]{:S(2)}) collective-permute-start(bf16[768,256]{1,0:T(8,128)(2,1)S(1)} %collective-permute-done.20.refs_0_), channel_id=1, source_target_pairs={{0,4},{1,5},{2,6},{3,7},{4,8},{5,9},{6,10},{7,11},{8,12},{9,13},{1... | collective-permute-start | bytes 1179656 | tf_op jit(solution)/shard_map/ppermute | solution.py:209
  149.1 19.1 %collective-permute-start.24 = (bf16[768,256]{1,0:T(8,128)(2,1)S(1)}, bf16[768,256]{1,0:T(8,128)(2,1)S(1)}, u32[]{:S(2)}, u32[]{:S(2)}) collective-permute-start(bf16[768,256]{1,0:T(8,128)(2,1)S(1)} %collective-permute-done.20.refs_0_), channel_id=1, source_target_pairs={{0,12},{1,13},{2,14},{3,15},{4,0},{5,1},{6,2},{7,3},{8,4},{9,5},{1... | collective-permute-start | bytes 1179656 | tf_op jit(solution)/shard_map/ppermute | solution.py:209
  152.2 16.0 %collective-permute-start.28 = (bf16[768,256]{1,0:T(8,128)(2,1)S(1)}, bf16[768,256]{1,0:T(8,128)(2,1)S(1)}, u32[]{:S(2)}, u32[]{:S(2)}) collective-permute-start(bf16[768,256]{1,0:T(8,128)(2,1)S(1)} %collective-permute-done.20.refs_0_), channel_id=1, source_target_pairs={{0,1},{1,0},{2,3},{3,2},{4,5},{5,4},{6,7},{7,6},{8,9},{9,8},{10,11... | collective-permute-start | bytes 1179656 | tf_op jit(solution)/shard_map/ppermute | solution.py:209
  152.2 19.9 %collective-permute-start.23 = (bf16[768,256]{1,0:T(8,128)(2,1)S(1)}, bf16[768,256]{1,0:T(8,128)(2,1)S(1)}, u32[]{:S(2)}, u32[]{:S(2)}) collective-permute-start(bf16[768,256]{1,0:T(8,128)(2,1)S(1)} %collective-permute-done.21.refs_1_), channel_id=1, source_target_pairs={{0,4},{1,5},{2,6},{3,7},{4,8},{5,9},{6,10},{7,11},{8,12},{9,13},{1... | collective-permute-start | bytes 1179656 | tf_op jit(solution)/shard_map/ppermute | solution.py:209
  159.1 13.1 %collective-permute-start.25 = (bf16[768,256]{1,0:T(8,128)(2,1)S(1)}, bf16[768,256]{1,0:T(8,128)(2,1)S(1)}, u32[]{:S(2)}, u32[]{:S(2)}) collective-permute-start(bf16[768,256]{1,0:T(8,128)(2,1)S(1)} %collective-permute-done.21.refs_1_), channel_id=1, source_target_pairs={{0,12},{1,13},{2,14},{3,15},{4,0},{5,1},{6,2},{7,3},{8,4},{9,5},{1... | collective-permute-start | bytes 1179656 | tf_op jit(solution)/shard_map/ppermute | solution.py:209
  167.0 9.3 %collective-permute-start.27 = (bf16[768,256]{1,0:T(8,128)(2,1)S(1)}, bf16[768,256]{1,0:T(8,128)(2,1)S(1)}, u32[]{:S(2)}, u32[]{:S(2)}) collective-permute-start(bf16[768,256]{1,0:T(8,128)(2,1)S(1)} %collective-permute-done.26.refs_6_), channel_id=1, source_target_pairs={{0,2},{1,3},{2,0},{3,1},{4,6},{5,7},{6,4},{7,5},{8,10},{9,11},{10,... | collective-permute-start | bytes 1179656 | tf_op jit(solution)/shard_map/ppermute | solution.py:209
  168.3 8.0 %collective-permute-start.29 = (bf16[768,256]{1,0:T(8,128)(2,1)S(1)}, bf16[768,256]{1,0:T(8,128)(2,1)S(1)}, u32[]{:S(2)}, u32[]{:S(2)}) collective-permute-start(bf16[768,256]{1,0:T(8,128)(2,1)S(1)} %collective-permute-done.21.refs_1_), channel_id=1, source_target_pairs={{0,1},{1,0},{2,3},{3,2},{4,5},{5,4},{6,7},{7,6},{8,9},{9,8},{10,11... | collective-permute-start | bytes 1179656 | tf_op jit(solution)/shard_map/ppermute | solution.py:209
  168.3 8.5 %collective-permute-start.30 = (bf16[768,256]{1,0:T(8,128)(2,1)S(1)}, bf16[768,256]{1,0:T(8,128)(2,1)S(1)}, u32[]{:S(2)}, u32[]{:S(2)}) collective-permute-start(bf16[768,256]{1,0:T(8,128)(2,1)S(1)} %collective-permute-done.22.refs_2_), channel_id=1, source_target_pairs={{0,1},{1,0},{2,3},{3,2},{4,5},{5,4},{6,7},{7,6},{8,9},{9,8},{10,11... | collective-permute-start | bytes 1179656 | tf_op jit(solution)/shard_map/ppermute | solution.py:209
  172.2 6.8 %collective-permute-start.34 = (bf16[768,256]{1,0:T(8,128)(2,1)S(1)}, bf16[768,256]{1,0:T(8,128)(2,1)}, u32[]{:S(2)}, u32[]{:S(2)}) collective-permute-start(bf16[768,256]{1,0:T(8,128)(2,1)S(1)} %collective-permute-done.26.refs_6_), channel_id=1, source_target_pairs={{0,1},{1,0},{2,3},{3,2},{4,5},{5,4},{6,7},{7,6},{8,9},{9,8},{10,11... | collective-permute-start | bytes 1179656 | tf_op jit(solution)/shard_map/ppermute | solution.py:209
  172.2 6.8 %collective-permute-start.32 = (bf16[768,256]{1,0:T(8,128)(2,1)S(1)}, bf16[768,256]{1,0:T(8,128)(2,1)}, u32[]{:S(2)}, u32[]{:S(2)}) collective-permute-start(bf16[768,256]{1,0:T(8,128)(2,1)S(1)} %collective-permute-done.24.refs_4_), channel_id=1, source_target_pairs={{0,1},{1,0},{2,3},{3,2},{4,5},{5,4},{6,7},{7,6},{8,9},{9,8},{10,11... | collective-permute-start | bytes 1179656 | tf_op jit(solution)/shard_map/ppermute | solution.py:209
  192.4 22.5 %collective-permute-start.36 = (bf16[768,512]{1,0:T(8,128)(2,1)}, bf16[768,512]{1,0:T(8,128)(2,1)S(1)}, u32[]{:S(2)}, u32[]{:S(2)}) collective-permute-start(bf16[768,512]{1,0:T(8,128)(2,1)} %get-tuple-element.25), channel_id=1, source_target_pairs={{0,32},{16,48},{32,64},{48,80},{64,96},{80,112},{96,0},{112,16},{1... | collective-permute-start | bytes 2359304 | tf_op jit(solution)/shard_map/ppermute | solution.py:214
  192.5 22.5 %collective-permute-start.37 = (bf16[768,512]{1,0:T(8,128)(2,1)}, bf16[768,512]{1,0:T(8,128)(2,1)S(1)}, u32[]{:S(2)}, u32[]{:S(2)}) collective-permute-start(bf16[768,512]{1,0:T(8,128)(2,1)} %get-tuple-element.25), channel_id=1, source_target_pairs={{0,96},{16,112},{32,0},{48,16},{64,32},{80,48},{96,64},{112,80},{1... | collective-permute-start | bytes 2359304 | tf_op jit(solution)/shard_map/ppermute | solution.py:214
  196.8 22.3 %collective-permute-start.38 = (bf16[768,512]{1,0:T(8,128)(2,1)}, bf16[768,512]{1,0:T(8,128)(2,1)S(1)}, u32[]{:S(2)}, u32[]{:S(2)}) collective-permute-start(bf16[768,512]{1,0:T(8,128)(2,1)} %get-tuple-element.25), channel_id=1, source_target_pairs={{0,16},{16,0},{32,48},{48,32},{64,80},{80,64},{96,112},{112,96},{1... | collective-permute-start | bytes 2359304 | tf_op jit(solution)/shard_map/ppermute | solution.py:214
  214.9 13.3 %collective-permute-start.39 = (bf16[384,512]{1,0:T(8,128)(2,1)S(1)}, bf16[384,512]{1,0:T(8,128)(2,1)S(1)}, u32[]{:S(2)}, u32[]{:S(2)}) collective-permute-start(bf16[384,512]{1,0:T(8,128)(2,1)S(1)} %slice.92), channel_id=1, source_target_pairs={{0,32},{16,48},{32,64},{48,80},{64,96},{80,112},{96,0},{112,16},{1... | collective-permute-start | bytes 1179656 | tf_op jit(solution)/shard_map/ppermute | solution.py:214
  215.8 13.1 %collective-permute-start.40 = (bf16[384,512]{1,0:T(8,128)(2,1)}, bf16[384,512]{1,0:T(8,128)(2,1)S(1)}, u32[]{:S(2)}, u32[]{:S(2)}) collective-permute-start(bf16[384,512]{1,0:T(8,128)(2,1)} %slice.93), channel_id=1, source_target_pairs={{0,96},{16,112},{32,0},{48,16},{64,32},{80,48},{96,64},{112,80},{1... | collective-permute-start | bytes 1179656 | tf_op jit(solution)/shard_map/ppermute | solution.py:214
  219.0 24.8 %collective-permute-start.41 = (bf16[768,512]{1,0:T(8,128)(2,1)S(1)}, bf16[768,512]{1,0:T(8,128)(2,1)S(1)}, u32[]{:S(2)}, u32[]{:S(2)}) collective-permute-start(bf16[768,512]{1,0:T(8,128)(2,1)S(1)} %collective-permute-done.38), channel_id=1, source_target_pairs={{0,32},{16,48},{32,64},{48,80},{64,96},{80,112},{96,0},{112,16},{1... | collective-permute-start | bytes 2359304 | tf_op jit(solution)/shard_map/ppermute | solution.py:214
  221.1 23.7 %collective-permute-start.42 = (bf16[768,512]{1,0:T(8,128)(2,1)S(1)}, bf16[768,512]{1,0:T(8,128)(2,1)S(1)}, u32[]{:S(2)}, u32[]{:S(2)}) collective-permute-start(bf16[768,512]{1,0:T(8,128)(2,1)S(1)} %collective-permute-done.38), channel_id=1, source_target_pairs={{0,96},{16,112},{32,0},{48,16},{64,32},{80,48},{96,64},{112,80},{1... | collective-permute-start | bytes 2359304 | tf_op jit(solution)/shard_map/ppermute | solution.py:214
  228.9 19.2 %collective-permute-start.43 = (bf16[768,512]{1,0:T(8,128)(2,1)S(1)}, bf16[768,512]{1,0:T(8,128)(2,1)S(1)}, u32[]{:S(2)}, u32[]{:S(2)}) collective-permute-start(bf16[768,512]{1,0:T(8,128)(2,1)S(1)} %pad_maximum_fusion), channel_id=1, source_target_pairs={{0,16},{16,0},{32,48},{48,32},{64,80},{80,64},{96,112},{112,96},{1... | collective-permute-start | bytes 2359304 | tf_op jit(solution)/shard_map/ppermute | solution.py:214
  (38 other events, 428.0 us)
Sparse Core Ops, SparseCore 0:
  16.7 55.4 all-gather.2
  84.6 53.1 all-gather.4

commit v5 on v4

--- a/solution.py
+++ b/solution.py
@@ -108,7 +108,7 @@
         cross_ref[s] = jnp.sum(jnp.where(eye, crossed[s], 0.0), axis=0, keepdims=True)
 
 
-def attention(lens, weights, scales, merged, squares, gain, taps, slots=2):
+def attention(lens, weights, scales, merged, squares, gain, taps, slots=4):
     count, span, wide = merged.shape
     scalar = pl.BlockSpec(memory_space=pltpu.SMEM)
     block = pl.BlockSpec((slots, span, wide), lambda i: (i, 0, 0))
@@ -333,16 +333,14 @@
     up_across = send(up_across, 1, 0)
     down_across = send(down_across, 3, 0)
     second = chip_sums(rows_now, ORDER[1])
-    far_across, rows_now = lax.optimization_barrier((far_across, rows_now))
-    rows_across = row_major(to_group(rows_now, 0, 1))
     up = send(second[1, 0], 1, 0).astype(f32)
     down = send(second[3, 0], 3, 0).astype(f32)
     far = send(second[2, 0] + far_across.astype(f32), 2, 0).astype(f32)
     across = send(second[0, 1] + up_across.astype(f32) + down_across.astype(f32), 0, 1).astype(f32)
     merged = (second[0, 0] + up + down + far + across) * (1.0 / SEND)
     merged = merged.reshape(slots, span, wide)
-    merged, rows_across = lax.optimization_barrier((merged, rows_across))
-    taps_across = gather_taps(rows_across)
+    merged, rows_now = lax.optimization_barrier((merged, rows_now))
+    rows_across = row_major(to_group(rows_now, 0, 1))
     squares = sum_over_tr(jnp.sum(merged * merged, axis=2))
 
     scaled, crossed = attention(
@@ -354,6 +352,8 @@
         norm_gain.reshape(1, wide),
         taps[:, :, 2, :],
     )
+    crossed, rows_across = lax.optimization_barrier((crossed, rows_across))
+    taps_across = gather_taps(rows_across)
     crossed = sum_over_tr(crossed.reshape(slots, span))
     inverse = lax.rsqrt(squares / width_all + epsilon)
     merged_grad = (

time: 258 us -> 258 us (level)
  Pallas kernels: 42 us -> 37.6 us
  waiting for transfers between devices: 84.4 us -> 88.7 us
    ppermute x9, starting transfers between devices: 21.2 us -> 15.4 us  [to_group(): return lax.ppermute(value, 'rep', pairs)]
    ppermute x34, starting transfers between devices: 57.2 us -> 61.8 us  [to_chip(): return lax.ppermute(value, 'tr', pairs)]
    pallas_call x1, Pallas kernels: 15.8 us -> 11.3 us  [attention(): pl.pallas_call(attention_kernel, grid=(count // slots,), in_specs=[scalar...]
    ppermute x34, waiting for transfers between devices: 57.3 us -> 60.2 us  [to_chip(): return lax.ppermute(value, 'tr', pairs)]
  transfers between devices with their start and end apart: 46 -> 46, of which waited for: 24 -> 23; matrix products, arithmetic and copies ran while one was open for 8% -> 9% of each run, Pallas kernels for 10% -> 8%
where the time goes in v5:
time: 258 us; the launch traced here: 256 us
  waiting for transfers between devices  88.7 us (34%)
  starting transfers between devices  78 us (30%)
  Pallas kernels  37.6 us (15%)
  local copies, waits for them, and re-layouts  25.7 us (10%)
  between operations  14.6 us (6%)
  other arithmetic  11.5 us (4%)
    ppermute x34, starting transfers between devices, to_chip(): return lax.ppermute(value, 'tr', pairs)  61.8 us
    ppermute x34, waiting for transfers between devices, to_chip(): return lax.ppermute(value, 'tr', pairs)  60.2 us
    ppermute x9, waiting for transfers between devices, to_group(): return lax.ppermute(value, 'rep', pairs)  28.5 us
    ppermute x9, starting transfers between devices, to_group(): return lax.ppermute(value, 'rep', pairs)  15.4 us
    pallas_call x4, Pallas kernels, products(): pl.pallas_call(product_kernel, grid_spec=pltpu.PrefetchScalarGridSpec(num...  13.7 us
    pallas_call x1, Pallas kernels, gradient(): pl.pallas_call(gradient_kernel, grid_spec=pltpu.PrefetchScalarGridSpec(nu...  12.6 us
    unnamed x49, local copies, waits for them, and re-layouts  11.4 us
    pallas_call x1, Pallas kernels, attention(): pl.pallas_call(attention_kernel, grid=(count // slots,), in_specs=[scalar...  11.3 us
  transfers between devices with their start and end apart: 46, of which 23 were waited for; matrix products, arithmetic and copies ran while one was open for 9% of the time, Pallas kernels for 8%

profile of v5, /device:TPU:0, one launch (start us, length us, event | category | flops | bytes accessed | tf_op | source)
XLA Modules:
  0.0 256.1 jit_solution(13089813110230021593)
XLA Ops:
  7.3 2.3 copy.16
  10.0 3.1 %copy-done = bf16[3,256,4096]{2,1,0:T(8,128)(2,1)S(1)} copy-done((bf16[3,256,4096]{2,1,0:T(8,128)(2,1)S(1)}, bf16[3,256,4096]{2,1,0:T(8,128)(2,1)}, u32[]{:S(2)}) %copy-start) | copy-done | bytes 6291480
  13.1 3.4 %shard_map.78 = f32[3,768,256]{2,1,0:T(8,128)} custom-call(s32[3]{0:T(128)S(1)} %pad_add_fusion.1.blocks_ref, bf16[768,768]{1,0:T(8,128)(2,1)S(1)} %bitcast.84, bf16[768,4096]{1,0:T(8,128)(2,1)S(1)} %bitcast.78), custom_call_target="tpu_custom_call" | custom-call | flops 905969664 | bytes 4718592 | tf_op jit(solution)/shard_map/pallas_call | solution.py:260
  16.9 2.8 %copy-done.1 = bf16[3,256,4096]{2,1,0:T(8,128)(2,1)S(1)} copy-done((bf16[3,256,4096]{2,1,0:T(8,128)(2,1)S(1)}, bf16[3,256,4096]{2,1,0:T(8,128)(2,1)}, u32[]{:S(2)}) %copy-start.1) | copy-done | bytes 6291480
  23.2 2.9 %fusion.28 = (f16[768,256]{1,0:T(8,128)(2,1)}, f16[768,256]{1,0:T(8,128)(2,1)}, f16[768,256]{1,0:T(8,128)(2,1)}) fusion(f32[3,768,256]{2,1,0:T(8,128)} %collective-permute-done, f32[3,768,256]{2,1,0:T(8,128)S(1)} %shard_map.77), kind=kLoop, calls=%fused_computation.39 | loop fusion | flops 1769472 | bytes 5898240 | tf_op jit(solution)/shard_map/convert_element_type | solution.py:330
  26.1 4.8 %shard_map.80 = f32[5,768,256]{2,1,0:T(8,128)} custom-call(s32[5]{0:T(128)S(1)} %stack.111.blocks_ref, bf16[768,768]{1,0:T(8,128)(2,1)S(1)} %bitcast.87, bf16[768,4096]{1,0:T(8,128)(2,1)S(1)} %bitcast.82), custom_call_target="tpu_custom_call" | custom-call | flops 1509949440 | bytes 7077888 | tf_op jit(solution)/shard_map/pallas_call | solution.py:260
  31.5 3.1 %collective-permute-start.4 = (f16[768,256]{1,0:T(8,128)(2,1)}, f16[768,256]{1,0:T(8,128)(2,1)S(1)}, u32[]{:S(2)}, u32[]{:S(2)}) collective-permute-start(f16[768,256]{1,0:T(8,128)(2,1)} %get-tuple-element.15), channel_id=1, source_target_pairs={{0,2},{1,3},{2,0},{3,1},{4,6},{5,7},{6,4},{7,5},{8,10},{9,11},{10,... | collective-permute-start | bytes 1179656 | tf_op jit(solution)/shard_map/ppermute | solution.py:209
  37.9 2.9 %copy-done.2 = bf16[3,256,4096]{2,1,0:T(8,128)(2,1)S(1)} copy-done((bf16[3,256,4096]{2,1,0:T(8,128)(2,1)S(1)}, bf16[3,256,4096]{2,1,0:T(8,128)(2,1)}, u32[]{:S(2)}) %copy-start.2) | copy-done | bytes 6291480
  40.7 3.3 %shard_map.79 = f32[5,768,256]{2,1,0:T(8,128)S(1)} custom-call(s32[5]{0:T(128)S(1)} %stack.97.blocks_ref, bf16[768,768]{1,0:T(8,128)(2,1)S(1)} %bitcast.88, bf16[768,4096]{1,0:T(8,128)(2,1)S(1)} %bitcast.83), custom_call_target="tpu_custom_call" | custom-call | flops 1509949440 | bytes 7077888 | tf_op jit(solution)/shard_map/pallas_call | solution.py:260
  44.1 3.8 %fusion.29 = (f16[768,256]{1,0:T(8,128)(2,1)}, f16[768,256]{1,0:T(8,128)(2,1)}) fusion(f32[5,768,256]{2,1,0:T(8,128)} %collective-permute-done.1, f32[5,768,256]{2,1,0:T(8,128)S(1)} %shard_map.79), kind=kLoop, calls=%fused_computation.40 | loop fusion | flops 1179648 | bytes 3932160 | tf_op jit(solution)/shard_map/convert_element_type | solution.py:326
  48.3 2.9 %collective-permute-start.3 = (f16[768,256]{1,0:T(8,128)(2,1)}, f16[768,256]{1,0:T(8,128)(2,1)}, u32[]{:S(2)}, u32[]{:S(2)}) collective-permute-start(f16[768,256]{1,0:T(8,128)(2,1)} %get-tuple-element.29), channel_id=1, source_target_pairs={{0,12},{1,13},{2,14},{3,15},{4,0},{5,1},{6,2},{7,3},{8,4},{9,5},{1... | collective-permute-start | bytes 1179656 | tf_op jit(solution)/shard_map/ppermute | solution.py:209
  55.3 12.9 %collective-permute-done.2 = f16[768,256]{1,0:T(8,128)(2,1)} collective-permute-done((f16[768,256]{1,0:T(8,128)(2,1)}, f16[768,256]{1,0:T(8,128)(2,1)}, u32[]{:S(2)}, u32[]{:S(2)}) %collective-permute-start.2) | collective-permute-done | bytes 393248 | tf_op jit(solution)/shard_map/ppermute | solution.py:209
  74.3 22.5 %collective-permute-done.10 = f32[8,96]{1,0:T(8,128)S(1)} collective-permute-done((f32[8,96]{1,0:T(8,128)S(1)}, f32[8,96]{1,0:T(8,128)S(1)}, u32[]{:S(2)}, u32[]{:S(2)}) %collective-permute-start.10) | collective-permute-done | bytes 3104 | tf_op jit(solution)/shard_map/ppermute | solution.py:209
  103.2 11.3 %shard_map.81 = (f32[8,96,256]{2,1,0:T(8,128)S(1)}, f32[8,1,96]{2,1,0:T(1,128)S(1)}) custom-call(s32[8]{0:T(128)S(1)} %dynamic_slice.6.lens_ref, f32[8]{0:T(128)S(1)} %convert_divide_fusion.weights_ref, f32[2]{0:T(128)S(1)} %copy-done.8, f32[8,96,256]{2,1,0:T(8,128)S(1)} %bitcast.91, f32[8,1,96]{2,1,0:T(1,128)S(1)} %bitcast.93, f32[1,256]{1,0:T(1,128)S(1)} %bitcast.96, ...), custom_call_target="tpu_custom_call" | custom-call | flops 2000000000 | bytes 3000000 | tf_op jit(solution)/shard_map/pallas_call | solution.py:116
  117.5 3.5 %collective-permute-done.16 = f32[8,96]{1,0:T(8,128)S(1)} collective-permute-done((f32[8,96]{1,0:T(8,128)S(1)}, f32[8,96]{1,0:T(8,128)S(1)}, u32[]{:S(2)}, u32[]{:S(2)}) %collective-permute-start.16) | collective-permute-done | bytes 3104 | tf_op jit(solution)/shard_map/ppermute | solution.py:209
  129.1 11.2 %collective-permute-start.21 = (bf16[768,256]{1,0:T(8,128)(2,1)S(1)}, bf16[768,256]{1,0:T(8,128)(2,1)S(1)}, u32[]{:S(2)}, u32[]{:S(2)}) collective-permute-start(bf16[768,256]{1,0:T(8,128)(2,1)S(1)} %collective-permute-done.20.refs_0_), channel_id=1, source_target_pairs={{0,2},{1,3},{2,0},{3,1},{4,6},{5,7},{6,4},{7,5},{8,10},{9,11},{10,... | collective-permute-start | bytes 1179656 | tf_op jit(solution)/shard_map/ppermute | solution.py:209
  140.4 12.0 %collective-permute-start.26 = (bf16[768,256]{1,0:T(8,128)(2,1)S(1)}, bf16[768,256]{1,0:T(8,128)(2,1)S(1)}, u32[]{:S(2)}, u32[]{:S(2)}) collective-permute-start(bf16[768,256]{1,0:T(8,128)(2,1)S(1)} %collective-permute-done.20.refs_0_), channel_id=1, source_target_pairs={{0,8},{1,9},{2,10},{3,11},{4,12},{5,13},{6,14},{7,15},{8,0},{9,1},... | collective-permute-start | bytes 1179656 | tf_op jit(solution)/shard_map/ppermute | solution.py:209
  155.6 3.2 %collective-permute-start.23 = (bf16[768,256]{1,0:T(8,128)(2,1)S(1)}, bf16[768,256]{1,0:T(8,128)(2,1)S(1)}, u32[]{:S(2)}, u32[]{:S(2)}) collective-permute-start(bf16[768,256]{1,0:T(8,128)(2,1)S(1)} %collective-permute-done.21.refs_1_), channel_id=1, source_target_pairs={{0,4},{1,5},{2,6},{3,7},{4,8},{5,9},{6,10},{7,11},{8,12},{9,13},{1... | collective-permute-start | bytes 1179656 | tf_op jit(solution)/shard_map/ppermute | solution.py:209
  158.8 3.6 %collective-permute-done.26.refs_6_ = bf16[768,256]{1,0:T(8,128)(2,1)S(1)} collective-permute-done((bf16[768,256]{1,0:T(8,128)(2,1)S(1)}, bf16[768,256]{1,0:T(8,128)(2,1)S(1)}, u32[]{:S(2)}, u32[]{:S(2)}) %collective-permute-start.26) | collective-permute-done | bytes 393248 | tf_op jit(solution)/shard_map/ppermute | solution.py:209
  162.4 4.2 %collective-permute-start.25 = (bf16[768,256]{1,0:T(8,128)(2,1)S(1)}, bf16[768,256]{1,0:T(8,128)(2,1)S(1)}, u32[]{:S(2)}, u32[]{:S(2)}) collective-permute-start(bf16[768,256]{1,0:T(8,128)(2,1)S(1)} %collective-permute-done.21.refs_1_), channel_id=1, source_target_pairs={{0,12},{1,13},{2,14},{3,15},{4,0},{5,1},{6,2},{7,3},{8,4},{9,5},{1... | collective-permute-start | bytes 1179656 | tf_op jit(solution)/shard_map/ppermute | solution.py:209
  166.7 3.7 %collective-permute-done.22.refs_2_ = bf16[768,256]{1,0:T(8,128)(2,1)S(1)} collective-permute-done((bf16[768,256]{1,0:T(8,128)(2,1)S(1)}, bf16[768,256]{1,0:T(8,128)(2,1)S(1)}, u32[]{:S(2)}, u32[]{:S(2)}) %collective-permute-start.22) | collective-permute-done | bytes 393248 | tf_op jit(solution)/shard_map/ppermute | solution.py:209
  170.4 3.2 %collective-permute-start.27 = (bf16[768,256]{1,0:T(8,128)(2,1)S(1)}, bf16[768,256]{1,0:T(8,128)(2,1)S(1)}, u32[]{:S(2)}, u32[]{:S(2)}) collective-permute-start(bf16[768,256]{1,0:T(8,128)(2,1)S(1)} %collective-permute-done.26.refs_6_), channel_id=1, source_target_pairs={{0,2},{1,3},{2,0},{3,1},{4,6},{5,7},{6,4},{7,5},{8,10},{9,11},{10,... | collective-permute-start | bytes 1179656 | tf_op jit(solution)/shard_map/ppermute | solution.py:209
  176.3 3.3 %collective-permute-done.27.refs_7_ = bf16[768,256]{1,0:T(8,128)(2,1)S(1)} collective-permute-done((bf16[768,256]{1,0:T(8,128)(2,1)S(1)}, bf16[768,256]{1,0:T(8,128)(2,1)S(1)}, u32[]{:S(2)}, u32[]{:S(2)}) %collective-permute-start.27) | collective-permute-done | bytes 393248 | tf_op jit(solution)/shard_map/ppermute | solution.py:209
  183.2 12.6 %shard_map.82 = (f32[768,512]{1,0:T(8,128)}, bf16[768,512]{1,0:T(8,128)(2,1)}) custom-call(s32[7]{0:T(128)} %stack.91.places_ref, bf16[3072,768]{1,0:T(8,128)(2,1)} %all-gather.3.cloned.1.call-done.here_ref, bf16[3072,768]{1,0:T(8,128)(2,1)} %all-gather.5.cloned.1.call-done.across_ref, bf16[768,256]{1,0:T(8,128)(2,1)} %copy-done.9, ...), custom_call_target="tpu_custom_call" | custom-call | flops 4831838208 | bytes 20971520 | tf_op jit(solution)/shard_map/pallas_call | solution.py:167
  195.8 3.2 %collective-permute-start.37 = (bf16[768,512]{1,0:T(8,128)(2,1)}, bf16[768,512]{1,0:T(8,128)(2,1)S(1)}, u32[]{:S(2)}, u32[]{:S(2)}) collective-permute-start(bf16[768,512]{1,0:T(8,128)(2,1)} %get-tuple-element.25), channel_id=1, source_target_pairs={{0,96},{16,112},{32,0},{48,16},{64,32},{80,48},{96,64},{112,80},{1... | collective-permute-start | bytes 2359304 | tf_op jit(solution)/shard_map/ppermute | solution.py:214
  199.0 2.7 %collective-permute-start.38 = (bf16[768,512]{1,0:T(8,128)(2,1)}, bf16[768,512]{1,0:T(8,128)(2,1)S(1)}, u32[]{:S(2)}, u32[]{:S(2)}) collective-permute-start(bf16[768,512]{1,0:T(8,128)(2,1)} %get-tuple-element.25), channel_id=1, source_target_pairs={{0,16},{16,0},{32,48},{48,32},{64,80},{80,64},{96,112},{112,96},{1... | collective-permute-start | bytes 2359304 | tf_op jit(solution)/shard_map/ppermute | solution.py:214
  201.7 15.2 %collective-permute-done.36 = bf16[768,512]{1,0:T(8,128)(2,1)S(1)} collective-permute-done((bf16[768,512]{1,0:T(8,128)(2,1)}, bf16[768,512]{1,0:T(8,128)(2,1)S(1)}, u32[]{:S(2)}, u32[]{:S(2)}) %collective-permute-start.36) | collective-permute-done | bytes 786464 | tf_op jit(solution)/shard_map/ppermute | solution.py:214
  218.5 2.6 %collective-permute-start.40 = (bf16[384,512]{1,0:T(8,128)(2,1)}, bf16[384,512]{1,0:T(8,128)(2,1)S(1)}, u32[]{:S(2)}, u32[]{:S(2)}) collective-permute-start(bf16[384,512]{1,0:T(8,128)(2,1)} %slice.93), channel_id=1, source_target_pairs={{0,96},{16,112},{32,0},{48,16},{64,32},{80,48},{96,64},{112,80},{1... | collective-permute-start | bytes 1179656 | tf_op jit(solution)/shard_map/ppermute | solution.py:214
  223.1 3.2 %collective-permute-start.42 = (bf16[768,512]{1,0:T(8,128)(2,1)S(1)}, bf16[768,512]{1,0:T(8,128)(2,1)S(1)}, u32[]{:S(2)}, u32[]{:S(2)}) collective-permute-start(bf16[768,512]{1,0:T(8,128)(2,1)S(1)} %collective-permute-done.38), channel_id=1, source_target_pairs={{0,96},{16,112},{32,0},{48,16},{64,32},{80,48},{96,64},{112,80},{1... | collective-permute-start | bytes 2359304 | tf_op jit(solution)/shard_map/ppermute | solution.py:214
  226.4 3.9 %collective-permute-done.39 = bf16[384,512]{1,0:T(8,128)(2,1)S(1)} collective-permute-done((bf16[384,512]{1,0:T(8,128)(2,1)S(1)}, bf16[384,512]{1,0:T(8,128)(2,1)S(1)}, u32[]{:S(2)}, u32[]{:S(2)}) %collective-permute-start.39) | collective-permute-done | bytes 393248 | tf_op jit(solution)/shard_map/ppermute | solution.py:214
  231.0 2.8 %collective-permute-start.43 = (bf16[768,512]{1,0:T(8,128)(2,1)S(1)}, bf16[768,512]{1,0:T(8,128)(2,1)S(1)}, u32[]{:S(2)}, u32[]{:S(2)}) collective-permute-start(bf16[768,512]{1,0:T(8,128)(2,1)S(1)} %pad_maximum_fusion), channel_id=1, source_target_pairs={{0,16},{16,0},{32,48},{48,32},{64,80},{80,64},{96,112},{112,96},{1... | collective-permute-start | bytes 2359304 | tf_op jit(solution)/shard_map/ppermute | solution.py:214
  238.1 7.5 %collective-permute-done.41 = bf16[768,512]{1,0:T(8,128)(2,1)S(1)} collective-permute-done((bf16[768,512]{1,0:T(8,128)(2,1)S(1)}, bf16[768,512]{1,0:T(8,128)(2,1)S(1)}, u32[]{:S(2)}, u32[]{:S(2)}) %collective-permute-start.41) | collective-permute-done | bytes 786464 | tf_op jit(solution)/shard_map/ppermute | solution.py:214
  (155 shorter events, 57.7 us)
Async XLA Ops:
  7.2 175.1 %all-gather.3.cloned.1.call-start = ((), (), s32[]{:S(2)}) async-start(), calls=%async_computation | async-start | bytes 5898240 | tf_op jit(solution)/shard_map/all_gather | solution.py:312
  16.5 6.6 %collective-permute-start = (f32[3,768,256]{2,1,0:T(8,128)}, f32[3,768,256]{2,1,0:T(8,128)}, u32[]{:S(2)}, u32[]{:S(2)}) collective-permute-start(f32[3,768,256]{2,1,0:T(8,128)} %shard_map.78), channel_id=1, source_target_pairs={{0,1},{1,0},{2,3},{3,2},{4,5},{5,4},{6,7},{7,6},{8,9},{9,8},{10,11... | collective-permute-start | bytes 7077896 | tf_op jit(solution)/shard_map/ppermute | solution.py:209
  16.6 166.6 %all-gather.5.cloned.1.call-start = ((), (), s32[]{:S(2)}) async-start(), calls=%async_computation.1 | async-start | bytes 5898240 | tf_op jit(solution)/shard_map/all_gather | solution.py:312
  30.9 13.1 %collective-permute-start.1 = (f32[5,768,256]{2,1,0:T(8,128)}, f32[5,768,256]{2,1,0:T(8,128)}, u32[]{:S(2)}, u32[]{:S(2)}) collective-permute-start(f32[5,768,256]{2,1,0:T(8,128)} %shard_map.80), channel_id=1, source_target_pairs={{0,1},{1,0},{2,3},{3,2},{4,5},{5,4},{6,7},{7,6},{8,9},{9,8},{10,11... | collective-permute-start | bytes 11796488 | tf_op jit(solution)/shard_map/ppermute | solution.py:209
  31.5 19.7 %collective-permute-start.4 = (f16[768,256]{1,0:T(8,128)(2,1)}, f16[768,256]{1,0:T(8,128)(2,1)S(1)}, u32[]{:S(2)}, u32[]{:S(2)}) collective-permute-start(f16[768,256]{1,0:T(8,128)(2,1)} %get-tuple-element.15), channel_id=1, source_target_pairs={{0,2},{1,3},{2,0},{3,1},{4,6},{5,7},{6,4},{7,5},{8,10},{9,11},{10,... | collective-permute-start | bytes 1179656 | tf_op jit(solution)/shard_map/ppermute | solution.py:209
  34.6 16.6 %collective-permute-start.6 = (f16[768,256]{1,0:T(8,128)(2,1)}, f16[768,256]{1,0:T(8,128)(2,1)S(1)}, u32[]{:S(2)}, u32[]{:S(2)}) collective-permute-start(f16[768,256]{1,0:T(8,128)(2,1)} %get-tuple-element.16), channel_id=1, source_target_pairs={{0,4},{1,5},{2,6},{3,7},{4,8},{5,9},{6,10},{7,11},{8,12},{9,13},{1... | collective-permute-start | bytes 1179656 | tf_op jit(solution)/shard_map/ppermute | solution.py:209
  36.2 15.0 %collective-permute-start.7 = (f16[768,256]{1,0:T(8,128)(2,1)}, f16[768,256]{1,0:T(8,128)(2,1)S(1)}, u32[]{:S(2)}, u32[]{:S(2)}) collective-permute-start(f16[768,256]{1,0:T(8,128)(2,1)} %get-tuple-element.17), channel_id=1, source_target_pairs={{0,12},{1,13},{2,14},{3,15},{4,0},{5,1},{6,2},{7,3},{8,4},{9,5},{1... | collective-permute-start | bytes 1179656 | tf_op jit(solution)/shard_map/ppermute | solution.py:209
  47.9 20.3 %collective-permute-start.2 = (f16[768,256]{1,0:T(8,128)(2,1)}, f16[768,256]{1,0:T(8,128)(2,1)}, u32[]{:S(2)}, u32[]{:S(2)}) collective-permute-start(f16[768,256]{1,0:T(8,128)(2,1)} %get-tuple-element.28), channel_id=1, source_target_pairs={{0,4},{1,5},{2,6},{3,7},{4,8},{5,9},{6,10},{7,11},{8,12},{9,13},{1... | collective-permute-start | bytes 1179656 | tf_op jit(solution)/shard_map/ppermute | solution.py:209
  48.3 19.9 %collective-permute-start.3 = (f16[768,256]{1,0:T(8,128)(2,1)}, f16[768,256]{1,0:T(8,128)(2,1)}, u32[]{:S(2)}, u32[]{:S(2)}) collective-permute-start(f16[768,256]{1,0:T(8,128)(2,1)} %get-tuple-element.29), channel_id=1, source_target_pairs={{0,12},{1,13},{2,14},{3,15},{4,0},{5,1},{6,2},{7,3},{8,4},{9,5},{1... | collective-permute-start | bytes 1179656 | tf_op jit(solution)/shard_map/ppermute | solution.py:209
  53.1 15.1 %collective-permute-start.5 = (f16[768,256]{1,0:T(8,128)(2,1)S(1)}, f16[768,256]{1,0:T(8,128)(2,1)S(1)}, u32[]{:S(2)}, u32[]{:S(2)}) collective-permute-start(f16[768,256]{1,0:T(8,128)(2,1)S(1)} %get-tuple-element.30), channel_id=1, source_target_pairs={{0,8},{1,9},{2,10},{3,11},{4,12},{5,13},{6,14},{7,15},{8,0},{9,1},... | collective-permute-start | bytes 1179656 | tf_op jit(solution)/shard_map/ppermute | solution.py:209
  53.8 14.4 %collective-permute-start.8 = (f16[768,256]{1,0:T(8,128)(2,1)S(1)}, f16[768,256]{1,0:T(8,128)(2,1)}, u32[]{:S(2)}, u32[]{:S(2)}) collective-permute-start(f16[768,256]{1,0:T(8,128)(2,1)S(1)} %get-tuple-element.31), channel_id=1, source_target_pairs={{0,2},{1,3},{2,0},{3,1},{4,6},{5,7},{6,4},{7,5},{8,10},{9,11},{10,... | collective-permute-start | bytes 1179656 | tf_op jit(solution)/shard_map/ppermute | solution.py:209
  70.2 44.3 %collective-permute-start.14 = (bf16[768,768]{1,0:T(8,128)(2,1)S(1)}, bf16[768,768]{1,0:T(8,128)(2,1)}, u32[]{:S(2)}, u32[]{:S(2)}) collective-permute-start(bf16[768,768]{1,0:T(8,128)(2,1)S(1)} %bitcast.89), channel_id=1, source_target_pairs={{0,16},{16,0},{32,48},{48,32},{64,80},{80,64},{96,112},{112,96},{1... | collective-permute-start | bytes 3538952 | tf_op jit(solution)/shard_map/ppermute | solution.py:214
  72.2 24.7 %collective-permute-start.10 = (f32[8,96]{1,0:T(8,128)S(1)}, f32[8,96]{1,0:T(8,128)S(1)}, u32[]{:S(2)}, u32[]{:S(2)}) collective-permute-start(f32[8,96]{1,0:T(8,128)S(1)} %add.447), channel_id=1, source_target_pairs={{0,2},{1,3},{2,0},{3,1},{4,6},{5,7},{6,4},{7,5},{8,10},{9,11},{10,... | collective-permute-start | bytes 9224 | tf_op jit(solution)/shard_map/ppermute | solution.py:209
  129.1 26.5 %collective-permute-start.21 = (bf16[768,256]{1,0:T(8,128)(2,1)S(1)}, bf16[768,256]{1,0:T(8,128)(2,1)S(1)}, u32[]{:S(2)}, u32[]{:S(2)}) collective-permute-start(bf16[768,256]{1,0:T(8,128)(2,1)S(1)} %collective-permute-done.20.refs_0_), channel_id=1, source_target_pairs={{0,2},{1,3},{2,0},{3,1},{4,6},{5,7},{6,4},{7,5},{8,10},{9,11},{10,... | collective-permute-start | bytes 1179656 | tf_op jit(solution)/shard_map/ppermute | solution.py:209
  140.4 22.1 %collective-permute-start.26 = (bf16[768,256]{1,0:T(8,128)(2,1)S(1)}, bf16[768,256]{1,0:T(8,128)(2,1)S(1)}, u32[]{:S(2)}, u32[]{:S(2)}) collective-permute-start(bf16[768,256]{1,0:T(8,128)(2,1)S(1)} %collective-permute-done.20.refs_0_), channel_id=1, source_target_pairs={{0,8},{1,9},{2,10},{3,11},{4,12},{5,13},{6,14},{7,15},{8,0},{9,1},... | collective-permute-start | bytes 1179656 | tf_op jit(solution)/shard_map/ppermute | solution.py:209
  152.4 18.0 %collective-permute-start.22 = (bf16[768,256]{1,0:T(8,128)(2,1)S(1)}, bf16[768,256]{1,0:T(8,128)(2,1)S(1)}, u32[]{:S(2)}, u32[]{:S(2)}) collective-permute-start(bf16[768,256]{1,0:T(8,128)(2,1)S(1)} %collective-permute-done.20.refs_0_), channel_id=1, source_target_pairs={{0,4},{1,5},{2,6},{3,7},{4,8},{5,9},{6,10},{7,11},{8,12},{9,13},{1... | collective-permute-start | bytes 1179656 | tf_op jit(solution)/shard_map/ppermute | solution.py:209
  154.0 19.6 %collective-permute-start.24 = (bf16[768,256]{1,0:T(8,128)(2,1)S(1)}, bf16[768,256]{1,0:T(8,128)(2,1)S(1)}, u32[]{:S(2)}, u32[]{:S(2)}) collective-permute-start(bf16[768,256]{1,0:T(8,128)(2,1)S(1)} %collective-permute-done.20.refs_0_), channel_id=1, source_target_pairs={{0,12},{1,13},{2,14},{3,15},{4,0},{5,1},{6,2},{7,3},{8,4},{9,5},{1... | collective-permute-start | bytes 1179656 | tf_op jit(solution)/shard_map/ppermute | solution.py:209
  155.6 18.0 %collective-permute-start.28 = (bf16[768,256]{1,0:T(8,128)(2,1)S(1)}, bf16[768,256]{1,0:T(8,128)(2,1)S(1)}, u32[]{:S(2)}, u32[]{:S(2)}) collective-permute-start(bf16[768,256]{1,0:T(8,128)(2,1)S(1)} %collective-permute-done.20.refs_0_), channel_id=1, source_target_pairs={{0,1},{1,0},{2,3},{3,2},{4,5},{5,4},{6,7},{7,6},{8,9},{9,8},{10,11... | collective-permute-start | bytes 1179656 | tf_op jit(solution)/shard_map/ppermute | solution.py:209
  155.6 19.6 %collective-permute-start.23 = (bf16[768,256]{1,0:T(8,128)(2,1)S(1)}, bf16[768,256]{1,0:T(8,128)(2,1)S(1)}, u32[]{:S(2)}, u32[]{:S(2)}) collective-permute-start(bf16[768,256]{1,0:T(8,128)(2,1)S(1)} %collective-permute-done.21.refs_1_), channel_id=1, source_target_pairs={{0,4},{1,5},{2,6},{3,7},{4,8},{5,9},{6,10},{7,11},{8,12},{9,13},{1... | collective-permute-start | bytes 1179656 | tf_op jit(solution)/shard_map/ppermute | solution.py:209
  162.4 13.9 %collective-permute-start.25 = (bf16[768,256]{1,0:T(8,128)(2,1)S(1)}, bf16[768,256]{1,0:T(8,128)(2,1)S(1)}, u32[]{:S(2)}, u32[]{:S(2)}) collective-permute-start(bf16[768,256]{1,0:T(8,128)(2,1)S(1)} %collective-permute-done.21.refs_1_), channel_id=1, source_target_pairs={{0,12},{1,13},{2,14},{3,15},{4,0},{5,1},{6,2},{7,3},{8,4},{9,5},{1... | collective-permute-start | bytes 1179656 | tf_op jit(solution)/shard_map/ppermute | solution.py:209
  170.4 9.3 %collective-permute-start.27 = (bf16[768,256]{1,0:T(8,128)(2,1)S(1)}, bf16[768,256]{1,0:T(8,128)(2,1)S(1)}, u32[]{:S(2)}, u32[]{:S(2)}) collective-permute-start(bf16[768,256]{1,0:T(8,128)(2,1)S(1)} %collective-permute-done.26.refs_6_), channel_id=1, source_target_pairs={{0,2},{1,3},{2,0},{3,1},{4,6},{5,7},{6,4},{7,5},{8,10},{9,11},{10,... | collective-permute-start | bytes 1179656 | tf_op jit(solution)/shard_map/ppermute | solution.py:209
  173.6 6.1 %collective-permute-start.29 = (bf16[768,256]{1,0:T(8,128)(2,1)S(1)}, bf16[768,256]{1,0:T(8,128)(2,1)S(1)}, u32[]{:S(2)}, u32[]{:S(2)}) collective-permute-start(bf16[768,256]{1,0:T(8,128)(2,1)S(1)} %collective-permute-done.21.refs_1_), channel_id=1, source_target_pairs={{0,1},{1,0},{2,3},{3,2},{4,5},{5,4},{6,7},{7,6},{8,9},{9,8},{10,11... | collective-permute-start | bytes 1179656 | tf_op jit(solution)/shard_map/ppermute | solution.py:209
  173.6 6.5 %collective-permute-start.30 = (bf16[768,256]{1,0:T(8,128)(2,1)S(1)}, bf16[768,256]{1,0:T(8,128)(2,1)S(1)}, u32[]{:S(2)}, u32[]{:S(2)}) collective-permute-start(bf16[768,256]{1,0:T(8,128)(2,1)S(1)} %collective-permute-done.22.refs_2_), channel_id=1, source_target_pairs={{0,1},{1,0},{2,3},{3,2},{4,5},{5,4},{6,7},{7,6},{8,9},{9,8},{10,11... | collective-permute-start | bytes 1179656 | tf_op jit(solution)/shard_map/ppermute | solution.py:209
  175.2 7.0 %collective-permute-start.34 = (bf16[768,256]{1,0:T(8,128)(2,1)S(1)}, bf16[768,256]{1,0:T(8,128)(2,1)}, u32[]{:S(2)}, u32[]{:S(2)}) collective-permute-start(bf16[768,256]{1,0:T(8,128)(2,1)S(1)} %collective-permute-done.26.refs_6_), channel_id=1, source_target_pairs={{0,1},{1,0},{2,3},{3,2},{4,5},{5,4},{6,7},{7,6},{8,9},{9,8},{10,11... | collective-permute-start | bytes 1179656 | tf_op jit(solution)/shard_map/ppermute | solution.py:209
  195.8 21.1 %collective-permute-start.36 = (bf16[768,512]{1,0:T(8,128)(2,1)}, bf16[768,512]{1,0:T(8,128)(2,1)S(1)}, u32[]{:S(2)}, u32[]{:S(2)}) collective-permute-start(bf16[768,512]{1,0:T(8,128)(2,1)} %get-tuple-element.25), channel_id=1, source_target_pairs={{0,32},{16,48},{32,64},{48,80},{64,96},{80,112},{96,0},{112,16},{1... | collective-permute-start | bytes 2359304 | tf_op jit(solution)/shard_map/ppermute | solution.py:214
  195.8 21.9 %collective-permute-start.37 = (bf16[768,512]{1,0:T(8,128)(2,1)}, bf16[768,512]{1,0:T(8,128)(2,1)S(1)}, u32[]{:S(2)}, u32[]{:S(2)}) collective-permute-start(bf16[768,512]{1,0:T(8,128)(2,1)} %get-tuple-element.25), channel_id=1, source_target_pairs={{0,96},{16,112},{32,0},{48,16},{64,32},{80,48},{96,64},{112,80},{1... | collective-permute-start | bytes 2359304 | tf_op jit(solution)/shard_map/ppermute | solution.py:214
  199.0 22.0 %collective-permute-start.38 = (bf16[768,512]{1,0:T(8,128)(2,1)}, bf16[768,512]{1,0:T(8,128)(2,1)S(1)}, u32[]{:S(2)}, u32[]{:S(2)}) collective-permute-start(bf16[768,512]{1,0:T(8,128)(2,1)} %get-tuple-element.25), channel_id=1, source_target_pairs={{0,16},{16,0},{32,48},{48,32},{64,80},{80,64},{96,112},{112,96},{1... | collective-permute-start | bytes 2359304 | tf_op jit(solution)/shard_map/ppermute | solution.py:214
  217.0 13.3 %collective-permute-start.39 = (bf16[384,512]{1,0:T(8,128)(2,1)S(1)}, bf16[384,512]{1,0:T(8,128)(2,1)S(1)}, u32[]{:S(2)}, u32[]{:S(2)}) collective-permute-start(bf16[384,512]{1,0:T(8,128)(2,1)S(1)} %slice.92), channel_id=1, source_target_pairs={{0,32},{16,48},{32,64},{48,80},{64,96},{80,112},{96,0},{112,16},{1... | collective-permute-start | bytes 1179656 | tf_op jit(solution)/shard_map/ppermute | solution.py:214
  218.5 12.5 %collective-permute-start.40 = (bf16[384,512]{1,0:T(8,128)(2,1)}, bf16[384,512]{1,0:T(8,128)(2,1)S(1)}, u32[]{:S(2)}, u32[]{:S(2)}) collective-permute-start(bf16[384,512]{1,0:T(8,128)(2,1)} %slice.93), channel_id=1, source_target_pairs={{0,96},{16,112},{32,0},{48,16},{64,32},{80,48},{96,64},{112,80},{1... | collective-permute-start | bytes 1179656 | tf_op jit(solution)/shard_map/ppermute | solution.py:214
  221.1 24.5 %collective-permute-start.41 = (bf16[768,512]{1,0:T(8,128)(2,1)S(1)}, bf16[768,512]{1,0:T(8,128)(2,1)S(1)}, u32[]{:S(2)}, u32[]{:S(2)}) collective-permute-start(bf16[768,512]{1,0:T(8,128)(2,1)S(1)} %collective-permute-done.38), channel_id=1, source_target_pairs={{0,32},{16,48},{32,64},{48,80},{64,96},{80,112},{96,0},{112,16},{1... | collective-permute-start | bytes 2359304 | tf_op jit(solution)/shard_map/ppermute | solution.py:214
  223.1 23.4 %collective-permute-start.42 = (bf16[768,512]{1,0:T(8,128)(2,1)S(1)}, bf16[768,512]{1,0:T(8,128)(2,1)S(1)}, u32[]{:S(2)}, u32[]{:S(2)}) collective-permute-start(bf16[768,512]{1,0:T(8,128)(2,1)S(1)} %collective-permute-done.38), channel_id=1, source_target_pairs={{0,96},{16,112},{32,0},{48,16},{64,32},{80,48},{96,64},{112,80},{1... | collective-permute-start | bytes 2359304 | tf_op jit(solution)/shard_map/ppermute | solution.py:214
  231.0 17.3 %collective-permute-start.43 = (bf16[768,512]{1,0:T(8,128)(2,1)S(1)}, bf16[768,512]{1,0:T(8,128)(2,1)S(1)}, u32[]{:S(2)}, u32[]{:S(2)}) collective-permute-start(bf16[768,512]{1,0:T(8,128)(2,1)S(1)} %pad_maximum_fusion), channel_id=1, source_target_pairs={{0,16},{16,0},{32,48},{48,32},{64,80},{80,64},{96,112},{112,96},{1... | collective-permute-start | bytes 2359304 | tf_op jit(solution)/shard_map/ppermute | solution.py:214
  (38 other events, 410.3 us)
Sparse Core Ops, SparseCore 0:
  16.7 55.4 all-gather.2
  114.7 60.8 all-gather.4

commit v6 on v4

--- a/solution.py
+++ b/solution.py
@@ -108,7 +108,7 @@
         cross_ref[s] = jnp.sum(jnp.where(eye, crossed[s], 0.0), axis=0, keepdims=True)
 
 
-def attention(lens, weights, scales, merged, squares, gain, taps, slots=2):
+def attention(lens, weights, scales, merged, squares, gain, taps, slots=4):
     count, span, wide = merged.shape
     scalar = pl.BlockSpec(memory_space=pltpu.SMEM)
     block = pl.BlockSpec((slots, span, wide), lambda i: (i, 0, 0))
@@ -311,6 +311,7 @@
     def gather_taps(value):
         return row_major(lax.all_gather(value, "rep", axis=0, tiled=True, axis_index_groups=along_z))
 
+    rows_across = row_major(to_group(rows, 0, 1))
     taps_here = gather_taps(rows)
 
     def sums(rows, offsets, parity):
@@ -333,8 +334,6 @@
     up_across = send(up_across, 1, 0)
     down_across = send(down_across, 3, 0)
     second = chip_sums(rows_now, ORDER[1])
-    far_across, rows_now = lax.optimization_barrier((far_across, rows_now))
-    rows_across = row_major(to_group(rows_now, 0, 1))
     up = send(second[1, 0], 1, 0).astype(f32)
     down = send(second[3, 0], 3, 0).astype(f32)
     far = send(second[2, 0] + far_across.astype(f32), 2, 0).astype(f32)

time: 258 us -> 259 us (level)
  waiting for transfers between devices: 84.4 us -> 93 us
  Pallas kernels: 42 us -> 37.5 us
    ppermute x9, starting transfers between devices: 21.2 us -> 14.6 us  [to_group(): return lax.ppermute(value, 'rep', pairs)]
    ppermute x34, waiting for transfers between devices: 57.3 us -> 63.5 us  [to_chip(): return lax.ppermute(value, 'tr', pairs)]
    ppermute x34, starting transfers between devices: 57.2 us -> 61.8 us  [to_chip(): return lax.ppermute(value, 'tr', pairs)]
    pallas_call x1, Pallas kernels: 15.8 us -> 11.3 us  [attention(): pl.pallas_call(attention_kernel, grid=(count // slots,), in_specs=[scalar...]
  transfers between devices with their start and end apart: 46 -> 46, of which waited for: 24 -> 21; matrix products, arithmetic and copies ran while one was open for 8% -> 8% of each run, Pallas kernels for 10% -> 8%
where the time goes in v6:
time: 259 us; the launch traced here: 258 us
  waiting for transfers between devices  93 us (36%)
  starting transfers between devices  77.1 us (30%)
  Pallas kernels  37.5 us (14%)
  local copies, waits for them, and re-layouts  26.7 us (10%)
  between operations  14.7 us (6%)
  other arithmetic  8.91 us (3%)
    ppermute x34, waiting for transfers between devices, to_chip(): return lax.ppermute(value, 'tr', pairs)  63.5 us
    ppermute x34, starting transfers between devices, to_chip(): return lax.ppermute(value, 'tr', pairs)  61.8 us
    ppermute x9, waiting for transfers between devices, to_group(): return lax.ppermute(value, 'rep', pairs)  29.6 us
    ppermute x9, starting transfers between devices, to_group(): return lax.ppermute(value, 'rep', pairs)  14.6 us
    pallas_call x4, Pallas kernels, products(): pl.pallas_call(product_kernel, grid_spec=pltpu.PrefetchScalarGridSpec(num...  13.7 us
    pallas_call x1, Pallas kernels, gradient(): pl.pallas_call(gradient_kernel, grid_spec=pltpu.PrefetchScalarGridSpec(nu...  12.6 us
    unnamed x49, local copies, waits for them, and re-layouts  12.4 us
    pallas_call x1, Pallas kernels, attention(): pl.pallas_call(attention_kernel, grid=(count // slots,), in_specs=[scalar...  11.3 us
  transfers between devices with their start and end apart: 46, of which 21 were waited for; matrix products, arithmetic and copies ran while one was open for 8% of the time, Pallas kernels for 8%

profile of v6, /device:TPU:0, one launch (start us, length us, event | category | flops | bytes accessed | tf_op | source)
XLA Modules:
  0.0 258.0 jit_solution(2414152961705164812)
XLA Ops:
  7.3 2.3 copy.16
  10.0 3.1 %copy-done = bf16[3,256,4096]{2,1,0:T(8,128)(2,1)S(1)} copy-done((bf16[3,256,4096]{2,1,0:T(8,128)(2,1)S(1)}, bf16[3,256,4096]{2,1,0:T(8,128)(2,1)}, u32[]{:S(2)}) %copy-start) | copy-done | bytes 6291480
  13.1 3.4 %shard_map.78 = f32[3,768,256]{2,1,0:T(8,128)} custom-call(s32[3]{0:T(128)S(1)} %pad_add_fusion.1.blocks_ref, bf16[768,768]{1,0:T(8,128)(2,1)S(1)} %bitcast.84, bf16[768,4096]{1,0:T(8,128)(2,1)S(1)} %bitcast.78), custom_call_target="tpu_custom_call" | custom-call | flops 905969664 | bytes 4718592 | tf_op jit(solution)/shard_map/pallas_call | solution.py:260
  16.9 2.8 %copy-done.1 = bf16[3,256,4096]{2,1,0:T(8,128)(2,1)S(1)} copy-done((bf16[3,256,4096]{2,1,0:T(8,128)(2,1)S(1)}, bf16[3,256,4096]{2,1,0:T(8,128)(2,1)}, u32[]{:S(2)}) %copy-start.1) | copy-done | bytes 6291480
  23.2 3.0 %fusion.28 = (f16[768,256]{1,0:T(8,128)(2,1)}, f16[768,256]{1,0:T(8,128)(2,1)}, f16[768,256]{1,0:T(8,128)(2,1)}) fusion(f32[3,768,256]{2,1,0:T(8,128)} %collective-permute-done, f32[3,768,256]{2,1,0:T(8,128)S(1)} %shard_map.77), kind=kLoop, calls=%fused_computation.39 | loop fusion | flops 1769472 | bytes 5898240 | tf_op jit(solution)/shard_map/convert_element_type | solution.py:331
  26.1 4.8 %shard_map.80 = f32[5,768,256]{2,1,0:T(8,128)} custom-call(s32[5]{0:T(128)S(1)} %stack.111.blocks_ref, bf16[768,768]{1,0:T(8,128)(2,1)S(1)} %bitcast.87, bf16[768,4096]{1,0:T(8,128)(2,1)S(1)} %bitcast.82), custom_call_target="tpu_custom_call" | custom-call | flops 1509949440 | bytes 7077888 | tf_op jit(solution)/shard_map/pallas_call | solution.py:260
  33.1 2.7 %collective-permute-start.4 = (f16[768,256]{1,0:T(8,128)(2,1)}, f16[768,256]{1,0:T(8,128)(2,1)S(1)}, u32[]{:S(2)}, u32[]{:S(2)}) collective-permute-start(f16[768,256]{1,0:T(8,128)(2,1)} %get-tuple-element.13), channel_id=1, source_target_pairs={{0,2},{1,3},{2,0},{3,1},{4,6},{5,7},{6,4},{7,5},{8,10},{9,11},{10,... | collective-permute-start | bytes 1179656 | tf_op jit(solution)/shard_map/ppermute | solution.py:209
  39.1 2.8 %copy-done.2 = bf16[3,256,4096]{2,1,0:T(8,128)(2,1)S(1)} copy-done((bf16[3,256,4096]{2,1,0:T(8,128)(2,1)S(1)}, bf16[3,256,4096]{2,1,0:T(8,128)(2,1)}, u32[]{:S(2)}) %copy-start.2) | copy-done | bytes 6291480
  41.9 3.3 %shard_map.79 = f32[5,768,256]{2,1,0:T(8,128)S(1)} custom-call(s32[5]{0:T(128)S(1)} %stack.97.blocks_ref, bf16[768,768]{1,0:T(8,128)(2,1)S(1)} %bitcast.89, bf16[768,4096]{1,0:T(8,128)(2,1)S(1)} %bitcast.83), custom_call_target="tpu_custom_call" | custom-call | flops 1509949440 | bytes 7077888 | tf_op jit(solution)/shard_map/pallas_call | solution.py:260
  47.5 22.6 %collective-permute-done.4 = f16[768,256]{1,0:T(8,128)(2,1)S(1)} collective-permute-done((f16[768,256]{1,0:T(8,128)(2,1)}, f16[768,256]{1,0:T(8,128)(2,1)S(1)}, u32[]{:S(2)}, u32[]{:S(2)}) %collective-permute-start.4) | collective-permute-done | bytes 393248 | tf_op jit(solution)/shard_map/ppermute | solution.py:209
  70.0 3.0 %collective-permute-start.3 = (f16[768,256]{1,0:T(8,128)(2,1)S(1)}, f16[768,256]{1,0:T(8,128)(2,1)S(1)}, u32[]{:S(2)}, u32[]{:S(2)}) collective-permute-start(f16[768,256]{1,0:T(8,128)(2,1)S(1)} %get-tuple-element.25), channel_id=1, source_target_pairs={{0,12},{1,13},{2,14},{3,15},{4,0},{5,1},{6,2},{7,3},{8,4},{9,5},{1... | collective-permute-start | bytes 1179656 | tf_op jit(solution)/shard_map/ppermute | solution.py:209
  76.4 12.8 %collective-permute-done.3 = f16[768,256]{1,0:T(8,128)(2,1)S(1)} collective-permute-done((f16[768,256]{1,0:T(8,128)(2,1)S(1)}, f16[768,256]{1,0:T(8,128)(2,1)S(1)}, u32[]{:S(2)}, u32[]{:S(2)}) %collective-permute-start.3) | collective-permute-done | bytes 393248 | tf_op jit(solution)/shard_map/ppermute | solution.py:209
  95.3 4.0 %collective-permute-done.11 = f32[8,96]{1,0:T(8,128)S(1)} collective-permute-done((f32[8,96]{1,0:T(8,128)S(1)}, f32[8,96]{1,0:T(8,128)S(1)}, u32[]{:S(2)}, u32[]{:S(2)}) %collective-permute-start.11) | collective-permute-done | bytes 3104 | tf_op jit(solution)/shard_map/ppermute | solution.py:209
  101.4 3.1 %collective-permute-start.13 = (f32[8,96]{1,0:T(8,128)S(1)}, f32[8,96]{1,0:T(8,128)S(1)}, u32[]{:S(2)}, u32[]{:S(2)}) collective-permute-start(f32[8,96]{1,0:T(8,128)S(1)} %add.448), channel_id=1, source_target_pairs={{0,8},{1,9},{2,10},{3,11},{4,12},{5,13},{6,14},{7,15},{8,0},{9,1},... | collective-permute-start | bytes 9224 | tf_op jit(solution)/shard_map/ppermute | solution.py:209
  108.2 11.3 %shard_map.81 = (f32[8,96,256]{2,1,0:T(8,128)S(1)}, f32[8,1,96]{2,1,0:T(1,128)S(1)}) custom-call(s32[8]{0:T(128)S(1)} %dynamic_slice.6.lens_ref, f32[8]{0:T(128)S(1)} %convert_divide_fusion.weights_ref, f32[2]{0:T(128)S(1)} %copy-done.7, f32[8,96,256]{2,1,0:T(8,128)S(1)} %bitcast.91, f32[8,1,96]{2,1,0:T(1,128)S(1)} %bitcast.93, f32[1,256]{1,0:T(1,128)S(1)} %bitcast.96, ...), custom_call_target="tpu_custom_call" | custom-call | flops 2000000000 | bytes 3000000 | tf_op jit(solution)/shard_map/pallas_call | solution.py:116
  121.6 4.2 %collective-permute-done.16 = f32[8,96]{1,0:T(8,128)S(1)} collective-permute-done((f32[8,96]{1,0:T(8,128)S(1)}, f32[8,96]{1,0:T(8,128)S(1)}, u32[]{:S(2)}, u32[]{:S(2)}) %collective-permute-start.16) | collective-permute-done | bytes 3104 | tf_op jit(solution)/shard_map/ppermute | solution.py:209
  125.8 2.7 %collective-permute-start.18 = (f32[8,96]{1,0:T(8,128)S(1)}, f32[8,96]{1,0:T(8,128)S(1)}, u32[]{:S(2)}, u32[]{:S(2)}) collective-permute-start(f32[8,96]{1,0:T(8,128)S(1)} %add.455), channel_id=1, source_target_pairs={{0,8},{1,9},{2,10},{3,11},{4,12},{5,13},{6,14},{7,15},{8,0},{9,1},... | collective-permute-start | bytes 9224 | tf_op jit(solution)/shard_map/ppermute | solution.py:209
  133.1 11.2 %collective-permute-start.21 = (bf16[768,256]{1,0:T(8,128)(2,1)S(1)}, bf16[768,256]{1,0:T(8,128)(2,1)S(1)}, u32[]{:S(2)}, u32[]{:S(2)}) collective-permute-start(bf16[768,256]{1,0:T(8,128)(2,1)S(1)} %collective-permute-done.20.refs_0_), channel_id=1, source_target_pairs={{0,2},{1,3},{2,0},{3,1},{4,6},{5,7},{6,4},{7,5},{8,10},{9,11},{10,... | collective-permute-start | bytes 1179656 | tf_op jit(solution)/shard_map/ppermute | solution.py:209
  144.3 8.8 %collective-permute-start.26 = (bf16[768,256]{1,0:T(8,128)(2,1)S(1)}, bf16[768,256]{1,0:T(8,128)(2,1)S(1)}, u32[]{:S(2)}, u32[]{:S(2)}) collective-permute-start(bf16[768,256]{1,0:T(8,128)(2,1)S(1)} %collective-permute-done.20.refs_0_), channel_id=1, source_target_pairs={{0,8},{1,9},{2,10},{3,11},{4,12},{5,13},{6,14},{7,15},{8,0},{9,1},... | collective-permute-start | bytes 1179656 | tf_op jit(solution)/shard_map/ppermute | solution.py:209
  156.4 6.8 %collective-permute-start.23 = (bf16[768,256]{1,0:T(8,128)(2,1)S(1)}, bf16[768,256]{1,0:T(8,128)(2,1)S(1)}, u32[]{:S(2)}, u32[]{:S(2)}) collective-permute-start(bf16[768,256]{1,0:T(8,128)(2,1)S(1)} %collective-permute-done.21.refs_1_), channel_id=1, source_target_pairs={{0,4},{1,5},{2,6},{3,7},{4,8},{5,9},{6,10},{7,11},{8,12},{9,13},{1... | collective-permute-start | bytes 1179656 | tf_op jit(solution)/shard_map/ppermute | solution.py:209
  163.2 4.0 %collective-permute-start.25 = (bf16[768,256]{1,0:T(8,128)(2,1)S(1)}, bf16[768,256]{1,0:T(8,128)(2,1)S(1)}, u32[]{:S(2)}, u32[]{:S(2)}) collective-permute-start(bf16[768,256]{1,0:T(8,128)(2,1)S(1)} %collective-permute-done.21.refs_1_), channel_id=1, source_target_pairs={{0,12},{1,13},{2,14},{3,15},{4,0},{5,1},{6,2},{7,3},{8,4},{9,5},{1... | collective-permute-start | bytes 1179656 | tf_op jit(solution)/shard_map/ppermute | solution.py:209
  167.2 4.0 %collective-permute-done.22.refs_2_ = bf16[768,256]{1,0:T(8,128)(2,1)S(1)} collective-permute-done((bf16[768,256]{1,0:T(8,128)(2,1)S(1)}, bf16[768,256]{1,0:T(8,128)(2,1)S(1)}, u32[]{:S(2)}, u32[]{:S(2)}) %collective-permute-start.22) | collective-permute-done | bytes 393248 | tf_op jit(solution)/shard_map/ppermute | solution.py:209
  171.1 3.5 %collective-permute-start.27 = (bf16[768,256]{1,0:T(8,128)(2,1)S(1)}, bf16[768,256]{1,0:T(8,128)(2,1)S(1)}, u32[]{:S(2)}, u32[]{:S(2)}) collective-permute-start(bf16[768,256]{1,0:T(8,128)(2,1)S(1)} %collective-permute-done.26.refs_6_), channel_id=1, source_target_pairs={{0,2},{1,3},{2,0},{3,1},{4,6},{5,7},{6,4},{7,5},{8,10},{9,11},{10,... | collective-permute-start | bytes 1179656 | tf_op jit(solution)/shard_map/ppermute | solution.py:209
  175.2 3.1 %collective-permute-done.23.refs_3_ = bf16[768,256]{1,0:T(8,128)(2,1)S(1)} collective-permute-done((bf16[768,256]{1,0:T(8,128)(2,1)S(1)}, bf16[768,256]{1,0:T(8,128)(2,1)S(1)}, u32[]{:S(2)}, u32[]{:S(2)}) %collective-permute-start.23) | collective-permute-done | bytes 393248 | tf_op jit(solution)/shard_map/ppermute | solution.py:209
  179.4 3.0 %collective-permute-done.27.refs_7_ = bf16[768,256]{1,0:T(8,128)(2,1)S(1)} collective-permute-done((bf16[768,256]{1,0:T(8,128)(2,1)S(1)}, bf16[768,256]{1,0:T(8,128)(2,1)S(1)}, u32[]{:S(2)}, u32[]{:S(2)}) %collective-permute-start.27) | collective-permute-done | bytes 393248 | tf_op jit(solution)/shard_map/ppermute | solution.py:209
  186.0 12.6 %shard_map.82 = (f32[768,512]{1,0:T(8,128)}, bf16[768,512]{1,0:T(8,128)(2,1)}) custom-call(s32[7]{0:T(128)} %stack.91.places_ref, bf16[3072,768]{1,0:T(8,128)(2,1)} %all-gather.3.cloned.1.call-done.here_ref, bf16[3072,768]{1,0:T(8,128)(2,1)} %all-gather.5.cloned.1.call-done.across_ref, bf16[768,256]{1,0:T(8,128)(2,1)} %copy-done.9, ...), custom_call_target="tpu_custom_call" | custom-call | flops 4831838208 | bytes 20971520 | tf_op jit(solution)/shard_map/pallas_call | solution.py:167
  198.5 3.2 %collective-permute-start.37 = (bf16[768,512]{1,0:T(8,128)(2,1)}, bf16[768,512]{1,0:T(8,128)(2,1)S(1)}, u32[]{:S(2)}, u32[]{:S(2)}) collective-permute-start(bf16[768,512]{1,0:T(8,128)(2,1)} %get-tuple-element.21), channel_id=1, source_target_pairs={{0,96},{16,112},{32,0},{48,16},{64,32},{80,48},{96,64},{112,80},{1... | collective-permute-start | bytes 2359304 | tf_op jit(solution)/shard_map/ppermute | solution.py:214
  203.5 16.2 %collective-permute-done.36 = bf16[768,512]{1,0:T(8,128)(2,1)S(1)} collective-permute-done((bf16[768,512]{1,0:T(8,128)(2,1)}, bf16[768,512]{1,0:T(8,128)(2,1)S(1)}, u32[]{:S(2)}, u32[]{:S(2)}) %collective-permute-start.36) | collective-permute-done | bytes 786464 | tf_op jit(solution)/shard_map/ppermute | solution.py:214
  221.2 2.6 %collective-permute-start.40 = (bf16[384,512]{1,0:T(8,128)(2,1)}, bf16[384,512]{1,0:T(8,128)(2,1)S(1)}, u32[]{:S(2)}, u32[]{:S(2)}) collective-permute-start(bf16[384,512]{1,0:T(8,128)(2,1)} %slice.93), channel_id=1, source_target_pairs={{0,96},{16,112},{32,0},{48,16},{64,32},{80,48},{96,64},{112,80},{1... | collective-permute-start | bytes 1179656 | tf_op jit(solution)/shard_map/ppermute | solution.py:214
  225.9 3.2 %collective-permute-start.42 = (bf16[768,512]{1,0:T(8,128)(2,1)S(1)}, bf16[768,512]{1,0:T(8,128)(2,1)S(1)}, u32[]{:S(2)}, u32[]{:S(2)}) collective-permute-start(bf16[768,512]{1,0:T(8,128)(2,1)S(1)} %collective-permute-done.38), channel_id=1, source_target_pairs={{0,96},{16,112},{32,0},{48,16},{64,32},{80,48},{96,64},{112,80},{1... | collective-permute-start | bytes 2359304 | tf_op jit(solution)/shard_map/ppermute | solution.py:214
  229.1 3.9 %collective-permute-done.39 = bf16[384,512]{1,0:T(8,128)(2,1)S(1)} collective-permute-done((bf16[384,512]{1,0:T(8,128)(2,1)S(1)}, bf16[384,512]{1,0:T(8,128)(2,1)S(1)}, u32[]{:S(2)}, u32[]{:S(2)}) %collective-permute-start.39) | collective-permute-done | bytes 393248 | tf_op jit(solution)/shard_map/ppermute | solution.py:214
  239.9 8.5 %collective-permute-done.41 = bf16[768,512]{1,0:T(8,128)(2,1)S(1)} collective-permute-done((bf16[768,512]{1,0:T(8,128)(2,1)S(1)}, bf16[768,512]{1,0:T(8,128)(2,1)S(1)}, u32[]{:S(2)}, u32[]{:S(2)}) %collective-permute-start.41) | collective-permute-done | bytes 786464 | tf_op jit(solution)/shard_map/ppermute | solution.py:214
  (155 shorter events, 56.9 us)
Async XLA Ops:
  7.2 177.9 %all-gather.3.cloned.1.call-start = ((), (), s32[]{:S(2)}) async-start(), calls=%async_computation | async-start | bytes 5898240 | tf_op jit(solution)/shard_map/all_gather | solution.py:312
  16.5 6.6 %collective-permute-start = (f32[3,768,256]{2,1,0:T(8,128)}, f32[3,768,256]{2,1,0:T(8,128)}, u32[]{:S(2)}, u32[]{:S(2)}) collective-permute-start(f32[3,768,256]{2,1,0:T(8,128)} %shard_map.78), channel_id=1, source_target_pairs={{0,1},{1,0},{2,3},{3,2},{4,5},{5,4},{6,7},{7,6},{8,9},{9,8},{10,11... | collective-permute-start | bytes 7077896 | tf_op jit(solution)/shard_map/ppermute | solution.py:209
  16.6 169.3 %all-gather.5.cloned.1.call-start = ((), (), s32[]{:S(2)}) async-start(), calls=%async_computation.1 | async-start | bytes 5898240 | tf_op jit(solution)/shard_map/all_gather | solution.py:312
  31.0 14.3 %collective-permute-start.1 = (f32[5,768,256]{2,1,0:T(8,128)}, f32[5,768,256]{2,1,0:T(8,128)}, u32[]{:S(2)}, u32[]{:S(2)}) collective-permute-start(f32[5,768,256]{2,1,0:T(8,128)} %shard_map.80), channel_id=1, source_target_pairs={{0,1},{1,0},{2,3},{3,2},{4,5},{5,4},{6,7},{7,6},{8,9},{9,8},{10,11... | collective-permute-start | bytes 11796488 | tf_op jit(solution)/shard_map/ppermute | solution.py:209
  31.5 59.2 %collective-permute-start.9 = (bf16[768,768]{1,0:T(8,128)(2,1)S(1)}, bf16[768,768]{1,0:T(8,128)(2,1)S(1)}, u32[]{:S(2)}, u32[]{:S(2)}) collective-permute-start(bf16[768,768]{1,0:T(8,128)(2,1)S(1)} %bitcast.88), channel_id=1, source_target_pairs={{0,16},{16,0},{32,48},{48,32},{64,80},{80,64},{96,112},{112,96},{1... | collective-permute-start | bytes 3538952 | tf_op jit(solution)/shard_map/ppermute | solution.py:214
  33.1 36.9 %collective-permute-start.4 = (f16[768,256]{1,0:T(8,128)(2,1)}, f16[768,256]{1,0:T(8,128)(2,1)S(1)}, u32[]{:S(2)}, u32[]{:S(2)}) collective-permute-start(f16[768,256]{1,0:T(8,128)(2,1)} %get-tuple-element.13), channel_id=1, source_target_pairs={{0,2},{1,3},{2,0},{3,1},{4,6},{5,7},{6,4},{7,5},{8,10},{9,11},{10,... | collective-permute-start | bytes 1179656 | tf_op jit(solution)/shard_map/ppermute | solution.py:209
  35.9 37.2 %collective-permute-start.6 = (f16[768,256]{1,0:T(8,128)(2,1)}, f16[768,256]{1,0:T(8,128)(2,1)S(1)}, u32[]{:S(2)}, u32[]{:S(2)}) collective-permute-start(f16[768,256]{1,0:T(8,128)(2,1)} %get-tuple-element.14), channel_id=1, source_target_pairs={{0,4},{1,5},{2,6},{3,7},{4,8},{5,9},{6,10},{7,11},{8,12},{9,13},{1... | collective-permute-start | bytes 1179656 | tf_op jit(solution)/shard_map/ppermute | solution.py:209
  37.4 35.6 %collective-permute-start.7 = (f16[768,256]{1,0:T(8,128)(2,1)}, f16[768,256]{1,0:T(8,128)(2,1)S(1)}, u32[]{:S(2)}, u32[]{:S(2)}) collective-permute-start(f16[768,256]{1,0:T(8,128)(2,1)} %get-tuple-element.15), channel_id=1, source_target_pairs={{0,12},{1,13},{2,14},{3,15},{4,0},{5,1},{6,2},{7,3},{8,4},{9,5},{1... | collective-permute-start | bytes 1179656 | tf_op jit(solution)/shard_map/ppermute | solution.py:209
  47.0 29.4 %collective-permute-start.2 = (f16[768,256]{1,0:T(8,128)(2,1)S(1)}, f16[768,256]{1,0:T(8,128)(2,1)S(1)}, u32[]{:S(2)}, u32[]{:S(2)}) collective-permute-start(f16[768,256]{1,0:T(8,128)(2,1)S(1)} %get-tuple-element.24), channel_id=1, source_target_pairs={{0,4},{1,5},{2,6},{3,7},{4,8},{5,9},{6,10},{7,11},{8,12},{9,13},{1... | collective-permute-start | bytes 1179656 | tf_op jit(solution)/shard_map/ppermute | solution.py:209
  70.0 19.1 %collective-permute-start.3 = (f16[768,256]{1,0:T(8,128)(2,1)S(1)}, f16[768,256]{1,0:T(8,128)(2,1)S(1)}, u32[]{:S(2)}, u32[]{:S(2)}) collective-permute-start(f16[768,256]{1,0:T(8,128)(2,1)S(1)} %get-tuple-element.25), channel_id=1, source_target_pairs={{0,12},{1,13},{2,14},{3,15},{4,0},{5,1},{6,2},{7,3},{8,4},{9,5},{1... | collective-permute-start | bytes 1179656 | tf_op jit(solution)/shard_map/ppermute | solution.py:209
  74.9 14.3 %collective-permute-start.5 = (f16[768,256]{1,0:T(8,128)(2,1)S(1)}, f16[768,256]{1,0:T(8,128)(2,1)S(1)}, u32[]{:S(2)}, u32[]{:S(2)}) collective-permute-start(f16[768,256]{1,0:T(8,128)(2,1)S(1)} %get-tuple-element.26), channel_id=1, source_target_pairs={{0,8},{1,9},{2,10},{3,11},{4,12},{5,13},{6,14},{7,15},{8,0},{9,1},... | collective-permute-start | bytes 1179656 | tf_op jit(solution)/shard_map/ppermute | solution.py:209
  75.6 13.6 %collective-permute-start.8 = (f16[768,256]{1,0:T(8,128)(2,1)S(1)}, f16[768,256]{1,0:T(8,128)(2,1)S(1)}, u32[]{:S(2)}, u32[]{:S(2)}) collective-permute-start(f16[768,256]{1,0:T(8,128)(2,1)S(1)} %get-tuple-element.27), channel_id=1, source_target_pairs={{0,2},{1,3},{2,0},{3,1},{4,6},{5,7},{6,4},{7,5},{8,10},{9,11},{10,... | collective-permute-start | bytes 1179656 | tf_op jit(solution)/shard_map/ppermute | solution.py:209
  133.1 23.2 %collective-permute-start.21 = (bf16[768,256]{1,0:T(8,128)(2,1)S(1)}, bf16[768,256]{1,0:T(8,128)(2,1)S(1)}, u32[]{:S(2)}, u32[]{:S(2)}) collective-permute-start(bf16[768,256]{1,0:T(8,128)(2,1)S(1)} %collective-permute-done.20.refs_0_), channel_id=1, source_target_pairs={{0,2},{1,3},{2,0},{3,1},{4,6},{5,7},{6,4},{7,5},{8,10},{9,11},{10,... | collective-permute-start | bytes 1179656 | tf_op jit(solution)/shard_map/ppermute | solution.py:209
  144.3 18.9 %collective-permute-start.26 = (bf16[768,256]{1,0:T(8,128)(2,1)S(1)}, bf16[768,256]{1,0:T(8,128)(2,1)S(1)}, u32[]{:S(2)}, u32[]{:S(2)}) collective-permute-start(bf16[768,256]{1,0:T(8,128)(2,1)S(1)} %collective-permute-done.20.refs_0_), channel_id=1, source_target_pairs={{0,8},{1,9},{2,10},{3,11},{4,12},{5,13},{6,14},{7,15},{8,0},{9,1},... | collective-permute-start | bytes 1179656 | tf_op jit(solution)/shard_map/ppermute | solution.py:209
  153.1 18.0 %collective-permute-start.22 = (bf16[768,256]{1,0:T(8,128)(2,1)S(1)}, bf16[768,256]{1,0:T(8,128)(2,1)S(1)}, u32[]{:S(2)}, u32[]{:S(2)}) collective-permute-start(bf16[768,256]{1,0:T(8,128)(2,1)S(1)} %collective-permute-done.20.refs_0_), channel_id=1, source_target_pairs={{0,4},{1,5},{2,6},{3,7},{4,8},{5,9},{6,10},{7,11},{8,12},{9,13},{1... | collective-permute-start | bytes 1179656 | tf_op jit(solution)/shard_map/ppermute | solution.py:209
  154.4 20.2 %collective-permute-start.24 = (bf16[768,256]{1,0:T(8,128)(2,1)S(1)}, bf16[768,256]{1,0:T(8,128)(2,1)S(1)}, u32[]{:S(2)}, u32[]{:S(2)}) collective-permute-start(bf16[768,256]{1,0:T(8,128)(2,1)S(1)} %collective-permute-done.20.refs_0_), channel_id=1, source_target_pairs={{0,12},{1,13},{2,14},{3,15},{4,0},{5,1},{6,2},{7,3},{8,4},{9,5},{1... | collective-permute-start | bytes 1179656 | tf_op jit(solution)/shard_map/ppermute | solution.py:209
  156.4 18.3 %collective-permute-start.28 = (bf16[768,256]{1,0:T(8,128)(2,1)S(1)}, bf16[768,256]{1,0:T(8,128)(2,1)S(1)}, u32[]{:S(2)}, u32[]{:S(2)}) collective-permute-start(bf16[768,256]{1,0:T(8,128)(2,1)S(1)} %collective-permute-done.20.refs_0_), channel_id=1, source_target_pairs={{0,1},{1,0},{2,3},{3,2},{4,5},{5,4},{6,7},{7,6},{8,9},{9,8},{10,11... | collective-permute-start | bytes 1179656 | tf_op jit(solution)/shard_map/ppermute | solution.py:209
  156.4 21.9 %collective-permute-start.23 = (bf16[768,256]{1,0:T(8,128)(2,1)S(1)}, bf16[768,256]{1,0:T(8,128)(2,1)S(1)}, u32[]{:S(2)}, u32[]{:S(2)}) collective-permute-start(bf16[768,256]{1,0:T(8,128)(2,1)S(1)} %collective-permute-done.21.refs_1_), channel_id=1, source_target_pairs={{0,4},{1,5},{2,6},{3,7},{4,8},{5,9},{6,10},{7,11},{8,12},{9,13},{1... | collective-permute-start | bytes 1179656 | tf_op jit(solution)/shard_map/ppermute | solution.py:209
  163.2 16.1 %collective-permute-start.25 = (bf16[768,256]{1,0:T(8,128)(2,1)S(1)}, bf16[768,256]{1,0:T(8,128)(2,1)S(1)}, u32[]{:S(2)}, u32[]{:S(2)}) collective-permute-start(bf16[768,256]{1,0:T(8,128)(2,1)S(1)} %collective-permute-done.21.refs_1_), channel_id=1, source_target_pairs={{0,12},{1,13},{2,14},{3,15},{4,0},{5,1},{6,2},{7,3},{8,4},{9,5},{1... | collective-permute-start | bytes 1179656 | tf_op jit(solution)/shard_map/ppermute | solution.py:209
  171.1 11.2 %collective-permute-start.27 = (bf16[768,256]{1,0:T(8,128)(2,1)S(1)}, bf16[768,256]{1,0:T(8,128)(2,1)S(1)}, u32[]{:S(2)}, u32[]{:S(2)}) collective-permute-start(bf16[768,256]{1,0:T(8,128)(2,1)S(1)} %collective-permute-done.26.refs_6_), channel_id=1, source_target_pairs={{0,2},{1,3},{2,0},{3,1},{4,6},{5,7},{6,4},{7,5},{8,10},{9,11},{10,... | collective-permute-start | bytes 1179656 | tf_op jit(solution)/shard_map/ppermute | solution.py:209
  174.7 7.7 %collective-permute-start.29 = (bf16[768,256]{1,0:T(8,128)(2,1)S(1)}, bf16[768,256]{1,0:T(8,128)(2,1)S(1)}, u32[]{:S(2)}, u32[]{:S(2)}) collective-permute-start(bf16[768,256]{1,0:T(8,128)(2,1)S(1)} %collective-permute-done.21.refs_1_), channel_id=1, source_target_pairs={{0,1},{1,0},{2,3},{3,2},{4,5},{5,4},{6,7},{7,6},{8,9},{9,8},{10,11... | collective-permute-start | bytes 1179656 | tf_op jit(solution)/shard_map/ppermute | solution.py:209
  174.7 8.2 %collective-permute-start.30 = (bf16[768,256]{1,0:T(8,128)(2,1)S(1)}, bf16[768,256]{1,0:T(8,128)(2,1)S(1)}, u32[]{:S(2)}, u32[]{:S(2)}) collective-permute-start(bf16[768,256]{1,0:T(8,128)(2,1)S(1)} %collective-permute-done.22.refs_2_), channel_id=1, source_target_pairs={{0,1},{1,0},{2,3},{3,2},{4,5},{5,4},{6,7},{7,6},{8,9},{9,8},{10,11... | collective-permute-start | bytes 1179656 | tf_op jit(solution)/shard_map/ppermute | solution.py:209
  178.3 6.8 %collective-permute-start.34 = (bf16[768,256]{1,0:T(8,128)(2,1)S(1)}, bf16[768,256]{1,0:T(8,128)(2,1)}, u32[]{:S(2)}, u32[]{:S(2)}) collective-permute-start(bf16[768,256]{1,0:T(8,128)(2,1)S(1)} %collective-permute-done.26.refs_6_), channel_id=1, source_target_pairs={{0,1},{1,0},{2,3},{3,2},{4,5},{5,4},{6,7},{7,6},{8,9},{9,8},{10,11... | collective-permute-start | bytes 1179656 | tf_op jit(solution)/shard_map/ppermute | solution.py:209
  179.4 5.7 %collective-permute-start.32 = (bf16[768,256]{1,0:T(8,128)(2,1)S(1)}, bf16[768,256]{1,0:T(8,128)(2,1)}, u32[]{:S(2)}, u32[]{:S(2)}) collective-permute-start(bf16[768,256]{1,0:T(8,128)(2,1)S(1)} %collective-permute-done.24.refs_4_), channel_id=1, source_target_pairs={{0,1},{1,0},{2,3},{3,2},{4,5},{5,4},{6,7},{7,6},{8,9},{9,8},{10,11... | collective-permute-start | bytes 1179656 | tf_op jit(solution)/shard_map/ppermute | solution.py:209
  198.5 21.2 %collective-permute-start.36 = (bf16[768,512]{1,0:T(8,128)(2,1)}, bf16[768,512]{1,0:T(8,128)(2,1)S(1)}, u32[]{:S(2)}, u32[]{:S(2)}) collective-permute-start(bf16[768,512]{1,0:T(8,128)(2,1)} %get-tuple-element.21), channel_id=1, source_target_pairs={{0,32},{16,48},{32,64},{48,80},{64,96},{80,112},{96,0},{112,16},{1... | collective-permute-start | bytes 2359304 | tf_op jit(solution)/shard_map/ppermute | solution.py:214
  198.5 21.9 %collective-permute-start.37 = (bf16[768,512]{1,0:T(8,128)(2,1)}, bf16[768,512]{1,0:T(8,128)(2,1)S(1)}, u32[]{:S(2)}, u32[]{:S(2)}) collective-permute-start(bf16[768,512]{1,0:T(8,128)(2,1)} %get-tuple-element.21), channel_id=1, source_target_pairs={{0,96},{16,112},{32,0},{48,16},{64,32},{80,48},{96,64},{112,80},{1... | collective-permute-start | bytes 2359304 | tf_op jit(solution)/shard_map/ppermute | solution.py:214
  201.8 22.1 %collective-permute-start.38 = (bf16[768,512]{1,0:T(8,128)(2,1)}, bf16[768,512]{1,0:T(8,128)(2,1)S(1)}, u32[]{:S(2)}, u32[]{:S(2)}) collective-permute-start(bf16[768,512]{1,0:T(8,128)(2,1)} %get-tuple-element.21), channel_id=1, source_target_pairs={{0,16},{16,0},{32,48},{48,32},{64,80},{80,64},{96,112},{112,96},{1... | collective-permute-start | bytes 2359304 | tf_op jit(solution)/shard_map/ppermute | solution.py:214
  219.7 13.3 %collective-permute-start.39 = (bf16[384,512]{1,0:T(8,128)(2,1)S(1)}, bf16[384,512]{1,0:T(8,128)(2,1)S(1)}, u32[]{:S(2)}, u32[]{:S(2)}) collective-permute-start(bf16[384,512]{1,0:T(8,128)(2,1)S(1)} %slice.92), channel_id=1, source_target_pairs={{0,32},{16,48},{32,64},{48,80},{64,96},{80,112},{96,0},{112,16},{1... | collective-permute-start | bytes 1179656 | tf_op jit(solution)/shard_map/ppermute | solution.py:214
  221.2 12.5 %collective-permute-start.40 = (bf16[384,512]{1,0:T(8,128)(2,1)}, bf16[384,512]{1,0:T(8,128)(2,1)S(1)}, u32[]{:S(2)}, u32[]{:S(2)}) collective-permute-start(bf16[384,512]{1,0:T(8,128)(2,1)} %slice.93), channel_id=1, source_target_pairs={{0,96},{16,112},{32,0},{48,16},{64,32},{80,48},{96,64},{112,80},{1... | collective-permute-start | bytes 1179656 | tf_op jit(solution)/shard_map/ppermute | solution.py:214
  223.8 24.5 %collective-permute-start.41 = (bf16[768,512]{1,0:T(8,128)(2,1)S(1)}, bf16[768,512]{1,0:T(8,128)(2,1)S(1)}, u32[]{:S(2)}, u32[]{:S(2)}) collective-permute-start(bf16[768,512]{1,0:T(8,128)(2,1)S(1)} %collective-permute-done.38), channel_id=1, source_target_pairs={{0,32},{16,48},{32,64},{48,80},{64,96},{80,112},{96,0},{112,16},{1... | collective-permute-start | bytes 2359304 | tf_op jit(solution)/shard_map/ppermute | solution.py:214
  225.9 23.4 %collective-permute-start.42 = (bf16[768,512]{1,0:T(8,128)(2,1)S(1)}, bf16[768,512]{1,0:T(8,128)(2,1)S(1)}, u32[]{:S(2)}, u32[]{:S(2)}) collective-permute-start(bf16[768,512]{1,0:T(8,128)(2,1)S(1)} %collective-permute-done.38), channel_id=1, source_target_pairs={{0,96},{16,112},{32,0},{48,16},{64,32},{80,48},{96,64},{112,80},{1... | collective-permute-start | bytes 2359304 | tf_op jit(solution)/shard_map/ppermute | solution.py:214
  233.7 16.5 %collective-permute-start.43 = (bf16[768,512]{1,0:T(8,128)(2,1)S(1)}, bf16[768,512]{1,0:T(8,128)(2,1)S(1)}, u32[]{:S(2)}, u32[]{:S(2)}) collective-permute-start(bf16[768,512]{1,0:T(8,128)(2,1)S(1)} %pad_maximum_fusion), channel_id=1, source_target_pairs={{0,16},{16,0},{32,48},{48,32},{64,80},{80,64},{96,112},{112,96},{1... | collective-permute-start | bytes 2359304 | tf_op jit(solution)/shard_map/ppermute | solution.py:214
  (38 other events, 466.0 us)
Sparse Core Ops, SparseCore 0:
  16.7 55.4 all-gather.2
  91.8 61.3 all-gather.4

commit v7 on v6

--- a/solution.py
+++ b/solution.py
@@ -127,7 +127,7 @@
     )(lens, weights, scales, merged, squares, gain, taps)
 
 
-def gradient_kernel(places_ref, here_ref, across_ref, *refs):
+def gradient_kernel(places_ref, here_ref, first_ref, last_ref, *refs):
     number = 2 * len(GRAD_ORDER)
     own, other, old_ref, grad_ref, new_ref = refs[:number], refs[number : 2 * number], *refs[2 * number :]
     step = pl.program_id(0)
@@ -147,21 +147,25 @@
                 here = jnp.where(same == 1, straight, crossed)
                 across = jnp.where(same == 1, crossed, straight)
                 columns = pl.ds(pl.multiple_of(parity * wide, wide), wide)
-                grad_ref[:, columns] += lax.dot_general(
-                    here_ref[...], here, COLS_COLS, preferred_element_type=f32
-                ) + lax.dot_general(across_ref[...], across, COLS_COLS, preferred_element_type=f32)
+                part = first_ref.shape[0]
+                grad_ref[:, columns] += (
+                    lax.dot_general(here_ref[...], here, COLS_COLS, preferred_element_type=f32)
+                    + lax.dot_general(first_ref[...], across[:part], COLS_COLS, preferred_element_type=f32)
+                    + lax.dot_general(last_ref[...], across[part:], COLS_COLS, preferred_element_type=f32)
+                )
 
     @pl.when(step == len(GRAD_ORDER) - 1)
     def _():
         new_ref[...] = (old_ref[...].astype(f32) - step_size * grad_ref[...]).astype(bf16)
 
 
-def gradient(places, here, across, own, other, weight):
+def gradient(places, here, first, last, own, other, weight):
     steps = len(GRAD_ORDER)
     rows, wide = own[0].shape
     depth = weight.shape[0]
     piece = pl.BlockSpec((rows, wide), lambda i, places: (0, 0))
     taps = pl.BlockSpec((rows, depth), lambda i, places: (places[i], 0))
+    half = pl.BlockSpec((rows // 2, depth), lambda i, places: (places[i], 0))
     out = pl.BlockSpec((depth, 2 * wide), lambda i, places: (0, 0))
     old = pl.BlockSpec((depth, 2 * wide), lambda i, places: (0, places[steps + 2]))
     return pl.pallas_call(
@@ -169,7 +173,7 @@
         grid_spec=pltpu.PrefetchScalarGridSpec(
             num_scalar_prefetch=1,
             grid=(steps,),
-            in_specs=[taps, taps] + [piece] * (4 * steps) + [old],
+            in_specs=[taps, half, half] + [piece] * (4 * steps) + [old],
             out_specs=[out, out],
         ),
         out_shape=[
@@ -180,7 +184,7 @@
         cost_estimate=pl.CostEstimate(
             flops=8 * steps * rows * depth * wide, bytes_accessed=20 * 2**20, transcendentals=0
         ),
-    )(places, here, across, *own, *other, weight)
+    )(places, here, first, last, *own, *other, weight)
 
 
 def row_major(a):
@@ -280,8 +284,8 @@
 
 def sum_over_tr(value):
     value = value + to_sibling(value)
-    value = value + to_chip(value, 0, 1)
-    return value + to_chip(value, 1, 0) + to_chip(value, 2, 0) + to_chip(value, 3, 0)
+    value = value + to_chip(value, 1, 0) + to_chip(value, 2, 0) + to_chip(value, 3, 0)
+    return value + to_chip(value, 0, 1)
 
 
 def per_device(taps, routes, lengths, merge_weight, norm_gain, head_scale):
@@ -311,7 +315,6 @@
     def gather_taps(value):
         return row_major(lax.all_gather(value, "rep", axis=0, tiled=True, axis_index_groups=along_z))
 
-    rows_across = row_major(to_group(rows, 0, 1))
     taps_here = gather_taps(rows)
 
     def sums(rows, offsets, parity):
@@ -331,6 +334,9 @@
         tuple(first[offset].astype(f16) for offset in ORDER[0]) + (rows,)
     )
     far_across = send(far_across, 0, 1)
+    far_across, rows_now = lax.optimization_barrier((far_across, rows_now))
+    part = slots * span // 2
+    first_across = row_major(to_group(rows_now[:part], 0, 1))
     up_across = send(up_across, 1, 0)
     down_across = send(down_across, 3, 0)
     second = chip_sums(rows_now, ORDER[1])
@@ -340,9 +346,10 @@
     across = send(second[0, 1] + up_across.astype(f32) + down_across.astype(f32), 0, 1).astype(f32)
     merged = (second[0, 0] + up + down + far + across) * (1.0 / SEND)
     merged = merged.reshape(slots, span, wide)
-    merged, rows_across = lax.optimization_barrier((merged, rows_across))
-    taps_across = gather_taps(rows_across)
     squares = sum_over_tr(jnp.sum(merged * merged, axis=2))
+    squares, first_across, rows_now = lax.optimization_barrier((squares, first_across, rows_now))
+    taps_first = gather_taps(first_across)
+    last_across = row_major(to_group(rows_now[part:], 0, 1))
 
     scaled, crossed = attention(
         lens,
@@ -353,6 +360,8 @@
         norm_gain.reshape(1, wide),
         taps[:, :, 2, :],
     )
+    crossed, last_across = lax.optimization_barrier((crossed, last_across))
+    taps_last = gather_taps(last_across)
     crossed = sum_over_tr(crossed.reshape(slots, span))
     inverse = lax.rsqrt(squares / width_all + epsilon)
     merged_grad = (
@@ -381,7 +390,8 @@
     grad, new_block = gradient(
         jnp.stack(places).astype(jnp.int32),
         taps_here,
-        taps_across,
+        taps_first,
+        taps_last,
         [own_half[k] for k in offsets],
         [other_half[k] for k in offsets],
         weight,

time: 259 us -> 248 us (0.958)
  starting transfers between devices: 77.1 us -> 70.8 us
  waiting for transfers between devices: 93 us -> 86.7 us
  local copies, waits for them, and re-layouts: 26.7 us -> 30.2 us
    ppermute x34, waiting for transfers between devices: 63.5 us -> 53.4 us  [to_chip(): return lax.ppermute(value, 'tr', pairs)]
    ppermute x34, starting transfers between devices: 61.8 us -> 57 us  [to_chip(): return lax.ppermute(value, 'tr', pairs)]
    ppermute x9 -> x10, waiting for transfers between devices: 29.6 us -> 33.2 us  [to_group(): return lax.ppermute(value, 'rep', pairs)]
    unnamed x49, local copies, waits for them, and re-layouts: 12.4 us -> 15.8 us
    ppermute x9 -> x10, starting transfers between devices: 14.6 us -> 13 us  [to_group(): return lax.ppermute(value, 'rep', pairs)]
  transfers between devices with their start and end apart: 46 -> 48, of which waited for: 21 -> 23; matrix products, arithmetic and copies ran while one was open for 8% -> 8% of each run, Pallas kernels for 8% -> 9%
where the time goes in v7:
time: 248 us; the launch traced here: 247 us
  waiting for transfers between devices  86.7 us (35%)
  starting transfers between devices  70.8 us (29%)
  Pallas kernels  37.3 us (15%)
  local copies, waits for them, and re-layouts  30.2 us (12%)
  between operations  14.3 us (6%)
  other arithmetic  7.92 us (3%)
    ppermute x34, starting transfers between devices, to_chip(): return lax.ppermute(value, 'tr', pairs)  57 us
    ppermute x34, waiting for transfers between devices, to_chip(): return lax.ppermute(value, 'tr', pairs)  53.4 us
    ppermute x10, waiting for transfers between devices, to_group(): return lax.ppermute(value, 'rep', pairs)  33.2 us
    unnamed x49, local copies, waits for them, and re-layouts  15.8 us
    pallas_call x1, Pallas kernels, gradient(): pl.pallas_call(gradient_kernel, grid_spec=pltpu.PrefetchScalarGridSpec(nu...  13.5 us
    ppermute x10, starting transfers between devices, to_group(): return lax.ppermute(value, 'rep', pairs)  13 us
    pallas_call x4, Pallas kernels, products(): pl.pallas_call(product_kernel, grid_spec=pltpu.PrefetchScalarGridSpec(num...  12.5 us
    pallas_call x1, Pallas kernels, attention(): pl.pallas_call(attention_kernel, grid=(count // slots,), in_specs=[scalar...  11.3 us
  transfers between devices with their start and end apart: 48, of which 23 were waited for; matrix products, arithmetic and copies ran while one was open for 8% of the time, Pallas kernels for 9%

profile of v7, /device:TPU:0, one launch (start us, length us, event | category | flops | bytes accessed | tf_op | source)
XLA Modules:
  0.0 247.3 jit_solution(11873080693746142256)
XLA Ops:
  7.3 2.3 copy.16
  10.0 3.1 %copy-done = bf16[3,256,4096]{2,1,0:T(8,128)(2,1)S(1)} copy-done((bf16[3,256,4096]{2,1,0:T(8,128)(2,1)S(1)}, bf16[3,256,4096]{2,1,0:T(8,128)(2,1)}, u32[]{:S(2)}) %copy-start) | copy-done | bytes 6291480
  15.6 2.8 %copy-done.1 = bf16[3,256,4096]{2,1,0:T(8,128)(2,1)S(1)} copy-done((bf16[3,256,4096]{2,1,0:T(8,128)(2,1)S(1)}, bf16[3,256,4096]{2,1,0:T(8,128)(2,1)}, u32[]{:S(2)}) %copy-start.1) | copy-done | bytes 6291480
  24.0 3.2 %collective-permute-start.1 = (f16[768,256]{1,0:T(8,128)(2,1)S(1)}, f16[768,256]{1,0:T(8,128)(2,1)S(1)}, u32[]{:S(2)}, u32[]{:S(2)}) collective-permute-start(f16[768,256]{1,0:T(8,128)(2,1)S(1)} %get-tuple-element.17), channel_id=1, source_target_pairs={{0,2},{1,3},{2,0},{3,1},{4,6},{5,7},{6,4},{7,5},{8,10},{9,11},{10,... | collective-permute-start | bytes 1179656 | tf_op jit(solution)/shard_map/ppermute | solution.py:213
  27.3 9.8 %collective-permute-done.1 = f16[768,256]{1,0:T(8,128)(2,1)S(1)} collective-permute-done((f16[768,256]{1,0:T(8,128)(2,1)S(1)}, f16[768,256]{1,0:T(8,128)(2,1)S(1)}, u32[]{:S(2)}, u32[]{:S(2)}) %collective-permute-start.1) | collective-permute-done | bytes 393248 | tf_op jit(solution)/shard_map/ppermute | solution.py:213
  37.1 2.8 %copy-done.2 = bf16[3,256,4096]{2,1,0:T(8,128)(2,1)S(1)} copy-done((bf16[3,256,4096]{2,1,0:T(8,128)(2,1)S(1)}, bf16[3,256,4096]{2,1,0:T(8,128)(2,1)}, u32[]{:S(2)}) %copy-start.2) | copy-done | bytes 6291480
  40.0 4.8 %shard_map.80 = f32[5,768,256]{2,1,0:T(8,128)} custom-call(s32[5]{0:T(128)S(1)} %stack.111.blocks_ref, bf16[768,768]{1,0:T(8,128)(2,1)S(1)} %bitcast.86, bf16[768,4096]{1,0:T(8,128)(2,1)S(1)} %bitcast.81), custom_call_target="tpu_custom_call" | custom-call | flops 1509949440 | bytes 7077888 | tf_op jit(solution)/shard_map/pallas_call | solution.py:264
  48.1 2.8 %copy-done.3 = bf16[3,256,4096]{2,1,0:T(8,128)(2,1)S(1)} copy-done((bf16[3,256,4096]{2,1,0:T(8,128)(2,1)S(1)}, bf16[3,256,4096]{2,1,0:T(8,128)(2,1)}, u32[]{:S(2)}) %copy-start.3) | copy-done | bytes 6291480
  50.9 3.3 %shard_map.79 = f32[5,768,256]{2,1,0:T(8,128)S(1)} custom-call(s32[5]{0:T(128)S(1)} %stack.97.blocks_ref, bf16[768,768]{1,0:T(8,128)(2,1)S(1)} %bitcast.87, bf16[768,4096]{1,0:T(8,128)(2,1)S(1)} %bitcast.82), custom_call_target="tpu_custom_call" | custom-call | flops 1509949440 | bytes 7077888 | tf_op jit(solution)/shard_map/pallas_call | solution.py:264
  56.5 2.8 %collective-permute-start.4 = (f16[768,256]{1,0:T(8,128)(2,1)S(1)}, f16[768,256]{1,0:T(8,128)(2,1)S(1)}, u32[]{:S(2)}, u32[]{:S(2)}) collective-permute-start(f16[768,256]{1,0:T(8,128)(2,1)S(1)} %get-tuple-element.35), channel_id=1, source_target_pairs={{0,12},{1,13},{2,14},{3,15},{4,0},{5,1},{6,2},{7,3},{8,4},{9,5},{1... | collective-permute-start | bytes 1179656 | tf_op jit(solution)/shard_map/ppermute | solution.py:213
  62.5 3.0 %collective-permute-start.8 = (f16[768,256]{1,0:T(8,128)(2,1)S(1)}, f16[768,256]{1,0:T(8,128)(2,1)S(1)}, u32[]{:S(2)}, u32[]{:S(2)}) collective-permute-start(f16[768,256]{1,0:T(8,128)(2,1)S(1)} %get-tuple-element.37), channel_id=1, source_target_pairs={{0,2},{1,3},{2,0},{3,1},{4,6},{5,7},{6,4},{7,5},{8,10},{9,11},{10,... | collective-permute-start | bytes 1179656 | tf_op jit(solution)/shard_map/ppermute | solution.py:213
  66.3 10.6 %collective-permute-done.3 = f16[768,256]{1,0:T(8,128)(2,1)S(1)} collective-permute-done((f16[768,256]{1,0:T(8,128)(2,1)S(1)}, f16[768,256]{1,0:T(8,128)(2,1)S(1)}, u32[]{:S(2)}, u32[]{:S(2)}) %collective-permute-start.3) | collective-permute-done | bytes 393248 | tf_op jit(solution)/shard_map/ppermute | solution.py:213
  80.7 3.5 %collective-permute-start.11 = (f32[8,96]{1,0:T(8,128)S(1)}, f32[8,96]{1,0:T(8,128)S(1)}, u32[]{:S(2)}, u32[]{:S(2)}) collective-permute-start(f32[8,96]{1,0:T(8,128)S(1)} %add.444), channel_id=1, source_target_pairs={{0,8},{1,9},{2,10},{3,11},{4,12},{5,13},{6,14},{7,15},{8,0},{9,1},... | collective-permute-start | bytes 9224 | tf_op jit(solution)/shard_map/ppermute | solution.py:213
  87.8 3.0 %collective-permute-start.13 = (f32[8,96]{1,0:T(8,128)S(1)}, f32[8,96]{1,0:T(8,128)S(1)}, u32[]{:S(2)}, u32[]{:S(2)}) collective-permute-start(f32[8,96]{1,0:T(8,128)S(1)} %add_add_fusion.1), channel_id=1, source_target_pairs={{0,2},{1,3},{2,0},{3,1},{4,6},{5,7},{6,4},{7,5},{8,10},{9,11},{10,... | collective-permute-start | bytes 9224 | tf_op jit(solution)/shard_map/ppermute | solution.py:213
  97.0 11.3 %shard_map.81 = (f32[8,96,256]{2,1,0:T(8,128)S(1)}, f32[8,1,96]{2,1,0:T(1,128)S(1)}) custom-call(s32[8]{0:T(128)S(1)} %dynamic_slice.6.lens_ref, f32[8]{0:T(128)S(1)} %convert_divide_fusion.weights_ref, f32[2]{0:T(128)S(1)} %copy-done.8, f32[8,96,256]{2,1,0:T(8,128)S(1)} %bitcast.90, f32[8,1,96]{2,1,0:T(1,128)S(1)} %bitcast.92, f32[1,256]{1,0:T(1,128)S(1)} %bitcast.95, ...), custom_call_target="tpu_custom_call" | custom-call | flops 2000000000 | bytes 3000000 | tf_op jit(solution)/shard_map/pallas_call | solution.py:116
  110.4 2.6 %collective-permute-start.18 = (f32[8,96]{1,0:T(8,128)S(1)}, f32[8,96]{1,0:T(8,128)S(1)}, u32[]{:S(2)}, u32[]{:S(2)}) collective-permute-start(f32[8,96]{1,0:T(8,128)S(1)} %add.454), channel_id=1, source_target_pairs={{0,8},{1,9},{2,10},{3,11},{4,12},{5,13},{6,14},{7,15},{8,0},{9,1},... | collective-permute-start | bytes 9224 | tf_op jit(solution)/shard_map/ppermute | solution.py:213
  116.7 2.7 %collective-permute-start.20 = (f32[8,96]{1,0:T(8,128)S(1)}, f32[8,96]{1,0:T(8,128)S(1)}, u32[]{:S(2)}, u32[]{:S(2)}) collective-permute-start(f32[8,96]{1,0:T(8,128)S(1)} %add_add_fusion), channel_id=1, source_target_pairs={{0,2},{1,3},{2,0},{3,1},{4,6},{5,7},{6,4},{7,5},{8,10},{9,11},{10,... | collective-permute-start | bytes 9224 | tf_op jit(solution)/shard_map/ppermute | solution.py:213
  119.4 2.4 collective-permute-done.20
  122.8 13.0 %collective-permute-start.22 = (bf16[768,256]{1,0:T(8,128)(2,1)S(1)}, bf16[768,256]{1,0:T(8,128)(2,1)S(1)}, u32[]{:S(2)}, u32[]{:S(2)}) collective-permute-start(bf16[768,256]{1,0:T(8,128)(2,1)S(1)} %collective-permute-done.21.refs_0_), channel_id=1, source_target_pairs={{0,2},{1,3},{2,0},{3,1},{4,6},{5,7},{6,4},{7,5},{8,10},{9,11},{10,... | collective-permute-start | bytes 1179656 | tf_op jit(solution)/shard_map/ppermute | solution.py:213
  135.8 6.7 %collective-permute-start.27 = (bf16[768,256]{1,0:T(8,128)(2,1)S(1)}, bf16[768,256]{1,0:T(8,128)(2,1)S(1)}, u32[]{:S(2)}, u32[]{:S(2)}) collective-permute-start(bf16[768,256]{1,0:T(8,128)(2,1)S(1)} %collective-permute-done.21.refs_0_), channel_id=1, source_target_pairs={{0,8},{1,9},{2,10},{3,11},{4,12},{5,13},{6,14},{7,15},{8,0},{9,1},... | collective-permute-start | bytes 1179656 | tf_op jit(solution)/shard_map/ppermute | solution.py:213
  145.8 6.7 %collective-permute-done.27.refs_6_ = bf16[768,256]{1,0:T(8,128)(2,1)S(1)} collective-permute-done((bf16[768,256]{1,0:T(8,128)(2,1)S(1)}, bf16[768,256]{1,0:T(8,128)(2,1)S(1)}, u32[]{:S(2)}, u32[]{:S(2)}) %collective-permute-start.27) | collective-permute-done | bytes 393248 | tf_op jit(solution)/shard_map/ppermute | solution.py:213
  152.6 3.8 %collective-permute-start.26 = (bf16[768,256]{1,0:T(8,128)(2,1)S(1)}, bf16[768,256]{1,0:T(8,128)(2,1)S(1)}, u32[]{:S(2)}, u32[]{:S(2)}) collective-permute-start(bf16[768,256]{1,0:T(8,128)(2,1)S(1)} %collective-permute-done.22.refs_1_), channel_id=1, source_target_pairs={{0,12},{1,13},{2,14},{3,15},{4,0},{5,1},{6,2},{7,3},{8,4},{9,5},{1... | collective-permute-start | bytes 1179656 | tf_op jit(solution)/shard_map/ppermute | solution.py:213
  156.4 4.1 %collective-permute-done.23.refs_2_ = bf16[768,256]{1,0:T(8,128)(2,1)S(1)} collective-permute-done((bf16[768,256]{1,0:T(8,128)(2,1)S(1)}, bf16[768,256]{1,0:T(8,128)(2,1)S(1)}, u32[]{:S(2)}, u32[]{:S(2)}) %collective-permute-start.23) | collective-permute-done | bytes 393248 | tf_op jit(solution)/shard_map/ppermute | solution.py:213
  162.7 3.2 %collective-permute-done.24.refs_3_ = bf16[768,256]{1,0:T(8,128)(2,1)S(1)} collective-permute-done((bf16[768,256]{1,0:T(8,128)(2,1)S(1)}, bf16[768,256]{1,0:T(8,128)(2,1)S(1)}, u32[]{:S(2)}, u32[]{:S(2)}) %collective-permute-start.24) | collective-permute-done | bytes 393248 | tf_op jit(solution)/shard_map/ppermute | solution.py:213
  166.5 3.3 %collective-permute-done.28.refs_7_ = bf16[768,256]{1,0:T(8,128)(2,1)S(1)} collective-permute-done((bf16[768,256]{1,0:T(8,128)(2,1)S(1)}, bf16[768,256]{1,0:T(8,128)(2,1)S(1)}, u32[]{:S(2)}, u32[]{:S(2)}) %collective-permute-start.28) | collective-permute-done | bytes 393248 | tf_op jit(solution)/shard_map/ppermute | solution.py:213
  173.4 13.5 %shard_map.82 = (f32[768,512]{1,0:T(8,128)}, bf16[768,512]{1,0:T(8,128)(2,1)}) custom-call(s32[7]{0:T(128)} %stack.91.places_ref, bf16[3072,768]{1,0:T(8,128)(2,1)} %all-gather.4.cloned.1.call-done.here_ref, bf16[1536,768]{1,0:T(8,128)(2,1)} %all-gather.6.cloned.1.call-done.first_ref, bf16[1536,768]{1,0:T(8,128)(2,1)} %all-gather.8.cloned.1.call-done.last_ref, ...), custom_call_target="tpu_custom_call" | custom-call | flops 4831838208 | bytes 20971520 | tf_op jit(solution)/shard_map/pallas_call | solution.py:171
  187.2 3.6 %collective-permute-start.38 = (bf16[768,512]{1,0:T(8,128)(2,1)}, bf16[768,512]{1,0:T(8,128)(2,1)S(1)}, u32[]{:S(2)}, u32[]{:S(2)}) collective-permute-start(bf16[768,512]{1,0:T(8,128)(2,1)} %get-tuple-element.31), channel_id=1, source_target_pairs={{0,96},{16,112},{32,0},{48,16},{64,32},{80,48},{96,64},{112,80},{1... | collective-permute-start | bytes 2359304 | tf_op jit(solution)/shard_map/ppermute | solution.py:218
  190.9 18.1 %collective-permute-done.37 = bf16[768,512]{1,0:T(8,128)(2,1)S(1)} collective-permute-done((bf16[768,512]{1,0:T(8,128)(2,1)}, bf16[768,512]{1,0:T(8,128)(2,1)S(1)}, u32[]{:S(2)}, u32[]{:S(2)}) %collective-permute-start.37) | collective-permute-done | bytes 786464 | tf_op jit(solution)/shard_map/ppermute | solution.py:218
  209.9 3.2 %collective-permute-start.41 = (bf16[384,512]{1,0:T(8,128)(2,1)}, bf16[384,512]{1,0:T(8,128)(2,1)S(1)}, u32[]{:S(2)}, u32[]{:S(2)}) collective-permute-start(bf16[384,512]{1,0:T(8,128)(2,1)} %slice.101), channel_id=1, source_target_pairs={{0,96},{16,112},{32,0},{48,16},{64,32},{80,48},{96,64},{112,80},{1... | collective-permute-start | bytes 1179656 | tf_op jit(solution)/shard_map/ppermute | solution.py:218
  215.2 3.2 %collective-permute-start.43 = (bf16[768,512]{1,0:T(8,128)(2,1)S(1)}, bf16[768,512]{1,0:T(8,128)(2,1)S(1)}, u32[]{:S(2)}, u32[]{:S(2)}) collective-permute-start(bf16[768,512]{1,0:T(8,128)(2,1)S(1)} %collective-permute-done.39), channel_id=1, source_target_pairs={{0,96},{16,112},{32,0},{48,16},{64,32},{80,48},{96,64},{112,80},{1... | collective-permute-start | bytes 2359304 | tf_op jit(solution)/shard_map/ppermute | solution.py:218
  218.4 3.9 %collective-permute-done.40 = bf16[384,512]{1,0:T(8,128)(2,1)S(1)} collective-permute-done((bf16[384,512]{1,0:T(8,128)(2,1)S(1)}, bf16[384,512]{1,0:T(8,128)(2,1)S(1)}, u32[]{:S(2)}, u32[]{:S(2)}) %collective-permute-start.40) | collective-permute-done | bytes 393248 | tf_op jit(solution)/shard_map/ppermute | solution.py:218
  227.5 10.5 %collective-permute-done.42 = bf16[768,512]{1,0:T(8,128)(2,1)S(1)} collective-permute-done((bf16[768,512]{1,0:T(8,128)(2,1)S(1)}, bf16[768,512]{1,0:T(8,128)(2,1)S(1)}, u32[]{:S(2)}, u32[]{:S(2)}) %collective-permute-start.42) | collective-permute-done | bytes 786464 | tf_op jit(solution)/shard_map/ppermute | solution.py:218
  (161 shorter events, 59.0 us)
Async XLA Ops:
  7.2 165.3 %all-gather.4.cloned.1.call-start = ((), (), s32[]{:S(2)}) async-start(), calls=%async_computation | async-start | bytes 5898240 | tf_op jit(solution)/shard_map/all_gather | solution.py:316
  15.5 157.8 %all-gather.6.cloned.1.call-start = ((), (), s32[]{:S(2)}) async-start(), calls=%async_computation.1 | async-start | bytes 2949120 | tf_op jit(solution)/shard_map/all_gather | solution.py:316
  24.0 13.1 %collective-permute-start.1 = (f16[768,256]{1,0:T(8,128)(2,1)S(1)}, f16[768,256]{1,0:T(8,128)(2,1)S(1)}, u32[]{:S(2)}, u32[]{:S(2)}) collective-permute-start(f16[768,256]{1,0:T(8,128)(2,1)S(1)} %get-tuple-element.17), channel_id=1, source_target_pairs={{0,2},{1,3},{2,0},{3,1},{4,6},{5,7},{6,4},{7,5},{8,10},{9,11},{10,... | collective-permute-start | bytes 1179656 | tf_op jit(solution)/shard_map/ppermute | solution.py:213
  44.8 9.5 %collective-permute-start.2 = (f32[5,768,256]{2,1,0:T(8,128)}, f32[5,768,256]{2,1,0:T(8,128)}, u32[]{:S(2)}, u32[]{:S(2)}) collective-permute-start(f32[5,768,256]{2,1,0:T(8,128)} %shard_map.80), channel_id=1, source_target_pairs={{0,1},{1,0},{2,3},{3,2},{4,5},{5,4},{6,7},{7,6},{8,9},{9,8},{10,11... | collective-permute-start | bytes 11796488 | tf_op jit(solution)/shard_map/ppermute | solution.py:213
  44.9 14.4 %collective-permute-start.6 = (f16[768,256]{1,0:T(8,128)(2,1)S(1)}, f16[768,256]{1,0:T(8,128)(2,1)S(1)}, u32[]{:S(2)}, u32[]{:S(2)}) collective-permute-start(f16[768,256]{1,0:T(8,128)(2,1)S(1)} %get-tuple-element.21), channel_id=1, source_target_pairs={{0,4},{1,5},{2,6},{3,7},{4,8},{5,9},{6,10},{7,11},{8,12},{9,13},{1... | collective-permute-start | bytes 1179656 | tf_op jit(solution)/shard_map/ppermute | solution.py:213
  46.5 12.8 %collective-permute-start.7 = (f16[768,256]{1,0:T(8,128)(2,1)S(1)}, f16[768,256]{1,0:T(8,128)(2,1)S(1)}, u32[]{:S(2)}, u32[]{:S(2)}) collective-permute-start(f16[768,256]{1,0:T(8,128)(2,1)S(1)} %get-tuple-element.22), channel_id=1, source_target_pairs={{0,12},{1,13},{2,14},{3,15},{4,0},{5,1},{6,2},{7,3},{8,4},{9,5},{1... | collective-permute-start | bytes 1179656 | tf_op jit(solution)/shard_map/ppermute | solution.py:213
  56.0 20.9 %collective-permute-start.3 = (f16[768,256]{1,0:T(8,128)(2,1)S(1)}, f16[768,256]{1,0:T(8,128)(2,1)S(1)}, u32[]{:S(2)}, u32[]{:S(2)}) collective-permute-start(f16[768,256]{1,0:T(8,128)(2,1)S(1)} %get-tuple-element.34), channel_id=1, source_target_pairs={{0,4},{1,5},{2,6},{3,7},{4,8},{5,9},{6,10},{7,11},{8,12},{9,13},{1... | collective-permute-start | bytes 1179656 | tf_op jit(solution)/shard_map/ppermute | solution.py:213
  56.5 20.4 %collective-permute-start.4 = (f16[768,256]{1,0:T(8,128)(2,1)S(1)}, f16[768,256]{1,0:T(8,128)(2,1)S(1)}, u32[]{:S(2)}, u32[]{:S(2)}) collective-permute-start(f16[768,256]{1,0:T(8,128)(2,1)S(1)} %get-tuple-element.35), channel_id=1, source_target_pairs={{0,12},{1,13},{2,14},{3,15},{4,0},{5,1},{6,2},{7,3},{8,4},{9,5},{1... | collective-permute-start | bytes 1179656 | tf_op jit(solution)/shard_map/ppermute | solution.py:213
  61.1 15.8 %collective-permute-start.5 = (f16[768,256]{1,0:T(8,128)(2,1)S(1)}, f16[768,256]{1,0:T(8,128)(2,1)S(1)}, u32[]{:S(2)}, u32[]{:S(2)}) collective-permute-start(f16[768,256]{1,0:T(8,128)(2,1)S(1)} %get-tuple-element.36), channel_id=1, source_target_pairs={{0,8},{1,9},{2,10},{3,11},{4,12},{5,13},{6,14},{7,15},{8,0},{9,1},... | collective-permute-start | bytes 1179656 | tf_op jit(solution)/shard_map/ppermute | solution.py:213
  62.5 14.4 %collective-permute-start.8 = (f16[768,256]{1,0:T(8,128)(2,1)S(1)}, f16[768,256]{1,0:T(8,128)(2,1)S(1)}, u32[]{:S(2)}, u32[]{:S(2)}) collective-permute-start(f16[768,256]{1,0:T(8,128)(2,1)S(1)} %get-tuple-element.37), channel_id=1, source_target_pairs={{0,2},{1,3},{2,0},{3,1},{4,6},{5,7},{6,4},{7,5},{8,10},{9,11},{10,... | collective-permute-start | bytes 1179656 | tf_op jit(solution)/shard_map/ppermute | solution.py:213
  65.6 27.3 %collective-permute-start.14 = (bf16[384,768]{1,0:T(8,128)(2,1)S(1)}, bf16[384,768]{1,0:T(8,128)(2,1)S(1)}, u32[]{:S(2)}, u32[]{:S(2)}) collective-permute-start(bf16[384,768]{1,0:T(8,128)(2,1)S(1)} %slice.79), channel_id=1, source_target_pairs={{0,16},{16,0},{32,48},{48,32},{64,80},{80,64},{96,112},{112,96},{1... | collective-permute-start | bytes 1769480 | tf_op jit(solution)/shard_map/ppermute | solution.py:218
  93.7 79.6 %all-gather.8.cloned.1.call-start = ((), (), s32[]{:S(2)}) async-start(), calls=%async_computation.2 | async-start | bytes 2949120 | tf_op jit(solution)/shard_map/all_gather | solution.py:316
  94.2 14.1 %collective-permute-start.15 = (bf16[384,768]{1,0:T(8,128)(2,1)S(1)}, bf16[384,768]{1,0:T(8,128)(2,1)S(1)}, u32[]{:S(2)}, u32[]{:S(2)}) collective-permute-start(bf16[384,768]{1,0:T(8,128)(2,1)S(1)} %slice.81), channel_id=1, source_target_pairs={{0,16},{16,0},{32,48},{48,32},{64,80},{80,64},{96,112},{112,96},{1... | collective-permute-start | bytes 1769480 | tf_op jit(solution)/shard_map/ppermute | solution.py:218
  122.8 23.0 %collective-permute-start.22 = (bf16[768,256]{1,0:T(8,128)(2,1)S(1)}, bf16[768,256]{1,0:T(8,128)(2,1)S(1)}, u32[]{:S(2)}, u32[]{:S(2)}) collective-permute-start(bf16[768,256]{1,0:T(8,128)(2,1)S(1)} %collective-permute-done.21.refs_0_), channel_id=1, source_target_pairs={{0,2},{1,3},{2,0},{3,1},{4,6},{5,7},{6,4},{7,5},{8,10},{9,11},{10,... | collective-permute-start | bytes 1179656 | tf_op jit(solution)/shard_map/ppermute | solution.py:213
  135.8 16.7 %collective-permute-start.27 = (bf16[768,256]{1,0:T(8,128)(2,1)S(1)}, bf16[768,256]{1,0:T(8,128)(2,1)S(1)}, u32[]{:S(2)}, u32[]{:S(2)}) collective-permute-start(bf16[768,256]{1,0:T(8,128)(2,1)S(1)} %collective-permute-done.21.refs_0_), channel_id=1, source_target_pairs={{0,8},{1,9},{2,10},{3,11},{4,12},{5,13},{6,14},{7,15},{8,0},{9,1},... | collective-permute-start | bytes 1179656 | tf_op jit(solution)/shard_map/ppermute | solution.py:213
  142.5 18.0 %collective-permute-start.23 = (bf16[768,256]{1,0:T(8,128)(2,1)S(1)}, bf16[768,256]{1,0:T(8,128)(2,1)S(1)}, u32[]{:S(2)}, u32[]{:S(2)}) collective-permute-start(bf16[768,256]{1,0:T(8,128)(2,1)S(1)} %collective-permute-done.21.refs_0_), channel_id=1, source_target_pairs={{0,4},{1,5},{2,6},{3,7},{4,8},{5,9},{6,10},{7,11},{8,12},{9,13},{1... | collective-permute-start | bytes 1179656 | tf_op jit(solution)/shard_map/ppermute | solution.py:213
  143.7 18.5 %collective-permute-start.25 = (bf16[768,256]{1,0:T(8,128)(2,1)S(1)}, bf16[768,256]{1,0:T(8,128)(2,1)S(1)}, u32[]{:S(2)}, u32[]{:S(2)}) collective-permute-start(bf16[768,256]{1,0:T(8,128)(2,1)S(1)} %collective-permute-done.21.refs_0_), channel_id=1, source_target_pairs={{0,12},{1,13},{2,14},{3,15},{4,0},{5,1},{6,2},{7,3},{8,4},{9,5},{1... | collective-permute-start | bytes 1179656 | tf_op jit(solution)/shard_map/ppermute | solution.py:213
  145.7 16.4 %collective-permute-start.29 = (bf16[768,256]{1,0:T(8,128)(2,1)S(1)}, bf16[768,256]{1,0:T(8,128)(2,1)S(1)}, u32[]{:S(2)}, u32[]{:S(2)}) collective-permute-start(bf16[768,256]{1,0:T(8,128)(2,1)S(1)} %collective-permute-done.21.refs_0_), channel_id=1, source_target_pairs={{0,1},{1,0},{2,3},{3,2},{4,5},{5,4},{6,7},{7,6},{8,9},{9,8},{10,11... | collective-permute-start | bytes 1179656 | tf_op jit(solution)/shard_map/ppermute | solution.py:213
  145.8 20.1 %collective-permute-start.24 = (bf16[768,256]{1,0:T(8,128)(2,1)S(1)}, bf16[768,256]{1,0:T(8,128)(2,1)S(1)}, u32[]{:S(2)}, u32[]{:S(2)}) collective-permute-start(bf16[768,256]{1,0:T(8,128)(2,1)S(1)} %collective-permute-done.22.refs_1_), channel_id=1, source_target_pairs={{0,4},{1,5},{2,6},{3,7},{4,8},{5,9},{6,10},{7,11},{8,12},{9,13},{1... | collective-permute-start | bytes 1179656 | tf_op jit(solution)/shard_map/ppermute | solution.py:213
  152.6 13.9 %collective-permute-start.26 = (bf16[768,256]{1,0:T(8,128)(2,1)S(1)}, bf16[768,256]{1,0:T(8,128)(2,1)S(1)}, u32[]{:S(2)}, u32[]{:S(2)}) collective-permute-start(bf16[768,256]{1,0:T(8,128)(2,1)S(1)} %collective-permute-done.22.refs_1_), channel_id=1, source_target_pairs={{0,12},{1,13},{2,14},{3,15},{4,0},{5,1},{6,2},{7,3},{8,4},{9,5},{1... | collective-permute-start | bytes 1179656 | tf_op jit(solution)/shard_map/ppermute | solution.py:213
  160.5 9.3 %collective-permute-start.28 = (bf16[768,256]{1,0:T(8,128)(2,1)S(1)}, bf16[768,256]{1,0:T(8,128)(2,1)S(1)}, u32[]{:S(2)}, u32[]{:S(2)}) collective-permute-start(bf16[768,256]{1,0:T(8,128)(2,1)S(1)} %collective-permute-done.27.refs_6_), channel_id=1, source_target_pairs={{0,2},{1,3},{2,0},{3,1},{4,6},{5,7},{6,4},{7,5},{8,10},{9,11},{10,... | collective-permute-start | bytes 1179656 | tf_op jit(solution)/shard_map/ppermute | solution.py:213
  162.1 7.7 %collective-permute-start.30 = (bf16[768,256]{1,0:T(8,128)(2,1)S(1)}, bf16[768,256]{1,0:T(8,128)(2,1)S(1)}, u32[]{:S(2)}, u32[]{:S(2)}) collective-permute-start(bf16[768,256]{1,0:T(8,128)(2,1)S(1)} %collective-permute-done.22.refs_1_), channel_id=1, source_target_pairs={{0,1},{1,0},{2,3},{3,2},{4,5},{5,4},{6,7},{7,6},{8,9},{9,8},{10,11... | collective-permute-start | bytes 1179656 | tf_op jit(solution)/shard_map/ppermute | solution.py:213
  162.2 8.2 %collective-permute-start.31 = (bf16[768,256]{1,0:T(8,128)(2,1)S(1)}, bf16[768,256]{1,0:T(8,128)(2,1)S(1)}, u32[]{:S(2)}, u32[]{:S(2)}) collective-permute-start(bf16[768,256]{1,0:T(8,128)(2,1)S(1)} %collective-permute-done.23.refs_2_), channel_id=1, source_target_pairs={{0,1},{1,0},{2,3},{3,2},{4,5},{5,4},{6,7},{7,6},{8,9},{9,8},{10,11... | collective-permute-start | bytes 1179656 | tf_op jit(solution)/shard_map/ppermute | solution.py:213
  165.8 6.6 %collective-permute-start.35 = (bf16[768,256]{1,0:T(8,128)(2,1)S(1)}, bf16[768,256]{1,0:T(8,128)(2,1)}, u32[]{:S(2)}, u32[]{:S(2)}) collective-permute-start(bf16[768,256]{1,0:T(8,128)(2,1)S(1)} %collective-permute-done.27.refs_6_), channel_id=1, source_target_pairs={{0,1},{1,0},{2,3},{3,2},{4,5},{5,4},{6,7},{7,6},{8,9},{9,8},{10,11... | collective-permute-start | bytes 1179656 | tf_op jit(solution)/shard_map/ppermute | solution.py:213
  186.9 22.1 %collective-permute-start.37 = (bf16[768,512]{1,0:T(8,128)(2,1)}, bf16[768,512]{1,0:T(8,128)(2,1)S(1)}, u32[]{:S(2)}, u32[]{:S(2)}) collective-permute-start(bf16[768,512]{1,0:T(8,128)(2,1)} %get-tuple-element.31), channel_id=1, source_target_pairs={{0,32},{16,48},{32,64},{48,80},{64,96},{80,112},{96,0},{112,16},{1... | collective-permute-start | bytes 2359304 | tf_op jit(solution)/shard_map/ppermute | solution.py:218
  187.2 21.9 %collective-permute-start.38 = (bf16[768,512]{1,0:T(8,128)(2,1)}, bf16[768,512]{1,0:T(8,128)(2,1)S(1)}, u32[]{:S(2)}, u32[]{:S(2)}) collective-permute-start(bf16[768,512]{1,0:T(8,128)(2,1)} %get-tuple-element.31), channel_id=1, source_target_pairs={{0,96},{16,112},{32,0},{48,16},{64,32},{80,48},{96,64},{112,80},{1... | collective-permute-start | bytes 2359304 | tf_op jit(solution)/shard_map/ppermute | solution.py:218
  190.8 22.3 %collective-permute-start.39 = (bf16[768,512]{1,0:T(8,128)(2,1)}, bf16[768,512]{1,0:T(8,128)(2,1)S(1)}, u32[]{:S(2)}, u32[]{:S(2)}) collective-permute-start(bf16[768,512]{1,0:T(8,128)(2,1)} %get-tuple-element.31), channel_id=1, source_target_pairs={{0,16},{16,0},{32,48},{48,32},{64,80},{80,64},{96,112},{112,96},{1... | collective-permute-start | bytes 2359304 | tf_op jit(solution)/shard_map/ppermute | solution.py:218
  209.0 13.3 %collective-permute-start.40 = (bf16[384,512]{1,0:T(8,128)(2,1)S(1)}, bf16[384,512]{1,0:T(8,128)(2,1)S(1)}, u32[]{:S(2)}, u32[]{:S(2)}) collective-permute-start(bf16[384,512]{1,0:T(8,128)(2,1)S(1)} %slice.100), channel_id=1, source_target_pairs={{0,32},{16,48},{32,64},{48,80},{64,96},{80,112},{96,0},{112,16},{1... | collective-permute-start | bytes 1179656 | tf_op jit(solution)/shard_map/ppermute | solution.py:218
  209.9 13.1 %collective-permute-start.41 = (bf16[384,512]{1,0:T(8,128)(2,1)}, bf16[384,512]{1,0:T(8,128)(2,1)S(1)}, u32[]{:S(2)}, u32[]{:S(2)}) collective-permute-start(bf16[384,512]{1,0:T(8,128)(2,1)} %slice.101), channel_id=1, source_target_pairs={{0,96},{16,112},{32,0},{48,16},{64,32},{80,48},{96,64},{112,80},{1... | collective-permute-start | bytes 1179656 | tf_op jit(solution)/shard_map/ppermute | solution.py:218
  213.1 24.9 %collective-permute-start.42 = (bf16[768,512]{1,0:T(8,128)(2,1)S(1)}, bf16[768,512]{1,0:T(8,128)(2,1)S(1)}, u32[]{:S(2)}, u32[]{:S(2)}) collective-permute-start(bf16[768,512]{1,0:T(8,128)(2,1)S(1)} %collective-permute-done.39), channel_id=1, source_target_pairs={{0,32},{16,48},{32,64},{48,80},{64,96},{80,112},{96,0},{112,16},{1... | collective-permute-start | bytes 2359304 | tf_op jit(solution)/shard_map/ppermute | solution.py:218
  215.2 23.7 %collective-permute-start.43 = (bf16[768,512]{1,0:T(8,128)(2,1)S(1)}, bf16[768,512]{1,0:T(8,128)(2,1)S(1)}, u32[]{:S(2)}, u32[]{:S(2)}) collective-permute-start(bf16[768,512]{1,0:T(8,128)(2,1)S(1)} %collective-permute-done.39), channel_id=1, source_target_pairs={{0,96},{16,112},{32,0},{48,16},{64,32},{80,48},{96,64},{112,80},{1... | collective-permute-start | bytes 2359304 | tf_op jit(solution)/shard_map/ppermute | solution.py:218
  223.0 16.8 %collective-permute-start.44 = (bf16[768,512]{1,0:T(8,128)(2,1)S(1)}, bf16[768,512]{1,0:T(8,128)(2,1)S(1)}, u32[]{:S(2)}, u32[]{:S(2)}) collective-permute-start(bf16[768,512]{1,0:T(8,128)(2,1)S(1)} %pad_maximum_fusion), channel_id=1, source_target_pairs={{0,16},{16,0},{32,48},{48,32},{64,80},{80,64},{96,112},{112,96},{1... | collective-permute-start | bytes 2359304 | tf_op jit(solution)/shard_map/ppermute | solution.py:218
  (40 other events, 408.0 us)
Sparse Core Ops, SparseCore 0:
  15.6 55.4 all-gather.3
  93.9 33.9 all-gather.5
  129.6 40.2 all-gather.7

commit v8 on v7

--- a/solution.py
+++ b/solution.py
@@ -334,16 +334,17 @@
         tuple(first[offset].astype(f16) for offset in ORDER[0]) + (rows,)
     )
     far_across = send(far_across, 0, 1)
-    far_across, rows_now = lax.optimization_barrier((far_across, rows_now))
-    part = slots * span // 2
-    first_across = row_major(to_group(rows_now[:part], 0, 1))
     up_across = send(up_across, 1, 0)
     down_across = send(down_across, 3, 0)
     second = chip_sums(rows_now, ORDER[1])
     up = send(second[1, 0], 1, 0).astype(f32)
     down = send(second[3, 0], 3, 0).astype(f32)
     far = send(second[2, 0] + far_across.astype(f32), 2, 0).astype(f32)
-    across = send(second[0, 1] + up_across.astype(f32) + down_across.astype(f32), 0, 1).astype(f32)
+    second_across = (second[0, 1] + up_across.astype(f32) + down_across.astype(f32)).astype(f16)
+    second_across, rows_now = lax.optimization_barrier((second_across, rows_now))
+    across = send(second_across, 0, 1).astype(f32)
+    part = slots * span // 2
+    first_across = row_major(to_group(rows_now[:part], 0, 1))
     merged = (second[0, 0] + up + down + far + across) * (1.0 / SEND)
     merged = merged.reshape(slots, span, wide)
     squares = sum_over_tr(jnp.sum(merged * merged, axis=2))

time: 248 us -> 236 us (0.952)
  starting transfers between devices: 70.8 us -> 64.5 us
  waiting for transfers between devices: 86.7 us -> 80.5 us
    ppermute x34, starting transfers between devices: 57 us -> 50.5 us  [to_chip(): return lax.ppermute(value, 'tr', pairs)]
    ppermute x34, waiting for transfers between devices: 53.4 us -> 47.3 us  [to_chip(): return lax.ppermute(value, 'tr', pairs)]
    unnamed x49 -> x51, local copies, waits for them, and re-layouts: 15.8 us -> 13.1 us
  transfers between devices with their start and end apart: 48 -> 48, of which waited for: 23 -> 24; matrix products, arithmetic and copies ran while one was open for 8% -> 9% of each run, Pallas kernels for 9% -> 9%
where the time goes in v8:
time: 236 us; the launch traced here: 235 us
  waiting for transfers between devices  80.5 us (34%)
  starting transfers between devices  64.5 us (27%)
  Pallas kernels  38.5 us (16%)
  local copies, waits for them, and re-layouts  28.3 us (12%)
  between operations  14.4 us (6%)
  other arithmetic  8.81 us (4%)
    ppermute x34, starting transfers between devices, to_chip(): return lax.ppermute(value, 'tr', pairs)  50.5 us
    ppermute x34, waiting for transfers between devices, to_chip(): return lax.ppermute(value, 'tr', pairs)  47.3 us
    ppermute x10, waiting for transfers between devices, to_group(): return lax.ppermute(value, 'rep', pairs)  33.2 us
    pallas_call x4, Pallas kernels, products(): pl.pallas_call(product_kernel, grid_spec=pltpu.PrefetchScalarGridSpec(num...  13.7 us
    pallas_call x1, Pallas kernels, gradient(): pl.pallas_call(gradient_kernel, grid_spec=pltpu.PrefetchScalarGridSpec(nu...  13.5 us
    ppermute x10, starting transfers between devices, to_group(): return lax.ppermute(value, 'rep', pairs)  13.2 us
    unnamed x51, local copies, waits for them, and re-layouts  13.1 us
    pallas_call x1, Pallas kernels, attention(): pl.pallas_call(attention_kernel, grid=(count // slots,), in_specs=[scalar...  11.3 us
  transfers between devices with their start and end apart: 48, of which 24 were waited for; matrix products, arithmetic and copies ran while one was open for 9% of the time, Pallas kernels for 9%

profile of v8, /device:TPU:0, one launch (start us, length us, event | category | flops | bytes accessed | tf_op | source)
XLA Modules:
  0.0 235.1 jit_solution(8541886101631023316)
XLA Ops:
  7.3 2.3 copy.16
  10.0 3.1 %copy-done = bf16[3,256,4096]{2,1,0:T(8,128)(2,1)S(1)} copy-done((bf16[3,256,4096]{2,1,0:T(8,128)(2,1)S(1)}, bf16[3,256,4096]{2,1,0:T(8,128)(2,1)}, u32[]{:S(2)}) %copy-start) | copy-done | bytes 6291480
  13.1 3.4 %shard_map.78 = f32[3,768,256]{2,1,0:T(8,128)} custom-call(s32[3]{0:T(128)S(1)} %pad_add_fusion.1.blocks_ref, bf16[768,768]{1,0:T(8,128)(2,1)S(1)} %bitcast.85, bf16[768,4096]{1,0:T(8,128)(2,1)S(1)} %bitcast.79), custom_call_target="tpu_custom_call" | custom-call | flops 905969664 | bytes 4718592 | tf_op jit(solution)/shard_map/pallas_call | solution.py:264
  16.9 2.8 %copy-done.1 = bf16[3,256,4096]{2,1,0:T(8,128)(2,1)S(1)} copy-done((bf16[3,256,4096]{2,1,0:T(8,128)(2,1)S(1)}, bf16[3,256,4096]{2,1,0:T(8,128)(2,1)}, u32[]{:S(2)}) %copy-start.1) | copy-done | bytes 6291480
  20.9 2.2 shard_map.77
  23.2 3.0 %fusion.28 = (f16[768,256]{1,0:T(8,128)(2,1)}, f16[768,256]{1,0:T(8,128)(2,1)}, f16[768,256]{1,0:T(8,128)(2,1)}) fusion(f32[3,768,256]{2,1,0:T(8,128)} %collective-permute-done, f32[3,768,256]{2,1,0:T(8,128)S(1)} %shard_map.77), kind=kLoop, calls=%fused_computation.39 | loop fusion | flops 1769472 | bytes 5898240 | tf_op jit(solution)/shard_map/convert_element_type | solution.py:334
  26.1 4.8 %shard_map.80 = f32[5,768,256]{2,1,0:T(8,128)} custom-call(s32[5]{0:T(128)S(1)} %stack.111.blocks_ref, bf16[768,768]{1,0:T(8,128)(2,1)S(1)} %bitcast.88, bf16[768,4096]{1,0:T(8,128)(2,1)S(1)} %bitcast.83), custom_call_target="tpu_custom_call" | custom-call | flops 1509949440 | bytes 7077888 | tf_op jit(solution)/shard_map/pallas_call | solution.py:264
  31.5 3.1 %collective-permute-start.4 = (f16[768,256]{1,0:T(8,128)(2,1)}, f16[768,256]{1,0:T(8,128)(2,1)S(1)}, u32[]{:S(2)}, u32[]{:S(2)}) collective-permute-start(f16[768,256]{1,0:T(8,128)(2,1)} %get-tuple-element.18), channel_id=1, source_target_pairs={{0,2},{1,3},{2,0},{3,1},{4,6},{5,7},{6,4},{7,5},{8,10},{9,11},{10,... | collective-permute-start | bytes 1179656 | tf_op jit(solution)/shard_map/ppermute | solution.py:213
  37.9 2.9 %copy-done.2 = bf16[3,256,4096]{2,1,0:T(8,128)(2,1)S(1)} copy-done((bf16[3,256,4096]{2,1,0:T(8,128)(2,1)S(1)}, bf16[3,256,4096]{2,1,0:T(8,128)(2,1)}, u32[]{:S(2)}) %copy-start.2) | copy-done | bytes 6291480
  40.8 3.3 %shard_map.79 = f32[5,768,256]{2,1,0:T(8,128)S(1)} custom-call(s32[5]{0:T(128)S(1)} %stack.97.blocks_ref, bf16[768,768]{1,0:T(8,128)(2,1)S(1)} %bitcast.89, bf16[768,4096]{1,0:T(8,128)(2,1)S(1)} %bitcast.84), custom_call_target="tpu_custom_call" | custom-call | flops 1509949440 | bytes 7077888 | tf_op jit(solution)/shard_map/pallas_call | solution.py:264
  46.2 2.9 %collective-permute-start.3 = (f16[768,256]{1,0:T(8,128)(2,1)S(1)}, f16[768,256]{1,0:T(8,128)(2,1)S(1)}, u32[]{:S(2)}, u32[]{:S(2)}) collective-permute-start(f16[768,256]{1,0:T(8,128)(2,1)S(1)} %get-tuple-element.35), channel_id=1, source_target_pairs={{0,12},{1,13},{2,14},{3,15},{4,0},{5,1},{6,2},{7,3},{8,4},{9,5},{1... | collective-permute-start | bytes 1179656 | tf_op jit(solution)/shard_map/ppermute | solution.py:213
  54.6 4.6 %collective-permute-done.2 = f16[768,256]{1,0:T(8,128)(2,1)S(1)} collective-permute-done((f16[768,256]{1,0:T(8,128)(2,1)S(1)}, f16[768,256]{1,0:T(8,128)(2,1)S(1)}, u32[]{:S(2)}, u32[]{:S(2)}) %collective-permute-start.2) | collective-permute-done | bytes 393248 | tf_op jit(solution)/shard_map/ppermute | solution.py:213
  59.2 5.8 %collective-permute-done.3 = f16[768,256]{1,0:T(8,128)(2,1)S(1)} collective-permute-done((f16[768,256]{1,0:T(8,128)(2,1)S(1)}, f16[768,256]{1,0:T(8,128)(2,1)S(1)}, u32[]{:S(2)}, u32[]{:S(2)}) %collective-permute-start.3) | collective-permute-done | bytes 393248 | tf_op jit(solution)/shard_map/ppermute | solution.py:213
  69.7 3.4 %collective-permute-start.11 = (f32[8,96]{1,0:T(8,128)S(1)}, f32[8,96]{1,0:T(8,128)S(1)}, u32[]{:S(2)}, u32[]{:S(2)}) collective-permute-start(f32[8,96]{1,0:T(8,128)S(1)} %add.444), channel_id=1, source_target_pairs={{0,8},{1,9},{2,10},{3,11},{4,12},{5,13},{6,14},{7,15},{8,0},{9,1},... | collective-permute-start | bytes 9224 | tf_op jit(solution)/shard_map/ppermute | solution.py:213
  77.1 4.7 %collective-permute-done.13 = f32[8,96]{1,0:T(8,128)S(1)} collective-permute-done((f32[8,96]{1,0:T(8,128)S(1)}, f32[8,96]{1,0:T(8,128)S(1)}, u32[]{:S(2)}, u32[]{:S(2)}) %collective-permute-start.13) | collective-permute-done | bytes 3104 | tf_op jit(solution)/shard_map/ppermute | solution.py:213
  84.9 11.3 %shard_map.81 = (f32[8,96,256]{2,1,0:T(8,128)S(1)}, f32[8,1,96]{2,1,0:T(1,128)S(1)}) custom-call(s32[8]{0:T(128)S(1)} %dynamic_slice.6.lens_ref, f32[8]{0:T(128)S(1)} %convert_divide_fusion.weights_ref, f32[2]{0:T(128)S(1)} %copy-done.7, f32[8,96,256]{2,1,0:T(8,128)S(1)} %bitcast.92, f32[8,1,96]{2,1,0:T(1,128)S(1)} %bitcast.94, f32[1,256]{1,0:T(1,128)S(1)} %bitcast.97, ...), custom_call_target="tpu_custom_call" | custom-call | flops 2000000000 | bytes 3000000 | tf_op jit(solution)/shard_map/pallas_call | solution.py:116
  98.3 2.9 %collective-permute-start.18 = (f32[8,96]{1,0:T(8,128)S(1)}, f32[8,96]{1,0:T(8,128)S(1)}, u32[]{:S(2)}, u32[]{:S(2)}) collective-permute-start(f32[8,96]{1,0:T(8,128)S(1)} %add.454), channel_id=1, source_target_pairs={{0,8},{1,9},{2,10},{3,11},{4,12},{5,13},{6,14},{7,15},{8,0},{9,1},... | collective-permute-start | bytes 9224 | tf_op jit(solution)/shard_map/ppermute | solution.py:213
  106.6 3.3 %collective-permute-done.20 = f32[8,96]{1,0:T(8,128)S(1)} collective-permute-done((f32[8,96]{1,0:T(8,128)S(1)}, f32[8,96]{1,0:T(8,128)S(1)}, u32[]{:S(2)}, u32[]{:S(2)}) %collective-permute-start.20) | collective-permute-done | bytes 3104 | tf_op jit(solution)/shard_map/ppermute | solution.py:213
  110.9 12.1 %collective-permute-start.22 = (bf16[768,256]{1,0:T(8,128)(2,1)S(1)}, bf16[768,256]{1,0:T(8,128)(2,1)S(1)}, u32[]{:S(2)}, u32[]{:S(2)}) collective-permute-start(bf16[768,256]{1,0:T(8,128)(2,1)S(1)} %collective-permute-done.21.refs_0_), channel_id=1, source_target_pairs={{0,2},{1,3},{2,0},{3,1},{4,6},{5,7},{6,4},{7,5},{8,10},{9,11},{10,... | collective-permute-start | bytes 1179656 | tf_op jit(solution)/shard_map/ppermute | solution.py:213
  123.0 6.7 %collective-permute-start.27 = (bf16[768,256]{1,0:T(8,128)(2,1)S(1)}, bf16[768,256]{1,0:T(8,128)(2,1)S(1)}, u32[]{:S(2)}, u32[]{:S(2)}) collective-permute-start(bf16[768,256]{1,0:T(8,128)(2,1)S(1)} %collective-permute-done.21.refs_0_), channel_id=1, source_target_pairs={{0,8},{1,9},{2,10},{3,11},{4,12},{5,13},{6,14},{7,15},{8,0},{9,1},... | collective-permute-start | bytes 1179656 | tf_op jit(solution)/shard_map/ppermute | solution.py:213
  133.0 6.7 %collective-permute-done.27.refs_6_ = bf16[768,256]{1,0:T(8,128)(2,1)S(1)} collective-permute-done((bf16[768,256]{1,0:T(8,128)(2,1)S(1)}, bf16[768,256]{1,0:T(8,128)(2,1)S(1)}, u32[]{:S(2)}, u32[]{:S(2)}) %collective-permute-start.27) | collective-permute-done | bytes 393248 | tf_op jit(solution)/shard_map/ppermute | solution.py:213
  139.8 3.8 %collective-permute-start.26 = (bf16[768,256]{1,0:T(8,128)(2,1)S(1)}, bf16[768,256]{1,0:T(8,128)(2,1)S(1)}, u32[]{:S(2)}, u32[]{:S(2)}) collective-permute-start(bf16[768,256]{1,0:T(8,128)(2,1)S(1)} %collective-permute-done.22.refs_1_), channel_id=1, source_target_pairs={{0,12},{1,13},{2,14},{3,15},{4,0},{5,1},{6,2},{7,3},{8,4},{9,5},{1... | collective-permute-start | bytes 1179656 | tf_op jit(solution)/shard_map/ppermute | solution.py:213
  143.6 4.1 %collective-permute-done.23.refs_2_ = bf16[768,256]{1,0:T(8,128)(2,1)S(1)} collective-permute-done((bf16[768,256]{1,0:T(8,128)(2,1)S(1)}, bf16[768,256]{1,0:T(8,128)(2,1)S(1)}, u32[]{:S(2)}, u32[]{:S(2)}) %collective-permute-start.23) | collective-permute-done | bytes 393248 | tf_op jit(solution)/shard_map/ppermute | solution.py:213
  149.9 3.2 %collective-permute-done.24.refs_3_ = bf16[768,256]{1,0:T(8,128)(2,1)S(1)} collective-permute-done((bf16[768,256]{1,0:T(8,128)(2,1)S(1)}, bf16[768,256]{1,0:T(8,128)(2,1)S(1)}, u32[]{:S(2)}, u32[]{:S(2)}) %collective-permute-start.24) | collective-permute-done | bytes 393248 | tf_op jit(solution)/shard_map/ppermute | solution.py:213
  153.7 3.3 %collective-permute-done.28.refs_7_ = bf16[768,256]{1,0:T(8,128)(2,1)S(1)} collective-permute-done((bf16[768,256]{1,0:T(8,128)(2,1)S(1)}, bf16[768,256]{1,0:T(8,128)(2,1)S(1)}, u32[]{:S(2)}, u32[]{:S(2)}) %collective-permute-start.28) | collective-permute-done | bytes 393248 | tf_op jit(solution)/shard_map/ppermute | solution.py:213
  160.6 13.5 %shard_map.82 = (f32[768,512]{1,0:T(8,128)}, bf16[768,512]{1,0:T(8,128)(2,1)}) custom-call(s32[7]{0:T(128)} %stack.91.places_ref, bf16[3072,768]{1,0:T(8,128)(2,1)} %all-gather.4.cloned.1.call-done.here_ref, bf16[1536,768]{1,0:T(8,128)(2,1)} %all-gather.6.cloned.1.call-done.first_ref, bf16[1536,768]{1,0:T(8,128)(2,1)} %all-gather.8.cloned.1.call-done.last_ref, ...), custom_call_target="tpu_custom_call" | custom-call | flops 4831838208 | bytes 20971520 | tf_op jit(solution)/shard_map/pallas_call | solution.py:171
  174.8 3.8 %collective-permute-start.38 = (bf16[768,512]{1,0:T(8,128)(2,1)}, bf16[768,512]{1,0:T(8,128)(2,1)S(1)}, u32[]{:S(2)}, u32[]{:S(2)}) collective-permute-start(bf16[768,512]{1,0:T(8,128)(2,1)} %get-tuple-element.31), channel_id=1, source_target_pairs={{0,96},{16,112},{32,0},{48,16},{64,32},{80,48},{96,64},{112,80},{1... | collective-permute-start | bytes 2359304 | tf_op jit(solution)/shard_map/ppermute | solution.py:218
  178.6 18.1 %collective-permute-done.37 = bf16[768,512]{1,0:T(8,128)(2,1)S(1)} collective-permute-done((bf16[768,512]{1,0:T(8,128)(2,1)}, bf16[768,512]{1,0:T(8,128)(2,1)S(1)}, u32[]{:S(2)}, u32[]{:S(2)}) %collective-permute-start.37) | collective-permute-done | bytes 786464 | tf_op jit(solution)/shard_map/ppermute | solution.py:218
  197.7 3.2 %collective-permute-start.41 = (bf16[384,512]{1,0:T(8,128)(2,1)}, bf16[384,512]{1,0:T(8,128)(2,1)S(1)}, u32[]{:S(2)}, u32[]{:S(2)}) collective-permute-start(bf16[384,512]{1,0:T(8,128)(2,1)} %slice.101), channel_id=1, source_target_pairs={{0,96},{16,112},{32,0},{48,16},{64,32},{80,48},{96,64},{112,80},{1... | collective-permute-start | bytes 1179656 | tf_op jit(solution)/shard_map/ppermute | solution.py:218
  203.0 3.2 %collective-permute-start.43 = (bf16[768,512]{1,0:T(8,128)(2,1)S(1)}, bf16[768,512]{1,0:T(8,128)(2,1)S(1)}, u32[]{:S(2)}, u32[]{:S(2)}) collective-permute-start(bf16[768,512]{1,0:T(8,128)(2,1)S(1)} %collective-permute-done.39), channel_id=1, source_target_pairs={{0,96},{16,112},{32,0},{48,16},{64,32},{80,48},{96,64},{112,80},{1... | collective-permute-start | bytes 2359304 | tf_op jit(solution)/shard_map/ppermute | solution.py:218
  206.2 3.9 %collective-permute-done.40 = bf16[384,512]{1,0:T(8,128)(2,1)S(1)} collective-permute-done((bf16[384,512]{1,0:T(8,128)(2,1)S(1)}, bf16[384,512]{1,0:T(8,128)(2,1)S(1)}, u32[]{:S(2)}, u32[]{:S(2)}) %collective-permute-start.40) | collective-permute-done | bytes 393248 | tf_op jit(solution)/shard_map/ppermute | solution.py:218
  215.3 10.5 %collective-permute-done.42 = bf16[768,512]{1,0:T(8,128)(2,1)S(1)} collective-permute-done((bf16[768,512]{1,0:T(8,128)(2,1)S(1)}, bf16[768,512]{1,0:T(8,128)(2,1)S(1)}, u32[]{:S(2)}, u32[]{:S(2)}) %collective-permute-start.42) | collective-permute-done | bytes 786464 | tf_op jit(solution)/shard_map/ppermute | solution.py:218
  (164 shorter events, 54.8 us)
Async XLA Ops:
  7.2 152.5 %all-gather.4.cloned.1.call-start = ((), (), s32[]{:S(2)}) async-start(), calls=%async_computation | async-start | bytes 5898240 | tf_op jit(solution)/shard_map/all_gather | solution.py:316
  16.6 143.9 %all-gather.6.cloned.1.call-start = ((), (), s32[]{:S(2)}) async-start(), calls=%async_computation.1 | async-start | bytes 2949120 | tf_op jit(solution)/shard_map/all_gather | solution.py:316
  30.9 13.1 %collective-permute-start.1 = (f32[5,768,256]{2,1,0:T(8,128)}, f32[5,768,256]{2,1,0:T(8,128)}, u32[]{:S(2)}, u32[]{:S(2)}) collective-permute-start(f32[5,768,256]{2,1,0:T(8,128)} %shard_map.80), channel_id=1, source_target_pairs={{0,1},{1,0},{2,3},{3,2},{4,5},{5,4},{6,7},{7,6},{8,9},{9,8},{10,11... | collective-permute-start | bytes 11796488 | tf_op jit(solution)/shard_map/ppermute | solution.py:213
  31.5 17.6 %collective-permute-start.4 = (f16[768,256]{1,0:T(8,128)(2,1)}, f16[768,256]{1,0:T(8,128)(2,1)S(1)}, u32[]{:S(2)}, u32[]{:S(2)}) collective-permute-start(f16[768,256]{1,0:T(8,128)(2,1)} %get-tuple-element.18), channel_id=1, source_target_pairs={{0,2},{1,3},{2,0},{3,1},{4,6},{5,7},{6,4},{7,5},{8,10},{9,11},{10,... | collective-permute-start | bytes 1179656 | tf_op jit(solution)/shard_map/ppermute | solution.py:213
  34.6 14.5 %collective-permute-start.6 = (f16[768,256]{1,0:T(8,128)(2,1)}, f16[768,256]{1,0:T(8,128)(2,1)S(1)}, u32[]{:S(2)}, u32[]{:S(2)}) collective-permute-start(f16[768,256]{1,0:T(8,128)(2,1)} %get-tuple-element.19), channel_id=1, source_target_pairs={{0,4},{1,5},{2,6},{3,7},{4,8},{5,9},{6,10},{7,11},{8,12},{9,13},{1... | collective-permute-start | bytes 1179656 | tf_op jit(solution)/shard_map/ppermute | solution.py:213
  36.2 12.9 %collective-permute-start.7 = (f16[768,256]{1,0:T(8,128)(2,1)}, f16[768,256]{1,0:T(8,128)(2,1)S(1)}, u32[]{:S(2)}, u32[]{:S(2)}) collective-permute-start(f16[768,256]{1,0:T(8,128)(2,1)} %get-tuple-element.20), channel_id=1, source_target_pairs={{0,12},{1,13},{2,14},{3,15},{4,0},{5,1},{6,2},{7,3},{8,4},{9,5},{1... | collective-permute-start | bytes 1179656 | tf_op jit(solution)/shard_map/ppermute | solution.py:213
  45.8 13.4 %collective-permute-start.2 = (f16[768,256]{1,0:T(8,128)(2,1)S(1)}, f16[768,256]{1,0:T(8,128)(2,1)S(1)}, u32[]{:S(2)}, u32[]{:S(2)}) collective-permute-start(f16[768,256]{1,0:T(8,128)(2,1)S(1)} %get-tuple-element.34), channel_id=1, source_target_pairs={{0,4},{1,5},{2,6},{3,7},{4,8},{5,9},{6,10},{7,11},{8,12},{9,13},{1... | collective-permute-start | bytes 1179656 | tf_op jit(solution)/shard_map/ppermute | solution.py:213
  46.2 18.8 %collective-permute-start.3 = (f16[768,256]{1,0:T(8,128)(2,1)S(1)}, f16[768,256]{1,0:T(8,128)(2,1)S(1)}, u32[]{:S(2)}, u32[]{:S(2)}) collective-permute-start(f16[768,256]{1,0:T(8,128)(2,1)S(1)} %get-tuple-element.35), channel_id=1, source_target_pairs={{0,12},{1,13},{2,14},{3,15},{4,0},{5,1},{6,2},{7,3},{8,4},{9,5},{1... | collective-permute-start | bytes 1179656 | tf_op jit(solution)/shard_map/ppermute | solution.py:213
  51.0 14.0 %collective-permute-start.8 = (f16[768,256]{1,0:T(8,128)(2,1)S(1)}, f16[768,256]{1,0:T(8,128)(2,1)S(1)}, u32[]{:S(2)}, u32[]{:S(2)}) collective-permute-start(f16[768,256]{1,0:T(8,128)(2,1)S(1)} %get-tuple-element.21), channel_id=1, source_target_pairs={{0,2},{1,3},{2,0},{3,1},{4,6},{5,7},{6,4},{7,5},{8,10},{9,11},{10,... | collective-permute-start | bytes 1179656 | tf_op jit(solution)/shard_map/ppermute | solution.py:213
  51.4 14.4 %collective-permute-start.5 = (f16[768,256]{1,0:T(8,128)(2,1)S(1)}, f16[768,256]{1,0:T(8,128)(2,1)S(1)}, u32[]{:S(2)}, u32[]{:S(2)}) collective-permute-start(f16[768,256]{1,0:T(8,128)(2,1)S(1)} %get-tuple-element.36), channel_id=1, source_target_pairs={{0,8},{1,9},{2,10},{3,11},{4,12},{5,13},{6,14},{7,15},{8,0},{9,1},... | collective-permute-start | bytes 1179656 | tf_op jit(solution)/shard_map/ppermute | solution.py:213
  53.4 28.4 %collective-permute-start.14 = (bf16[384,768]{1,0:T(8,128)(2,1)}, bf16[384,768]{1,0:T(8,128)(2,1)S(1)}, u32[]{:S(2)}, u32[]{:S(2)}) collective-permute-start(bf16[384,768]{1,0:T(8,128)(2,1)} %slice.79), channel_id=1, source_target_pairs={{0,16},{16,0},{32,48},{48,32},{64,80},{80,64},{96,112},{112,96},{1... | collective-permute-start | bytes 1769480 | tf_op jit(solution)/shard_map/ppermute | solution.py:218
  82.6 77.9 %all-gather.8.cloned.1.call-start = ((), (), s32[]{:S(2)}) async-start(), calls=%async_computation.2 | async-start | bytes 2949120 | tf_op jit(solution)/shard_map/all_gather | solution.py:316
  83.1 13.2 %collective-permute-start.15 = (bf16[384,768]{1,0:T(8,128)(2,1)S(1)}, bf16[384,768]{1,0:T(8,128)(2,1)S(1)}, u32[]{:S(2)}, u32[]{:S(2)}) collective-permute-start(bf16[384,768]{1,0:T(8,128)(2,1)S(1)} %slice.81), channel_id=1, source_target_pairs={{0,16},{16,0},{32,48},{48,32},{64,80},{80,64},{96,112},{112,96},{1... | collective-permute-start | bytes 1769480 | tf_op jit(solution)/shard_map/ppermute | solution.py:218
  110.9 22.0 %collective-permute-start.22 = (bf16[768,256]{1,0:T(8,128)(2,1)S(1)}, bf16[768,256]{1,0:T(8,128)(2,1)S(1)}, u32[]{:S(2)}, u32[]{:S(2)}) collective-permute-start(bf16[768,256]{1,0:T(8,128)(2,1)S(1)} %collective-permute-done.21.refs_0_), channel_id=1, source_target_pairs={{0,2},{1,3},{2,0},{3,1},{4,6},{5,7},{6,4},{7,5},{8,10},{9,11},{10,... | collective-permute-start | bytes 1179656 | tf_op jit(solution)/shard_map/ppermute | solution.py:213
  123.0 16.7 %collective-permute-start.27 = (bf16[768,256]{1,0:T(8,128)(2,1)S(1)}, bf16[768,256]{1,0:T(8,128)(2,1)S(1)}, u32[]{:S(2)}, u32[]{:S(2)}) collective-permute-start(bf16[768,256]{1,0:T(8,128)(2,1)S(1)} %collective-permute-done.21.refs_0_), channel_id=1, source_target_pairs={{0,8},{1,9},{2,10},{3,11},{4,12},{5,13},{6,14},{7,15},{8,0},{9,1},... | collective-permute-start | bytes 1179656 | tf_op jit(solution)/shard_map/ppermute | solution.py:213
  129.7 18.0 %collective-permute-start.23 = (bf16[768,256]{1,0:T(8,128)(2,1)S(1)}, bf16[768,256]{1,0:T(8,128)(2,1)S(1)}, u32[]{:S(2)}, u32[]{:S(2)}) collective-permute-start(bf16[768,256]{1,0:T(8,128)(2,1)S(1)} %collective-permute-done.21.refs_0_), channel_id=1, source_target_pairs={{0,4},{1,5},{2,6},{3,7},{4,8},{5,9},{6,10},{7,11},{8,12},{9,13},{1... | collective-permute-start | bytes 1179656 | tf_op jit(solution)/shard_map/ppermute | solution.py:213
  130.9 18.5 %collective-permute-start.25 = (bf16[768,256]{1,0:T(8,128)(2,1)S(1)}, bf16[768,256]{1,0:T(8,128)(2,1)S(1)}, u32[]{:S(2)}, u32[]{:S(2)}) collective-permute-start(bf16[768,256]{1,0:T(8,128)(2,1)S(1)} %collective-permute-done.21.refs_0_), channel_id=1, source_target_pairs={{0,12},{1,13},{2,14},{3,15},{4,0},{5,1},{6,2},{7,3},{8,4},{9,5},{1... | collective-permute-start | bytes 1179656 | tf_op jit(solution)/shard_map/ppermute | solution.py:213
  132.9 16.4 %collective-permute-start.29 = (bf16[768,256]{1,0:T(8,128)(2,1)S(1)}, bf16[768,256]{1,0:T(8,128)(2,1)S(1)}, u32[]{:S(2)}, u32[]{:S(2)}) collective-permute-start(bf16[768,256]{1,0:T(8,128)(2,1)S(1)} %collective-permute-done.21.refs_0_), channel_id=1, source_target_pairs={{0,1},{1,0},{2,3},{3,2},{4,5},{5,4},{6,7},{7,6},{8,9},{9,8},{10,11... | collective-permute-start | bytes 1179656 | tf_op jit(solution)/shard_map/ppermute | solution.py:213
  132.9 20.1 %collective-permute-start.24 = (bf16[768,256]{1,0:T(8,128)(2,1)S(1)}, bf16[768,256]{1,0:T(8,128)(2,1)S(1)}, u32[]{:S(2)}, u32[]{:S(2)}) collective-permute-start(bf16[768,256]{1,0:T(8,128)(2,1)S(1)} %collective-permute-done.22.refs_1_), channel_id=1, source_target_pairs={{0,4},{1,5},{2,6},{3,7},{4,8},{5,9},{6,10},{7,11},{8,12},{9,13},{1... | collective-permute-start | bytes 1179656 | tf_op jit(solution)/shard_map/ppermute | solution.py:213
  139.8 13.9 %collective-permute-start.26 = (bf16[768,256]{1,0:T(8,128)(2,1)S(1)}, bf16[768,256]{1,0:T(8,128)(2,1)S(1)}, u32[]{:S(2)}, u32[]{:S(2)}) collective-permute-start(bf16[768,256]{1,0:T(8,128)(2,1)S(1)} %collective-permute-done.22.refs_1_), channel_id=1, source_target_pairs={{0,12},{1,13},{2,14},{3,15},{4,0},{5,1},{6,2},{7,3},{8,4},{9,5},{1... | collective-permute-start | bytes 1179656 | tf_op jit(solution)/shard_map/ppermute | solution.py:213
  147.7 9.3 %collective-permute-start.28 = (bf16[768,256]{1,0:T(8,128)(2,1)S(1)}, bf16[768,256]{1,0:T(8,128)(2,1)S(1)}, u32[]{:S(2)}, u32[]{:S(2)}) collective-permute-start(bf16[768,256]{1,0:T(8,128)(2,1)S(1)} %collective-permute-done.27.refs_6_), channel_id=1, source_target_pairs={{0,2},{1,3},{2,0},{3,1},{4,6},{5,7},{6,4},{7,5},{8,10},{9,11},{10,... | collective-permute-start | bytes 1179656 | tf_op jit(solution)/shard_map/ppermute | solution.py:213
  149.3 7.6 %collective-permute-start.30 = (bf16[768,256]{1,0:T(8,128)(2,1)S(1)}, bf16[768,256]{1,0:T(8,128)(2,1)S(1)}, u32[]{:S(2)}, u32[]{:S(2)}) collective-permute-start(bf16[768,256]{1,0:T(8,128)(2,1)S(1)} %collective-permute-done.22.refs_1_), channel_id=1, source_target_pairs={{0,1},{1,0},{2,3},{3,2},{4,5},{5,4},{6,7},{7,6},{8,9},{9,8},{10,11... | collective-permute-start | bytes 1179656 | tf_op jit(solution)/shard_map/ppermute | solution.py:213
  149.4 8.1 %collective-permute-start.31 = (bf16[768,256]{1,0:T(8,128)(2,1)S(1)}, bf16[768,256]{1,0:T(8,128)(2,1)S(1)}, u32[]{:S(2)}, u32[]{:S(2)}) collective-permute-start(bf16[768,256]{1,0:T(8,128)(2,1)S(1)} %collective-permute-done.23.refs_2_), channel_id=1, source_target_pairs={{0,1},{1,0},{2,3},{3,2},{4,5},{5,4},{6,7},{7,6},{8,9},{9,8},{10,11... | collective-permute-start | bytes 1179656 | tf_op jit(solution)/shard_map/ppermute | solution.py:213
  153.0 6.6 %collective-permute-start.35 = (bf16[768,256]{1,0:T(8,128)(2,1)S(1)}, bf16[768,256]{1,0:T(8,128)(2,1)}, u32[]{:S(2)}, u32[]{:S(2)}) collective-permute-start(bf16[768,256]{1,0:T(8,128)(2,1)S(1)} %collective-permute-done.27.refs_6_), channel_id=1, source_target_pairs={{0,1},{1,0},{2,3},{3,2},{4,5},{5,4},{6,7},{7,6},{8,9},{9,8},{10,11... | collective-permute-start | bytes 1179656 | tf_op jit(solution)/shard_map/ppermute | solution.py:213
  174.1 22.7 %collective-permute-start.37 = (bf16[768,512]{1,0:T(8,128)(2,1)}, bf16[768,512]{1,0:T(8,128)(2,1)S(1)}, u32[]{:S(2)}, u32[]{:S(2)}) collective-permute-start(bf16[768,512]{1,0:T(8,128)(2,1)} %get-tuple-element.31), channel_id=1, source_target_pairs={{0,32},{16,48},{32,64},{48,80},{64,96},{80,112},{96,0},{112,16},{1... | collective-permute-start | bytes 2359304 | tf_op jit(solution)/shard_map/ppermute | solution.py:218
  174.8 22.1 %collective-permute-start.38 = (bf16[768,512]{1,0:T(8,128)(2,1)}, bf16[768,512]{1,0:T(8,128)(2,1)S(1)}, u32[]{:S(2)}, u32[]{:S(2)}) collective-permute-start(bf16[768,512]{1,0:T(8,128)(2,1)} %get-tuple-element.31), channel_id=1, source_target_pairs={{0,96},{16,112},{32,0},{48,16},{64,32},{80,48},{96,64},{112,80},{1... | collective-permute-start | bytes 2359304 | tf_op jit(solution)/shard_map/ppermute | solution.py:218
  178.6 22.3 %collective-permute-start.39 = (bf16[768,512]{1,0:T(8,128)(2,1)}, bf16[768,512]{1,0:T(8,128)(2,1)S(1)}, u32[]{:S(2)}, u32[]{:S(2)}) collective-permute-start(bf16[768,512]{1,0:T(8,128)(2,1)} %get-tuple-element.31), channel_id=1, source_target_pairs={{0,16},{16,0},{32,48},{48,32},{64,80},{80,64},{96,112},{112,96},{1... | collective-permute-start | bytes 2359304 | tf_op jit(solution)/shard_map/ppermute | solution.py:218
  196.8 13.3 %collective-permute-start.40 = (bf16[384,512]{1,0:T(8,128)(2,1)S(1)}, bf16[384,512]{1,0:T(8,128)(2,1)S(1)}, u32[]{:S(2)}, u32[]{:S(2)}) collective-permute-start(bf16[384,512]{1,0:T(8,128)(2,1)S(1)} %slice.100), channel_id=1, source_target_pairs={{0,32},{16,48},{32,64},{48,80},{64,96},{80,112},{96,0},{112,16},{1... | collective-permute-start | bytes 1179656 | tf_op jit(solution)/shard_map/ppermute | solution.py:218
  197.7 13.1 %collective-permute-start.41 = (bf16[384,512]{1,0:T(8,128)(2,1)}, bf16[384,512]{1,0:T(8,128)(2,1)S(1)}, u32[]{:S(2)}, u32[]{:S(2)}) collective-permute-start(bf16[384,512]{1,0:T(8,128)(2,1)} %slice.101), channel_id=1, source_target_pairs={{0,96},{16,112},{32,0},{48,16},{64,32},{80,48},{96,64},{112,80},{1... | collective-permute-start | bytes 1179656 | tf_op jit(solution)/shard_map/ppermute | solution.py:218
  200.9 24.8 %collective-permute-start.42 = (bf16[768,512]{1,0:T(8,128)(2,1)S(1)}, bf16[768,512]{1,0:T(8,128)(2,1)S(1)}, u32[]{:S(2)}, u32[]{:S(2)}) collective-permute-start(bf16[768,512]{1,0:T(8,128)(2,1)S(1)} %collective-permute-done.39), channel_id=1, source_target_pairs={{0,32},{16,48},{32,64},{48,80},{64,96},{80,112},{96,0},{112,16},{1... | collective-permute-start | bytes 2359304 | tf_op jit(solution)/shard_map/ppermute | solution.py:218
  203.0 23.7 %collective-permute-start.43 = (bf16[768,512]{1,0:T(8,128)(2,1)S(1)}, bf16[768,512]{1,0:T(8,128)(2,1)S(1)}, u32[]{:S(2)}, u32[]{:S(2)}) collective-permute-start(bf16[768,512]{1,0:T(8,128)(2,1)S(1)} %collective-permute-done.39), channel_id=1, source_target_pairs={{0,96},{16,112},{32,0},{48,16},{64,32},{80,48},{96,64},{112,80},{1... | collective-permute-start | bytes 2359304 | tf_op jit(solution)/shard_map/ppermute | solution.py:218
  210.8 16.8 %collective-permute-start.44 = (bf16[768,512]{1,0:T(8,128)(2,1)S(1)}, bf16[768,512]{1,0:T(8,128)(2,1)S(1)}, u32[]{:S(2)}, u32[]{:S(2)}) collective-permute-start(bf16[768,512]{1,0:T(8,128)(2,1)S(1)} %pad_maximum_fusion), channel_id=1, source_target_pairs={{0,16},{16,0},{32,48},{48,32},{64,80},{80,64},{96,112},{112,96},{1... | collective-permute-start | bytes 2359304 | tf_op jit(solution)/shard_map/ppermute | solution.py:218
  (41 other events, 405.9 us)
Sparse Core Ops, SparseCore 0:
  16.7 55.4 all-gather.3
  82.7 32.0 all-gather.5
  116.5 40.2 all-gather.7

commit v9 on v8

--- a/solution.py
+++ b/solution.py
@@ -282,10 +282,9 @@
     )(blocks, rows, weight)
 
 
-def sum_over_tr(value):
+def sum_over_y(value):
     value = value + to_sibling(value)
-    value = value + to_chip(value, 1, 0) + to_chip(value, 2, 0) + to_chip(value, 3, 0)
-    return value + to_chip(value, 0, 1)
+    return value + to_chip(value, 1, 0) + to_chip(value, 2, 0) + to_chip(value, 3, 0)
 
 
 def per_device(taps, routes, lengths, merge_weight, norm_gain, head_scale):
@@ -347,9 +346,11 @@
     first_across = row_major(to_group(rows_now[:part], 0, 1))
     merged = (second[0, 0] + up + down + far + across) * (1.0 / SEND)
     merged = merged.reshape(slots, span, wide)
-    squares = sum_over_tr(jnp.sum(merged * merged, axis=2))
-    squares, first_across, rows_now = lax.optimization_barrier((squares, first_across, rows_now))
+    squares = sum_over_y(jnp.sum(merged * merged, axis=2))
+    squares, first_across = lax.optimization_barrier((squares, first_across))
     taps_first = gather_taps(first_across)
+    squares = squares + to_chip(squares, 0, 1)
+    squares, rows_now = lax.optimization_barrier((squares, rows_now))
     last_across = row_major(to_group(rows_now[part:], 0, 1))
 
     scaled, crossed = attention(
@@ -362,8 +363,8 @@
         taps[:, :, 2, :],
     )
     crossed, last_across = lax.optimization_barrier((crossed, last_across))
-    taps_last = gather_taps(last_across)
-    crossed = sum_over_tr(crossed.reshape(slots, span))
+    crossed = sum_over_y(crossed.reshape(slots, span))
+    crossed = crossed + to_chip(crossed, 0, 1)
     inverse = lax.rsqrt(squares / width_all + epsilon)
     merged_grad = (
         scaled * inverse[:, :, None]
@@ -383,6 +384,8 @@
         for at_core in range(2)
     ]
     turned = lax.ppermute(merged_grad.reshape(slots * span, wide), ("rep", "tr"), pairs)
+    turned, last_across = lax.optimization_barrier((turned, last_across))
+    taps_last = gather_taps(last_across)
     own_half = gather(turned, to_chip)
     other_half = {k: to_sibling(v) for k, v in own_half.items()}
 

time: 236 us -> 234 us (level)
  waiting for transfers between devices: 80.5 us -> 77.4 us
    ppermute x10, waiting for transfers between devices: 33.2 us -> 29.2 us  [to_group(): return lax.ppermute(value, 'rep', pairs)]
  transfers between devices with their start and end apart: 48 -> 48, of which waited for: 24 -> 25; matrix products, arithmetic and copies ran while one was open for 9% -> 9% of each run, Pallas kernels for 9% -> 9%
where the time goes in v9:
time: 234 us; the launch traced here: 233 us
  waiting for transfers between devices  77.4 us (33%)
  starting transfers between devices  66 us (28%)
  Pallas kernels  38.5 us (16%)
  local copies, waits for them, and re-layouts  27.5 us (12%)
  between operations  14.4 us (6%)
  other arithmetic  8.81 us (4%)
    ppermute x34, starting transfers between devices, to_chip(): return lax.ppermute(value, 'tr', pairs)  50.6 us
    ppermute x34, waiting for transfers between devices, to_chip(): return lax.ppermute(value, 'tr', pairs)  47.1 us
    ppermute x10, waiting for transfers between devices, to_group(): return lax.ppermute(value, 'rep', pairs)  29.2 us
    ppermute x10, starting transfers between devices, to_group(): return lax.ppermute(value, 'rep', pairs)  14.7 us
    pallas_call x4, Pallas kernels, products(): pl.pallas_call(product_kernel, grid_spec=pltpu.PrefetchScalarGridSpec(num...  13.7 us
    pallas_call x1, Pallas kernels, gradient(): pl.pallas_call(gradient_kernel, grid_spec=pltpu.PrefetchScalarGridSpec(nu...  13.5 us
    unnamed x51, local copies, waits for them, and re-layouts  12.2 us
    pallas_call x1, Pallas kernels, attention(): pl.pallas_call(attention_kernel, grid=(count // slots,), in_specs=[scalar...  11.3 us
  transfers between devices with their start and end apart: 48, of which 25 were waited for; matrix products, arithmetic and copies ran while one was open for 9% of the time, Pallas kernels for 9%

profile of v9, /device:TPU:0, one launch (start us, length us, event | category | flops | bytes accessed | tf_op | source)
XLA Modules:
  0.0 232.6 jit_solution(11126232437056112292)
XLA Ops:
  7.3 2.3 copy.16
  10.0 3.1 %copy-done = bf16[3,256,4096]{2,1,0:T(8,128)(2,1)S(1)} copy-done((bf16[3,256,4096]{2,1,0:T(8,128)(2,1)S(1)}, bf16[3,256,4096]{2,1,0:T(8,128)(2,1)}, u32[]{:S(2)}) %copy-start) | copy-done | bytes 6291480
  13.1 3.4 %shard_map.78 = f32[3,768,256]{2,1,0:T(8,128)} custom-call(s32[3]{0:T(128)S(1)} %pad_add_fusion.1.blocks_ref, bf16[768,768]{1,0:T(8,128)(2,1)S(1)} %bitcast.85, bf16[768,4096]{1,0:T(8,128)(2,1)S(1)} %bitcast.79), custom_call_target="tpu_custom_call" | custom-call | flops 905969664 | bytes 4718592 | tf_op jit(solution)/shard_map/pallas_call | solution.py:264
  16.9 2.8 %copy-done.1 = bf16[3,256,4096]{2,1,0:T(8,128)(2,1)S(1)} copy-done((bf16[3,256,4096]{2,1,0:T(8,128)(2,1)S(1)}, bf16[3,256,4096]{2,1,0:T(8,128)(2,1)}, u32[]{:S(2)}) %copy-start.1) | copy-done | bytes 6291480
  20.9 2.2 shard_map.77
  23.2 3.0 %fusion.28 = (f16[768,256]{1,0:T(8,128)(2,1)}, f16[768,256]{1,0:T(8,128)(2,1)}, f16[768,256]{1,0:T(8,128)(2,1)}) fusion(f32[3,768,256]{2,1,0:T(8,128)} %collective-permute-done, f32[3,768,256]{2,1,0:T(8,128)S(1)} %shard_map.77), kind=kLoop, calls=%fused_computation.39 | loop fusion | flops 1769472 | bytes 5898240 | tf_op jit(solution)/shard_map/convert_element_type | solution.py:333
  26.1 4.8 %shard_map.80 = f32[5,768,256]{2,1,0:T(8,128)} custom-call(s32[5]{0:T(128)S(1)} %stack.111.blocks_ref, bf16[768,768]{1,0:T(8,128)(2,1)S(1)} %bitcast.88, bf16[768,4096]{1,0:T(8,128)(2,1)S(1)} %bitcast.83), custom_call_target="tpu_custom_call" | custom-call | flops 1509949440 | bytes 7077888 | tf_op jit(solution)/shard_map/pallas_call | solution.py:264
  31.5 3.1 %collective-permute-start.4 = (f16[768,256]{1,0:T(8,128)(2,1)}, f16[768,256]{1,0:T(8,128)(2,1)S(1)}, u32[]{:S(2)}, u32[]{:S(2)}) collective-permute-start(f16[768,256]{1,0:T(8,128)(2,1)} %get-tuple-element.21), channel_id=1, source_target_pairs={{0,2},{1,3},{2,0},{3,1},{4,6},{5,7},{6,4},{7,5},{8,10},{9,11},{10,... | collective-permute-start | bytes 1179656 | tf_op jit(solution)/shard_map/ppermute | solution.py:213
  37.9 2.9 %copy-done.2 = bf16[3,256,4096]{2,1,0:T(8,128)(2,1)S(1)} copy-done((bf16[3,256,4096]{2,1,0:T(8,128)(2,1)S(1)}, bf16[3,256,4096]{2,1,0:T(8,128)(2,1)}, u32[]{:S(2)}) %copy-start.2) | copy-done | bytes 6291480
  40.8 3.3 %shard_map.79 = f32[5,768,256]{2,1,0:T(8,128)S(1)} custom-call(s32[5]{0:T(128)S(1)} %stack.97.blocks_ref, bf16[768,768]{1,0:T(8,128)(2,1)S(1)} %bitcast.89, bf16[768,4096]{1,0:T(8,128)(2,1)S(1)} %bitcast.84), custom_call_target="tpu_custom_call" | custom-call | flops 1509949440 | bytes 7077888 | tf_op jit(solution)/shard_map/pallas_call | solution.py:264
  46.2 2.9 %collective-permute-start.3 = (f16[768,256]{1,0:T(8,128)(2,1)S(1)}, f16[768,256]{1,0:T(8,128)(2,1)S(1)}, u32[]{:S(2)}, u32[]{:S(2)}) collective-permute-start(f16[768,256]{1,0:T(8,128)(2,1)S(1)} %get-tuple-element.41), channel_id=1, source_target_pairs={{0,12},{1,13},{2,14},{3,15},{4,0},{5,1},{6,2},{7,3},{8,4},{9,5},{1... | collective-permute-start | bytes 1179656 | tf_op jit(solution)/shard_map/ppermute | solution.py:213
  54.6 4.6 %collective-permute-done.2 = f16[768,256]{1,0:T(8,128)(2,1)S(1)} collective-permute-done((f16[768,256]{1,0:T(8,128)(2,1)S(1)}, f16[768,256]{1,0:T(8,128)(2,1)S(1)}, u32[]{:S(2)}, u32[]{:S(2)}) %collective-permute-start.2) | collective-permute-done | bytes 393248 | tf_op jit(solution)/shard_map/ppermute | solution.py:213
  59.2 5.8 %collective-permute-done.3 = f16[768,256]{1,0:T(8,128)(2,1)S(1)} collective-permute-done((f16[768,256]{1,0:T(8,128)(2,1)S(1)}, f16[768,256]{1,0:T(8,128)(2,1)S(1)}, u32[]{:S(2)}, u32[]{:S(2)}) %collective-permute-start.3) | collective-permute-done | bytes 393248 | tf_op jit(solution)/shard_map/ppermute | solution.py:213
  69.7 3.4 %collective-permute-start.11 = (f32[8,96]{1,0:T(8,128)S(1)}, f32[8,96]{1,0:T(8,128)S(1)}, u32[]{:S(2)}, u32[]{:S(2)}) collective-permute-start(f32[8,96]{1,0:T(8,128)S(1)} %add.444), channel_id=1, source_target_pairs={{0,8},{1,9},{2,10},{3,11},{4,12},{5,13},{6,14},{7,15},{8,0},{9,1},... | collective-permute-start | bytes 9224 | tf_op jit(solution)/shard_map/ppermute | solution.py:213
  78.4 4.4 %collective-permute-done.14 = f32[8,96]{1,0:T(8,128)S(1)} collective-permute-done((f32[8,96]{1,0:T(8,128)S(1)}, f32[8,96]{1,0:T(8,128)S(1)}, u32[]{:S(2)}, u32[]{:S(2)}) %collective-permute-start.14) | collective-permute-done | bytes 3104 | tf_op jit(solution)/shard_map/ppermute | solution.py:213
  84.7 11.3 %shard_map.81 = (f32[8,96,256]{2,1,0:T(8,128)S(1)}, f32[8,1,96]{2,1,0:T(1,128)S(1)}) custom-call(s32[8]{0:T(128)S(1)} %dynamic_slice.6.lens_ref, f32[8]{0:T(128)S(1)} %convert_divide_fusion.weights_ref, f32[2]{0:T(128)S(1)} %copy-done.7, f32[8,96,256]{2,1,0:T(8,128)S(1)} %bitcast.92, f32[8,1,96]{2,1,0:T(1,128)S(1)} %bitcast.94, f32[1,256]{1,0:T(1,128)S(1)} %bitcast.97, ...), custom_call_target="tpu_custom_call" | custom-call | flops 2000000000 | bytes 3000000 | tf_op jit(solution)/shard_map/pallas_call | solution.py:116
  97.3 2.8 %collective-permute-start.18 = (f32[8,96]{1,0:T(8,128)S(1)}, f32[8,96]{1,0:T(8,128)S(1)}, u32[]{:S(2)}, u32[]{:S(2)}) collective-permute-start(f32[8,96]{1,0:T(8,128)S(1)} %add.454), channel_id=1, source_target_pairs={{0,8},{1,9},{2,10},{3,11},{4,12},{5,13},{6,14},{7,15},{8,0},{9,1},... | collective-permute-start | bytes 9224 | tf_op jit(solution)/shard_map/ppermute | solution.py:213
  105.6 3.3 %collective-permute-done.20 = f32[8,96]{1,0:T(8,128)S(1)} collective-permute-done((f32[8,96]{1,0:T(8,128)S(1)}, f32[8,96]{1,0:T(8,128)S(1)}, u32[]{:S(2)}, u32[]{:S(2)}) %collective-permute-start.20) | collective-permute-done | bytes 3104 | tf_op jit(solution)/shard_map/ppermute | solution.py:213
  109.9 12.2 %collective-permute-start.22 = (bf16[768,256]{1,0:T(8,128)(2,1)S(1)}, bf16[768,256]{1,0:T(8,128)(2,1)S(1)}, u32[]{:S(2)}, u32[]{:S(2)}) collective-permute-start(bf16[768,256]{1,0:T(8,128)(2,1)S(1)} %collective-permute-done.21.refs_0_), channel_id=1, source_target_pairs={{0,2},{1,3},{2,0},{3,1},{4,6},{5,7},{6,4},{7,5},{8,10},{9,11},{10,... | collective-permute-start | bytes 1179656 | tf_op jit(solution)/shard_map/ppermute | solution.py:213
  122.1 6.7 %collective-permute-start.27 = (bf16[768,256]{1,0:T(8,128)(2,1)S(1)}, bf16[768,256]{1,0:T(8,128)(2,1)S(1)}, u32[]{:S(2)}, u32[]{:S(2)}) collective-permute-start(bf16[768,256]{1,0:T(8,128)(2,1)S(1)} %collective-permute-done.21.refs_0_), channel_id=1, source_target_pairs={{0,8},{1,9},{2,10},{3,11},{4,12},{5,13},{6,14},{7,15},{8,0},{9,1},... | collective-permute-start | bytes 1179656 | tf_op jit(solution)/shard_map/ppermute | solution.py:213
  132.1 6.7 %collective-permute-done.27.refs_6_ = bf16[768,256]{1,0:T(8,128)(2,1)S(1)} collective-permute-done((bf16[768,256]{1,0:T(8,128)(2,1)S(1)}, bf16[768,256]{1,0:T(8,128)(2,1)S(1)}, u32[]{:S(2)}, u32[]{:S(2)}) %collective-permute-start.27) | collective-permute-done | bytes 393248 | tf_op jit(solution)/shard_map/ppermute | solution.py:213
  138.8 3.7 %collective-permute-start.26 = (bf16[768,256]{1,0:T(8,128)(2,1)S(1)}, bf16[768,256]{1,0:T(8,128)(2,1)S(1)}, u32[]{:S(2)}, u32[]{:S(2)}) collective-permute-start(bf16[768,256]{1,0:T(8,128)(2,1)S(1)} %collective-permute-done.22.refs_1_), channel_id=1, source_target_pairs={{0,12},{1,13},{2,14},{3,15},{4,0},{5,1},{6,2},{7,3},{8,4},{9,5},{1... | collective-permute-start | bytes 1179656 | tf_op jit(solution)/shard_map/ppermute | solution.py:213
  142.6 4.2 %collective-permute-done.23.refs_2_ = bf16[768,256]{1,0:T(8,128)(2,1)S(1)} collective-permute-done((bf16[768,256]{1,0:T(8,128)(2,1)S(1)}, bf16[768,256]{1,0:T(8,128)(2,1)S(1)}, u32[]{:S(2)}, u32[]{:S(2)}) %collective-permute-start.23) | collective-permute-done | bytes 393248 | tf_op jit(solution)/shard_map/ppermute | solution.py:213
  148.9 3.2 %collective-permute-done.24.refs_3_ = bf16[768,256]{1,0:T(8,128)(2,1)S(1)} collective-permute-done((bf16[768,256]{1,0:T(8,128)(2,1)S(1)}, bf16[768,256]{1,0:T(8,128)(2,1)S(1)}, u32[]{:S(2)}, u32[]{:S(2)}) %collective-permute-start.24) | collective-permute-done | bytes 393248 | tf_op jit(solution)/shard_map/ppermute | solution.py:213
  152.7 3.4 %collective-permute-done.28.refs_7_ = bf16[768,256]{1,0:T(8,128)(2,1)S(1)} collective-permute-done((bf16[768,256]{1,0:T(8,128)(2,1)S(1)}, bf16[768,256]{1,0:T(8,128)(2,1)S(1)}, u32[]{:S(2)}, u32[]{:S(2)}) %collective-permute-start.28) | collective-permute-done | bytes 393248 | tf_op jit(solution)/shard_map/ppermute | solution.py:213
  160.7 13.5 %shard_map.82 = (f32[768,512]{1,0:T(8,128)}, bf16[768,512]{1,0:T(8,128)(2,1)}) custom-call(s32[7]{0:T(128)} %stack.91.places_ref, bf16[3072,768]{1,0:T(8,128)(2,1)} %all-gather.4.cloned.1.call-done.here_ref, bf16[1536,768]{1,0:T(8,128)(2,1)} %all-gather.6.cloned.1.call-done.first_ref, bf16[1536,768]{1,0:T(8,128)(2,1)} %all-gather.8.cloned.1.call-done.last_ref, ...), custom_call_target="tpu_custom_call" | custom-call | flops 4831838208 | bytes 20971520 | tf_op jit(solution)/shard_map/pallas_call | solution.py:171
  174.7 2.7 %collective-permute-start.38 = (bf16[768,512]{1,0:T(8,128)(2,1)}, bf16[768,512]{1,0:T(8,128)(2,1)S(1)}, u32[]{:S(2)}, u32[]{:S(2)}) collective-permute-start(bf16[768,512]{1,0:T(8,128)(2,1)} %get-tuple-element.37), channel_id=1, source_target_pairs={{0,96},{16,112},{32,0},{48,16},{64,32},{80,48},{96,64},{112,80},{1... | collective-permute-start | bytes 2359304 | tf_op jit(solution)/shard_map/ppermute | solution.py:218
  178.9 16.1 %collective-permute-done.37 = bf16[768,512]{1,0:T(8,128)(2,1)S(1)} collective-permute-done((bf16[768,512]{1,0:T(8,128)(2,1)}, bf16[768,512]{1,0:T(8,128)(2,1)S(1)}, u32[]{:S(2)}, u32[]{:S(2)}) %collective-permute-start.37) | collective-permute-done | bytes 786464 | tf_op jit(solution)/shard_map/ppermute | solution.py:218
  195.9 3.2 %collective-permute-start.41 = (bf16[384,512]{1,0:T(8,128)(2,1)}, bf16[384,512]{1,0:T(8,128)(2,1)S(1)}, u32[]{:S(2)}, u32[]{:S(2)}) collective-permute-start(bf16[384,512]{1,0:T(8,128)(2,1)} %slice.101), channel_id=1, source_target_pairs={{0,96},{16,112},{32,0},{48,16},{64,32},{80,48},{96,64},{112,80},{1... | collective-permute-start | bytes 1179656 | tf_op jit(solution)/shard_map/ppermute | solution.py:218
  201.2 3.2 %collective-permute-start.43 = (bf16[768,512]{1,0:T(8,128)(2,1)S(1)}, bf16[768,512]{1,0:T(8,128)(2,1)S(1)}, u32[]{:S(2)}, u32[]{:S(2)}) collective-permute-start(bf16[768,512]{1,0:T(8,128)(2,1)S(1)} %collective-permute-done.39), channel_id=1, source_target_pairs={{0,96},{16,112},{32,0},{48,16},{64,32},{80,48},{96,64},{112,80},{1... | collective-permute-start | bytes 2359304 | tf_op jit(solution)/shard_map/ppermute | solution.py:218
  204.5 3.9 %collective-permute-done.40 = bf16[384,512]{1,0:T(8,128)(2,1)S(1)} collective-permute-done((bf16[384,512]{1,0:T(8,128)(2,1)S(1)}, bf16[384,512]{1,0:T(8,128)(2,1)S(1)}, u32[]{:S(2)}, u32[]{:S(2)}) %collective-permute-start.40) | collective-permute-done | bytes 393248 | tf_op jit(solution)/shard_map/ppermute | solution.py:218
  214.8 8.5 %collective-permute-done.42 = bf16[768,512]{1,0:T(8,128)(2,1)S(1)} collective-permute-done((bf16[768,512]{1,0:T(8,128)(2,1)S(1)}, bf16[768,512]{1,0:T(8,128)(2,1)S(1)}, u32[]{:S(2)}, u32[]{:S(2)}) %collective-permute-start.42) | collective-permute-done | bytes 786464 | tf_op jit(solution)/shard_map/ppermute | solution.py:218
  (164 shorter events, 57.5 us)
Async XLA Ops:
  7.2 151.6 %all-gather.4.cloned.1.call-start = ((), (), s32[]{:S(2)}) async-start(), calls=%async_computation | async-start | bytes 5898240 | tf_op jit(solution)/shard_map/all_gather | solution.py:315
  16.6 143.0 %all-gather.6.cloned.1.call-start = ((), (), s32[]{:S(2)}) async-start(), calls=%async_computation.1 | async-start | bytes 2949120 | tf_op jit(solution)/shard_map/all_gather | solution.py:315
  30.9 13.1 %collective-permute-start.1 = (f32[5,768,256]{2,1,0:T(8,128)}, f32[5,768,256]{2,1,0:T(8,128)}, u32[]{:S(2)}, u32[]{:S(2)}) collective-permute-start(f32[5,768,256]{2,1,0:T(8,128)} %shard_map.80), channel_id=1, source_target_pairs={{0,1},{1,0},{2,3},{3,2},{4,5},{5,4},{6,7},{7,6},{8,9},{9,8},{10,11... | collective-permute-start | bytes 11796488 | tf_op jit(solution)/shard_map/ppermute | solution.py:213
  31.5 17.6 %collective-permute-start.4 = (f16[768,256]{1,0:T(8,128)(2,1)}, f16[768,256]{1,0:T(8,128)(2,1)S(1)}, u32[]{:S(2)}, u32[]{:S(2)}) collective-permute-start(f16[768,256]{1,0:T(8,128)(2,1)} %get-tuple-element.21), channel_id=1, source_target_pairs={{0,2},{1,3},{2,0},{3,1},{4,6},{5,7},{6,4},{7,5},{8,10},{9,11},{10,... | collective-permute-start | bytes 1179656 | tf_op jit(solution)/shard_map/ppermute | solution.py:213
  34.6 14.5 %collective-permute-start.6 = (f16[768,256]{1,0:T(8,128)(2,1)}, f16[768,256]{1,0:T(8,128)(2,1)S(1)}, u32[]{:S(2)}, u32[]{:S(2)}) collective-permute-start(f16[768,256]{1,0:T(8,128)(2,1)} %get-tuple-element.22), channel_id=1, source_target_pairs={{0,4},{1,5},{2,6},{3,7},{4,8},{5,9},{6,10},{7,11},{8,12},{9,13},{1... | collective-permute-start | bytes 1179656 | tf_op jit(solution)/shard_map/ppermute | solution.py:213
  36.2 12.9 %collective-permute-start.7 = (f16[768,256]{1,0:T(8,128)(2,1)}, f16[768,256]{1,0:T(8,128)(2,1)S(1)}, u32[]{:S(2)}, u32[]{:S(2)}) collective-permute-start(f16[768,256]{1,0:T(8,128)(2,1)} %get-tuple-element.23), channel_id=1, source_target_pairs={{0,12},{1,13},{2,14},{3,15},{4,0},{5,1},{6,2},{7,3},{8,4},{9,5},{1... | collective-permute-start | bytes 1179656 | tf_op jit(solution)/shard_map/ppermute | solution.py:213
  45.8 13.4 %collective-permute-start.2 = (f16[768,256]{1,0:T(8,128)(2,1)S(1)}, f16[768,256]{1,0:T(8,128)(2,1)S(1)}, u32[]{:S(2)}, u32[]{:S(2)}) collective-permute-start(f16[768,256]{1,0:T(8,128)(2,1)S(1)} %get-tuple-element.40), channel_id=1, source_target_pairs={{0,4},{1,5},{2,6},{3,7},{4,8},{5,9},{6,10},{7,11},{8,12},{9,13},{1... | collective-permute-start | bytes 1179656 | tf_op jit(solution)/shard_map/ppermute | solution.py:213
  46.2 18.8 %collective-permute-start.3 = (f16[768,256]{1,0:T(8,128)(2,1)S(1)}, f16[768,256]{1,0:T(8,128)(2,1)S(1)}, u32[]{:S(2)}, u32[]{:S(2)}) collective-permute-start(f16[768,256]{1,0:T(8,128)(2,1)S(1)} %get-tuple-element.41), channel_id=1, source_target_pairs={{0,12},{1,13},{2,14},{3,15},{4,0},{5,1},{6,2},{7,3},{8,4},{9,5},{1... | collective-permute-start | bytes 1179656 | tf_op jit(solution)/shard_map/ppermute | solution.py:213
  51.0 14.0 %collective-permute-start.8 = (f16[768,256]{1,0:T(8,128)(2,1)S(1)}, f16[768,256]{1,0:T(8,128)(2,1)S(1)}, u32[]{:S(2)}, u32[]{:S(2)}) collective-permute-start(f16[768,256]{1,0:T(8,128)(2,1)S(1)} %get-tuple-element.24), channel_id=1, source_target_pairs={{0,2},{1,3},{2,0},{3,1},{4,6},{5,7},{6,4},{7,5},{8,10},{9,11},{10,... | collective-permute-start | bytes 1179656 | tf_op jit(solution)/shard_map/ppermute | solution.py:213
  51.4 14.4 %collective-permute-start.5 = (f16[768,256]{1,0:T(8,128)(2,1)S(1)}, f16[768,256]{1,0:T(8,128)(2,1)S(1)}, u32[]{:S(2)}, u32[]{:S(2)}) collective-permute-start(f16[768,256]{1,0:T(8,128)(2,1)S(1)} %get-tuple-element.42), channel_id=1, source_target_pairs={{0,8},{1,9},{2,10},{3,11},{4,12},{5,13},{6,14},{7,15},{8,0},{9,1},... | collective-permute-start | bytes 1179656 | tf_op jit(solution)/shard_map/ppermute | solution.py:213
  53.4 23.3 %collective-permute-start.13 = (bf16[384,768]{1,0:T(8,128)(2,1)}, bf16[384,768]{1,0:T(8,128)(2,1)S(1)}, u32[]{:S(2)}, u32[]{:S(2)}) collective-permute-start(bf16[384,768]{1,0:T(8,128)(2,1)} %slice.79), channel_id=1, source_target_pairs={{0,16},{16,0},{32,48},{48,32},{64,80},{80,64},{96,112},{112,96},{1... | collective-permute-start | bytes 1769480 | tf_op jit(solution)/shard_map/ppermute | solution.py:218
  77.5 83.1 %all-gather.8.cloned.1.call-start = ((), (), s32[]{:S(2)}) async-start(), calls=%async_computation.2 | async-start | bytes 2949120 | tf_op jit(solution)/shard_map/all_gather | solution.py:315
  82.9 13.2 %collective-permute-start.15 = (bf16[384,768]{1,0:T(8,128)(2,1)S(1)}, bf16[384,768]{1,0:T(8,128)(2,1)S(1)}, u32[]{:S(2)}, u32[]{:S(2)}) collective-permute-start(bf16[384,768]{1,0:T(8,128)(2,1)S(1)} %slice.81), channel_id=1, source_target_pairs={{0,16},{16,0},{32,48},{48,32},{64,80},{80,64},{96,112},{112,96},{1... | collective-permute-start | bytes 1769480 | tf_op jit(solution)/shard_map/ppermute | solution.py:218
  109.9 22.2 %collective-permute-start.22 = (bf16[768,256]{1,0:T(8,128)(2,1)S(1)}, bf16[768,256]{1,0:T(8,128)(2,1)S(1)}, u32[]{:S(2)}, u32[]{:S(2)}) collective-permute-start(bf16[768,256]{1,0:T(8,128)(2,1)S(1)} %collective-permute-done.21.refs_0_), channel_id=1, source_target_pairs={{0,2},{1,3},{2,0},{3,1},{4,6},{5,7},{6,4},{7,5},{8,10},{9,11},{10,... | collective-permute-start | bytes 1179656 | tf_op jit(solution)/shard_map/ppermute | solution.py:213
  122.1 16.7 %collective-permute-start.27 = (bf16[768,256]{1,0:T(8,128)(2,1)S(1)}, bf16[768,256]{1,0:T(8,128)(2,1)S(1)}, u32[]{:S(2)}, u32[]{:S(2)}) collective-permute-start(bf16[768,256]{1,0:T(8,128)(2,1)S(1)} %collective-permute-done.21.refs_0_), channel_id=1, source_target_pairs={{0,8},{1,9},{2,10},{3,11},{4,12},{5,13},{6,14},{7,15},{8,0},{9,1},... | collective-permute-start | bytes 1179656 | tf_op jit(solution)/shard_map/ppermute | solution.py:213
  128.8 18.0 %collective-permute-start.23 = (bf16[768,256]{1,0:T(8,128)(2,1)S(1)}, bf16[768,256]{1,0:T(8,128)(2,1)S(1)}, u32[]{:S(2)}, u32[]{:S(2)}) collective-permute-start(bf16[768,256]{1,0:T(8,128)(2,1)S(1)} %collective-permute-done.21.refs_0_), channel_id=1, source_target_pairs={{0,4},{1,5},{2,6},{3,7},{4,8},{5,9},{6,10},{7,11},{8,12},{9,13},{1... | collective-permute-start | bytes 1179656 | tf_op jit(solution)/shard_map/ppermute | solution.py:213
  129.9 18.5 %collective-permute-start.25 = (bf16[768,256]{1,0:T(8,128)(2,1)S(1)}, bf16[768,256]{1,0:T(8,128)(2,1)S(1)}, u32[]{:S(2)}, u32[]{:S(2)}) collective-permute-start(bf16[768,256]{1,0:T(8,128)(2,1)S(1)} %collective-permute-done.21.refs_0_), channel_id=1, source_target_pairs={{0,12},{1,13},{2,14},{3,15},{4,0},{5,1},{6,2},{7,3},{8,4},{9,5},{1... | collective-permute-start | bytes 1179656 | tf_op jit(solution)/shard_map/ppermute | solution.py:213
  132.0 16.3 %collective-permute-start.29 = (bf16[768,256]{1,0:T(8,128)(2,1)S(1)}, bf16[768,256]{1,0:T(8,128)(2,1)S(1)}, u32[]{:S(2)}, u32[]{:S(2)}) collective-permute-start(bf16[768,256]{1,0:T(8,128)(2,1)S(1)} %collective-permute-done.21.refs_0_), channel_id=1, source_target_pairs={{0,1},{1,0},{2,3},{3,2},{4,5},{5,4},{6,7},{7,6},{8,9},{9,8},{10,11... | collective-permute-start | bytes 1179656 | tf_op jit(solution)/shard_map/ppermute | solution.py:213
  132.0 20.1 %collective-permute-start.24 = (bf16[768,256]{1,0:T(8,128)(2,1)S(1)}, bf16[768,256]{1,0:T(8,128)(2,1)S(1)}, u32[]{:S(2)}, u32[]{:S(2)}) collective-permute-start(bf16[768,256]{1,0:T(8,128)(2,1)S(1)} %collective-permute-done.22.refs_1_), channel_id=1, source_target_pairs={{0,4},{1,5},{2,6},{3,7},{4,8},{5,9},{6,10},{7,11},{8,12},{9,13},{1... | collective-permute-start | bytes 1179656 | tf_op jit(solution)/shard_map/ppermute | solution.py:213
  138.8 13.8 %collective-permute-start.26 = (bf16[768,256]{1,0:T(8,128)(2,1)S(1)}, bf16[768,256]{1,0:T(8,128)(2,1)S(1)}, u32[]{:S(2)}, u32[]{:S(2)}) collective-permute-start(bf16[768,256]{1,0:T(8,128)(2,1)S(1)} %collective-permute-done.22.refs_1_), channel_id=1, source_target_pairs={{0,12},{1,13},{2,14},{3,15},{4,0},{5,1},{6,2},{7,3},{8,4},{9,5},{1... | collective-permute-start | bytes 1179656 | tf_op jit(solution)/shard_map/ppermute | solution.py:213
  146.8 9.3 %collective-permute-start.28 = (bf16[768,256]{1,0:T(8,128)(2,1)S(1)}, bf16[768,256]{1,0:T(8,128)(2,1)S(1)}, u32[]{:S(2)}, u32[]{:S(2)}) collective-permute-start(bf16[768,256]{1,0:T(8,128)(2,1)S(1)} %collective-permute-done.27.refs_6_), channel_id=1, source_target_pairs={{0,2},{1,3},{2,0},{3,1},{4,6},{5,7},{6,4},{7,5},{8,10},{9,11},{10,... | collective-permute-start | bytes 1179656 | tf_op jit(solution)/shard_map/ppermute | solution.py:213
  148.3 7.7 %collective-permute-start.30 = (bf16[768,256]{1,0:T(8,128)(2,1)S(1)}, bf16[768,256]{1,0:T(8,128)(2,1)S(1)}, u32[]{:S(2)}, u32[]{:S(2)}) collective-permute-start(bf16[768,256]{1,0:T(8,128)(2,1)S(1)} %collective-permute-done.22.refs_1_), channel_id=1, source_target_pairs={{0,1},{1,0},{2,3},{3,2},{4,5},{5,4},{6,7},{7,6},{8,9},{9,8},{10,11... | collective-permute-start | bytes 1179656 | tf_op jit(solution)/shard_map/ppermute | solution.py:213
  148.4 8.2 %collective-permute-start.31 = (bf16[768,256]{1,0:T(8,128)(2,1)S(1)}, bf16[768,256]{1,0:T(8,128)(2,1)S(1)}, u32[]{:S(2)}, u32[]{:S(2)}) collective-permute-start(bf16[768,256]{1,0:T(8,128)(2,1)S(1)} %collective-permute-done.23.refs_2_), channel_id=1, source_target_pairs={{0,1},{1,0},{2,3},{3,2},{4,5},{5,4},{6,7},{7,6},{8,9},{9,8},{10,11... | collective-permute-start | bytes 1179656 | tf_op jit(solution)/shard_map/ppermute | solution.py:213
  152.1 6.6 %collective-permute-start.35 = (bf16[768,256]{1,0:T(8,128)(2,1)S(1)}, bf16[768,256]{1,0:T(8,128)(2,1)}, u32[]{:S(2)}, u32[]{:S(2)}) collective-permute-start(bf16[768,256]{1,0:T(8,128)(2,1)S(1)} %collective-permute-done.27.refs_6_), channel_id=1, source_target_pairs={{0,1},{1,0},{2,3},{3,2},{4,5},{5,4},{6,7},{7,6},{8,9},{9,8},{10,11... | collective-permute-start | bytes 1179656 | tf_op jit(solution)/shard_map/ppermute | solution.py:213
  174.2 20.8 %collective-permute-start.37 = (bf16[768,512]{1,0:T(8,128)(2,1)}, bf16[768,512]{1,0:T(8,128)(2,1)S(1)}, u32[]{:S(2)}, u32[]{:S(2)}) collective-permute-start(bf16[768,512]{1,0:T(8,128)(2,1)} %get-tuple-element.37), channel_id=1, source_target_pairs={{0,32},{16,48},{32,64},{48,80},{64,96},{80,112},{96,0},{112,16},{1... | collective-permute-start | bytes 2359304 | tf_op jit(solution)/shard_map/ppermute | solution.py:218
  174.7 20.4 %collective-permute-start.38 = (bf16[768,512]{1,0:T(8,128)(2,1)}, bf16[768,512]{1,0:T(8,128)(2,1)S(1)}, u32[]{:S(2)}, u32[]{:S(2)}) collective-permute-start(bf16[768,512]{1,0:T(8,128)(2,1)} %get-tuple-element.37), channel_id=1, source_target_pairs={{0,96},{16,112},{32,0},{48,16},{64,32},{80,48},{96,64},{112,80},{1... | collective-permute-start | bytes 2359304 | tf_op jit(solution)/shard_map/ppermute | solution.py:218
  177.4 21.7 %collective-permute-start.39 = (bf16[768,512]{1,0:T(8,128)(2,1)}, bf16[768,512]{1,0:T(8,128)(2,1)S(1)}, u32[]{:S(2)}, u32[]{:S(2)}) collective-permute-start(bf16[768,512]{1,0:T(8,128)(2,1)} %get-tuple-element.37), channel_id=1, source_target_pairs={{0,16},{16,0},{32,48},{48,32},{64,80},{80,64},{96,112},{112,96},{1... | collective-permute-start | bytes 2359304 | tf_op jit(solution)/shard_map/ppermute | solution.py:218
  195.0 13.3 %collective-permute-start.40 = (bf16[384,512]{1,0:T(8,128)(2,1)S(1)}, bf16[384,512]{1,0:T(8,128)(2,1)S(1)}, u32[]{:S(2)}, u32[]{:S(2)}) collective-permute-start(bf16[384,512]{1,0:T(8,128)(2,1)S(1)} %slice.100), channel_id=1, source_target_pairs={{0,32},{16,48},{32,64},{48,80},{64,96},{80,112},{96,0},{112,16},{1... | collective-permute-start | bytes 1179656 | tf_op jit(solution)/shard_map/ppermute | solution.py:218
  195.9 13.1 %collective-permute-start.41 = (bf16[384,512]{1,0:T(8,128)(2,1)}, bf16[384,512]{1,0:T(8,128)(2,1)S(1)}, u32[]{:S(2)}, u32[]{:S(2)}) collective-permute-start(bf16[384,512]{1,0:T(8,128)(2,1)} %slice.101), channel_id=1, source_target_pairs={{0,96},{16,112},{32,0},{48,16},{64,32},{80,48},{96,64},{112,80},{1... | collective-permute-start | bytes 1179656 | tf_op jit(solution)/shard_map/ppermute | solution.py:218
  199.2 24.1 %collective-permute-start.42 = (bf16[768,512]{1,0:T(8,128)(2,1)S(1)}, bf16[768,512]{1,0:T(8,128)(2,1)S(1)}, u32[]{:S(2)}, u32[]{:S(2)}) collective-permute-start(bf16[768,512]{1,0:T(8,128)(2,1)S(1)} %collective-permute-done.39), channel_id=1, source_target_pairs={{0,32},{16,48},{32,64},{48,80},{64,96},{80,112},{96,0},{112,16},{1... | collective-permute-start | bytes 2359304 | tf_op jit(solution)/shard_map/ppermute | solution.py:218
  201.2 23.0 %collective-permute-start.43 = (bf16[768,512]{1,0:T(8,128)(2,1)S(1)}, bf16[768,512]{1,0:T(8,128)(2,1)S(1)}, u32[]{:S(2)}, u32[]{:S(2)}) collective-permute-start(bf16[768,512]{1,0:T(8,128)(2,1)S(1)} %collective-permute-done.39), channel_id=1, source_target_pairs={{0,96},{16,112},{32,0},{48,16},{64,32},{80,48},{96,64},{112,80},{1... | collective-permute-start | bytes 2359304 | tf_op jit(solution)/shard_map/ppermute | solution.py:218
  209.1 16.0 %collective-permute-start.44 = (bf16[768,512]{1,0:T(8,128)(2,1)S(1)}, bf16[768,512]{1,0:T(8,128)(2,1)S(1)}, u32[]{:S(2)}, u32[]{:S(2)}) collective-permute-start(bf16[768,512]{1,0:T(8,128)(2,1)S(1)} %pad_maximum_fusion), channel_id=1, source_target_pairs={{0,16},{16,0},{32,48},{48,32},{64,80},{80,64},{96,112},{112,96},{1... | collective-permute-start | bytes 2359304 | tf_op jit(solution)/shard_map/ppermute | solution.py:218
  (41 other events, 418.2 us)
Sparse Core Ops, SparseCore 0:
  16.7 55.4 all-gather.3
  77.6 31.9 all-gather.5
  111.3 49.2 all-gather.7
